TPU v7x, 32 devices: a whole 2x2x4 slice. The times are simulated.
32 devices in a mesh: az: 4 (over x, core), curve: 8 (over z, y).
Axes of the slice: x: 2, y: 2, z: 4, core: 2. Of those that a mesh axis runs over, the one named last changes fastest.
Arguments:
- fields: float32 [2, 256, 16, 1024], P(None, 'az', None, 'curve'), may hold values from -6 to 6
- impedance: float32 [2, 256, 1024], P(None, 'az', 'curve'), may hold values from 0.25 to 1.5
- tile_data: bfloat16 [256, 8, 3, 2, 128, 128], P('az', 'curve'), may hold values from -0.21875 to 0.21875
- tile_cols: int32 [256, 8, 3], P('az', 'curve'), may hold values from 0 to 7, as said below
- tile_count: int32 [256, 8], P('az', 'curve'), may hold values from 1 to 3
Outputs:
- applied: float32 [2, 256, 16, 1024], P(None, 'az', None, 'curve')
Inputs may be any that keep to these rules, and one draw needn't show every extreme that they name: `tile_cols`: for every mode and block row the 3 entries are distinct blocks lying within one block of the row's own block along the closed curve, indices taken modulo 8; only the first tile_count entries are used.
All inputs are finite; a program needn't handle non-finite values.
Results may differ from a plain program's by a relative error of at most 0.0021.
Values may be sent and summed in bfloat16 or wider, within the bound.
No kernel may reach another device: no remote copies, remote signals or barrier semaphores. Data moves between devices by JAX's collectives and lax.ppermute only.
A program may use at most 64 MiB of HBM per device.

v0:
```python
import functools

import jax
import jax.numpy as jnp
import numpy as np
from jax import lax
from jax.experimental import pallas as pl
from jax.experimental.pallas import tpu as pltpu
from jax.sharding import PartitionSpec as P

CHUNKS = 2
FIELD_BOUND = 6.0
CODE_TOP = 32767.0
VMEM_LIMIT = 40 * 1024 * 1024


def dft_tables(parts, local, order, inverse):
    period = parts * local
    own = np.arange(local)
    tables = np.zeros((parts, 2 * local, parts * 2 * local), np.float64)
    for a in range(parts):
        rows = a * local + own
        for j in range(parts):
            cols = order(a, j) * local + own
            angle = 2.0 * np.pi / period * ((rows[:, None] * cols[None, :]) % period)
            cosine, sine = np.cos(angle), np.sin(angle)
            if inverse:
                block = np.block([[cosine, -sine], [sine, cosine]])
            else:
                block = np.block([[cosine, sine], [-sine, cosine]]) / period
            tables[a, :, j * 2 * local : (j + 1) * 2 * local] = block
    tables = tables.astype(np.float32)
    high = tables.astype(jnp.bfloat16)
    low = (tables - high.astype(np.float32)).astype(jnp.bfloat16)
    return np.stack([high, low], axis=1)


def pack_kernel(rhs, fields_ref, *coded_refs):
    rows = fields_ref.shape[0] // rhs
    per = rhs // len(coded_refs)
    for r in range(rhs):
        x = fields_ref[pl.ds(r, rows, stride=rhs), :]
        root = jnp.sqrt(jnp.sqrt(jnp.abs(x) * (1.0 / FIELD_BOUND)))
        code = jnp.round(jnp.where(x < 0, -root, root) * CODE_TOP)
        coded_refs[r // per][r % per] = code.astype(jnp.int32).astype(jnp.int16)


def decoded(code):
    t = code.astype(jnp.int32).astype(jnp.float32) * (FIELD_BOUND**0.25 / CODE_TOP)
    return (t * jnp.abs(t)) * (t * t)


def forward_kernel(sources, az_ref, table_ref, *refs):
    coded_refs, modes_ref, held = refs[:sources], refs[sources], refs[sources + 1]
    rhs, rows, nodes = coded_refs[0].shape
    for r in range(0, rhs, 2):
        total = jnp.zeros((rows, 2 * nodes), jnp.float32)
        for j in range(sources):
            x = jnp.concatenate([decoded(coded_refs[j][r]), decoded(coded_refs[j][r + 1])], axis=1)
            high = x.astype(jnp.bfloat16)
            low = (x - high.astype(jnp.float32)).astype(jnp.bfloat16)
            cols = slice(j * rows, (j + 1) * rows)
            table_high, table_low = table_ref[0, 0, :, cols], table_ref[0, 1, :, cols]
            total += jnp.dot(table_high, high, preferred_element_type=jnp.float32)
            total += jnp.dot(table_low, high, preferred_element_type=jnp.float32)
            total += jnp.dot(table_high, low, preferred_element_type=jnp.float32)
        held[r * rows : (r + 1) * rows, :] = total[:, :nodes]
        held[(r + 1) * rows : (r + 2) * rows, :] = total[:, nodes:]
    local = rows // 2
    for k in range(local):
        real = held[pl.ds(k, rhs, stride=rows), :]
        imag = held[pl.ds(local + k, rhs, stride=rows), :]
        modes_ref[k] = jnp.concatenate([real, imag], axis=0).astype(jnp.bfloat16)


def near_kernel(pick_ref, tiles_ref, own_ref, side_ref, far_ref, near_ref, held):
    group, slots = tiles_ref.shape[0], tiles_ref.shape[2]
    block = tiles_ref.shape[-1]
    both = own_ref.shape[1]
    rhs = both // 2
    first = pl.program_id(0) * group
    for k in range(group):
        own, side, far = own_ref[k], side_ref[k], far_ref[k]
        values, tiles = [], []
        for t in range(slots):
            pick = pick_ref[(first + k) * slots + t]
            value = jnp.where(pick == 0, own, jnp.where(pick == 1, side, far))
            values.append(jnp.where(pick < 0, jnp.zeros_like(value), value))
            tiles.append(tiles_ref[k, 0, t].reshape(2 * block, block))
        product = lax.dot_general(
            jnp.concatenate(values, axis=1),
            jnp.concatenate(tiles, axis=1),
            (((1,), (1,)), ((), ())),
            preferred_element_type=jnp.float32,
        )
        held[k * both : k * both + rhs, :] = product[:rhs, :block] - product[rhs:, block:]
        held[k * both + rhs : (k + 1) * both, :] = product[rhs:, :block] + product[:rhs, block:]
    for r in range(rhs):
        for part in range(2):
            near_ref[r, part] = held[pl.ds(part * rhs + r, group, stride=both), :].astype(jnp.bfloat16)


def back_kernel(sources, rhs, az_ref, table_ref, fields_ref, impedance_ref, *refs):
    near_refs, out_ref = refs[:-1], refs[-1]
    per, _, local, nodes = near_refs[0].shape
    rows = 2 * local
    z_real, z_imag = impedance_ref[:local], impedance_ref[local:]
    for r in range(0, rhs, 2):
        total = jnp.zeros((rows, 2 * nodes), jnp.float32)
        for j in range(sources):
            source = near_refs[(r // per) * sources + j]
            x = jnp.concatenate(
                [source[r % per].reshape(rows, nodes), source[r % per + 1].reshape(rows, nodes)], axis=1
            )
            cols = slice(j * rows, (j + 1) * rows)
            total += jnp.dot(table_ref[0, 0, :, cols], x, preferred_element_type=jnp.float32)
            total += jnp.dot(table_ref[0, 1, :, cols], x, preferred_element_type=jnp.float32)
        for s in range(2):
            real, imag = total[:local, s * nodes : (s + 1) * nodes], total[local:, s * nodes : (s + 1) * nodes]
            at_real = pl.ds(r + s, local, stride=rhs)
            at_imag = pl.ds(local * rhs + r + s, local, stride=rhs)
            out_ref[at_real, :] = fields_ref[at_real, :] + z_real * real - z_imag * imag
            out_ref[at_imag, :] = fields_ref[at_imag, :] + z_real * imag + z_imag * real


def whole(x):
    return pl.BlockSpec(x.shape, lambda i, *s: (0,) * len(x.shape))


def table_spec(table):
    return pl.BlockSpec((1,) + table.shape[1:], lambda i, az: (az[0], 0, 0, 0))


def shared(x, parts):
    if parts == 4:
        peer = [(i, i ^ 1) for i in range(4)]
        across = [(i, i ^ 2) for i in range(4)]
        far = lax.ppermute(x, "az", across)
        near = lax.ppermute(x, "az", peer)
        return [x, near, far, lax.ppermute(far, "az", peer)]
    every = lax.all_gather(x, "az")
    return [every[j] for j in range(parts)]


def on_device(parts, ring, fields, impedance, tile_data, tile_cols, tile_count):
    _, local, rhs, nodes = fields.shape
    per = rhs // CHUNKS
    slots, block = tile_data.shape[2], tile_data.shape[-1]
    rows = 2 * local
    order = (lambda a, j: a ^ j) if parts == 4 else (lambda a, j: j)
    az = lax.axis_index("az").astype(jnp.int32)[None]
    place = lax.axis_index("curve")
    forward_table = jnp.asarray(dft_tables(parts, local, order, False))
    back_table = jnp.asarray(dft_tables(parts, local, order, True))
    flat_fields = fields.reshape(rows * rhs, nodes)
    params = pltpu.CompilerParams(vmem_limit_bytes=VMEM_LIMIT)

    even = jnp.mod(place, 2) == 0
    step = jnp.mod(tile_cols[:, 0, :] - place, ring)
    live = jnp.arange(slots, dtype=jnp.int32)[None, :] < tile_count
    pick = jnp.where(step == 0, 0, jnp.where((step == 1) == even, 1, 2))
    pick = jnp.where(live, pick, -1).astype(jnp.int32).reshape(-1)

    coded = pl.pallas_call(
        functools.partial(pack_kernel, rhs),
        out_shape=[jax.ShapeDtypeStruct((per, rows, nodes), jnp.int16)] * CHUNKS,
        compiler_params=params,
        name="pack",
    )(flat_fields)

    sides = [(i, i ^ 1) for i in range(ring)]
    onward = [(i, (i + 2 if i % 2 == 0 else i - 2) % ring) for i in range(ring)]
    group = min(16, local)
    near_all = []
    for chunk in coded:
        everyone = shared(chunk, parts)
        modes_shape = jax.ShapeDtypeStruct((local, 2 * per, nodes), jnp.bfloat16)
        own = pl.pallas_call(
            functools.partial(forward_kernel, parts),
            out_shape=modes_shape,
            grid_spec=pltpu.PrefetchScalarGridSpec(
                num_scalar_prefetch=1,
                grid=(1,),
                in_specs=[table_spec(forward_table)] + [whole(x) for x in everyone],
                out_specs=whole(modes_shape),
                scratch_shapes=[pltpu.VMEM((per * rows, nodes), jnp.float32)],
            ),
            compiler_params=params,
            name="forward",
        )(az, forward_table, *everyone)
        side = lax.ppermute(own, "curve", sides)
        far = lax.ppermute(side, "curve", onward)
        some_modes = pl.BlockSpec((group, 2 * per, nodes), lambda i, s: (i, 0, 0))
        near = pl.pallas_call(
            near_kernel,
            out_shape=jax.ShapeDtypeStruct((per, 2, local, nodes), jnp.bfloat16),
            grid_spec=pltpu.PrefetchScalarGridSpec(
                num_scalar_prefetch=1,
                grid=(local // group,),
                in_specs=[
                    pl.BlockSpec((group, 1, slots, 2, block, block), lambda i, s: (i, 0, 0, 0, 0, 0)),
                    some_modes,
                    some_modes,
                    some_modes,
                ],
                out_specs=pl.BlockSpec((per, 2, group, nodes), lambda i, s: (0, 0, i, 0)),
                scratch_shapes=[pltpu.VMEM((group * 2 * per, nodes), jnp.float32)],
            ),
            compiler_params=params,
            name="near",
        )(pick, tile_data, own, side, far)
        near_all += shared(near, parts)

    flat_impedance = impedance.reshape(rows, nodes)
    out_shape = jax.ShapeDtypeStruct(flat_fields.shape, jnp.float32)
    out = pl.pallas_call(
        functools.partial(back_kernel, parts, rhs),
        out_shape=out_shape,
        grid_spec=pltpu.PrefetchScalarGridSpec(
            num_scalar_prefetch=1,
            grid=(1,),
            in_specs=[table_spec(back_table), whole(flat_fields), whole(flat_impedance)]
            + [whole(x) for x in near_all],
            out_specs=whole(out_shape),
        ),
        compiler_params=params,
        name="back",
    )(az, back_table, flat_fields, flat_impedance, *near_all)
    return out.reshape(fields.shape)


def solution(mesh):
    placed = (
        P(None, "az", None, "curve"),
        P(None, "az", "curve"),
        P("az", "curve", None, None, None, None),
        P("az", "curve", None),
        P("az", "curve"),
    )
    return jax.shard_map(
        functools.partial(on_device, mesh.shape["az"], mesh.shape["curve"]),
        mesh=mesh,
        in_specs=placed,
        out_specs=P(None, "az", None, "curve"),
        check_vma=False,
    )
```

profile of v0, /device:TPU:0, one launch (start us, length us, event | category | flops | bytes accessed | tf_op | source)
XLA Modules:
  0.0 68.7 jit_solution(11676160261462609412)
XLA Ops:
  0.0 0.0 copy-start.3
  0.0 1.2 %copy-done.3 = f32[2,64,16,128]{3,2,1,0:T(8,128)S(1)} copy-done((f32[2,64,16,128]{3,2,1,0:T(8,128)S(1)}, f32[2,64,16,128]{3,2,1,0:T(8,128)}, u32[]{:S(2)}) %copy-start.3) | copy-done | bytes 1048600
  1.2 0.9 %pack.1 = (s16[8,128,128]{2,1,0:T(8,128)(2,1)S(1)}, s16[8,128,128]{2,1,0:T(8,128)(2,1)S(1)}) custom-call(f32[2048,128]{1,0:T(8,128)S(1)} %bitcast.7), custom_call_target="tpu_custom_call" | custom-call | tf_op jit(solution)/shard_map/pack/pallas_call | solution.py:164
  2.1 3.0 %collective-permute-start.1 = (s16[8,128,128]{2,1,0:T(8,128)(2,1)S(1)}, s16[8,128,128]{2,1,0:T(8,128)(2,1)S(1)}, u32[]{:S(2)}, u32[]{:S(2)}) collective-permute-start(s16[8,128,128]{2,1,0:T(8,128)(2,1)S(1)} %get-tuple-element.7.refs_0_), channel_id=1, source_target_pairs={{0,16},{8,24},{16,0},{24,8},{1,17},{9,25},{17,1},{25,9},{2,18},{10... | collective-permute-start | bytes 786440 | tf_op jit(solution)/shard_map/ppermute | solution.py:138
  5.1 0.1 collective-permute-start.9
  5.2 0.0 collective-permute-start
  5.2 7.1 %collective-permute-done.1.refs_2_ = s16[8,128,128]{2,1,0:T(8,128)(2,1)S(1)} collective-permute-done((s16[8,128,128]{2,1,0:T(8,128)(2,1)S(1)}, s16[8,128,128]{2,1,0:T(8,128)(2,1)S(1)}, u32[]{:S(2)}, u32[]{:S(2)}) %collective-permute-start.1) | collective-permute-done | bytes 262176 | tf_op jit(solution)/shard_map/ppermute | solution.py:138
  12.2 0.0 collective-permute-start.2
  12.2 0.5 collective-permute-start.8
  12.7 4.3 %collective-permute-done.9.refs_2_ = s16[8,128,128]{2,1,0:T(8,128)(2,1)S(1)} collective-permute-done((s16[8,128,128]{2,1,0:T(8,128)(2,1)S(1)}, s16[8,128,128]{2,1,0:T(8,128)(2,1)S(1)}, u32[]{:S(2)}, u32[]{:S(2)}) %collective-permute-start.9) | collective-permute-done | bytes 262176 | tf_op jit(solution)/shard_map/ppermute | solution.py:138
  17.0 0.0 collective-permute-start.10
  17.0 0.0 collective-permute-done.refs_1_
  17.0 0.0 collective-permute-done.2.refs_3_
  17.0 0.0 copy-start.2
  17.0 1.2 %copy-done.2 = bf16[4,2,128,512]{3,2,1,0:T(8,128)(2,1)S(1)} copy-done((bf16[4,2,128,512]{3,2,1,0:T(8,128)(2,1)S(1)}, bf16[4,2,128,512]{3,2,1,0:T(8,128)(2,1)}, u32[]{:S(2)}) %copy-start.2) | copy-done | bytes 1048600
  18.3 1.4 %forward.2.own_ref = bf16[64,16,128]{2,1,0:T(8,128)(2,1)S(1)} custom-call(s32[1]{0:T(128)} %bitcast.az_ref, bf16[4,2,128,512]{3,2,1,0:T(8,128)(2,1)S(1)} %copy-done.2, s16[8,128,128]{2,1,0:T(8,128)(2,1)S(1)} %get-tuple-element.7.refs_0_, s16[8,128,128]{2,1,0:T(8,128)(2,1)S(1)} %collective-permute-done.refs_1_, ...), custom_call_target="tpu_custom_call" | custom-call | tf_op jit(solution)/shard_map/forward/pallas_call | solution.py:178
  19.6 1.8 %collective-permute-start.3 = (bf16[64,16,128]{2,1,0:T(8,128)(2,1)S(1)}, bf16[64,16,128]{2,1,0:T(8,128)(2,1)S(1)}, u32[]{:S(2)}, u32[]{:S(2)}) collective-permute-start(bf16[64,16,128]{2,1,0:T(8,128)(2,1)S(1)} %forward.2.own_ref), channel_id=1, source_target_pairs={{0,1},{1,0},{2,3},{3,2},{4,5},{5,4},{6,7},{7,6},{8,9},{9,8},{10,11... | collective-permute-start | bytes 786440 | tf_op jit(solution)/shard_map/ppermute | solution.py:191
  21.5 0.0 collective-permute-done.8.refs_1_
  21.5 0.0 collective-permute-done.10.refs_3_
  21.5 1.4 %forward.3.own_ref = bf16[64,16,128]{2,1,0:T(8,128)(2,1)S(1)} custom-call(s32[1]{0:T(128)} %bitcast.az_ref, bf16[4,2,128,512]{3,2,1,0:T(8,128)(2,1)S(1)} %copy-done.2, s16[8,128,128]{2,1,0:T(8,128)(2,1)S(1)} %get-tuple-element.8.refs_0_, s16[8,128,128]{2,1,0:T(8,128)(2,1)S(1)} %collective-permute-done.8.refs_1_, ...), custom_call_target="tpu_custom_call" | custom-call | tf_op jit(solution)/shard_map/forward/pallas_call | solution.py:178
  22.8 0.3 collective-permute-start.11
  23.2 0.7 %iota_compare_fusion = pred[64,3]{1,0:T(8,128)(4,1)S(1)} fusion(s32[64]{0:T(128)} %bitcast.10), kind=kLoop, calls=%fused_computation | loop fusion | flops 192 | bytes 448 | tf_op jit(solution)/shard_map/lt | solution.py:160
  23.9 4.9 %collective-permute-done.3.side_ref = bf16[64,16,128]{2,1,0:T(8,128)(2,1)S(1)} collective-permute-done((bf16[64,16,128]{2,1,0:T(8,128)(2,1)S(1)}, bf16[64,16,128]{2,1,0:T(8,128)(2,1)S(1)}, u32[]{:S(2)}, u32[]{:S(2)}) %collective-permute-start.3) | collective-permute-done | bytes 262176 | tf_op jit(solution)/shard_map/ppermute | solution.py:191
  28.8 1.8 %collective-permute-start.4 = (bf16[64,16,128]{2,1,0:T(8,128)(2,1)S(1)}, bf16[64,16,128]{2,1,0:T(8,128)(2,1)S(1)}, u32[]{:S(2)}, u32[]{:S(2)}) collective-permute-start(bf16[64,16,128]{2,1,0:T(8,128)(2,1)S(1)} %collective-permute-done.3.side_ref), channel_id=1, source_target_pairs={{0,2},{1,7},{2,4},{3,1},{4,6},{5,3},{6,0},{7,5},{8,10},{9,15},{10,... | collective-permute-start | bytes 786440 | tf_op jit(solution)/shard_map/ppermute | solution.py:192
  30.6 3.4 %collective-permute-done.11.side_ref = bf16[64,16,128]{2,1,0:T(8,128)(2,1)S(1)} collective-permute-done((bf16[64,16,128]{2,1,0:T(8,128)(2,1)S(1)}, bf16[64,16,128]{2,1,0:T(8,128)(2,1)S(1)}, u32[]{:S(2)}, u32[]{:S(2)}) %collective-permute-start.11) | collective-permute-done | bytes 262176 | tf_op jit(solution)/shard_map/ppermute | solution.py:191
  34.0 1.8 %collective-permute-start.12 = (bf16[64,16,128]{2,1,0:T(8,128)(2,1)S(1)}, bf16[64,16,128]{2,1,0:T(8,128)(2,1)S(1)}, u32[]{:S(2)}, u32[]{:S(2)}) collective-permute-start(bf16[64,16,128]{2,1,0:T(8,128)(2,1)S(1)} %collective-permute-done.11.side_ref), channel_id=1, source_target_pairs={{0,2},{1,7},{2,4},{3,1},{4,6},{5,3},{6,0},{7,5},{8,10},{9,15},{10,... | collective-permute-start | bytes 786440 | tf_op jit(solution)/shard_map/ppermute | solution.py:192
  35.8 0.7 broadcast_subtract_fusion
  36.5 0.1 lt.35
  36.7 0.1 copy.8
  36.8 0.1 sub.12
  36.9 1.5 %collective-permute-done.4.far_ref = bf16[64,16,128]{2,1,0:T(8,128)(2,1)S(1)} collective-permute-done((bf16[64,16,128]{2,1,0:T(8,128)(2,1)S(1)}, bf16[64,16,128]{2,1,0:T(8,128)(2,1)S(1)}, u32[]{:S(2)}, u32[]{:S(2)}) %collective-permute-start.4) | collective-permute-done | bytes 262176 | tf_op jit(solution)/shard_map/ppermute | solution.py:192
  38.4 0.0 copy-start
  38.4 4.6 %copy-done = bf16[64,1,3,2,128,128]{5,4,3,2,1,0:T(8,128)(2,1)S(1)} copy-done((bf16[64,1,3,2,128,128]{5,4,3,2,1,0:T(8,128)(2,1)S(1)}, bf16[64,1,3,2,128,128]{5,4,3,2,1,0:T(8,128)(2,1)}, u32[]{:S(2)}) %copy-start) | copy-done | bytes 12582936
  43.0 0.0 copy-start.4
  43.0 0.0 copy-start.5
  43.0 0.0 copy-start.6
  43.0 4.4 %near.2.refs_0_ = bf16[8,2,64,128]{3,2,1,0:T(8,128)(2,1)S(1)} custom-call(s32[192]{0:T(256)S(1)} %fusion.pick_ref, bf16[64,1,3,2,128,128]{5,4,3,2,1,0:T(8,128)(2,1)S(1)} %copy-done, bf16[64,16,128]{2,1,0:T(8,128)(2,1)S(1)} %forward.2.own_ref, bf16[64,16,128]{2,1,0:T(8,128)(2,1)S(1)} %collective-permute-done.3.side_ref, ...), custom_call_target="tpu_custom_call" | custom-call | tf_op jit(solution)/shard_map/near/pallas_call | solution.py:194
  47.4 1.6 %collective-permute-start.6 = (bf16[8,2,64,128]{3,2,1,0:T(8,128)(2,1)S(1)}, bf16[8,2,64,128]{3,2,1,0:T(8,128)(2,1)S(1)}, u32[]{:S(2)}, u32[]{:S(2)}) collective-permute-start(bf16[8,2,64,128]{3,2,1,0:T(8,128)(2,1)S(1)} %near.2.refs_0_), channel_id=1, source_target_pairs={{0,16},{8,24},{16,0},{24,8},{1,17},{9,25},{17,1},{25,9},{2,18},{10... | collective-permute-start | bytes 786440 | tf_op jit(solution)/shard_map/ppermute | solution.py:138
  49.0 0.0 collective-permute-done.12.far_ref
  49.0 0.0 copy-start.1
  49.0 4.6 %copy-done.1 = bf16[64,1,3,2,128,128]{5,4,3,2,1,0:T(8,128)(2,1)S(1)} copy-done((bf16[64,1,3,2,128,128]{5,4,3,2,1,0:T(8,128)(2,1)S(1)}, bf16[64,1,3,2,128,128]{5,4,3,2,1,0:T(8,128)(2,1)}, u32[]{:S(2)}) %copy-start.1) | copy-done | bytes 12582936
  53.6 4.4 %near.3.refs_4_ = bf16[8,2,64,128]{3,2,1,0:T(8,128)(2,1)S(1)} custom-call(s32[192]{0:T(256)S(1)} %fusion.pick_ref, bf16[64,1,3,2,128,128]{5,4,3,2,1,0:T(8,128)(2,1)S(1)} %copy-done.1, bf16[64,16,128]{2,1,0:T(8,128)(2,1)S(1)} %forward.3.own_ref, bf16[64,16,128]{2,1,0:T(8,128)(2,1)S(1)} %collective-permute-done.11.side_ref, ...), custom_call_target="tpu_custom_call" | custom-call | tf_op jit(solution)/shard_map/near/pallas_call | solution.py:194
  58.0 0.6 collective-permute-start.14
  58.6 0.0 collective-permute-start.5
  58.6 0.5 collective-permute-start.13
  59.1 0.0 collective-permute-done.6.refs_2_
  59.1 0.0 collective-permute-start.7
  59.1 5.3 %collective-permute-done.14.refs_6_ = bf16[8,2,64,128]{3,2,1,0:T(8,128)(2,1)S(1)} collective-permute-done((bf16[8,2,64,128]{3,2,1,0:T(8,128)(2,1)S(1)}, bf16[8,2,64,128]{3,2,1,0:T(8,128)(2,1)S(1)}, u32[]{:S(2)}, u32[]{:S(2)}) %collective-permute-start.14) | collective-permute-done | bytes 262176 | tf_op jit(solution)/shard_map/ppermute | solution.py:138
  64.5 0.0 collective-permute-start.15
  64.5 0.0 collective-permute-done.5.refs_1_
  64.5 0.0 collective-permute-done.13.refs_5_
  64.5 0.0 collective-permute-done.7.refs_3_
  64.5 1.5 %collective-permute-done.15.refs_7_ = bf16[8,2,64,128]{3,2,1,0:T(8,128)(2,1)S(1)} collective-permute-done((bf16[8,2,64,128]{3,2,1,0:T(8,128)(2,1)S(1)}, bf16[8,2,64,128]{3,2,1,0:T(8,128)(2,1)S(1)}, u32[]{:S(2)}, u32[]{:S(2)}) %collective-permute-start.15) | collective-permute-done | bytes 262176 | tf_op jit(solution)/shard_map/ppermute | solution.py:140
  66.0 0.0 copy-done.4
  66.0 0.0 copy-done.5
  66.0 0.0 copy-done.6
  66.0 2.7 %back.1 = f32[2048,128]{1,0:T(8,128)} custom-call(s32[1]{0:T(128)} %bitcast.az_ref, bf16[4,2,128,512]{3,2,1,0:T(8,128)(2,1)S(1)} %copy-done.5, f32[2048,128]{1,0:T(8,128)S(1)} %bitcast.8, f32[128,128]{1,0:T(8,128)S(1)} %bitcast.9, bf16[8,2,64,128]{3,2,1,0:T(8,128)(2,1)S(1)} %near.2.refs_0_, bf16[8,2,64,128]{3,2,1,0:T(8,128)(2,1)S(1)} %collective-permute-done.5.refs_1_, ...), custom_call_target="tpu_custom_call" | custom-call | tf_op jit(solution)/shard_map/back/pallas_call | solution.py:216
  (1 shorter events, 0.0 us)
Async XLA Ops:
  0.0 1.2 %copy-start.3 = (f32[2,64,16,128]{3,2,1,0:T(8,128)S(1)}, f32[2,64,16,128]{3,2,1,0:T(8,128)}, u32[]{:S(2)}) copy-start(f32[2,64,16,128]{3,2,1,0:T(8,128)} %param.7) | copy-start | bytes 3145732
  2.1 10.1 %collective-permute-start.1 = (s16[8,128,128]{2,1,0:T(8,128)(2,1)S(1)}, s16[8,128,128]{2,1,0:T(8,128)(2,1)S(1)}, u32[]{:S(2)}, u32[]{:S(2)}) collective-permute-start(s16[8,128,128]{2,1,0:T(8,128)(2,1)S(1)} %get-tuple-element.7.refs_0_), channel_id=1, source_target_pairs={{0,16},{8,24},{16,0},{24,8},{1,17},{9,25},{17,1},{25,9},{2,18},{10... | collective-permute-start | bytes 786440 | tf_op jit(solution)/shard_map/ppermute | solution.py:138
  5.1 11.9 %collective-permute-start.9 = (s16[8,128,128]{2,1,0:T(8,128)(2,1)S(1)}, s16[8,128,128]{2,1,0:T(8,128)(2,1)S(1)}, u32[]{:S(2)}, u32[]{:S(2)}) collective-permute-start(s16[8,128,128]{2,1,0:T(8,128)(2,1)S(1)} %get-tuple-element.8.refs_0_), channel_id=1, source_target_pairs={{0,16},{8,24},{16,0},{24,8},{1,17},{9,25},{17,1},{25,9},{2,18},{10... | collective-permute-start | bytes 786440 | tf_op jit(solution)/shard_map/ppermute | solution.py:138
  5.2 11.9 %collective-permute-start = (s16[8,128,128]{2,1,0:T(8,128)(2,1)S(1)}, s16[8,128,128]{2,1,0:T(8,128)(2,1)S(1)}, u32[]{:S(2)}, u32[]{:S(2)}) collective-permute-start(s16[8,128,128]{2,1,0:T(8,128)(2,1)S(1)} %get-tuple-element.7.refs_0_), channel_id=1, source_target_pairs={{0,8},{8,0},{16,24},{24,16},{1,9},{9,1},{17,25},{25,17},{2,10},{10... | collective-permute-start | bytes 786440 | tf_op jit(solution)/shard_map/ppermute | solution.py:139
  12.2 4.8 %collective-permute-start.2 = (s16[8,128,128]{2,1,0:T(8,128)(2,1)S(1)}, s16[8,128,128]{2,1,0:T(8,128)(2,1)S(1)}, u32[]{:S(2)}, u32[]{:S(2)}) collective-permute-start(s16[8,128,128]{2,1,0:T(8,128)(2,1)S(1)} %collective-permute-done.1.refs_2_), channel_id=1, source_target_pairs={{0,8},{8,0},{16,24},{24,16},{1,9},{9,1},{17,25},{25,17},{2,10},{10... | collective-permute-start | bytes 786440 | tf_op jit(solution)/shard_map/ppermute | solution.py:140
  12.2 9.2 %collective-permute-start.8 = (s16[8,128,128]{2,1,0:T(8,128)(2,1)S(1)}, s16[8,128,128]{2,1,0:T(8,128)(2,1)S(1)}, u32[]{:S(2)}, u32[]{:S(2)}) collective-permute-start(s16[8,128,128]{2,1,0:T(8,128)(2,1)S(1)} %get-tuple-element.8.refs_0_), channel_id=1, source_target_pairs={{0,8},{8,0},{16,24},{24,16},{1,9},{9,1},{17,25},{25,17},{2,10},{10... | collective-permute-start | bytes 786440 | tf_op jit(solution)/shard_map/ppermute | solution.py:139
  17.0 4.4 %collective-permute-start.10 = (s16[8,128,128]{2,1,0:T(8,128)(2,1)S(1)}, s16[8,128,128]{2,1,0:T(8,128)(2,1)S(1)}, u32[]{:S(2)}, u32[]{:S(2)}) collective-permute-start(s16[8,128,128]{2,1,0:T(8,128)(2,1)S(1)} %collective-permute-done.9.refs_2_), channel_id=1, source_target_pairs={{0,8},{8,0},{16,24},{24,16},{1,9},{9,1},{17,25},{25,17},{2,10},{10... | collective-permute-start | bytes 786440 | tf_op jit(solution)/shard_map/ppermute | solution.py:140
  17.0 1.2 %copy-start.2 = (bf16[4,2,128,512]{3,2,1,0:T(8,128)(2,1)S(1)}, bf16[4,2,128,512]{3,2,1,0:T(8,128)(2,1)}, u32[]{:S(2)}) copy-start(bf16[4,2,128,512]{3,2,1,0:T(8,128)(2,1)} %constant.45.clone.table_ref) | copy-start | bytes 3145732
  19.6 9.2 %collective-permute-start.3 = (bf16[64,16,128]{2,1,0:T(8,128)(2,1)S(1)}, bf16[64,16,128]{2,1,0:T(8,128)(2,1)S(1)}, u32[]{:S(2)}, u32[]{:S(2)}) collective-permute-start(bf16[64,16,128]{2,1,0:T(8,128)(2,1)S(1)} %forward.2.own_ref), channel_id=1, source_target_pairs={{0,1},{1,0},{2,3},{3,2},{4,5},{5,4},{6,7},{7,6},{8,9},{9,8},{10,11... | collective-permute-start | bytes 786440 | tf_op jit(solution)/shard_map/ppermute | solution.py:191
  22.8 11.2 %collective-permute-start.11 = (bf16[64,16,128]{2,1,0:T(8,128)(2,1)S(1)}, bf16[64,16,128]{2,1,0:T(8,128)(2,1)S(1)}, u32[]{:S(2)}, u32[]{:S(2)}) collective-permute-start(bf16[64,16,128]{2,1,0:T(8,128)(2,1)S(1)} %forward.3.own_ref), channel_id=1, source_target_pairs={{0,1},{1,0},{2,3},{3,2},{4,5},{5,4},{6,7},{7,6},{8,9},{9,8},{10,11... | collective-permute-start | bytes 786440 | tf_op jit(solution)/shard_map/ppermute | solution.py:191
  28.8 9.7 %collective-permute-start.4 = (bf16[64,16,128]{2,1,0:T(8,128)(2,1)S(1)}, bf16[64,16,128]{2,1,0:T(8,128)(2,1)S(1)}, u32[]{:S(2)}, u32[]{:S(2)}) collective-permute-start(bf16[64,16,128]{2,1,0:T(8,128)(2,1)S(1)} %collective-permute-done.3.side_ref), channel_id=1, source_target_pairs={{0,2},{1,7},{2,4},{3,1},{4,6},{5,3},{6,0},{7,5},{8,10},{9,15},{10,... | collective-permute-start | bytes 786440 | tf_op jit(solution)/shard_map/ppermute | solution.py:192
  34.0 15.0 %collective-permute-start.12 = (bf16[64,16,128]{2,1,0:T(8,128)(2,1)S(1)}, bf16[64,16,128]{2,1,0:T(8,128)(2,1)S(1)}, u32[]{:S(2)}, u32[]{:S(2)}) collective-permute-start(bf16[64,16,128]{2,1,0:T(8,128)(2,1)S(1)} %collective-permute-done.11.side_ref), channel_id=1, source_target_pairs={{0,2},{1,7},{2,4},{3,1},{4,6},{5,3},{6,0},{7,5},{8,10},{9,15},{10,... | collective-permute-start | bytes 786440 | tf_op jit(solution)/shard_map/ppermute | solution.py:192
  38.4 4.6 %copy-start = (bf16[64,1,3,2,128,128]{5,4,3,2,1,0:T(8,128)(2,1)S(1)}, bf16[64,1,3,2,128,128]{5,4,3,2,1,0:T(8,128)(2,1)}, u32[]{:S(2)}) copy-start(bf16[64,1,3,2,128,128]{5,4,3,2,1,0:T(8,128)(2,1)} %tiles_ref.3) | copy-start | bytes 37748740
  43.0 23.0 %copy-start.4 = (f32[2,64,16,128]{3,2,1,0:T(8,128)S(1)}, f32[2,64,16,128]{3,2,1,0:T(8,128)}, u32[]{:S(2)}) copy-start(f32[2,64,16,128]{3,2,1,0:T(8,128)} %param.7) | copy-start | bytes 3145732
  43.0 23.0 %copy-start.5 = (bf16[4,2,128,512]{3,2,1,0:T(8,128)(2,1)S(1)}, bf16[4,2,128,512]{3,2,1,0:T(8,128)(2,1)}, u32[]{:S(2)}) copy-start(bf16[4,2,128,512]{3,2,1,0:T(8,128)(2,1)} %constant.46.clone.table_ref) | copy-start | bytes 3145732
  43.0 23.0 %copy-start.6 = (f32[2,64,128]{2,1,0:T(8,128)S(1)}, f32[2,64,128]{2,1,0:T(8,128)}, u32[]{:S(2)}) copy-start(f32[2,64,128]{2,1,0:T(8,128)} %param.8) | copy-start | bytes 196612
  47.4 11.7 %collective-permute-start.6 = (bf16[8,2,64,128]{3,2,1,0:T(8,128)(2,1)S(1)}, bf16[8,2,64,128]{3,2,1,0:T(8,128)(2,1)S(1)}, u32[]{:S(2)}, u32[]{:S(2)}) collective-permute-start(bf16[8,2,64,128]{3,2,1,0:T(8,128)(2,1)S(1)} %near.2.refs_0_), channel_id=1, source_target_pairs={{0,16},{8,24},{16,0},{24,8},{1,17},{9,25},{17,1},{25,9},{2,18},{10... | collective-permute-start | bytes 786440 | tf_op jit(solution)/shard_map/ppermute | solution.py:138
  49.0 4.6 %copy-start.1 = (bf16[64,1,3,2,128,128]{5,4,3,2,1,0:T(8,128)(2,1)S(1)}, bf16[64,1,3,2,128,128]{5,4,3,2,1,0:T(8,128)(2,1)}, u32[]{:S(2)}) copy-start(bf16[64,1,3,2,128,128]{5,4,3,2,1,0:T(8,128)(2,1)} %tiles_ref.3) | copy-start | bytes 37748740
  58.0 6.5 %collective-permute-start.14 = (bf16[8,2,64,128]{3,2,1,0:T(8,128)(2,1)S(1)}, bf16[8,2,64,128]{3,2,1,0:T(8,128)(2,1)S(1)}, u32[]{:S(2)}, u32[]{:S(2)}) collective-permute-start(bf16[8,2,64,128]{3,2,1,0:T(8,128)(2,1)S(1)} %near.3.refs_4_), channel_id=1, source_target_pairs={{0,16},{8,24},{16,0},{24,8},{1,17},{9,25},{17,1},{25,9},{2,18},{10... | collective-permute-start | bytes 786440 | tf_op jit(solution)/shard_map/ppermute | solution.py:138
  58.6 5.9 %collective-permute-start.5 = (bf16[8,2,64,128]{3,2,1,0:T(8,128)(2,1)S(1)}, bf16[8,2,64,128]{3,2,1,0:T(8,128)(2,1)S(1)}, u32[]{:S(2)}, u32[]{:S(2)}) collective-permute-start(bf16[8,2,64,128]{3,2,1,0:T(8,128)(2,1)S(1)} %near.2.refs_0_), channel_id=1, source_target_pairs={{0,8},{8,0},{16,24},{24,16},{1,9},{9,1},{17,25},{25,17},{2,10},{10... | collective-permute-start | bytes 786440 | tf_op jit(solution)/shard_map/ppermute | solution.py:139
  58.6 5.9 %collective-permute-start.13 = (bf16[8,2,64,128]{3,2,1,0:T(8,128)(2,1)S(1)}, bf16[8,2,64,128]{3,2,1,0:T(8,128)(2,1)S(1)}, u32[]{:S(2)}, u32[]{:S(2)}) collective-permute-start(bf16[8,2,64,128]{3,2,1,0:T(8,128)(2,1)S(1)} %near.3.refs_4_), channel_id=1, source_target_pairs={{0,8},{8,0},{16,24},{24,16},{1,9},{9,1},{17,25},{25,17},{2,10},{10... | collective-permute-start | bytes 786440 | tf_op jit(solution)/shard_map/ppermute | solution.py:139
  59.1 5.4 %collective-permute-start.7 = (bf16[8,2,64,128]{3,2,1,0:T(8,128)(2,1)S(1)}, bf16[8,2,64,128]{3,2,1,0:T(8,128)(2,1)S(1)}, u32[]{:S(2)}, u32[]{:S(2)}) collective-permute-start(bf16[8,2,64,128]{3,2,1,0:T(8,128)(2,1)S(1)} %collective-permute-done.6.refs_2_), channel_id=1, source_target_pairs={{0,8},{8,0},{16,24},{24,16},{1,9},{9,1},{17,25},{25,17},{2,10},{10... | collective-permute-start | bytes 786440 | tf_op jit(solution)/shard_map/ppermute | solution.py:140
  64.5 1.5 %collective-permute-start.15 = (bf16[8,2,64,128]{3,2,1,0:T(8,128)(2,1)S(1)}, bf16[8,2,64,128]{3,2,1,0:T(8,128)(2,1)S(1)}, u32[]{:S(2)}, u32[]{:S(2)}) collective-permute-start(bf16[8,2,64,128]{3,2,1,0:T(8,128)(2,1)S(1)} %collective-permute-done.14.refs_6_), channel_id=1, source_target_pairs={{0,8},{8,0},{16,24},{24,16},{1,9},{9,1},{17,25},{25,17},{2,10},{10... | collective-permute-start | bytes 786440 | tf_op jit(solution)/shard_map/ppermute | solution.py:140
where the time goes:
time: 69.3 us; the launch traced here: 68.7 us
  waiting for transfers between devices  28.1 us (41%)
  Pallas kernels  15.1 us (22%)
  starting transfers between devices  12.1 us (17%)
  local copies, waits for them, and re-layouts  12 us (17%)
  other arithmetic  1.42 us (2%)
    ppermute x4, waiting for transfers between devices, shared(): far = lax.ppermute(x, 'az', across)  16.7 us
    unnamed x14, local copies, waits for them, and re-layouts  11.6 us
    pallas_call x2, Pallas kernels, on_device(): pl.pallas_call(near_kernel, out_shape=jax.ShapeDtypeStruct((per, 2, local...  8.82 us
    ppermute x2, waiting for transfers between devices, on_device(): side = lax.ppermute(own, 'curve', sides)  8.33 us
    ppermute x4, starting transfers between devices, shared(): far = lax.ppermute(x, 'az', across)  5.24 us
    ppermute x2, starting transfers between devices, on_device(): far = lax.ppermute(side, 'curve', onward)  3.62 us
    pallas_call x2, Pallas kernels, on_device(): pl.pallas_call(functools.partial(forward_kernel, parts), out_shape=modes_...  2.71 us
    pallas_call x1, Pallas kernels, on_device(): pl.pallas_call(functools.partial(back_kernel, parts, rhs), out_shape=out_...  2.69 us
  transfers between devices with their start and end apart: 16, of which 7 were waited for; matrix products, arithmetic and copies ran while one was open for 3% of the time, Pallas kernels for 17%

commit v1 on v0

v1 whole, which is shorter than its diff:
```python
import functools

import jax
import jax.numpy as jnp
import numpy as np
from jax import lax
from jax.experimental import pallas as pl
from jax.experimental.pallas import tpu as pltpu
from jax.sharding import PartitionSpec as P

CHUNKS = 2
FIELD_BOUND = 6.0
CODE_TOP = 32767.0
VMEM_LIMIT = 24 * 1024 * 1024


def dft_tables(parts, local, order, inverse):
    period = parts * local
    own = np.arange(local)
    tables = np.zeros((parts, 2 * local, parts * 2 * local), np.float64)
    for a in range(parts):
        rows = a * local + own
        for j in range(parts):
            cols = order(a, j) * local + own
            angle = 2.0 * np.pi / period * ((rows[:, None] * cols[None, :]) % period)
            cosine, sine = np.cos(angle), np.sin(angle)
            if inverse:
                block = np.block([[cosine, -sine], [sine, cosine]])
            else:
                block = np.block([[cosine, sine], [-sine, cosine]]) / period
            tables[a, :, j * 2 * local : (j + 1) * 2 * local] = block
    tables = tables.astype(np.float32)
    high = tables.astype(jnp.bfloat16)
    low = (tables - high.astype(np.float32)).astype(jnp.bfloat16)
    return np.stack([high, low], axis=1)


def pack_kernel(rhs, fields_ref, *coded_refs):
    rows = fields_ref.shape[0] // rhs
    per = rhs // len(coded_refs)
    for r in range(rhs):
        x = fields_ref[pl.ds(r, rows, stride=rhs), :]
        root = jnp.sqrt(jnp.sqrt(jnp.abs(x) * (1.0 / FIELD_BOUND)))
        code = jnp.round(jnp.where(x < 0, -root, root) * CODE_TOP)
        coded_refs[r // per][r % per] = code.astype(jnp.int32).astype(jnp.int16)


def decoded(code):
    t = code.astype(jnp.int32).astype(jnp.float32) * (FIELD_BOUND**0.25 / CODE_TOP)
    return (t * jnp.abs(t)) * (t * t)


def forward_kernel(sources, table_ref, *refs):
    coded_refs, modes_ref, held = refs[:sources], refs[sources], refs[sources + 1]
    rhs, rows, nodes = coded_refs[0].shape
    for r in range(0, rhs, 2):
        total = jnp.zeros((rows, 2 * nodes), jnp.float32)
        for j in range(sources):
            x = jnp.concatenate([decoded(coded_refs[j][r]), decoded(coded_refs[j][r + 1])], axis=1)
            high = x.astype(jnp.bfloat16)
            low = (x - high.astype(jnp.float32)).astype(jnp.bfloat16)
            cols = slice(j * rows, (j + 1) * rows)
            table_high, table_low = table_ref[0, :, cols], table_ref[1, :, cols]
            total += jnp.dot(table_high, high, preferred_element_type=jnp.float32)
            total += jnp.dot(table_low, high, preferred_element_type=jnp.float32)
            total += jnp.dot(table_high, low, preferred_element_type=jnp.float32)
        held[r * rows : (r + 1) * rows, :] = total[:, :nodes]
        held[(r + 1) * rows : (r + 2) * rows, :] = total[:, nodes:]
    local = rows // 2
    for k in range(local):
        real = held[pl.ds(k, rhs, stride=rows), :]
        imag = held[pl.ds(local + k, rhs, stride=rows), :]
        modes_ref[k] = jnp.concatenate([real, imag], axis=0).astype(jnp.bfloat16)


def stage_kernel(ring, place_ref, cols_ref, count_ref, tiles_ref, forward_ref, back_ref,
                 sorted_ref, forward_out, back_out, sems):
    az, place = place_ref[0], place_ref[1]
    modes, _, slots = tiles_ref.shape[:3]
    tables = [
        pltpu.make_async_copy(forward_ref.at[az], forward_out, sems.at[0]),
        pltpu.make_async_copy(back_ref.at[az], back_out, sems.at[1]),
    ]
    for copy in tables:
        copy.start()

    def tile_copy(k, t):
        step = lax.rem(cols_ref[t, k] - place + ring, ring)
        matched = jnp.where(lax.rem(place, 2) == 0, step == 1, step != 1)
        role = jnp.where(step == 0, 0, jnp.where(matched, 1, 2))
        copy = pltpu.make_async_copy(tiles_ref.at[k, 0, t], sorted_ref.at[role, k], sems.at[2])
        return role, copy

    def begin(k, carry):
        for t in range(slots):
            role, copy = tile_copy(k, t)
            used = t < count_ref[k]

            @pl.when(used)
            def _():
                copy.start()

            @pl.when(jnp.logical_not(used))
            def _():
                sorted_ref[role, k] = jnp.zeros(sorted_ref.shape[2:], sorted_ref.dtype)

        return carry

    def end(k, carry):
        for t in range(slots):

            @pl.when(t < count_ref[k])
            def _():
                tile_copy(k, t)[1].wait()

        return carry

    lax.fori_loop(0, modes, begin, 0)
    lax.fori_loop(0, modes, end, 0)
    for copy in tables:
        copy.wait()


def tile_product(sorted_ref, roles, k, values):
    block = sorted_ref.shape[-1]
    rhs = values[0].shape[0] // 2
    tiles = [sorted_ref[role, k].reshape(2 * block, block) for role in roles]
    product = lax.dot_general(
        jnp.concatenate(values, axis=1),
        jnp.concatenate(tiles, axis=1),
        (((1,), (1,)), ((), ())),
        preferred_element_type=jnp.float32,
    )
    real = product[:rhs, :block] - product[rhs:, block:]
    imag = product[rhs:, :block] + product[:rhs, block:]
    return real, imag


def inner_kernel(sorted_ref, own_ref, side_ref, part_ref):
    modes, both = own_ref.shape[:2]
    for k in range(modes):
        real, imag = tile_product(sorted_ref, (0, 1), k, [own_ref[k], side_ref[k]])
        part_ref[k * both : k * both + both // 2, :] = real
        part_ref[k * both + both // 2 : (k + 1) * both, :] = imag


def outer_kernel(sorted_ref, far_ref, part_ref, near_ref, held):
    modes, both = far_ref.shape[:2]
    rhs = both // 2
    for k in range(modes):
        real, imag = tile_product(sorted_ref, (2,), k, [far_ref[k]])
        at_real, at_imag = slice(k * both, k * both + rhs), slice(k * both + rhs, (k + 1) * both)
        held[at_real, :] = real + part_ref[at_real, :]
        held[at_imag, :] = imag + part_ref[at_imag, :]
    for r in range(rhs):
        for part in range(2):
            rows = slice(part * modes, (part + 1) * modes)
            near_ref[r, rows, :] = held[pl.ds(part * rhs + r, modes, stride=both), :].astype(jnp.bfloat16)


def back_kernel(sources, rhs, chunk, table_ref, fields_ref, impedance_ref, *refs):
    near_refs, out_ref, held, sem = refs[:sources], refs[-3], refs[-2], refs[-1]
    per, rows, nodes = near_refs[0].shape
    local = rows // 2
    z_real, z_imag = impedance_ref[:local], impedance_ref[local:]
    for r in range(0, per, 2):
        total = jnp.zeros((rows, 2 * nodes), jnp.float32)
        for j in range(sources):
            x = jnp.concatenate([near_refs[j][r], near_refs[j][r + 1]], axis=1)
            cols = slice(j * rows, (j + 1) * rows)
            total += jnp.dot(table_ref[0, :, cols], x, preferred_element_type=jnp.float32)
            total += jnp.dot(table_ref[1, :, cols], x, preferred_element_type=jnp.float32)
        for s in range(2):
            real, imag = total[:local, s * nodes : (s + 1) * nodes], total[local:, s * nodes : (s + 1) * nodes]
            from_row = chunk * per + r + s
            f_real = fields_ref[pl.ds(from_row, local, stride=rhs), :]
            f_imag = fields_ref[pl.ds(local * rhs + from_row, local, stride=rhs), :]
            held[pl.ds(r + s, local, stride=per), :] = f_real + z_real * real - z_imag * imag
            held[pl.ds(local * per + r + s, local, stride=per), :] = f_imag + z_real * imag + z_imag * real
    copy = pltpu.make_async_copy(
        held.reshape(rows, per, nodes), out_ref.at[:, pl.ds(chunk * per, per), :], sem
    )
    copy.start()
    copy.wait()


def shared(x, parts):
    if parts == 4:
        peer = [(i, i ^ 1) for i in range(4)]
        across = [(i, i ^ 2) for i in range(4)]
        far = lax.ppermute(x, "az", across)
        near = lax.ppermute(x, "az", peer)
        return [x, near, far, lax.ppermute(far, "az", peer)]
    every = lax.all_gather(x, "az")
    return [every[j] for j in range(parts)]


def after(x, *earlier):
    return lax.optimization_barrier((x,) + earlier)[0]


def on_device(parts, ring, fields, impedance, tile_data, tile_cols, tile_count):
    _, local, rhs, nodes = fields.shape
    per = rhs // CHUNKS
    slots, block = tile_data.shape[2], tile_data.shape[-1]
    rows = 2 * local
    order = (lambda a, j: a ^ j) if parts == 4 else (lambda a, j: j)
    forward_tables = jnp.asarray(dft_tables(parts, local, order, False))
    back_tables = jnp.asarray(dft_tables(parts, local, order, True))
    flat_fields = fields.reshape(rows * rhs, nodes)
    flat_impedance = impedance.reshape(rows, nodes)
    params = pltpu.CompilerParams(vmem_limit_bytes=VMEM_LIMIT)
    vmem, smem = pl.BlockSpec(memory_space=pltpu.VMEM), pl.BlockSpec(memory_space=pltpu.SMEM)
    hbm = pl.BlockSpec(memory_space=pltpu.HBM)

    coded = pl.pallas_call(
        functools.partial(pack_kernel, rhs),
        out_shape=[jax.ShapeDtypeStruct((per, rows, nodes), jnp.int16)] * CHUNKS,
        compiler_params=params,
        name="pack",
    )(flat_fields)

    everyone = []
    for chunk in coded:
        if everyone:
            chunk = after(chunk, everyone[-1][2])
        everyone.append(shared(chunk, parts))

    place = jnp.stack([lax.axis_index("az"), lax.axis_index("curve")]).astype(jnp.int32)
    place = after(place, coded[0])
    sorted_tiles, forward_table, back_table = pl.pallas_call(
        functools.partial(stage_kernel, ring),
        out_shape=[
            jax.ShapeDtypeStruct((slots, local, 2, block, block), tile_data.dtype),
            jax.ShapeDtypeStruct(forward_tables.shape[1:], jnp.bfloat16),
            jax.ShapeDtypeStruct(back_tables.shape[1:], jnp.bfloat16),
        ],
        in_specs=[smem, smem, smem, hbm, hbm, hbm],
        out_specs=[vmem, vmem, vmem],
        scratch_shapes=[pltpu.SemaphoreType.DMA((3,))],
        compiler_params=params,
        name="stage",
    )(place, tile_cols[:, 0, :].T, tile_count.reshape(local), tile_data, forward_tables, back_tables)

    sides = [(i, i ^ 1) for i in range(ring)]
    onward = [(i, (i + 2 if i % 2 == 0 else i - 2) % ring) for i in range(ring)]
    out_shape = jax.ShapeDtypeStruct((rows, rhs, nodes), jnp.float32)
    out = []
    for index, sources in enumerate(everyone):
        own = pl.pallas_call(
            functools.partial(forward_kernel, parts),
            out_shape=jax.ShapeDtypeStruct((local, 2 * per, nodes), jnp.bfloat16),
            in_specs=[vmem] * (1 + parts),
            out_specs=vmem,
            scratch_shapes=[pltpu.VMEM((per * rows, nodes), jnp.float32)],
            compiler_params=params,
            name="forward",
        )(forward_table, *sources)
        side = lax.ppermute(own, "curve", sides)
        far = lax.ppermute(side, "curve", onward)
        inner = pl.pallas_call(
            inner_kernel,
            out_shape=jax.ShapeDtypeStruct((local * 2 * per, nodes), jnp.float32),
            in_specs=[vmem] * 3,
            out_specs=vmem,
            compiler_params=params,
            name="inner",
        )(sorted_tiles, own, side)
        near = pl.pallas_call(
            outer_kernel,
            out_shape=jax.ShapeDtypeStruct((per, rows, nodes), jnp.bfloat16),
            in_specs=[vmem] * 3,
            out_specs=vmem,
            scratch_shapes=[pltpu.VMEM((local * 2 * per, nodes), jnp.float32)],
            compiler_params=params,
            name="outer",
        )(sorted_tiles, far, inner)
        operands = [back_table, flat_fields, flat_impedance] + shared(near, parts) + out
        out = [
            pl.pallas_call(
                functools.partial(back_kernel, parts, rhs, index),
                out_shape=out_shape,
                in_specs=[vmem] * (3 + parts) + [hbm] * len(out),
                out_specs=hbm,
                scratch_shapes=[pltpu.VMEM((rows * per, nodes), jnp.float32), pltpu.SemaphoreType.DMA],
                input_output_aliases={3 + parts: 0} if out else {},
                compiler_params=params,
                name="back",
            )(*operands)
        ]
    return out[0].reshape(fields.shape)


def solution(mesh):
    placed = (
        P(None, "az", None, "curve"),
        P(None, "az", "curve"),
        P("az", "curve", None, None, None, None),
        P("az", "curve", None),
        P("az", "curve"),
    )
    return jax.shard_map(
        functools.partial(on_device, mesh.shape["az"], mesh.shape["curve"]),
        mesh=mesh,
        in_specs=placed,
        out_specs=P(None, "az", None, "curve"),
        check_vma=False,
    )
```

time: 69.3 us -> 84.3 us (1.22)
  Pallas kernels: 15.1 us -> 31 us
  starting transfers between devices: 12.1 us -> 16.1 us
  local copies, waits for them, and re-layouts: 12 us -> 9.6 us
  waiting for transfers between devices: 28.1 us -> 26.7 us
  other arithmetic: 1.42 us -> 0.07 us
    pallas_call x5 -> x9, Pallas kernels: 14.2 us -> 30.1 us  [the longest x1 17.1 us: on_device(): pl.pallas_call(functools.partial(stage_kernel, ring), out_shape=[jax.Shap...]
    ppermute x4, starting transfers between devices: 5.24 us -> 9.09 us  [shared(): far = lax.ppermute(x, 'az', across)]
    unnamed x14 -> x15, local copies, waits for them, and re-layouts: 11.6 us -> 9.6 us
    ppermute x2, waiting for transfers between devices: 1.52 us -> 0.01 us  [on_device(): far = lax.ppermute(side, 'curve', onward)]
    ppermute x4, waiting for transfers between devices: 1.52 us -> 0.01 us  [shared(): return [x, near, far, lax.ppermute(far, 'az', peer)]]
    ppermute x2, waiting for transfers between devices: 8.33 us -> 9.31 us  [on_device(): side = lax.ppermute(own, 'curve', sides)]
    ppermute x4, starting transfers between devices: 1.02 us -> 0.05 us  [shared(): near = lax.ppermute(x, 'az', peer)]
    ppermute x4, starting transfers between devices: 0.01 us -> 0.98 us  [shared(): return [x, near, far, lax.ppermute(far, 'az', peer)]]
  transfers between devices with their start and end apart: 16 -> 16, of which waited for: 7 -> 5; matrix products, arithmetic and copies ran while one was open for 3% -> 1% of each run, Pallas kernels for 17% -> 34%
where the time goes in v1:
time: 84.3 us; the launch traced here: 83.7 us
  Pallas kernels  31 us (37%)
  waiting for transfers between devices  26.7 us (32%)
  starting transfers between devices  16.1 us (19%)
  local copies, waits for them, and re-layouts  9.6 us (11%)
    ppermute x4, waiting for transfers between devices, shared(): far = lax.ppermute(x, 'az', across)  17.4 us
    pallas_call x1, Pallas kernels, on_device(): pl.pallas_call(functools.partial(stage_kernel, ring), out_shape=[jax.Shap...  17.1 us
    unnamed x15, local copies, waits for them, and re-layouts  9.6 us
    ppermute x2, waiting for transfers between devices, on_device(): side = lax.ppermute(own, 'curve', sides)  9.31 us
    ppermute x4, starting transfers between devices, shared(): far = lax.ppermute(x, 'az', across)  9.09 us
    pallas_call x2, Pallas kernels, on_device(): pl.pallas_call(inner_kernel, out_shape=jax.ShapeDtypeStruct((local * 2 *...  4.55 us
    pallas_call x2, Pallas kernels, on_device(): pl.pallas_call(functools.partial(back_kernel, parts, rhs, index), out_sha...  3.24 us
    ppermute x2, starting transfers between devices, on_device(): far = lax.ppermute(side, 'curve', onward)  3.22 us
  transfers between devices with their start and end apart: 16, of which 5 were waited for; matrix products, arithmetic and copies ran while one was open for 1% of the time, Pallas kernels for 34%

profile of v1, /device:TPU:0, one launch (start us, length us, event | category | flops | bytes accessed | tf_op | source)
XLA Modules:
  0.0 83.7 jit_solution(9081924226507129816)
XLA Ops:
  0.0 0.0 copy-start.1
  0.0 1.2 %copy-done.1 = f32[2,64,16,128]{3,2,1,0:T(8,128)S(1)} copy-done((f32[2,64,16,128]{3,2,1,0:T(8,128)S(1)}, f32[2,64,16,128]{3,2,1,0:T(8,128)}, u32[]{:S(2)}) %copy-start.1) | copy-done | bytes 1048600
  1.2 0.9 %pack.1 = (s16[8,128,128]{2,1,0:T(8,128)(2,1)S(1)}, s16[8,128,128]{2,1,0:T(8,128)(2,1)S(1)}) custom-call(f32[2048,128]{1,0:T(8,128)S(1)} %bitcast.11), custom_call_target="tpu_custom_call" | custom-call | tf_op jit(solution)/shard_map/pack/pallas_call | solution.py:216
  2.1 3.0 %collective-permute-start = (s16[8,128,128]{2,1,0:T(8,128)(2,1)S(1)}, s16[8,128,128]{2,1,0:T(8,128)(2,1)S(1)}, u32[]{:S(2)}, u32[]{:S(2)}) collective-permute-start(s16[8,128,128]{2,1,0:T(8,128)(2,1)S(1)} %get-tuple-element.12.refs_0_), channel_id=1, source_target_pairs={{0,16},{8,24},{16,0},{24,8},{1,17},{9,25},{17,1},{25,9},{2,18},{10... | collective-permute-start | bytes 786440 | tf_op jit(solution)/shard_map/ppermute | solution.py:191
  5.1 6.3 %collective-permute-done.refs_2_ = s16[8,128,128]{2,1,0:T(8,128)(2,1)S(1)} collective-permute-done((s16[8,128,128]{2,1,0:T(8,128)(2,1)S(1)}, s16[8,128,128]{2,1,0:T(8,128)(2,1)S(1)}, u32[]{:S(2)}, u32[]{:S(2)}) %collective-permute-start) | collective-permute-done | bytes 262176 | tf_op jit(solution)/shard_map/ppermute | solution.py:191
  11.4 1.7 %collective-permute-start.2 = (s16[8,128,128]{2,1,0:T(8,128)(2,1)S(1)}, s16[8,128,128]{2,1,0:T(8,128)(2,1)S(1)}, u32[]{:S(2)}, u32[]{:S(2)}) collective-permute-start(s16[8,128,128]{2,1,0:T(8,128)(2,1)S(1)} %get-tuple-element.18.refs_0_), channel_id=1, source_target_pairs={{0,16},{8,24},{16,0},{24,8},{1,17},{9,25},{17,1},{25,9},{2,18},{10... | collective-permute-start | bytes 786440 | tf_op jit(solution)/shard_map/ppermute | solution.py:191
  13.1 0.0 collective-permute-start.9
  13.1 0.5 collective-permute-start.10
  13.6 0.0 collective-permute-start.1
  13.7 5.2 %collective-permute-done.2.refs_2_ = s16[8,128,128]{2,1,0:T(8,128)(2,1)S(1)} collective-permute-done((s16[8,128,128]{2,1,0:T(8,128)(2,1)S(1)}, s16[8,128,128]{2,1,0:T(8,128)(2,1)S(1)}, u32[]{:S(2)}, u32[]{:S(2)}) %collective-permute-start.2) | collective-permute-done | bytes 262176 | tf_op jit(solution)/shard_map/ppermute | solution.py:191
  18.9 0.0 collective-permute-start.3
  18.9 0.1 pad_add_fusion.place_ref
  19.0 0.7 copy.11
  19.7 0.0 copy-start
  19.7 4.6 %copy-done = bf16[64,1,3,2,128,128]{5,4,3,2,1,0:T(8,128)(2,1)S(1)} copy-done((bf16[64,1,3,2,128,128]{5,4,3,2,1,0:T(8,128)(2,1)S(1)}, bf16[64,1,3,2,128,128]{5,4,3,2,1,0:T(8,128)(2,1)}, u32[]{:S(2)}) %copy-start) | copy-done | bytes 12582936
  24.2 0.0 copy-start.3
  24.2 1.2 %copy-done.3 = bf16[4,2,128,512]{3,2,1,0:T(8,128)(2,1)S(1)} copy-done((bf16[4,2,128,512]{3,2,1,0:T(8,128)(2,1)S(1)}, bf16[4,2,128,512]{3,2,1,0:T(8,128)(2,1)}, u32[]{:S(2)}) %copy-start.3) | copy-done | bytes 1048600
  25.5 0.0 copy-start.4
  25.5 1.2 %copy-done.4 = bf16[4,2,128,512]{3,2,1,0:T(8,128)(2,1)S(1)} copy-done((bf16[4,2,128,512]{3,2,1,0:T(8,128)(2,1)S(1)}, bf16[4,2,128,512]{3,2,1,0:T(8,128)(2,1)}, u32[]{:S(2)}) %copy-start.4) | copy-done | bytes 1048600
  26.7 0.0 copy-start.6
  26.7 0.7 copy-done.6
  27.3 17.1 %stage.1 = (bf16[3,64,2,128,128]{4,3,2,1,0:T(8,128)(2,1)S(1)}, bf16[2,128,512]{2,1,0:T(8,128)(2,1)S(1)}, bf16[2,128,512]{2,1,0:T(8,128)(2,1)S(1)}) custom-call(s32[2]{0:T(128)S(1)} %pad_add_fusion.place_ref, s32[3,64]{1,0:T(4,128)S(1)} %bitcast.16, s32[64]{0:T(128)S(1)} %bitcast.17, bf16[64,1,3,2,128,128]{5,4,3,2,1,0:T(8,128)(2,1)S(1)} %copy-done, ...), custom_call_target="tpu_custom_call" | custom-call | tf_op jit(solution)/shard_map/stage/pallas_call | solution.py:231
  44.4 0.0 collective-permute-done.9.refs_1_
  44.4 0.0 collective-permute-done.10.refs_3_
  44.4 1.4 %forward.3.own_ref = bf16[64,16,128]{2,1,0:T(8,128)(2,1)S(1)} custom-call(bf16[2,128,512]{2,1,0:T(8,128)(2,1)S(1)} %get-tuple-element.16.table_ref, s16[8,128,128]{2,1,0:T(8,128)(2,1)S(1)} %get-tuple-element.12.refs_0_, s16[8,128,128]{2,1,0:T(8,128)(2,1)S(1)} %collective-permute-done.9.refs_1_, s16[8,128,128]{2,1,0:T(8,128)(2,1)S(1)} %collective-permute-done.refs_2_, ...), custom_call_target="tpu_custom_call" | custom-call | tf_op jit(solution)/shard_map/forward/pallas_call | solution.py:250
  45.8 2.7 %collective-permute-start.11 = (bf16[64,16,128]{2,1,0:T(8,128)(2,1)S(1)}, bf16[64,16,128]{2,1,0:T(8,128)(2,1)S(1)}, u32[]{:S(2)}, u32[]{:S(2)}) collective-permute-start(bf16[64,16,128]{2,1,0:T(8,128)(2,1)S(1)} %forward.3.own_ref), channel_id=1, source_target_pairs={{0,1},{1,0},{2,3},{3,2},{4,5},{5,4},{6,7},{7,6},{8,9},{9,8},{10,11... | collective-permute-start | bytes 786440 | tf_op jit(solution)/shard_map/ppermute | solution.py:259
  48.5 0.0 collective-permute-done.1.refs_1_
  48.5 0.0 collective-permute-done.3.refs_3_
  48.5 1.4 %forward.2.own_ref = bf16[64,16,128]{2,1,0:T(8,128)(2,1)S(1)} custom-call(bf16[2,128,512]{2,1,0:T(8,128)(2,1)S(1)} %get-tuple-element.16.table_ref, s16[8,128,128]{2,1,0:T(8,128)(2,1)S(1)} %get-tuple-element.18.refs_0_, s16[8,128,128]{2,1,0:T(8,128)(2,1)S(1)} %collective-permute-done.1.refs_1_, s16[8,128,128]{2,1,0:T(8,128)(2,1)S(1)} %collective-permute-done.2.refs_2_, ...), custom_call_target="tpu_custom_call" | custom-call | tf_op jit(solution)/shard_map/forward/pallas_call | solution.py:250
  49.9 0.1 collective-permute-start.4
  50.0 5.6 %collective-permute-done.11.side_ref = bf16[64,16,128]{2,1,0:T(8,128)(2,1)S(1)} collective-permute-done((bf16[64,16,128]{2,1,0:T(8,128)(2,1)S(1)}, bf16[64,16,128]{2,1,0:T(8,128)(2,1)S(1)}, u32[]{:S(2)}, u32[]{:S(2)}) %collective-permute-start.11) | collective-permute-done | bytes 262176 | tf_op jit(solution)/shard_map/ppermute | solution.py:259
  55.6 1.4 %collective-permute-start.12 = (bf16[64,16,128]{2,1,0:T(8,128)(2,1)S(1)}, bf16[64,16,128]{2,1,0:T(8,128)(2,1)S(1)}, u32[]{:S(2)}, u32[]{:S(2)}) collective-permute-start(bf16[64,16,128]{2,1,0:T(8,128)(2,1)S(1)} %collective-permute-done.11.side_ref), channel_id=1, source_target_pairs={{0,2},{1,7},{2,4},{3,1},{4,6},{5,3},{6,0},{7,5},{8,10},{9,15},{10,... | collective-permute-start | bytes 786440 | tf_op jit(solution)/shard_map/ppermute | solution.py:260
  57.0 3.7 %collective-permute-done.4.side_ref = bf16[64,16,128]{2,1,0:T(8,128)(2,1)S(1)} collective-permute-done((bf16[64,16,128]{2,1,0:T(8,128)(2,1)S(1)}, bf16[64,16,128]{2,1,0:T(8,128)(2,1)S(1)}, u32[]{:S(2)}, u32[]{:S(2)}) %collective-permute-start.4) | collective-permute-done | bytes 262176 | tf_op jit(solution)/shard_map/ppermute | solution.py:259
  60.7 1.8 %collective-permute-start.5 = (bf16[64,16,128]{2,1,0:T(8,128)(2,1)S(1)}, bf16[64,16,128]{2,1,0:T(8,128)(2,1)S(1)}, u32[]{:S(2)}, u32[]{:S(2)}) collective-permute-start(bf16[64,16,128]{2,1,0:T(8,128)(2,1)S(1)} %collective-permute-done.4.side_ref), channel_id=1, source_target_pairs={{0,2},{1,7},{2,4},{3,1},{4,6},{5,3},{6,0},{7,5},{8,10},{9,15},{10,... | collective-permute-start | bytes 786440 | tf_op jit(solution)/shard_map/ppermute | solution.py:260
  62.5 2.3 %inner.3.part_ref = f32[1024,128]{1,0:T(8,128)S(1)} custom-call(bf16[3,64,2,128,128]{4,3,2,1,0:T(8,128)(2,1)S(1)} %get-tuple-element.15.sorted_ref, bf16[64,16,128]{2,1,0:T(8,128)(2,1)S(1)} %forward.3.own_ref, bf16[64,16,128]{2,1,0:T(8,128)(2,1)S(1)} %collective-permute-done.11.side_ref), custom_call_target="tpu_custom_call" | custom-call | tf_op jit(solution)/shard_map/inner/pallas_call | solution.py:261
  64.8 0.0 collective-permute-done.12.far_ref
  64.8 1.3 %outer.3.refs_0_ = bf16[8,128,128]{2,1,0:T(8,128)(2,1)S(1)} custom-call(bf16[3,64,2,128,128]{4,3,2,1,0:T(8,128)(2,1)S(1)} %get-tuple-element.15.sorted_ref, bf16[64,16,128]{2,1,0:T(8,128)(2,1)S(1)} %collective-permute-done.12.far_ref, f32[1024,128]{1,0:T(8,128)S(1)} %inner.3.part_ref), custom_call_target="tpu_custom_call" | custom-call | tf_op jit(solution)/shard_map/outer/pallas_call | solution.py:269
  66.1 0.0 copy-start.2
  66.1 0.0 copy-start.5
  66.1 2.5 %collective-permute-start.14 = (bf16[8,128,128]{2,1,0:T(8,128)(2,1)S(1)}, bf16[8,128,128]{2,1,0:T(8,128)(2,1)S(1)}, u32[]{:S(2)}, u32[]{:S(2)}) collective-permute-start(bf16[8,128,128]{2,1,0:T(8,128)(2,1)S(1)} %outer.3.refs_0_), channel_id=1, source_target_pairs={{0,16},{8,24},{16,0},{24,8},{1,17},{9,25},{17,1},{25,9},{2,18},{10... | collective-permute-start | bytes 786440 | tf_op jit(solution)/shard_map/ppermute | solution.py:191
  68.6 2.3 %inner.2.part_ref = f32[1024,128]{1,0:T(8,128)S(1)} custom-call(bf16[3,64,2,128,128]{4,3,2,1,0:T(8,128)(2,1)S(1)} %get-tuple-element.15.sorted_ref, bf16[64,16,128]{2,1,0:T(8,128)(2,1)S(1)} %forward.2.own_ref, bf16[64,16,128]{2,1,0:T(8,128)(2,1)S(1)} %collective-permute-done.4.side_ref), custom_call_target="tpu_custom_call" | custom-call | tf_op jit(solution)/shard_map/inner/pallas_call | solution.py:261
  70.9 0.0 collective-permute-done.5.far_ref
  70.9 1.3 %outer.2.refs_0_ = bf16[8,128,128]{2,1,0:T(8,128)(2,1)S(1)} custom-call(bf16[3,64,2,128,128]{4,3,2,1,0:T(8,128)(2,1)S(1)} %get-tuple-element.15.sorted_ref, bf16[64,16,128]{2,1,0:T(8,128)(2,1)S(1)} %collective-permute-done.5.far_ref, f32[1024,128]{1,0:T(8,128)S(1)} %inner.2.part_ref), custom_call_target="tpu_custom_call" | custom-call | tf_op jit(solution)/shard_map/outer/pallas_call | solution.py:269
  72.2 1.8 %collective-permute-start.7 = (bf16[8,128,128]{2,1,0:T(8,128)(2,1)S(1)}, bf16[8,128,128]{2,1,0:T(8,128)(2,1)S(1)}, u32[]{:S(2)}, u32[]{:S(2)}) collective-permute-start(bf16[8,128,128]{2,1,0:T(8,128)(2,1)S(1)} %outer.2.refs_0_), channel_id=1, source_target_pairs={{0,16},{8,24},{16,0},{24,8},{1,17},{9,25},{17,1},{25,9},{2,18},{10... | collective-permute-start | bytes 786440 | tf_op jit(solution)/shard_map/ppermute | solution.py:191
  74.0 0.0 collective-permute-start.13
  74.0 0.0 collective-permute-done.14.refs_2_
  74.1 0.5 collective-permute-start.15
  74.5 0.0 collective-permute-start.6
  74.6 5.8 %collective-permute-done.7.refs_2_ = bf16[8,128,128]{2,1,0:T(8,128)(2,1)S(1)} collective-permute-done((bf16[8,128,128]{2,1,0:T(8,128)(2,1)S(1)}, bf16[8,128,128]{2,1,0:T(8,128)(2,1)S(1)}, u32[]{:S(2)}, u32[]{:S(2)}) %collective-permute-start.7) | collective-permute-done | bytes 262176 | tf_op jit(solution)/shard_map/ppermute | solution.py:191
  80.4 0.0 collective-permute-start.8
  80.4 0.0 collective-permute-done.13.refs_1_
  80.4 0.0 collective-permute-done.15.refs_3_
  80.4 0.0 copy-done.2
  80.4 0.0 copy-done.5
  80.4 1.6 %back.2.refs_4_ = f32[128,16,128]{2,1,0:T(8,128)} custom-call(bf16[2,128,512]{2,1,0:T(8,128)(2,1)S(1)} %get-tuple-element.14.table_ref, f32[2048,128]{1,0:T(8,128)S(1)} %bitcast.12, f32[128,128]{1,0:T(8,128)S(1)} %bitcast.14, bf16[8,128,128]{2,1,0:T(8,128)(2,1)S(1)} %outer.3.refs_0_, bf16[8,128,128]{2,1,0:T(8,128)(2,1)S(1)} %collective-permute-done.13.refs_1_, ...), custom_call_target="tpu_custom_call" | custom-call | tf_op jit(solution)/shard_map/back/pallas_call | solution.py:280
  82.1 0.0 collective-permute-done.6.refs_1_
  82.1 0.0 collective-permute-done.8.refs_3_
  82.1 1.6 %back.3 = f32[128,16,128]{2,1,0:T(8,128)} custom-call(bf16[2,128,512]{2,1,0:T(8,128)(2,1)S(1)} %get-tuple-element.14.table_ref, f32[2048,128]{1,0:T(8,128)S(1)} %bitcast.13, f32[128,128]{1,0:T(8,128)S(1)} %bitcast.15, bf16[8,128,128]{2,1,0:T(8,128)(2,1)S(1)} %outer.2.refs_0_, ...), custom_call_target="tpu_custom_call", output_to_operand_aliasing={{}: (7, {})} | custom-call | tf_op jit(solution)/shard_map/back/pallas_call | solution.py:280
Async XLA Ops:
  0.0 1.2 %copy-start.1 = (f32[2,64,16,128]{3,2,1,0:T(8,128)S(1)}, f32[2,64,16,128]{3,2,1,0:T(8,128)}, u32[]{:S(2)}) copy-start(f32[2,64,16,128]{3,2,1,0:T(8,128)} %param.7) | copy-start | bytes 3145732
  2.1 9.3 %collective-permute-start = (s16[8,128,128]{2,1,0:T(8,128)(2,1)S(1)}, s16[8,128,128]{2,1,0:T(8,128)(2,1)S(1)}, u32[]{:S(2)}, u32[]{:S(2)}) collective-permute-start(s16[8,128,128]{2,1,0:T(8,128)(2,1)S(1)} %get-tuple-element.12.refs_0_), channel_id=1, source_target_pairs={{0,16},{8,24},{16,0},{24,8},{1,17},{9,25},{17,1},{25,9},{2,18},{10... | collective-permute-start | bytes 786440 | tf_op jit(solution)/shard_map/ppermute | solution.py:191
  11.4 7.5 %collective-permute-start.2 = (s16[8,128,128]{2,1,0:T(8,128)(2,1)S(1)}, s16[8,128,128]{2,1,0:T(8,128)(2,1)S(1)}, u32[]{:S(2)}, u32[]{:S(2)}) collective-permute-start(s16[8,128,128]{2,1,0:T(8,128)(2,1)S(1)} %get-tuple-element.18.refs_0_), channel_id=1, source_target_pairs={{0,16},{8,24},{16,0},{24,8},{1,17},{9,25},{17,1},{25,9},{2,18},{10... | collective-permute-start | bytes 786440 | tf_op jit(solution)/shard_map/ppermute | solution.py:191
  13.1 31.3 %collective-permute-start.9 = (s16[8,128,128]{2,1,0:T(8,128)(2,1)S(1)}, s16[8,128,128]{2,1,0:T(8,128)(2,1)S(1)}, u32[]{:S(2)}, u32[]{:S(2)}) collective-permute-start(s16[8,128,128]{2,1,0:T(8,128)(2,1)S(1)} %get-tuple-element.12.refs_0_), channel_id=1, source_target_pairs={{0,8},{8,0},{16,24},{24,16},{1,9},{9,1},{17,25},{25,17},{2,10},{10... | collective-permute-start | bytes 786440 | tf_op jit(solution)/shard_map/ppermute | solution.py:192
  13.1 31.3 %collective-permute-start.10 = (s16[8,128,128]{2,1,0:T(8,128)(2,1)S(1)}, s16[8,128,128]{2,1,0:T(8,128)(2,1)S(1)}, u32[]{:S(2)}, u32[]{:S(2)}) collective-permute-start(s16[8,128,128]{2,1,0:T(8,128)(2,1)S(1)} %collective-permute-done.refs_2_), channel_id=1, source_target_pairs={{0,8},{8,0},{16,24},{24,16},{1,9},{9,1},{17,25},{25,17},{2,10},{10... | collective-permute-start | bytes 786440 | tf_op jit(solution)/shard_map/ppermute | solution.py:193
  13.6 34.9 %collective-permute-start.1 = (s16[8,128,128]{2,1,0:T(8,128)(2,1)S(1)}, s16[8,128,128]{2,1,0:T(8,128)(2,1)S(1)}, u32[]{:S(2)}, u32[]{:S(2)}) collective-permute-start(s16[8,128,128]{2,1,0:T(8,128)(2,1)S(1)} %get-tuple-element.18.refs_0_), channel_id=1, source_target_pairs={{0,8},{8,0},{16,24},{24,16},{1,9},{9,1},{17,25},{25,17},{2,10},{10... | collective-permute-start | bytes 786440 | tf_op jit(solution)/shard_map/ppermute | solution.py:192
  18.9 29.6 %collective-permute-start.3 = (s16[8,128,128]{2,1,0:T(8,128)(2,1)S(1)}, s16[8,128,128]{2,1,0:T(8,128)(2,1)S(1)}, u32[]{:S(2)}, u32[]{:S(2)}) collective-permute-start(s16[8,128,128]{2,1,0:T(8,128)(2,1)S(1)} %collective-permute-done.2.refs_2_), channel_id=1, source_target_pairs={{0,8},{8,0},{16,24},{24,16},{1,9},{9,1},{17,25},{25,17},{2,10},{10... | collective-permute-start | bytes 786440 | tf_op jit(solution)/shard_map/ppermute | solution.py:193
  19.7 4.6 %copy-start = (bf16[64,1,3,2,128,128]{5,4,3,2,1,0:T(8,128)(2,1)S(1)}, bf16[64,1,3,2,128,128]{5,4,3,2,1,0:T(8,128)(2,1)}, u32[]{:S(2)}) copy-start(bf16[64,1,3,2,128,128]{5,4,3,2,1,0:T(8,128)(2,1)} %tiles_ref.1) | copy-start | bytes 37748740
  24.2 1.2 %copy-start.3 = (bf16[4,2,128,512]{3,2,1,0:T(8,128)(2,1)S(1)}, bf16[4,2,128,512]{3,2,1,0:T(8,128)(2,1)}, u32[]{:S(2)}) copy-start(bf16[4,2,128,512]{3,2,1,0:T(8,128)(2,1)} %constant.12.clone.forward_ref) | copy-start | bytes 3145732
  25.5 1.2 %copy-start.4 = (bf16[4,2,128,512]{3,2,1,0:T(8,128)(2,1)S(1)}, bf16[4,2,128,512]{3,2,1,0:T(8,128)(2,1)}, u32[]{:S(2)}) copy-start(bf16[4,2,128,512]{3,2,1,0:T(8,128)(2,1)} %constant.13.clone.back_ref) | copy-start | bytes 3145732
  26.7 0.7 copy-start.6
  45.8 9.8 %collective-permute-start.11 = (bf16[64,16,128]{2,1,0:T(8,128)(2,1)S(1)}, bf16[64,16,128]{2,1,0:T(8,128)(2,1)S(1)}, u32[]{:S(2)}, u32[]{:S(2)}) collective-permute-start(bf16[64,16,128]{2,1,0:T(8,128)(2,1)S(1)} %forward.3.own_ref), channel_id=1, source_target_pairs={{0,1},{1,0},{2,3},{3,2},{4,5},{5,4},{6,7},{7,6},{8,9},{9,8},{10,11... | collective-permute-start | bytes 786440 | tf_op jit(solution)/shard_map/ppermute | solution.py:259
  49.9 10.8 %collective-permute-start.4 = (bf16[64,16,128]{2,1,0:T(8,128)(2,1)S(1)}, bf16[64,16,128]{2,1,0:T(8,128)(2,1)S(1)}, u32[]{:S(2)}, u32[]{:S(2)}) collective-permute-start(bf16[64,16,128]{2,1,0:T(8,128)(2,1)S(1)} %forward.2.own_ref), channel_id=1, source_target_pairs={{0,1},{1,0},{2,3},{3,2},{4,5},{5,4},{6,7},{7,6},{8,9},{9,8},{10,11... | collective-permute-start | bytes 786440 | tf_op jit(solution)/shard_map/ppermute | solution.py:259
  55.6 9.2 %collective-permute-start.12 = (bf16[64,16,128]{2,1,0:T(8,128)(2,1)S(1)}, bf16[64,16,128]{2,1,0:T(8,128)(2,1)S(1)}, u32[]{:S(2)}, u32[]{:S(2)}) collective-permute-start(bf16[64,16,128]{2,1,0:T(8,128)(2,1)S(1)} %collective-permute-done.11.side_ref), channel_id=1, source_target_pairs={{0,2},{1,7},{2,4},{3,1},{4,6},{5,3},{6,0},{7,5},{8,10},{9,15},{10,... | collective-permute-start | bytes 786440 | tf_op jit(solution)/shard_map/ppermute | solution.py:260
  60.7 10.2 %collective-permute-start.5 = (bf16[64,16,128]{2,1,0:T(8,128)(2,1)S(1)}, bf16[64,16,128]{2,1,0:T(8,128)(2,1)S(1)}, u32[]{:S(2)}, u32[]{:S(2)}) collective-permute-start(bf16[64,16,128]{2,1,0:T(8,128)(2,1)S(1)} %collective-permute-done.4.side_ref), channel_id=1, source_target_pairs={{0,2},{1,7},{2,4},{3,1},{4,6},{5,3},{6,0},{7,5},{8,10},{9,15},{10,... | collective-permute-start | bytes 786440 | tf_op jit(solution)/shard_map/ppermute | solution.py:260
  66.1 14.3 %copy-start.2 = (f32[2,64,16,128]{3,2,1,0:T(8,128)S(1)}, f32[2,64,16,128]{3,2,1,0:T(8,128)}, u32[]{:S(2)}) copy-start(f32[2,64,16,128]{3,2,1,0:T(8,128)} %param.7) | copy-start | bytes 3145732
  66.1 14.3 %copy-start.5 = (f32[2,64,128]{2,1,0:T(8,128)S(1)}, f32[2,64,128]{2,1,0:T(8,128)}, u32[]{:S(2)}) copy-start(f32[2,64,128]{2,1,0:T(8,128)} %param.8) | copy-start | bytes 196612
  66.1 8.0 %collective-permute-start.14 = (bf16[8,128,128]{2,1,0:T(8,128)(2,1)S(1)}, bf16[8,128,128]{2,1,0:T(8,128)(2,1)S(1)}, u32[]{:S(2)}, u32[]{:S(2)}) collective-permute-start(bf16[8,128,128]{2,1,0:T(8,128)(2,1)S(1)} %outer.3.refs_0_), channel_id=1, source_target_pairs={{0,16},{8,24},{16,0},{24,8},{1,17},{9,25},{17,1},{25,9},{2,18},{10... | collective-permute-start | bytes 786440 | tf_op jit(solution)/shard_map/ppermute | solution.py:191
  72.2 8.2 %collective-permute-start.7 = (bf16[8,128,128]{2,1,0:T(8,128)(2,1)S(1)}, bf16[8,128,128]{2,1,0:T(8,128)(2,1)S(1)}, u32[]{:S(2)}, u32[]{:S(2)}) collective-permute-start(bf16[8,128,128]{2,1,0:T(8,128)(2,1)S(1)} %outer.2.refs_0_), channel_id=1, source_target_pairs={{0,16},{8,24},{16,0},{24,8},{1,17},{9,25},{17,1},{25,9},{2,18},{10... | collective-permute-start | bytes 786440 | tf_op jit(solution)/shard_map/ppermute | solution.py:191
  74.0 6.4 %collective-permute-start.13 = (bf16[8,128,128]{2,1,0:T(8,128)(2,1)S(1)}, bf16[8,128,128]{2,1,0:T(8,128)(2,1)S(1)}, u32[]{:S(2)}, u32[]{:S(2)}) collective-permute-start(bf16[8,128,128]{2,1,0:T(8,128)(2,1)S(1)} %outer.3.refs_0_), channel_id=1, source_target_pairs={{0,8},{8,0},{16,24},{24,16},{1,9},{9,1},{17,25},{25,17},{2,10},{10... | collective-permute-start | bytes 786440 | tf_op jit(solution)/shard_map/ppermute | solution.py:192
  74.1 6.3 %collective-permute-start.15 = (bf16[8,128,128]{2,1,0:T(8,128)(2,1)S(1)}, bf16[8,128,128]{2,1,0:T(8,128)(2,1)S(1)}, u32[]{:S(2)}, u32[]{:S(2)}) collective-permute-start(bf16[8,128,128]{2,1,0:T(8,128)(2,1)S(1)} %collective-permute-done.14.refs_2_), channel_id=1, source_target_pairs={{0,8},{8,0},{16,24},{24,16},{1,9},{9,1},{17,25},{25,17},{2,10},{10... | collective-permute-start | bytes 786440 | tf_op jit(solution)/shard_map/ppermute | solution.py:193
  74.5 7.5 %collective-permute-start.6 = (bf16[8,128,128]{2,1,0:T(8,128)(2,1)S(1)}, bf16[8,128,128]{2,1,0:T(8,128)(2,1)S(1)}, u32[]{:S(2)}, u32[]{:S(2)}) collective-permute-start(bf16[8,128,128]{2,1,0:T(8,128)(2,1)S(1)} %outer.2.refs_0_), channel_id=1, source_target_pairs={{0,8},{8,0},{16,24},{24,16},{1,9},{9,1},{17,25},{25,17},{2,10},{10... | collective-permute-start | bytes 786440 | tf_op jit(solution)/shard_map/ppermute | solution.py:192
  80.4 1.7 %collective-permute-start.8 = (bf16[8,128,128]{2,1,0:T(8,128)(2,1)S(1)}, bf16[8,128,128]{2,1,0:T(8,128)(2,1)S(1)}, u32[]{:S(2)}, u32[]{:S(2)}) collective-permute-start(bf16[8,128,128]{2,1,0:T(8,128)(2,1)S(1)} %collective-permute-done.7.refs_2_), channel_id=1, source_target_pairs={{0,8},{8,0},{16,24},{24,16},{1,9},{9,1},{17,25},{25,17},{2,10},{10... | collective-permute-start | bytes 786440 | tf_op jit(solution)/shard_map/ppermute | solution.py:193

commit v2 on v1

v2 whole, which is shorter than its diff:
```python
import functools

import jax
import jax.numpy as jnp
import numpy as np
from jax import lax
from jax.experimental import pallas as pl
from jax.experimental.pallas import tpu as pltpu
from jax.sharding import PartitionSpec as P

CHUNKS = 2
FIELD_BOUND = 6.0
CODE_TOP = 32767.0
VMEM_LIMIT = 24 * 1024 * 1024
STAGE_VMEM_LIMIT = 36 * 1024 * 1024


def dft_tables(parts, local, order, inverse):
    period = parts * local
    own = np.arange(local)
    tables = np.zeros((parts, 2 * local, parts * 2 * local), np.float64)
    for a in range(parts):
        rows = a * local + own
        for j in range(parts):
            cols = order(a, j) * local + own
            angle = 2.0 * np.pi / period * ((rows[:, None] * cols[None, :]) % period)
            cosine, sine = np.cos(angle), np.sin(angle)
            if inverse:
                block = np.block([[cosine, -sine], [sine, cosine]])
            else:
                block = np.block([[cosine, sine], [-sine, cosine]]) / period
            tables[a, :, j * 2 * local : (j + 1) * 2 * local] = block
    tables = tables.astype(np.float32)
    high = tables.astype(jnp.bfloat16)
    low = (tables - high.astype(np.float32)).astype(jnp.bfloat16)
    return np.stack([high, low], axis=1)


def pack_kernel(rhs, fields_ref, all_ref, *chunk_refs):
    rows = fields_ref.shape[0] // rhs
    per = rhs // len(chunk_refs)
    for r in range(rhs):
        x = fields_ref[pl.ds(r, rows, stride=rhs), :]
        root = jnp.sqrt(jnp.sqrt(jnp.abs(x) * (1.0 / FIELD_BOUND)))
        code = jnp.round(jnp.where(x < 0, -root, root) * CODE_TOP)
        code = code.astype(jnp.int32).astype(jnp.int16)
        all_ref[r] = code
        chunk_refs[r // per][r % per] = code


def decoded(code):
    t = code.astype(jnp.int32).astype(jnp.float32) * (FIELD_BOUND**0.25 / CODE_TOP)
    return (t * jnp.abs(t)) * (t * t)


def forward_kernel(firsts, table_ref, *refs):
    sources = len(firsts)
    coded_refs, modes_ref, held = refs[:sources], refs[sources], refs[sources + 1]
    rhs = modes_ref.shape[1] // 2
    rows, nodes = coded_refs[0].shape[1:]
    for r in range(0, rhs, 2):
        total = jnp.zeros((rows, 2 * nodes), jnp.float32)
        for j in range(sources):
            at = firsts[j] + r
            x = jnp.concatenate([decoded(coded_refs[j][at]), decoded(coded_refs[j][at + 1])], axis=1)
            high = x.astype(jnp.bfloat16)
            low = (x - high.astype(jnp.float32)).astype(jnp.bfloat16)
            cols = slice(j * rows, (j + 1) * rows)
            table_high, table_low = table_ref[0, :, cols], table_ref[1, :, cols]
            total += jnp.dot(table_high, high, preferred_element_type=jnp.float32)
            total += jnp.dot(table_low, high, preferred_element_type=jnp.float32)
            total += jnp.dot(table_high, low, preferred_element_type=jnp.float32)
        held[r * rows : (r + 1) * rows, :] = total[:, :nodes]
        held[(r + 1) * rows : (r + 2) * rows, :] = total[:, nodes:]
    local = rows // 2
    for k in range(local):
        real = held[pl.ds(k, rhs, stride=rows), :]
        imag = held[pl.ds(local + k, rhs, stride=rows), :]
        modes_ref[k] = jnp.concatenate([real, imag], axis=0).astype(jnp.bfloat16)


def stage_kernel(ring, place_ref, cols_ref, count_ref, tiles_ref, forward_ref, back_ref,
                 tiles_out, forward_out, back_out, slot_out, sems):
    az, place = place_ref[0], place_ref[1]
    modes = tiles_ref.shape[0]
    copies = [
        pltpu.make_async_copy(forward_ref.at[az], forward_out, sems.at[0]),
        pltpu.make_async_copy(back_ref.at[az], back_out, sems.at[1]),
        pltpu.make_async_copy(tiles_ref, tiles_out, sems.at[2]),
    ]
    for copy in copies:
        copy.start()
    even = lax.rem(place, 2) == 0
    side = jnp.where(even, place + 1, place - 1)
    far = lax.rem(jnp.where(even, place - 1, place + 1) + ring, ring)

    def find(k, carry):
        for role, wanted in enumerate((place, side, far)):
            slot = jnp.where(cols_ref[0, k] == wanted, 0, jnp.where(cols_ref[1, k] == wanted, 1, 2))
            slot_out[role * modes + k] = jnp.where(slot < count_ref[k], slot, -1)
        return carry

    lax.fori_loop(0, modes, find, 0)
    for copy in copies:
        copy.wait()


def tile_product(slot_ref, tiles_ref, k, roles, values):
    modes, block = tiles_ref.shape[0], tiles_ref.shape[-1]
    rhs = values[0].shape[0] // 2
    tiles, kept = [], []
    for role, value in zip(roles, values):
        slot = slot_ref[role * modes + k]
        tiles.append(tiles_ref[k, 0, jnp.maximum(slot, 0)].reshape(2 * block, block))
        kept.append(jnp.where(slot < 0, jnp.zeros_like(value), value))
    product = lax.dot_general(
        jnp.concatenate(kept, axis=1),
        jnp.concatenate(tiles, axis=1),
        (((1,), (1,)), ((), ())),
        preferred_element_type=jnp.float32,
    )
    real = product[:rhs, :block] - product[rhs:, block:]
    imag = product[rhs:, :block] + product[:rhs, block:]
    return real, imag


def inner_kernel(slot_ref, tiles_ref, own_ref, side_ref, part_ref):
    modes, both = own_ref.shape[:2]
    for k in range(modes):
        real, imag = tile_product(slot_ref, tiles_ref, k, (0, 1), [own_ref[k], side_ref[k]])
        part_ref[k * both : k * both + both // 2, :] = real
        part_ref[k * both + both // 2 : (k + 1) * both, :] = imag


def outer_kernel(slot_ref, tiles_ref, far_ref, part_ref, near_ref, held):
    modes, both = far_ref.shape[:2]
    rhs = both // 2
    for k in range(modes):
        real, imag = tile_product(slot_ref, tiles_ref, k, (2,), [far_ref[k]])
        at_real, at_imag = slice(k * both, k * both + rhs), slice(k * both + rhs, (k + 1) * both)
        held[at_real, :] = real + part_ref[at_real, :]
        held[at_imag, :] = imag + part_ref[at_imag, :]
    for r in range(rhs):
        for part in range(2):
            rows = slice(part * modes, (part + 1) * modes)
            near_ref[r, rows, :] = held[pl.ds(part * rhs + r, modes, stride=both), :].astype(jnp.bfloat16)


def back_kernel(sources, rhs, chunk, table_ref, fields_ref, impedance_ref, *refs):
    near_refs, out_ref, held, sem = refs[:sources], refs[-3], refs[-2], refs[-1]
    per, rows, nodes = near_refs[0].shape
    local = rows // 2
    z_real, z_imag = impedance_ref[:local], impedance_ref[local:]
    for r in range(0, per, 2):
        total = jnp.zeros((rows, 2 * nodes), jnp.float32)
        for j in range(sources):
            x = jnp.concatenate([near_refs[j][r], near_refs[j][r + 1]], axis=1)
            cols = slice(j * rows, (j + 1) * rows)
            total += jnp.dot(table_ref[0, :, cols], x, preferred_element_type=jnp.float32)
            total += jnp.dot(table_ref[1, :, cols], x, preferred_element_type=jnp.float32)
        for s in range(2):
            real, imag = total[:local, s * nodes : (s + 1) * nodes], total[local:, s * nodes : (s + 1) * nodes]
            from_row = chunk * per + r + s
            f_real = fields_ref[pl.ds(from_row, local, stride=rhs), :]
            f_imag = fields_ref[pl.ds(local * rhs + from_row, local, stride=rhs), :]
            held[pl.ds(r + s, local, stride=per), :] = f_real + z_real * real - z_imag * imag
            held[pl.ds(local * per + r + s, local, stride=per), :] = f_imag + z_real * imag + z_imag * real
    copy = pltpu.make_async_copy(
        held.reshape(rows, per, nodes), out_ref.at[:, pl.ds(chunk * per, per), :], sem
    )
    copy.start()
    copy.wait()


PEER = [(i, i ^ 1) for i in range(4)]
ACROSS = [(i, i ^ 2) for i in range(4)]


def after(x, *earlier):
    return lax.optimization_barrier((x,) + earlier)[0]


def cost(flops, moved):
    return pl.CostEstimate(flops=flops, bytes_accessed=moved, transcendentals=0)


def on_device(parts, ring, fields, impedance, tile_data, tile_cols, tile_count):
    _, local, rhs, nodes = fields.shape
    per = rhs // CHUNKS
    slots, block = tile_data.shape[2], tile_data.shape[-1]
    rows = 2 * local
    paired = parts == 4
    order = (lambda a, j: a ^ j) if paired else (lambda a, j: j)
    forward_tables = jnp.asarray(dft_tables(parts, local, order, False))
    back_tables = jnp.asarray(dft_tables(parts, local, order, True))
    flat_fields = fields.reshape(rows * rhs, nodes)
    flat_impedance = impedance.reshape(rows, nodes)
    params = pltpu.CompilerParams(vmem_limit_bytes=VMEM_LIMIT)
    vmem, smem = pl.BlockSpec(memory_space=pltpu.VMEM), pl.BlockSpec(memory_space=pltpu.SMEM)
    hbm = pl.BlockSpec(memory_space=pltpu.HBM)
    move = 16 * fields.size
    multiply = 4 * rows * rows * parts * per * nodes

    coded, *chunks = pl.pallas_call(
        functools.partial(pack_kernel, rhs),
        out_shape=[jax.ShapeDtypeStruct((rhs, rows, nodes), jnp.int16)]
        + [jax.ShapeDtypeStruct((per, rows, nodes), jnp.int16)] * CHUNKS,
        cost_estimate=cost(0, move),
        compiler_params=params,
        name="pack",
    )(flat_fields)

    place = jnp.stack([lax.axis_index("az"), lax.axis_index("curve")]).astype(jnp.int32)
    place = after(place, coded)
    tiles, forward_table, back_table, slot = pl.pallas_call(
        functools.partial(stage_kernel, ring),
        out_shape=[
            jax.ShapeDtypeStruct(tile_data.shape, tile_data.dtype),
            jax.ShapeDtypeStruct(forward_tables.shape[1:], jnp.bfloat16),
            jax.ShapeDtypeStruct(back_tables.shape[1:], jnp.bfloat16),
            jax.ShapeDtypeStruct((slots * local,), jnp.int32),
        ],
        in_specs=[smem, smem, smem, hbm, hbm, hbm],
        out_specs=[vmem, vmem, vmem, smem],
        scratch_shapes=[pltpu.SemaphoreType.DMA((3,))],
        cost_estimate=cost(0, 2 * tile_data.size),
        compiler_params=pltpu.CompilerParams(vmem_limit_bytes=STAGE_VMEM_LIMIT),
        name="stage",
    )(place, tile_cols[:, 0, :].T, tile_count.reshape(local), tile_data, forward_tables, back_tables)

    sides = [(i, i ^ 1) for i in range(ring)]
    onward = [(i, (i + 2 if i % 2 == 0 else i - 2) % ring) for i in range(ring)]
    peer = lax.ppermute(coded, "az", PEER) if paired else None
    owns, ready = [], (tiles,)
    for index, chunk in enumerate(chunks):
        if paired:
            across = lax.ppermute(after(chunk, *ready) if index else chunk, "az", ACROSS)
            across = after(across, *ready) if index == 0 else after(across, owns[-1])
            ready = (across,)
            sources = [coded, peer, across, lax.ppermute(across, "az", PEER)]
            firsts = (index * per, index * per, 0, 0)
        else:
            every = lax.all_gather(chunk, "az")
            sources, firsts = [every[j] for j in range(parts)], (0,) * parts
        owns.append(
            pl.pallas_call(
                functools.partial(forward_kernel, firsts),
                out_shape=jax.ShapeDtypeStruct((local, 2 * per, nodes), jnp.bfloat16),
                in_specs=[vmem] * (1 + parts),
                out_specs=vmem,
                scratch_shapes=[pltpu.VMEM((per * rows, nodes), jnp.float32)],
                cost_estimate=cost(3 * multiply, move),
                compiler_params=params,
                name="forward",
            )(forward_table, *sources)
        )

    nears = []
    for own in owns:
        side = lax.ppermute(own, "curve", sides)
        far = lax.ppermute(side, "curve", onward)
        inner = pl.pallas_call(
            inner_kernel,
            out_shape=jax.ShapeDtypeStruct((local * 2 * per, nodes), jnp.float32),
            in_specs=[smem] + [vmem] * 3,
            out_specs=vmem,
            cost_estimate=cost(0, tile_data.size),
            compiler_params=params,
            name="inner",
        )(slot, tiles, own, side)
        far = after(far, inner)
        nears.append(
            pl.pallas_call(
                outer_kernel,
                out_shape=jax.ShapeDtypeStruct((per, rows, nodes), jnp.bfloat16),
                in_specs=[smem] + [vmem] * 3,
                out_specs=vmem,
                scratch_shapes=[pltpu.VMEM((local * 2 * per, nodes), jnp.float32)],
                cost_estimate=cost(0, tile_data.size // 2),
                compiler_params=params,
                name="outer",
            )(slot, tiles, far, inner)
        )

    out = None
    for index, near in enumerate(nears):
        if paired:
            across = lax.ppermute(near, "az", ACROSS)
            if out is not None:
                across, out = lax.optimization_barrier((across, out))
            sources = [near, lax.ppermute(near, "az", PEER), across, lax.ppermute(across, "az", PEER)]
        else:
            every = lax.all_gather(near, "az")
            sources = [every[j] for j in range(parts)]
        earlier = [] if out is None else [out]
        out = pl.pallas_call(
            functools.partial(back_kernel, parts, rhs, index),
            out_shape=jax.ShapeDtypeStruct((rows, rhs, nodes), jnp.float32),
            in_specs=[vmem] * (3 + parts) + [hbm] * len(earlier),
            out_specs=hbm,
            scratch_shapes=[pltpu.VMEM((rows * per, nodes), jnp.float32), pltpu.SemaphoreType.DMA],
            input_output_aliases={3 + parts: 0} if earlier else {},
            cost_estimate=cost(2 * multiply, move),
            compiler_params=params,
            name="back",
        )(back_table, flat_fields, flat_impedance, *sources, *earlier)
    return out.reshape(fields.shape)


def solution(mesh):
    placed = (
        P(None, "az", None, "curve"),
        P(None, "az", "curve"),
        P("az", "curve", None, None, None, None),
        P("az", "curve", None),
        P("az", "curve"),
    )
    return jax.shard_map(
        functools.partial(on_device, mesh.shape["az"], mesh.shape["curve"]),
        mesh=mesh,
        in_specs=placed,
        out_specs=P(None, "az", None, "curve"),
        check_vma=False,
    )
```

time: 84.3 us -> 62 us (0.74)
  Pallas kernels: 31 us -> 21.9 us
  local copies, waits for them, and re-layouts: 9.6 us -> 5.02 us
  starting transfers between devices: 16.1 us -> 11.6 us
  waiting for transfers between devices: 26.7 us -> 23 us
    pallas_call x1, Pallas kernels: 17.1 us -> 5.82 us  [on_device(): pl.pallas_call(functools.partial(stage_kernel, ring), out_shape=[jax.Shap...]
    ppermute x2, waiting for transfers between devices: 9.31 us -> 3.33 us  [on_device(): side = lax.ppermute(own, 'curve', sides)]
    ppermute x12 -> x11, starting transfers between devices: 10.1 us -> 4.8 us  [the longest x2 3.08 us: on_device(): lax.ppermute(after(chunk, *ready) if index else chunk, 'az', ACROSS)]
    unnamed x15 -> x13, local copies, waits for them, and re-layouts: 9.6 us -> 5.02 us
    ppermute x2, starting transfers between devices: 2.81 us -> 5.21 us  [on_device(): side = lax.ppermute(own, 'curve', sides)]
    ppermute x12 -> x11, waiting for transfers between devices: 17.4 us -> 19.4 us  [the longest x2 12.6 us: on_device(): across = lax.ppermute(near, 'az', ACROSS)]
    ppermute x2, starting transfers between devices: 3.22 us -> 1.58 us  [on_device(): far = lax.ppermute(side, 'curve', onward)]
    pallas_call x2, Pallas kernels: 4.55 us -> 5.66 us  [on_device(): pl.pallas_call(inner_kernel, out_shape=jax.ShapeDtypeStruct((local * 2 *...]
  transfers between devices with their start and end apart: 16 -> 15, of which waited for: 5 -> 8; matrix products, arithmetic and copies ran while one was open for 1% -> 1% of each run, Pallas kernels for 34% -> 32%
where the time goes in v2:
time: 62 us; the launch traced here: 61.7 us
  waiting for transfers between devices  23 us (37%)
  Pallas kernels  21.9 us (35%)
  starting transfers between devices  11.6 us (19%)
  local copies, waits for them, and re-layouts  5.02 us (8%)
    ppermute x2, waiting for transfers between devices, on_device(): across = lax.ppermute(near, 'az', ACROSS)  12.6 us
    pallas_call x1, Pallas kernels, on_device(): pl.pallas_call(functools.partial(stage_kernel, ring), out_shape=[jax.Shap...  5.82 us
    pallas_call x2, Pallas kernels, on_device(): pl.pallas_call(inner_kernel, out_shape=jax.ShapeDtypeStruct((local * 2 *...  5.66 us
    ppermute x2, starting transfers between devices, on_device(): side = lax.ppermute(own, 'curve', sides)  5.21 us
    unnamed x13, local copies, waits for them, and re-layouts  5.02 us
    ppermute x2, waiting for transfers between devices, on_device(): lax.ppermute(after(chunk, *ready) if index else chunk, 'az', ACROSS)  4.17 us
    pallas_call x2, Pallas kernels, on_device(): pl.pallas_call(outer_kernel, out_shape=jax.ShapeDtypeStruct((per, rows, n...  3.63 us
    ppermute x2, waiting for transfers between devices, on_device(): side = lax.ppermute(own, 'curve', sides)  3.33 us
  transfers between devices with their start and end apart: 15, of which 8 were waited for; matrix products, arithmetic and copies ran while one was open for 1% of the time, Pallas kernels for 32%

profile of v2, /device:TPU:0, one launch (start us, length us, event | category | flops | bytes accessed | tf_op | source)
XLA Modules:
  0.0 61.7 jit_solution(238358012669882013)
XLA Ops:
  0.0 0.0 copy-start
  0.0 1.2 %copy-done = f32[2,64,16,128]{3,2,1,0:T(8,128)S(1)} copy-done((f32[2,64,16,128]{3,2,1,0:T(8,128)S(1)}, f32[2,64,16,128]{3,2,1,0:T(8,128)}, u32[]{:S(2)}) %copy-start) | copy-done | bytes 1048600
  1.2 0.9 %pack.1 = (s16[16,128,128]{2,1,0:T(8,128)(2,1)S(1)}, s16[8,128,128]{2,1,0:T(8,128)(2,1)S(1)}, s16[8,128,128]{2,1,0:T(8,128)(2,1)S(1)}) custom-call(f32[2048,128]{1,0:T(8,128)S(1)} %bitcast.11), custom_call_target="tpu_custom_call" | custom-call | bytes 4194304 | tf_op jit(solution)/shard_map/pack/pallas_call | solution.py:204
  2.1 3.0 %collective-permute-start.1 = (s16[8,128,128]{2,1,0:T(8,128)(2,1)S(1)}, s16[8,128,128]{2,1,0:T(8,128)(2,1)S(1)}, u32[]{:S(2)}, u32[]{:S(2)}) collective-permute-start(s16[8,128,128]{2,1,0:T(8,128)(2,1)S(1)} %get-tuple-element.27), channel_id=1, source_target_pairs={{0,16},{8,24},{16,0},{24,8},{1,17},{9,25},{17,1},{25,9},{2,18},{10... | collective-permute-start | bytes 786440 | tf_op jit(solution)/shard_map/ppermute | solution.py:237
  5.1 0.0 collective-permute-start
  5.1 0.7 %copy.11 = s32[64,1,3]{0,2,1:T(4,128)S(1)} copy(s32[64,1,3]{0,1,2:T(1,128)} %param.10) | data formatting | bytes 1536
  5.8 0.1 pad_add_fusion.place_ref
  5.9 0.0 copy-start.2
  5.9 1.2 %copy-done.2 = bf16[4,2,128,512]{3,2,1,0:T(8,128)(2,1)S(1)} copy-done((bf16[4,2,128,512]{3,2,1,0:T(8,128)(2,1)S(1)}, bf16[4,2,128,512]{3,2,1,0:T(8,128)(2,1)}, u32[]{:S(2)}) %copy-start.2) | copy-done | bytes 1048600
  7.1 0.0 copy-start.3
  7.1 1.2 %copy-done.3 = bf16[4,2,128,512]{3,2,1,0:T(8,128)(2,1)S(1)} copy-done((bf16[4,2,128,512]{3,2,1,0:T(8,128)(2,1)S(1)}, bf16[4,2,128,512]{3,2,1,0:T(8,128)(2,1)}, u32[]{:S(2)}) %copy-start.3) | copy-done | bytes 1048600
  8.3 0.0 copy-start.5
  8.3 0.7 %copy-done.5 = s32[64,1]{0,1:T(1,128)S(1)} copy-done((s32[64,1]{0,1:T(1,128)S(1)}, s32[64,1]{0,1:T(1,128)}, u32[]{:S(2)}) %copy-start.5) | copy-done | bytes 280
  9.0 5.8 %stage.1 = (bf16[64,1,3,2,128,128]{5,4,3,2,1,0:T(8,128)(2,1)S(1)}, bf16[2,128,512]{2,1,0:T(8,128)(2,1)S(1)}, bf16[2,128,512]{2,1,0:T(8,128)(2,1)S(1)}, s32[192]{0:T(256)S(1)}) custom-call(s32[2]{0:T(128)S(1)} %pad_add_fusion.place_ref, s32[3,64]{1,0:T(4,128)S(1)} %bitcast.16, s32[64]{0:T(128)S(1)} %bitcast.17, bf16[64,1,3,2,128,128]{5,4,3,2,1,0:T(8,128)(2,1)} %tiles_ref.1, ...), custom_call_target="tpu_custom_call" | custom-call | bytes 12582912 | tf_op jit(solution)/shard_map/stage/pallas_call | solution.py:215
  14.8 0.0 collective-permute-done.1.refs_2_
  14.8 0.6 collective-permute-start.3
  15.4 0.1 collective-permute-start.2
  15.4 0.0 collective-permute-done.refs_1_
  15.5 1.1 %collective-permute-done.3.refs_3_ = s16[8,128,128]{2,1,0:T(8,128)(2,1)S(1)} collective-permute-done((s16[8,128,128]{2,1,0:T(8,128)(2,1)S(1)}, s16[8,128,128]{2,1,0:T(8,128)(2,1)S(1)}, u32[]{:S(2)}, u32[]{:S(2)}) %collective-permute-start.3) | collective-permute-done | bytes 262176 | tf_op jit(solution)/shard_map/ppermute | solution.py:240
  16.5 1.3 %forward.2.own_ref = bf16[64,16,128]{2,1,0:T(8,128)(2,1)S(1)} custom-call(bf16[2,128,512]{2,1,0:T(8,128)(2,1)S(1)} %get-tuple-element.25.table_ref, s16[16,128,128]{2,1,0:T(8,128)(2,1)S(1)} %get-tuple-element.20.refs_0_, s16[16,128,128]{2,1,0:T(8,128)(2,1)S(1)} %collective-permute-done.refs_1_, s16[8,128,128]{2,1,0:T(8,128)(2,1)S(1)} %collective-permute-done.1.refs_2_, ...), custom_call_target="tpu_custom_call" | custom-call | flops 805306368 | bytes 4194304 | tf_op jit(solution)/shard_map/forward/pallas_call | solution.py:246
  17.9 1.6 %collective-permute-start.9 = (bf16[64,16,128]{2,1,0:T(8,128)(2,1)S(1)}, bf16[64,16,128]{2,1,0:T(8,128)(2,1)S(1)}, u32[]{:S(2)}, u32[]{:S(2)}) collective-permute-start(bf16[64,16,128]{2,1,0:T(8,128)(2,1)S(1)} %forward.2.own_ref), channel_id=1, source_target_pairs={{0,1},{1,0},{2,3},{3,2},{4,5},{5,4},{6,7},{7,6},{8,9},{9,8},{10,11... | collective-permute-start | bytes 786440 | tf_op jit(solution)/shard_map/ppermute | solution.py:260
  19.5 4.2 %collective-permute-done.2.refs_2_ = s16[8,128,128]{2,1,0:T(8,128)(2,1)S(1)} collective-permute-done((s16[8,128,128]{2,1,0:T(8,128)(2,1)S(1)}, s16[8,128,128]{2,1,0:T(8,128)(2,1)S(1)}, u32[]{:S(2)}, u32[]{:S(2)}) %collective-permute-start.2) | collective-permute-done | bytes 262176 | tf_op jit(solution)/shard_map/ppermute | solution.py:237
  23.7 0.0 collective-permute-start.4
  23.7 2.9 %collective-permute-done.9.side_ref = bf16[64,16,128]{2,1,0:T(8,128)(2,1)S(1)} collective-permute-done((bf16[64,16,128]{2,1,0:T(8,128)(2,1)S(1)}, bf16[64,16,128]{2,1,0:T(8,128)(2,1)S(1)}, u32[]{:S(2)}, u32[]{:S(2)}) %collective-permute-start.9) | collective-permute-done | bytes 262176 | tf_op jit(solution)/shard_map/ppermute | solution.py:260
  26.5 1.6 %collective-permute-start.10 = (bf16[64,16,128]{2,1,0:T(8,128)(2,1)S(1)}, bf16[64,16,128]{2,1,0:T(8,128)(2,1)S(1)}, u32[]{:S(2)}, u32[]{:S(2)}) collective-permute-start(bf16[64,16,128]{2,1,0:T(8,128)(2,1)S(1)} %collective-permute-done.9.side_ref), channel_id=1, source_target_pairs={{0,2},{1,7},{2,4},{3,1},{4,6},{5,3},{6,0},{7,5},{8,10},{9,15},{10,... | collective-permute-start | bytes 786440 | tf_op jit(solution)/shard_map/ppermute | solution.py:261
  28.1 0.0 collective-permute-done.4.refs_3_
  28.1 1.4 %forward.3.own_ref = bf16[64,16,128]{2,1,0:T(8,128)(2,1)S(1)} custom-call(bf16[2,128,512]{2,1,0:T(8,128)(2,1)S(1)} %get-tuple-element.25.table_ref, s16[16,128,128]{2,1,0:T(8,128)(2,1)S(1)} %get-tuple-element.20.refs_0_, s16[16,128,128]{2,1,0:T(8,128)(2,1)S(1)} %collective-permute-done.refs_1_, s16[8,128,128]{2,1,0:T(8,128)(2,1)S(1)} %collective-permute-done.2.refs_2_, ...), custom_call_target="tpu_custom_call" | custom-call | flops 805306368 | bytes 4194304 | tf_op jit(solution)/shard_map/forward/pallas_call | solution.py:246
  29.5 3.6 %collective-permute-start.5 = (bf16[64,16,128]{2,1,0:T(8,128)(2,1)S(1)}, bf16[64,16,128]{2,1,0:T(8,128)(2,1)S(1)}, u32[]{:S(2)}, u32[]{:S(2)}) collective-permute-start(bf16[64,16,128]{2,1,0:T(8,128)(2,1)S(1)} %forward.3.own_ref), channel_id=1, source_target_pairs={{0,1},{1,0},{2,3},{3,2},{4,5},{5,4},{6,7},{7,6},{8,9},{9,8},{10,11... | collective-permute-start | bytes 786440 | tf_op jit(solution)/shard_map/ppermute | solution.py:260
  33.1 2.8 %inner.3.part_ref = f32[1024,128]{1,0:T(8,128)S(1)} custom-call(s32[192]{0:T(256)S(1)} %get-tuple-element.23.slot_ref, bf16[64,1,3,2,128,128]{5,4,3,2,1,0:T(8,128)(2,1)S(1)} %get-tuple-element.24.tiles_ref, bf16[64,16,128]{2,1,0:T(8,128)(2,1)S(1)} %forward.2.own_ref, bf16[64,16,128]{2,1,0:T(8,128)(2,1)S(1)} %collective-permute-done.9.side_ref), custom_call_target="tpu_custom_call" | custom-call | bytes 6291456 | tf_op jit(solution)/shard_map/inner/pallas_call | solution.py:262
  35.9 0.2 collective-permute-done.10.far_ref
  36.2 1.8 %outer.3.refs_0_ = bf16[8,128,128]{2,1,0:T(8,128)(2,1)S(1)} custom-call(s32[192]{0:T(256)S(1)} %get-tuple-element.23.slot_ref, bf16[64,1,3,2,128,128]{5,4,3,2,1,0:T(8,128)(2,1)S(1)} %get-tuple-element.24.tiles_ref, bf16[64,16,128]{2,1,0:T(8,128)(2,1)S(1)} %collective-permute-done.10.far_ref, f32[1024,128]{1,0:T(8,128)S(1)} %inner.3.part_ref), custom_call_target="tpu_custom_call" | custom-call | bytes 3145728 | tf_op jit(solution)/shard_map/outer/pallas_call | solution.py:273
  38.0 0.0 copy-start.1
  38.0 0.0 copy-start.4
  38.0 0.4 collective-permute-start.12
  38.4 0.5 collective-permute-done.5.side_ref
  38.8 0.0 collective-permute-start.6
  38.8 0.0 collective-permute-start.11
  38.8 6.2 %collective-permute-done.12.refs_2_ = bf16[8,128,128]{2,1,0:T(8,128)(2,1)S(1)} collective-permute-done((bf16[8,128,128]{2,1,0:T(8,128)(2,1)S(1)}, bf16[8,128,128]{2,1,0:T(8,128)(2,1)S(1)}, u32[]{:S(2)}, u32[]{:S(2)}) %collective-permute-start.12) | collective-permute-done | bytes 262176 | tf_op jit(solution)/shard_map/ppermute | solution.py:288
  45.1 0.0 collective-permute-start.13
  45.1 2.8 %inner.2.part_ref = f32[1024,128]{1,0:T(8,128)S(1)} custom-call(s32[192]{0:T(256)S(1)} %get-tuple-element.23.slot_ref, bf16[64,1,3,2,128,128]{5,4,3,2,1,0:T(8,128)(2,1)S(1)} %get-tuple-element.24.tiles_ref, bf16[64,16,128]{2,1,0:T(8,128)(2,1)S(1)} %forward.3.own_ref, bf16[64,16,128]{2,1,0:T(8,128)(2,1)S(1)} %collective-permute-done.5.side_ref), custom_call_target="tpu_custom_call" | custom-call | bytes 6291456 | tf_op jit(solution)/shard_map/inner/pallas_call | solution.py:262
  47.9 0.0 collective-permute-done.6.far_ref
  47.9 1.8 %outer.2.refs_0_ = bf16[8,128,128]{2,1,0:T(8,128)(2,1)S(1)} custom-call(s32[192]{0:T(256)S(1)} %get-tuple-element.23.slot_ref, bf16[64,1,3,2,128,128]{5,4,3,2,1,0:T(8,128)(2,1)S(1)} %get-tuple-element.24.tiles_ref, bf16[64,16,128]{2,1,0:T(8,128)(2,1)S(1)} %collective-permute-done.6.far_ref, f32[1024,128]{1,0:T(8,128)S(1)} %inner.2.part_ref), custom_call_target="tpu_custom_call" | custom-call | bytes 3145728 | tf_op jit(solution)/shard_map/outer/pallas_call | solution.py:273
  49.7 0.8 %collective-permute-start.8 = (bf16[8,128,128]{2,1,0:T(8,128)(2,1)S(1)}, bf16[8,128,128]{2,1,0:T(8,128)(2,1)S(1)}, u32[]{:S(2)}, u32[]{:S(2)}) collective-permute-start(bf16[8,128,128]{2,1,0:T(8,128)(2,1)S(1)} %outer.2.refs_0_), channel_id=1, source_target_pairs={{0,16},{8,24},{16,0},{24,8},{1,17},{9,25},{17,1},{25,9},{2,18},{10... | collective-permute-start | bytes 786440 | tf_op jit(solution)/shard_map/ppermute | solution.py:288
  50.5 0.0 collective-permute-start.7
  50.5 0.0 collective-permute-done.11.refs_1_
  50.5 0.0 collective-permute-done.13.refs_3_
  50.5 0.0 copy-done.1
  50.5 0.0 copy-done.4
  50.5 1.6 %back.2.refs_4_ = f32[128,16,128]{2,1,0:T(8,128)} custom-call(bf16[2,128,512]{2,1,0:T(8,128)(2,1)S(1)} %get-tuple-element.22.table_ref, f32[2048,128]{1,0:T(8,128)S(1)} %bitcast.12, f32[128,128]{1,0:T(8,128)S(1)} %bitcast.14, bf16[8,128,128]{2,1,0:T(8,128)(2,1)S(1)} %outer.3.refs_0_, bf16[8,128,128]{2,1,0:T(8,128)(2,1)S(1)} %collective-permute-done.11.refs_1_, ...), custom_call_target="tpu_custom_call" | custom-call | flops 536870912 | bytes 4194304 | tf_op jit(solution)/shard_map/back/pallas_call | solution.py:296
  52.2 6.4 %collective-permute-done.8.refs_2_ = bf16[8,128,128]{2,1,0:T(8,128)(2,1)S(1)} collective-permute-done((bf16[8,128,128]{2,1,0:T(8,128)(2,1)S(1)}, bf16[8,128,128]{2,1,0:T(8,128)(2,1)S(1)}, u32[]{:S(2)}, u32[]{:S(2)}) %collective-permute-start.8) | collective-permute-done | bytes 262176 | tf_op jit(solution)/shard_map/ppermute | solution.py:288
  58.5 0.0 collective-permute-start.14
  58.5 0.0 collective-permute-done.7.refs_1_
  58.5 1.5 %collective-permute-done.14.refs_3_ = bf16[8,128,128]{2,1,0:T(8,128)(2,1)S(1)} collective-permute-done((bf16[8,128,128]{2,1,0:T(8,128)(2,1)S(1)}, bf16[8,128,128]{2,1,0:T(8,128)(2,1)S(1)}, u32[]{:S(2)}, u32[]{:S(2)}) %collective-permute-start.14) | collective-permute-done | bytes 262176 | tf_op jit(solution)/shard_map/ppermute | solution.py:291
  60.1 1.6 %back.3 = f32[128,16,128]{2,1,0:T(8,128)} custom-call(bf16[2,128,512]{2,1,0:T(8,128)(2,1)S(1)} %get-tuple-element.22.table_ref, f32[2048,128]{1,0:T(8,128)S(1)} %bitcast.13, f32[128,128]{1,0:T(8,128)S(1)} %bitcast.15, bf16[8,128,128]{2,1,0:T(8,128)(2,1)S(1)} %outer.2.refs_0_, ...), custom_call_target="tpu_custom_call", output_to_operand_aliasing={{}: (7, {})} | custom-call | flops 536870912 | bytes 4194304 | tf_op jit(solution)/shard_map/back/pallas_call | solution.py:296
Async XLA Ops:
  0.0 1.2 %copy-start = (f32[2,64,16,128]{3,2,1,0:T(8,128)S(1)}, f32[2,64,16,128]{3,2,1,0:T(8,128)}, u32[]{:S(2)}) copy-start(f32[2,64,16,128]{3,2,1,0:T(8,128)} %param.7) | copy-start | bytes 3145732
  2.1 12.7 %collective-permute-start.1 = (s16[8,128,128]{2,1,0:T(8,128)(2,1)S(1)}, s16[8,128,128]{2,1,0:T(8,128)(2,1)S(1)}, u32[]{:S(2)}, u32[]{:S(2)}) collective-permute-start(s16[8,128,128]{2,1,0:T(8,128)(2,1)S(1)} %get-tuple-element.27), channel_id=1, source_target_pairs={{0,16},{8,24},{16,0},{24,8},{1,17},{9,25},{17,1},{25,9},{2,18},{10... | collective-permute-start | bytes 786440 | tf_op jit(solution)/shard_map/ppermute | solution.py:237
  5.1 10.4 %collective-permute-start = (s16[16,128,128]{2,1,0:T(8,128)(2,1)S(1)}, s16[16,128,128]{2,1,0:T(8,128)(2,1)S(1)}, u32[]{:S(2)}, u32[]{:S(2)}) collective-permute-start(s16[16,128,128]{2,1,0:T(8,128)(2,1)S(1)} %get-tuple-element.20.refs_0_), channel_id=1, source_target_pairs={{0,8},{8,0},{16,24},{24,16},{1,9},{9,1},{17,25},{25,17},{2,10},{10... | collective-permute-start | bytes 1572872 | tf_op jit(solution)/shard_map/ppermute | solution.py:233
  5.9 1.2 %copy-start.2 = (bf16[4,2,128,512]{3,2,1,0:T(8,128)(2,1)S(1)}, bf16[4,2,128,512]{3,2,1,0:T(8,128)(2,1)}, u32[]{:S(2)}) copy-start(bf16[4,2,128,512]{3,2,1,0:T(8,128)(2,1)} %constant.13.clone.back_ref) | copy-start | bytes 3145732
  7.1 1.2 %copy-start.3 = (bf16[4,2,128,512]{3,2,1,0:T(8,128)(2,1)S(1)}, bf16[4,2,128,512]{3,2,1,0:T(8,128)(2,1)}, u32[]{:S(2)}) copy-start(bf16[4,2,128,512]{3,2,1,0:T(8,128)(2,1)} %constant.12.clone.forward_ref) | copy-start | bytes 3145732
  8.3 0.7 %copy-start.5 = (s32[64,1]{0,1:T(1,128)S(1)}, s32[64,1]{0,1:T(1,128)}, u32[]{:S(2)}) copy-start(s32[64,1]{0,1:T(1,128)} %param.11) | copy-start | bytes 772
  14.8 1.7 %collective-permute-start.3 = (s16[8,128,128]{2,1,0:T(8,128)(2,1)S(1)}, s16[8,128,128]{2,1,0:T(8,128)(2,1)S(1)}, u32[]{:S(2)}, u32[]{:S(2)}) collective-permute-start(s16[8,128,128]{2,1,0:T(8,128)(2,1)S(1)} %collective-permute-done.1.refs_2_), channel_id=1, source_target_pairs={{0,8},{8,0},{16,24},{24,16},{1,9},{9,1},{17,25},{25,17},{2,10},{10... | collective-permute-start | bytes 786440 | tf_op jit(solution)/shard_map/ppermute | solution.py:240
  15.4 8.3 %collective-permute-start.2 = (s16[8,128,128]{2,1,0:T(8,128)(2,1)S(1)}, s16[8,128,128]{2,1,0:T(8,128)(2,1)S(1)}, u32[]{:S(2)}, u32[]{:S(2)}) collective-permute-start(s16[8,128,128]{2,1,0:T(8,128)(2,1)S(1)} %get-tuple-element.29), channel_id=1, source_target_pairs={{0,16},{8,24},{16,0},{24,8},{1,17},{9,25},{17,1},{25,9},{2,18},{10... | collective-permute-start | bytes 786440 | tf_op jit(solution)/shard_map/ppermute | solution.py:237
  17.9 8.7 %collective-permute-start.9 = (bf16[64,16,128]{2,1,0:T(8,128)(2,1)S(1)}, bf16[64,16,128]{2,1,0:T(8,128)(2,1)S(1)}, u32[]{:S(2)}, u32[]{:S(2)}) collective-permute-start(bf16[64,16,128]{2,1,0:T(8,128)(2,1)S(1)} %forward.2.own_ref), channel_id=1, source_target_pairs={{0,1},{1,0},{2,3},{3,2},{4,5},{5,4},{6,7},{7,6},{8,9},{9,8},{10,11... | collective-permute-start | bytes 786440 | tf_op jit(solution)/shard_map/ppermute | solution.py:260
  23.7 4.5 %collective-permute-start.4 = (s16[8,128,128]{2,1,0:T(8,128)(2,1)S(1)}, s16[8,128,128]{2,1,0:T(8,128)(2,1)S(1)}, u32[]{:S(2)}, u32[]{:S(2)}) collective-permute-start(s16[8,128,128]{2,1,0:T(8,128)(2,1)S(1)} %collective-permute-done.2.refs_2_), channel_id=1, source_target_pairs={{0,8},{8,0},{16,24},{24,16},{1,9},{9,1},{17,25},{25,17},{2,10},{10... | collective-permute-start | bytes 786440 | tf_op jit(solution)/shard_map/ppermute | solution.py:240
  26.5 9.6 %collective-permute-start.10 = (bf16[64,16,128]{2,1,0:T(8,128)(2,1)S(1)}, bf16[64,16,128]{2,1,0:T(8,128)(2,1)S(1)}, u32[]{:S(2)}, u32[]{:S(2)}) collective-permute-start(bf16[64,16,128]{2,1,0:T(8,128)(2,1)S(1)} %collective-permute-done.9.side_ref), channel_id=1, source_target_pairs={{0,2},{1,7},{2,4},{3,1},{4,6},{5,3},{6,0},{7,5},{8,10},{9,15},{10,... | collective-permute-start | bytes 786440 | tf_op jit(solution)/shard_map/ppermute | solution.py:261
  29.5 9.4 %collective-permute-start.5 = (bf16[64,16,128]{2,1,0:T(8,128)(2,1)S(1)}, bf16[64,16,128]{2,1,0:T(8,128)(2,1)S(1)}, u32[]{:S(2)}, u32[]{:S(2)}) collective-permute-start(bf16[64,16,128]{2,1,0:T(8,128)(2,1)S(1)} %forward.3.own_ref), channel_id=1, source_target_pairs={{0,1},{1,0},{2,3},{3,2},{4,5},{5,4},{6,7},{7,6},{8,9},{9,8},{10,11... | collective-permute-start | bytes 786440 | tf_op jit(solution)/shard_map/ppermute | solution.py:260
  38.0 12.5 %copy-start.1 = (f32[2,64,16,128]{3,2,1,0:T(8,128)S(1)}, f32[2,64,16,128]{3,2,1,0:T(8,128)}, u32[]{:S(2)}) copy-start(f32[2,64,16,128]{3,2,1,0:T(8,128)} %param.7) | copy-start | bytes 3145732
  38.0 12.5 %copy-start.4 = (f32[2,64,128]{2,1,0:T(8,128)S(1)}, f32[2,64,128]{2,1,0:T(8,128)}, u32[]{:S(2)}) copy-start(f32[2,64,128]{2,1,0:T(8,128)} %param.8) | copy-start | bytes 196612
  38.0 7.1 %collective-permute-start.12 = (bf16[8,128,128]{2,1,0:T(8,128)(2,1)S(1)}, bf16[8,128,128]{2,1,0:T(8,128)(2,1)S(1)}, u32[]{:S(2)}, u32[]{:S(2)}) collective-permute-start(bf16[8,128,128]{2,1,0:T(8,128)(2,1)S(1)} %outer.3.refs_0_), channel_id=1, source_target_pairs={{0,16},{8,24},{16,0},{24,8},{1,17},{9,25},{17,1},{25,9},{2,18},{10... | collective-permute-start | bytes 786440 | tf_op jit(solution)/shard_map/ppermute | solution.py:288
  38.8 9.1 %collective-permute-start.6 = (bf16[64,16,128]{2,1,0:T(8,128)(2,1)S(1)}, bf16[64,16,128]{2,1,0:T(8,128)(2,1)S(1)}, u32[]{:S(2)}, u32[]{:S(2)}) collective-permute-start(bf16[64,16,128]{2,1,0:T(8,128)(2,1)S(1)} %collective-permute-done.5.side_ref), channel_id=1, source_target_pairs={{0,2},{1,7},{2,4},{3,1},{4,6},{5,3},{6,0},{7,5},{8,10},{9,15},{10,... | collective-permute-start | bytes 786440 | tf_op jit(solution)/shard_map/ppermute | solution.py:261
  38.8 11.6 %collective-permute-start.11 = (bf16[8,128,128]{2,1,0:T(8,128)(2,1)S(1)}, bf16[8,128,128]{2,1,0:T(8,128)(2,1)S(1)}, u32[]{:S(2)}, u32[]{:S(2)}) collective-permute-start(bf16[8,128,128]{2,1,0:T(8,128)(2,1)S(1)} %outer.3.refs_0_), channel_id=1, source_target_pairs={{0,8},{8,0},{16,24},{24,16},{1,9},{9,1},{17,25},{25,17},{2,10},{10... | collective-permute-start | bytes 786440 | tf_op jit(solution)/shard_map/ppermute | solution.py:291
  45.1 5.4 %collective-permute-start.13 = (bf16[8,128,128]{2,1,0:T(8,128)(2,1)S(1)}, bf16[8,128,128]{2,1,0:T(8,128)(2,1)S(1)}, u32[]{:S(2)}, u32[]{:S(2)}) collective-permute-start(bf16[8,128,128]{2,1,0:T(8,128)(2,1)S(1)} %collective-permute-done.12.refs_2_), channel_id=1, source_target_pairs={{0,8},{8,0},{16,24},{24,16},{1,9},{9,1},{17,25},{25,17},{2,10},{10... | collective-permute-start | bytes 786440 | tf_op jit(solution)/shard_map/ppermute | solution.py:291
  49.7 8.8 %collective-permute-start.8 = (bf16[8,128,128]{2,1,0:T(8,128)(2,1)S(1)}, bf16[8,128,128]{2,1,0:T(8,128)(2,1)S(1)}, u32[]{:S(2)}, u32[]{:S(2)}) collective-permute-start(bf16[8,128,128]{2,1,0:T(8,128)(2,1)S(1)} %outer.2.refs_0_), channel_id=1, source_target_pairs={{0,16},{8,24},{16,0},{24,8},{1,17},{9,25},{17,1},{25,9},{2,18},{10... | collective-permute-start | bytes 786440 | tf_op jit(solution)/shard_map/ppermute | solution.py:288
  50.5 8.0 %collective-permute-start.7 = (bf16[8,128,128]{2,1,0:T(8,128)(2,1)S(1)}, bf16[8,128,128]{2,1,0:T(8,128)(2,1)S(1)}, u32[]{:S(2)}, u32[]{:S(2)}) collective-permute-start(bf16[8,128,128]{2,1,0:T(8,128)(2,1)S(1)} %outer.2.refs_0_), channel_id=1, source_target_pairs={{0,8},{8,0},{16,24},{24,16},{1,9},{9,1},{17,25},{25,17},{2,10},{10... | collective-permute-start | bytes 786440 | tf_op jit(solution)/shard_map/ppermute | solution.py:291
  58.5 1.5 %collective-permute-start.14 = (bf16[8,128,128]{2,1,0:T(8,128)(2,1)S(1)}, bf16[8,128,128]{2,1,0:T(8,128)(2,1)S(1)}, u32[]{:S(2)}, u32[]{:S(2)}) collective-permute-start(bf16[8,128,128]{2,1,0:T(8,128)(2,1)S(1)} %collective-permute-done.8.refs_2_), channel_id=1, source_target_pairs={{0,8},{8,0},{16,24},{24,16},{1,9},{9,1},{17,25},{25,17},{2,10},{10... | collective-permute-start | bytes 786440 | tf_op jit(solution)/shard_map/ppermute | solution.py:291

commit v3 on v2

--- a/solution.py
+++ b/solution.py
@@ -9,10 +9,13 @@
 from jax.sharding import PartitionSpec as P
 
 CHUNKS = 2
+SHARES = 2
 FIELD_BOUND = 6.0
 CODE_TOP = 32767.0
 VMEM_LIMIT = 24 * 1024 * 1024
-STAGE_VMEM_LIMIT = 36 * 1024 * 1024
+STAGE_VMEM_LIMIT = 46 * 1024 * 1024
+PACK_VMEM_LIMIT = 53 * 1024 * 1024
+LATER_VMEM_LIMIT = 50 * 1024 * 1024
 
 
 def dft_tables(parts, local, order, inverse):
@@ -36,16 +39,50 @@
     return np.stack([high, low], axis=1)
 
 
-def pack_kernel(rhs, fields_ref, all_ref, *chunk_refs):
-    rows = fields_ref.shape[0] // rhs
-    per = rhs // len(chunk_refs)
-    for r in range(rhs):
-        x = fields_ref[pl.ds(r, rows, stride=rhs), :]
+def code_rows(held, chunk_ref, all_ref, first):
+    per, rows = chunk_ref.shape[:2]
+    for r in range(per):
+        x = held[pl.ds(r, rows, stride=per), :]
         root = jnp.sqrt(jnp.sqrt(jnp.abs(x) * (1.0 / FIELD_BOUND)))
         code = jnp.round(jnp.where(x < 0, -root, root) * CODE_TOP)
         code = code.astype(jnp.int32).astype(jnp.int16)
-        all_ref[r] = code
-        chunk_refs[r // per][r % per] = code
+        chunk_ref[r] = code
+        if all_ref is not None:
+            all_ref[first + r] = code
+
+
+def chunk_copy(fields_ref, held, per, chunk, sem):
+    rows, _, nodes = fields_ref.shape
+    return pltpu.make_async_copy(
+        fields_ref.at[:, pl.ds(chunk * per, per), :], held.reshape(rows, per, nodes), sem
+    )
+
+
+def first_pack_kernel(fields_ref, chunk_ref, held, sem):
+    copy = chunk_copy(fields_ref, held, chunk_ref.shape[0], 0, sem)
+    copy.start()
+    copy.wait()
+    code_rows(held, chunk_ref, None, 0)
+
+
+def later_pack_kernel(az_ref, fields_ref, tables_ref, first_ref, *refs):
+    chunk_refs, (all_ref, forward_out, back_out, held, sems) = refs[:-5], refs[-5:]
+    per = first_ref.shape[0]
+    tables = [
+        pltpu.make_async_copy(tables_ref.at[az_ref[0], 0], forward_out, sems.at[0]),
+        pltpu.make_async_copy(tables_ref.at[az_ref[0], 1], back_out, sems.at[1]),
+    ]
+    for index, chunk_ref in enumerate(chunk_refs):
+        copy = chunk_copy(fields_ref, held, per, index + 1, sems.at[2])
+        copy.start()
+        if index == 0:
+            for table in tables:
+                table.start()
+            all_ref[:per] = first_ref[...]
+        copy.wait()
+        code_rows(held, chunk_ref, all_ref, (index + 1) * per)
+    for table in tables:
+        table.wait()
 
 
 def decoded(code):
@@ -79,43 +116,43 @@
         modes_ref[k] = jnp.concatenate([real, imag], axis=0).astype(jnp.bfloat16)
 
 
-def stage_kernel(ring, place_ref, cols_ref, count_ref, tiles_ref, forward_ref, back_ref,
-                 tiles_out, forward_out, back_out, slot_out, sems):
-    az, place = place_ref[0], place_ref[1]
-    modes = tiles_ref.shape[0]
-    copies = [
-        pltpu.make_async_copy(forward_ref.at[az], forward_out, sems.at[0]),
-        pltpu.make_async_copy(back_ref.at[az], back_out, sems.at[1]),
-        pltpu.make_async_copy(tiles_ref, tiles_out, sems.at[2]),
-    ]
-    for copy in copies:
-        copy.start()
+def stage_kernel(first, tiles_ref, out_ref, sem):
+    share = out_ref.shape[0] - 1
+    copy = pltpu.make_async_copy(tiles_ref.at[pl.ds(first, share)], out_ref.at[pl.ds(0, share)], sem)
+    copy.start()
+    out_ref[share] = jnp.zeros(out_ref.shape[1:], out_ref.dtype)
+    copy.wait()
+
+
+def find_kernel(ring, shares, place_ref, cols_ref, count_ref, tiles_ref, out_ref, slot_ref, sem):
+    slots, modes = cols_ref.shape
+    share = out_ref.shape[0] - 1
+    copy = pltpu.make_async_copy(tiles_ref.at[pl.ds(0, share)], out_ref.at[pl.ds(0, share)], sem)
+    copy.start()
+    out_ref[share] = jnp.zeros(out_ref.shape[1:], out_ref.dtype)
+    place = place_ref[0]
     even = lax.rem(place, 2) == 0
     side = jnp.where(even, place + 1, place - 1)
     far = lax.rem(jnp.where(even, place - 1, place + 1) + ring, ring)
 
     def find(k, carry):
+        base = lax.rem(k, modes // shares) * slots
         for role, wanted in enumerate((place, side, far)):
             slot = jnp.where(cols_ref[0, k] == wanted, 0, jnp.where(cols_ref[1, k] == wanted, 1, 2))
-            slot_out[role * modes + k] = jnp.where(slot < count_ref[k], slot, -1)
+            slot_ref[role * modes + k] = jnp.where(slot < count_ref[k], base + slot, share)
         return carry
 
     lax.fori_loop(0, modes, find, 0)
-    for copy in copies:
-        copy.wait()
-
-
-def tile_product(slot_ref, tiles_ref, k, roles, values):
-    modes, block = tiles_ref.shape[0], tiles_ref.shape[-1]
+    copy.wait()
+
+
+def tile_product(slot_ref, tile_refs, modes, k, roles, values):
+    tiles_ref = tile_refs[k * len(tile_refs) // modes]
+    block = tiles_ref.shape[-1]
     rhs = values[0].shape[0] // 2
-    tiles, kept = [], []
-    for role, value in zip(roles, values):
-        slot = slot_ref[role * modes + k]
-        tiles.append(tiles_ref[k, 0, jnp.maximum(slot, 0)].reshape(2 * block, block))
-        kept.append(jnp.where(slot < 0, jnp.zeros_like(value), value))
     product = lax.dot_general(
-        jnp.concatenate(kept, axis=1),
-        jnp.concatenate(tiles, axis=1),
+        jnp.concatenate(values, axis=1),
+        jnp.concatenate([tiles_ref[slot_ref[role * modes + k]] for role in roles], axis=1),
         (((1,), (1,)), ((), ())),
         preferred_element_type=jnp.float32,
     )
@@ -124,19 +161,21 @@
     return real, imag
 
 
-def inner_kernel(slot_ref, tiles_ref, own_ref, side_ref, part_ref):
+def inner_kernel(slot_ref, *refs):
+    tile_refs, (own_ref, side_ref, part_ref) = refs[:-3], refs[-3:]
     modes, both = own_ref.shape[:2]
     for k in range(modes):
-        real, imag = tile_product(slot_ref, tiles_ref, k, (0, 1), [own_ref[k], side_ref[k]])
+        real, imag = tile_product(slot_ref, tile_refs, modes, k, (0, 1), [own_ref[k], side_ref[k]])
         part_ref[k * both : k * both + both // 2, :] = real
         part_ref[k * both + both // 2 : (k + 1) * both, :] = imag
 
 
-def outer_kernel(slot_ref, tiles_ref, far_ref, part_ref, near_ref, held):
+def outer_kernel(slot_ref, *refs):
+    tile_refs, (far_ref, part_ref, near_ref, held) = refs[:-4], refs[-4:]
     modes, both = far_ref.shape[:2]
     rhs = both // 2
     for k in range(modes):
-        real, imag = tile_product(slot_ref, tiles_ref, k, (2,), [far_ref[k]])
+        real, imag = tile_product(slot_ref, tile_refs, modes, k, (2,), [far_ref[k]])
         at_real, at_imag = slice(k * both, k * both + rhs), slice(k * both + rhs, (k + 1) * both)
         held[at_real, :] = real + part_ref[at_real, :]
         held[at_imag, :] = imag + part_ref[at_imag, :]
@@ -191,95 +230,131 @@
     rows = 2 * local
     paired = parts == 4
     order = (lambda a, j: a ^ j) if paired else (lambda a, j: j)
-    forward_tables = jnp.asarray(dft_tables(parts, local, order, False))
-    back_tables = jnp.asarray(dft_tables(parts, local, order, True))
+    tables = jnp.asarray(
+        np.stack([dft_tables(parts, local, order, False), dft_tables(parts, local, order, True)], axis=1)
+    )
+    table_shape = jax.ShapeDtypeStruct(tables.shape[2:], jnp.bfloat16)
     flat_fields = fields.reshape(rows * rhs, nodes)
+    cut_fields = fields.reshape(rows, rhs, nodes)
     flat_impedance = impedance.reshape(rows, nodes)
+    flat_tiles = tile_data.reshape(local * slots, 2 * block, block)
+    share = local * slots // SHARES
+    tiles_shape = jax.ShapeDtypeStruct((share + 1, 2 * block, block), tile_data.dtype)
     params = pltpu.CompilerParams(vmem_limit_bytes=VMEM_LIMIT)
+    pack_params = pltpu.CompilerParams(vmem_limit_bytes=PACK_VMEM_LIMIT)
+    later_params = pltpu.CompilerParams(vmem_limit_bytes=LATER_VMEM_LIMIT)
+    stage_params = pltpu.CompilerParams(vmem_limit_bytes=STAGE_VMEM_LIMIT)
     vmem, smem = pl.BlockSpec(memory_space=pltpu.VMEM), pl.BlockSpec(memory_space=pltpu.SMEM)
     hbm = pl.BlockSpec(memory_space=pltpu.HBM)
     move = 16 * fields.size
     multiply = 4 * rows * rows * parts * per * nodes
-
-    coded, *chunks = pl.pallas_call(
-        functools.partial(pack_kernel, rhs),
-        out_shape=[jax.ShapeDtypeStruct((rhs, rows, nodes), jnp.int16)]
-        + [jax.ShapeDtypeStruct((per, rows, nodes), jnp.int16)] * CHUNKS,
+    chunk_shape = jax.ShapeDtypeStruct((per, rows, nodes), jnp.int16)
+
+    first = pl.pallas_call(
+        first_pack_kernel,
+        out_shape=chunk_shape,
+        in_specs=[hbm],
+        out_specs=vmem,
+        scratch_shapes=[pltpu.VMEM((rows * per, nodes), jnp.float32), pltpu.SemaphoreType.DMA],
+        cost_estimate=cost(0, move // 2),
+        compiler_params=pack_params,
+        name="pack",
+    )(cut_fields)
+    az = lax.axis_index("az").astype(jnp.int32)[None]
+    place = lax.axis_index("curve").astype(jnp.int32)[None]
+    *later, coded, forward_table, back_table = pl.pallas_call(
+        later_pack_kernel,
+        out_shape=[chunk_shape] * (CHUNKS - 1)
+        + [jax.ShapeDtypeStruct((rhs, rows, nodes), jnp.int16), table_shape, table_shape],
+        in_specs=[smem, hbm, hbm, vmem],
+        out_specs=[vmem] * (CHUNKS + 2),
+        scratch_shapes=[pltpu.VMEM((rows * per, nodes), jnp.float32), pltpu.SemaphoreType.DMA((3,))],
         cost_estimate=cost(0, move),
-        compiler_params=params,
-        name="pack",
-    )(flat_fields)
-
-    place = jnp.stack([lax.axis_index("az"), lax.axis_index("curve")]).astype(jnp.int32)
-    place = after(place, coded)
-    tiles, forward_table, back_table, slot = pl.pallas_call(
-        functools.partial(stage_kernel, ring),
-        out_shape=[
-            jax.ShapeDtypeStruct(tile_data.shape, tile_data.dtype),
-            jax.ShapeDtypeStruct(forward_tables.shape[1:], jnp.bfloat16),
-            jax.ShapeDtypeStruct(back_tables.shape[1:], jnp.bfloat16),
-            jax.ShapeDtypeStruct((slots * local,), jnp.int32),
-        ],
-        in_specs=[smem, smem, smem, hbm, hbm, hbm],
-        out_specs=[vmem, vmem, vmem, smem],
-        scratch_shapes=[pltpu.SemaphoreType.DMA((3,))],
-        cost_estimate=cost(0, 2 * tile_data.size),
-        compiler_params=pltpu.CompilerParams(vmem_limit_bytes=STAGE_VMEM_LIMIT),
-        name="stage",
-    )(place, tile_cols[:, 0, :].T, tile_count.reshape(local), tile_data, forward_tables, back_tables)
+        compiler_params=later_params,
+        name="later",
+    )(az, cut_fields, tables, first)
+    chunks = [first] + later
+
+    peer = lax.ppermute(coded, "az", PEER) if paired else None
+    tiles = []
+    head, slot = pl.pallas_call(
+        functools.partial(find_kernel, ring, SHARES),
+        out_shape=[tiles_shape, jax.ShapeDtypeStruct((slots * local,), jnp.int32)],
+        in_specs=[smem, smem, smem, hbm],
+        out_specs=[vmem, smem],
+        scratch_shapes=[pltpu.SemaphoreType.DMA],
+        cost_estimate=cost(0, 2 * tile_data.size // SHARES),
+        compiler_params=stage_params,
+        name="find",
+    )(after(place, coded), tile_cols[:, 0, :].T, tile_count.reshape(local), flat_tiles)
+    tiles.append(head)
 
     sides = [(i, i ^ 1) for i in range(ring)]
     onward = [(i, (i + 2 if i % 2 == 0 else i - 2) % ring) for i in range(ring)]
-    peer = lax.ppermute(coded, "az", PEER) if paired else None
-    owns, ready = [], (tiles,)
+    owns, ready = [], (head,)
     for index, chunk in enumerate(chunks):
         if paired:
             across = lax.ppermute(after(chunk, *ready) if index else chunk, "az", ACROSS)
-            across = after(across, *ready) if index == 0 else after(across, owns[-1])
+            across = after(across, *ready, *tiles[1:])
             ready = (across,)
             sources = [coded, peer, across, lax.ppermute(across, "az", PEER)]
             firsts = (index * per, index * per, 0, 0)
         else:
             every = lax.all_gather(chunk, "az")
             sources, firsts = [every[j] for j in range(parts)], (0,) * parts
-        owns.append(
-            pl.pallas_call(
-                functools.partial(forward_kernel, firsts),
-                out_shape=jax.ShapeDtypeStruct((local, 2 * per, nodes), jnp.bfloat16),
-                in_specs=[vmem] * (1 + parts),
-                out_specs=vmem,
-                scratch_shapes=[pltpu.VMEM((per * rows, nodes), jnp.float32)],
-                cost_estimate=cost(3 * multiply, move),
-                compiler_params=params,
-                name="forward",
-            )(forward_table, *sources)
-        )
-
-    nears = []
+        own = pl.pallas_call(
+            functools.partial(forward_kernel, firsts),
+            out_shape=jax.ShapeDtypeStruct((local, 2 * per, nodes), jnp.bfloat16),
+            in_specs=[vmem] * (1 + parts),
+            out_specs=vmem,
+            scratch_shapes=[pltpu.VMEM((per * rows, nodes), jnp.float32)],
+            cost_estimate=cost(3 * multiply, move),
+            compiler_params=params,
+            name="forward",
+        )(forward_table, *sources)
+        owns.append(own)
+        if index == 0:
+            for place_of in range(1, SHARES):
+                tail = pl.pallas_call(
+                    functools.partial(stage_kernel, place_of * share),
+                    out_shape=tiles_shape,
+                    in_specs=[hbm],
+                    out_specs=vmem,
+                    scratch_shapes=[pltpu.SemaphoreType.DMA],
+                    cost_estimate=cost(0, 2 * tile_data.size // SHARES),
+                    compiler_params=stage_params,
+                    name="stage",
+                )(after(flat_tiles, own))
+                tiles.append(tail)
+
+    halo = []
     for own in owns:
         side = lax.ppermute(own, "curve", sides)
         far = lax.ppermute(side, "curve", onward)
         inner = pl.pallas_call(
             inner_kernel,
             out_shape=jax.ShapeDtypeStruct((local * 2 * per, nodes), jnp.float32),
-            in_specs=[smem] + [vmem] * 3,
+            in_specs=[smem] + [vmem] * (2 + SHARES),
             out_specs=vmem,
             cost_estimate=cost(0, tile_data.size),
             compiler_params=params,
             name="inner",
-        )(slot, tiles, own, side)
-        far = after(far, inner)
+        )(slot, *tiles, own, side)
+        halo.append((inner, after(far, inner)))
+
+    nears = []
+    for inner, far in halo:
         nears.append(
             pl.pallas_call(
                 outer_kernel,
                 out_shape=jax.ShapeDtypeStruct((per, rows, nodes), jnp.bfloat16),
-                in_specs=[smem] + [vmem] * 3,
+                in_specs=[smem] + [vmem] * (2 + SHARES),
                 out_specs=vmem,
                 scratch_shapes=[pltpu.VMEM((local * 2 * per, nodes), jnp.float32)],
                 cost_estimate=cost(0, tile_data.size // 2),
                 compiler_params=params,
                 name="outer",
-            )(slot, tiles, far, inner)
+            )(slot, *tiles, far, inner)
         )
 
     out = None
@@ -288,6 +363,8 @@
             across = lax.ppermute(near, "az", ACROSS)
             if out is not None:
                 across, out = lax.optimization_barrier((across, out))
+            elif CHUNKS > 1:
+                across = after(across, halo[-1][0])
             sources = [near, lax.ppermute(near, "az", PEER), across, lax.ppermute(across, "az", PEER)]
         else:
             every = lax.all_gather(near, "az")

time: 62 us -> 56.5 us (0.911)
  waiting for transfers between devices: 23 us -> 17.2 us
  Pallas kernels: 21.9 us -> 24.4 us
  local copies, waits for them, and re-layouts: 5.02 us -> 2.57 us
    ppermute x2, waiting for transfers between devices: 12.6 us -> 6.99 us  [on_device(): across = lax.ppermute(near, 'az', ACROSS)]
    ppermute x2, waiting for transfers between devices: 4.17 us -> 1.38 us  [on_device(): lax.ppermute(after(chunk, *ready) if index else chunk, 'az', ACROSS)]
    pallas_call x2 -> x4, Pallas kernels: 6.68 us -> 9.29 us  [the longest x1 3.96 us: on_device(): pl.pallas_call(functools.partial(find_kernel, ring, SHARES), out_shape=[t...]
    ppermute x2, waiting for transfers between devices: 0.25 us -> 2.74 us  [on_device(): far = lax.ppermute(side, 'curve', onward)]
    unnamed x13 -> x9, local copies, waits for them, and re-layouts: 5.02 us -> 2.57 us
  transfers between devices with their start and end apart: 15 -> 15, of which waited for: 8 -> 9; matrix products, arithmetic and copies ran while one was open for 1% -> 1% of each run, Pallas kernels for 32% -> 38%
where the time goes in v3:
time: 56.5 us; the launch traced here: 56.2 us
  Pallas kernels  24.4 us (43%)
  waiting for transfers between devices  17.2 us (30%)
  starting transfers between devices  12 us (21%)
  local copies, waits for them, and re-layouts  2.57 us (5%)
    ppermute x2, waiting for transfers between devices, on_device(): across = lax.ppermute(near, 'az', ACROSS)  6.99 us
    pallas_call x2, Pallas kernels, on_device(): pl.pallas_call(inner_kernel, out_shape=jax.ShapeDtypeStruct((local * 2 *...  5.65 us
    ppermute x2, starting transfers between devices, on_device(): side = lax.ppermute(own, 'curve', sides)  5.21 us
    pallas_call x1, Pallas kernels, on_device(): pl.pallas_call(functools.partial(find_kernel, ring, SHARES), out_shape=[t...  3.96 us
    pallas_call x2, Pallas kernels, on_device(): pl.pallas_call(outer_kernel, out_shape=jax.ShapeDtypeStruct((per, rows, n...  3.56 us
    ppermute x2, waiting for transfers between devices, on_device(): side = lax.ppermute(own, 'curve', sides)  3.37 us
    pallas_call x2, Pallas kernels, on_device(): pl.pallas_call(functools.partial(back_kernel, parts, rhs, index), out_sha...  3.22 us
    ppermute x2, starting transfers between devices, on_device(): lax.ppermute(after(chunk, *ready) if index else chunk, 'az', ACROSS)  3.02 us
  transfers between devices with their start and end apart: 15, of which 9 were waited for; matrix products, arithmetic and copies ran while one was open for 1% of the time, Pallas kernels for 38%

profile of v3, /device:TPU:0, one launch (start us, length us, event | category | flops | bytes accessed | tf_op | source)
XLA Modules:
  0.0 56.2 jit_solution(13659170327536451330)
XLA Ops:
  0.0 1.4 %pack.1.first_ref = s16[8,128,128]{2,1,0:T(8,128)(2,1)S(1)} custom-call(f32[128,16,128]{2,1,0:T(8,128)} %bitcast.13), custom_call_target="tpu_custom_call" | custom-call | bytes 2097152 | tf_op jit(solution)/shard_map/pack/pallas_call | solution.py:253
  1.5 3.0 %collective-permute-start.1 = (s16[8,128,128]{2,1,0:T(8,128)(2,1)S(1)}, s16[8,128,128]{2,1,0:T(8,128)(2,1)S(1)}, u32[]{:S(2)}, u32[]{:S(2)}) collective-permute-start(s16[8,128,128]{2,1,0:T(8,128)(2,1)S(1)} %pack.1.first_ref), channel_id=1, source_target_pairs={{0,16},{8,24},{16,0},{24,8},{1,17},{9,25},{17,1},{25,9},{2,18},{10... | collective-permute-start | bytes 786440 | tf_op jit(solution)/shard_map/ppermute | solution.py:297
  4.5 0.0 copy-start
  4.5 1.2 %copy-done = f32[2,64,16,128]{3,2,1,0:T(8,128)S(1)} copy-done((f32[2,64,16,128]{3,2,1,0:T(8,128)S(1)}, f32[2,64,16,128]{3,2,1,0:T(8,128)}, u32[]{:S(2)}) %copy-start) | copy-done | bytes 1048600
  5.7 1.1 %later.1 = (s16[8,128,128]{2,1,0:T(8,128)(2,1)S(1)}, s16[16,128,128]{2,1,0:T(8,128)(2,1)S(1)}, bf16[2,128,512]{2,1,0:T(8,128)(2,1)S(1)}, bf16[2,128,512]{2,1,0:T(8,128)(2,1)S(1)}) custom-call(s32[1]{0:T(128)} %bitcast.az_ref, f32[128,16,128]{2,1,0:T(8,128)S(1)} %bitcast.14, bf16[4,2,2,128,512]{4,3,2,1,0:T(8,128)(2,1)} %constant.10.clone.tables_ref, ...), custom_call_target="tpu_custom_call" | custom-call | bytes 4194304 | tf_op jit(solution)/shard_map/later/pallas_call | solution.py:265
  6.8 0.1 collective-permute-start
  6.9 0.7 %copy.10 = s32[64,1,3]{0,2,1:T(4,128)S(1)} copy(s32[64,1,3]{0,1,2:T(1,128)} %param.9) | data formatting | bytes 1536
  7.5 0.0 copy-start.3
  7.6 0.7 %copy-done.3 = s32[64,1]{0,1:T(1,128)S(1)} copy-done((s32[64,1]{0,1:T(1,128)S(1)}, s32[64,1]{0,1:T(1,128)}, u32[]{:S(2)}) %copy-start.3) | copy-done | bytes 280
  8.2 4.0 %find.1 = (bf16[97,256,128]{2,1,0:T(8,128)(2,1)S(1)}, s32[192]{0:T(256)S(1)}) custom-call(s32[1]{0:T(128)} %bitcast.4.place_ref, s32[3,64]{1,0:T(4,128)S(1)} %bitcast.19, s32[64]{0:T(128)S(1)} %bitcast.20, bf16[192,256,128]{2,1,0:T(8,128)(2,1)} %bitcast.21), custom_call_target="tpu_custom_call" | custom-call | bytes 6291456 | tf_op jit(solution)/shard_map/find/pallas_call | solution.py:280
  12.2 0.0 collective-permute-done.1.refs_2_
  12.2 0.6 collective-permute-start.2
  12.7 0.0 collective-permute-start.3
  12.8 0.0 collective-permute-done.refs_1_
  12.8 1.1 %collective-permute-done.2.refs_3_ = s16[8,128,128]{2,1,0:T(8,128)(2,1)S(1)} collective-permute-done((s16[8,128,128]{2,1,0:T(8,128)(2,1)S(1)}, s16[8,128,128]{2,1,0:T(8,128)(2,1)S(1)}, u32[]{:S(2)}, u32[]{:S(2)}) %collective-permute-start.2) | collective-permute-done | bytes 262176 | tf_op jit(solution)/shard_map/ppermute | solution.py:300
  13.9 1.3 %forward.2.refs_2_ = bf16[64,16,128]{2,1,0:T(8,128)(2,1)S(1)} custom-call(bf16[2,128,512]{2,1,0:T(8,128)(2,1)S(1)} %get-tuple-element.26.table_ref, s16[16,128,128]{2,1,0:T(8,128)(2,1)S(1)} %get-tuple-element.22.refs_0_, s16[16,128,128]{2,1,0:T(8,128)(2,1)S(1)} %collective-permute-done.refs_1_, s16[8,128,128]{2,1,0:T(8,128)(2,1)S(1)} %collective-permute-done.1.refs_2_, ...), custom_call_target="tpu_custom_call" | custom-call | flops 805306368 | bytes 4194304 | tf_op jit(solution)/shard_map/forward/pallas_call | solution.py:305
  15.3 1.6 %collective-permute-start.9 = (bf16[64,16,128]{2,1,0:T(8,128)(2,1)S(1)}, bf16[64,16,128]{2,1,0:T(8,128)(2,1)S(1)}, u32[]{:S(2)}, u32[]{:S(2)}) collective-permute-start(bf16[64,16,128]{2,1,0:T(8,128)(2,1)S(1)} %forward.2.refs_2_), channel_id=1, source_target_pairs={{0,1},{1,0},{2,3},{3,2},{4,5},{5,4},{6,7},{7,6},{8,9},{9,8},{10,11... | collective-permute-start | bytes 786440 | tf_op jit(solution)/shard_map/ppermute | solution.py:332
  16.9 2.8 %stage.1.refs_1_ = bf16[97,256,128]{2,1,0:T(8,128)(2,1)S(1)} custom-call(bf16[192,256,128]{2,1,0:T(8,128)(2,1)} %bitcast.22), custom_call_target="tpu_custom_call" | custom-call | bytes 6291456 | tf_op jit(solution)/shard_map/stage/pallas_call | solution.py:318
  19.7 1.4 %collective-permute-done.3.refs_2_ = s16[8,128,128]{2,1,0:T(8,128)(2,1)S(1)} collective-permute-done((s16[8,128,128]{2,1,0:T(8,128)(2,1)S(1)}, s16[8,128,128]{2,1,0:T(8,128)(2,1)S(1)}, u32[]{:S(2)}, u32[]{:S(2)}) %collective-permute-start.3) | collective-permute-done | bytes 262176 | tf_op jit(solution)/shard_map/ppermute | solution.py:297
  21.0 0.0 collective-permute-start.4
  21.0 2.9 %collective-permute-done.9.refs_3_ = bf16[64,16,128]{2,1,0:T(8,128)(2,1)S(1)} collective-permute-done((bf16[64,16,128]{2,1,0:T(8,128)(2,1)S(1)}, bf16[64,16,128]{2,1,0:T(8,128)(2,1)S(1)}, u32[]{:S(2)}, u32[]{:S(2)}) %collective-permute-start.9) | collective-permute-done | bytes 262176 | tf_op jit(solution)/shard_map/ppermute | solution.py:332
  23.9 1.6 %collective-permute-start.10 = (bf16[64,16,128]{2,1,0:T(8,128)(2,1)S(1)}, bf16[64,16,128]{2,1,0:T(8,128)(2,1)S(1)}, u32[]{:S(2)}, u32[]{:S(2)}) collective-permute-start(bf16[64,16,128]{2,1,0:T(8,128)(2,1)S(1)} %collective-permute-done.9.refs_3_), channel_id=1, source_target_pairs={{0,2},{1,7},{2,4},{3,1},{4,6},{5,3},{6,0},{7,5},{8,10},{9,15},{10,... | collective-permute-start | bytes 786440 | tf_op jit(solution)/shard_map/ppermute | solution.py:333
  25.5 0.0 collective-permute-done.4.refs_3_
  25.5 1.3 %forward.3.refs_2_ = bf16[64,16,128]{2,1,0:T(8,128)(2,1)S(1)} custom-call(bf16[2,128,512]{2,1,0:T(8,128)(2,1)S(1)} %get-tuple-element.26.table_ref, s16[16,128,128]{2,1,0:T(8,128)(2,1)S(1)} %get-tuple-element.22.refs_0_, s16[16,128,128]{2,1,0:T(8,128)(2,1)S(1)} %collective-permute-done.refs_1_, s16[8,128,128]{2,1,0:T(8,128)(2,1)S(1)} %collective-permute-done.3.refs_2_, ...), custom_call_target="tpu_custom_call" | custom-call | flops 805306368 | bytes 4194304 | tf_op jit(solution)/shard_map/forward/pallas_call | solution.py:305
  26.8 3.6 %collective-permute-start.5 = (bf16[64,16,128]{2,1,0:T(8,128)(2,1)S(1)}, bf16[64,16,128]{2,1,0:T(8,128)(2,1)S(1)}, u32[]{:S(2)}, u32[]{:S(2)}) collective-permute-start(bf16[64,16,128]{2,1,0:T(8,128)(2,1)S(1)} %forward.3.refs_2_), channel_id=1, source_target_pairs={{0,1},{1,0},{2,3},{3,2},{4,5},{5,4},{6,7},{7,6},{8,9},{9,8},{10,11... | collective-permute-start | bytes 786440 | tf_op jit(solution)/shard_map/ppermute | solution.py:332
  30.5 2.8 %inner.3.refs_3_ = f32[1024,128]{1,0:T(8,128)S(1)} custom-call(s32[192]{0:T(256)S(1)} %get-tuple-element.24.slot_ref, bf16[97,256,128]{2,1,0:T(8,128)(2,1)S(1)} %get-tuple-element.25.refs_0_, bf16[97,256,128]{2,1,0:T(8,128)(2,1)S(1)} %stage.1.refs_1_, bf16[64,16,128]{2,1,0:T(8,128)(2,1)S(1)} %forward.2.refs_2_, ...), custom_call_target="tpu_custom_call" | custom-call | bytes 6291456 | tf_op jit(solution)/shard_map/inner/pallas_call | solution.py:334
  33.3 0.3 collective-permute-done.10.refs_2_
  33.5 1.8 %outer.3.refs_0_ = bf16[8,128,128]{2,1,0:T(8,128)(2,1)S(1)} custom-call(s32[192]{0:T(256)S(1)} %get-tuple-element.24.slot_ref, bf16[97,256,128]{2,1,0:T(8,128)(2,1)S(1)} %get-tuple-element.25.refs_0_, bf16[97,256,128]{2,1,0:T(8,128)(2,1)S(1)} %stage.1.refs_1_, bf16[64,16,128]{2,1,0:T(8,128)(2,1)S(1)} %collective-permute-done.10.refs_2_, ...), custom_call_target="tpu_custom_call" | custom-call | bytes 3145728 | tf_op jit(solution)/shard_map/outer/pallas_call | solution.py:348
  35.3 0.4 collective-permute-start.12
  35.7 0.5 collective-permute-done.5.refs_3_
  36.2 0.0 collective-permute-start.6
  36.2 0.0 collective-permute-start.11
  36.2 2.8 %inner.2.refs_3_ = f32[1024,128]{1,0:T(8,128)S(1)} custom-call(s32[192]{0:T(256)S(1)} %get-tuple-element.24.slot_ref, bf16[97,256,128]{2,1,0:T(8,128)(2,1)S(1)} %get-tuple-element.25.refs_0_, bf16[97,256,128]{2,1,0:T(8,128)(2,1)S(1)} %stage.1.refs_1_, bf16[64,16,128]{2,1,0:T(8,128)(2,1)S(1)} %forward.3.refs_2_, ...), custom_call_target="tpu_custom_call" | custom-call | bytes 6291456 | tf_op jit(solution)/shard_map/inner/pallas_call | solution.py:334
  39.0 0.0 copy-start.1
  39.0 0.0 copy-start.2
  39.0 3.3 %collective-permute-done.12.refs_2_ = bf16[8,128,128]{2,1,0:T(8,128)(2,1)S(1)} collective-permute-done((bf16[8,128,128]{2,1,0:T(8,128)(2,1)S(1)}, bf16[8,128,128]{2,1,0:T(8,128)(2,1)S(1)}, u32[]{:S(2)}, u32[]{:S(2)}) %collective-permute-start.12) | collective-permute-done | bytes 262176 | tf_op jit(solution)/shard_map/ppermute | solution.py:363
  42.4 0.0 collective-permute-start.13
  42.4 2.5 %collective-permute-done.6.refs_2_ = bf16[64,16,128]{2,1,0:T(8,128)(2,1)S(1)} collective-permute-done((bf16[64,16,128]{2,1,0:T(8,128)(2,1)S(1)}, bf16[64,16,128]{2,1,0:T(8,128)(2,1)S(1)}, u32[]{:S(2)}, u32[]{:S(2)}) %collective-permute-start.6) | collective-permute-done | bytes 262176 | tf_op jit(solution)/shard_map/ppermute | solution.py:333
  44.9 1.8 %outer.2.refs_0_ = bf16[8,128,128]{2,1,0:T(8,128)(2,1)S(1)} custom-call(s32[192]{0:T(256)S(1)} %get-tuple-element.24.slot_ref, bf16[97,256,128]{2,1,0:T(8,128)(2,1)S(1)} %get-tuple-element.25.refs_0_, bf16[97,256,128]{2,1,0:T(8,128)(2,1)S(1)} %stage.1.refs_1_, bf16[64,16,128]{2,1,0:T(8,128)(2,1)S(1)} %collective-permute-done.6.refs_2_, ...), custom_call_target="tpu_custom_call" | custom-call | bytes 3145728 | tf_op jit(solution)/shard_map/outer/pallas_call | solution.py:348
  46.6 1.1 %collective-permute-start.8 = (bf16[8,128,128]{2,1,0:T(8,128)(2,1)S(1)}, bf16[8,128,128]{2,1,0:T(8,128)(2,1)S(1)}, u32[]{:S(2)}, u32[]{:S(2)}) collective-permute-start(bf16[8,128,128]{2,1,0:T(8,128)(2,1)S(1)} %outer.2.refs_0_), channel_id=1, source_target_pairs={{0,16},{8,24},{16,0},{24,8},{1,17},{9,25},{17,1},{25,9},{2,18},{10... | collective-permute-start | bytes 786440 | tf_op jit(solution)/shard_map/ppermute | solution.py:363
  47.8 0.0 collective-permute-start.7
  47.8 0.0 collective-permute-done.11.refs_1_
  47.8 0.0 collective-permute-done.13.refs_3_
  47.8 0.0 copy-done.1
  47.8 0.0 copy-done.2
  47.8 1.6 %back.2.refs_4_ = f32[128,16,128]{2,1,0:T(8,128)} custom-call(bf16[2,128,512]{2,1,0:T(8,128)(2,1)S(1)} %get-tuple-element.21.table_ref, f32[2048,128]{1,0:T(8,128)S(1)} %bitcast.15, f32[128,128]{1,0:T(8,128)S(1)} %bitcast.17, bf16[8,128,128]{2,1,0:T(8,128)(2,1)S(1)} %outer.3.refs_0_, bf16[8,128,128]{2,1,0:T(8,128)(2,1)S(1)} %collective-permute-done.11.refs_1_, ...), custom_call_target="tpu_custom_call" | custom-call | flops 536870912 | bytes 4194304 | tf_op jit(solution)/shard_map/back/pallas_call | solution.py:373
  49.4 3.7 %collective-permute-done.8.refs_2_ = bf16[8,128,128]{2,1,0:T(8,128)(2,1)S(1)} collective-permute-done((bf16[8,128,128]{2,1,0:T(8,128)(2,1)S(1)}, bf16[8,128,128]{2,1,0:T(8,128)(2,1)S(1)}, u32[]{:S(2)}, u32[]{:S(2)}) %collective-permute-start.8) | collective-permute-done | bytes 262176 | tf_op jit(solution)/shard_map/ppermute | solution.py:363
  53.1 0.0 collective-permute-start.14
  53.1 0.0 collective-permute-done.7.refs_1_
  53.1 1.5 %collective-permute-done.14.refs_3_ = bf16[8,128,128]{2,1,0:T(8,128)(2,1)S(1)} collective-permute-done((bf16[8,128,128]{2,1,0:T(8,128)(2,1)S(1)}, bf16[8,128,128]{2,1,0:T(8,128)(2,1)S(1)}, u32[]{:S(2)}, u32[]{:S(2)}) %collective-permute-start.14) | collective-permute-done | bytes 262176 | tf_op jit(solution)/shard_map/ppermute | solution.py:368
  54.6 1.6 %back.3 = f32[128,16,128]{2,1,0:T(8,128)} custom-call(bf16[2,128,512]{2,1,0:T(8,128)(2,1)S(1)} %get-tuple-element.21.table_ref, f32[2048,128]{1,0:T(8,128)S(1)} %bitcast.16, f32[128,128]{1,0:T(8,128)S(1)} %bitcast.18, bf16[8,128,128]{2,1,0:T(8,128)(2,1)S(1)} %outer.2.refs_0_, ...), custom_call_target="tpu_custom_call", output_to_operand_aliasing={{}: (7, {})} | custom-call | flops 536870912 | bytes 4194304 | tf_op jit(solution)/shard_map/back/pallas_call | solution.py:373
Async XLA Ops:
  1.5 10.7 %collective-permute-start.1 = (s16[8,128,128]{2,1,0:T(8,128)(2,1)S(1)}, s16[8,128,128]{2,1,0:T(8,128)(2,1)S(1)}, u32[]{:S(2)}, u32[]{:S(2)}) collective-permute-start(s16[8,128,128]{2,1,0:T(8,128)(2,1)S(1)} %pack.1.first_ref), channel_id=1, source_target_pairs={{0,16},{8,24},{16,0},{24,8},{1,17},{9,25},{17,1},{25,9},{2,18},{10... | collective-permute-start | bytes 786440 | tf_op jit(solution)/shard_map/ppermute | solution.py:297
  4.5 1.2 %copy-start = (f32[2,64,16,128]{3,2,1,0:T(8,128)S(1)}, f32[2,64,16,128]{3,2,1,0:T(8,128)}, u32[]{:S(2)}) copy-start(f32[2,64,16,128]{3,2,1,0:T(8,128)} %param.6) | copy-start | bytes 3145732
  6.8 6.0 %collective-permute-start = (s16[16,128,128]{2,1,0:T(8,128)(2,1)S(1)}, s16[16,128,128]{2,1,0:T(8,128)(2,1)S(1)}, u32[]{:S(2)}, u32[]{:S(2)}) collective-permute-start(s16[16,128,128]{2,1,0:T(8,128)(2,1)S(1)} %get-tuple-element.22.refs_0_), channel_id=1, source_target_pairs={{0,8},{8,0},{16,24},{24,16},{1,9},{9,1},{17,25},{25,17},{2,10},{10... | collective-permute-start | bytes 1572872 | tf_op jit(solution)/shard_map/ppermute | solution.py:278
  7.5 0.7 %copy-start.3 = (s32[64,1]{0,1:T(1,128)S(1)}, s32[64,1]{0,1:T(1,128)}, u32[]{:S(2)}) copy-start(s32[64,1]{0,1:T(1,128)} %param.10) | copy-start | bytes 772
  12.2 1.7 %collective-permute-start.2 = (s16[8,128,128]{2,1,0:T(8,128)(2,1)S(1)}, s16[8,128,128]{2,1,0:T(8,128)(2,1)S(1)}, u32[]{:S(2)}, u32[]{:S(2)}) collective-permute-start(s16[8,128,128]{2,1,0:T(8,128)(2,1)S(1)} %collective-permute-done.1.refs_2_), channel_id=1, source_target_pairs={{0,8},{8,0},{16,24},{24,16},{1,9},{9,1},{17,25},{25,17},{2,10},{10... | collective-permute-start | bytes 786440 | tf_op jit(solution)/shard_map/ppermute | solution.py:300
  12.7 8.3 %collective-permute-start.3 = (s16[8,128,128]{2,1,0:T(8,128)(2,1)S(1)}, s16[8,128,128]{2,1,0:T(8,128)(2,1)S(1)}, u32[]{:S(2)}, u32[]{:S(2)}) collective-permute-start(s16[8,128,128]{2,1,0:T(8,128)(2,1)S(1)} %get-tuple-element.30), channel_id=1, source_target_pairs={{0,16},{8,24},{16,0},{24,8},{1,17},{9,25},{17,1},{25,9},{2,18},{10... | collective-permute-start | bytes 786440 | tf_op jit(solution)/shard_map/ppermute | solution.py:297
  15.3 8.7 %collective-permute-start.9 = (bf16[64,16,128]{2,1,0:T(8,128)(2,1)S(1)}, bf16[64,16,128]{2,1,0:T(8,128)(2,1)S(1)}, u32[]{:S(2)}, u32[]{:S(2)}) collective-permute-start(bf16[64,16,128]{2,1,0:T(8,128)(2,1)S(1)} %forward.2.refs_2_), channel_id=1, source_target_pairs={{0,1},{1,0},{2,3},{3,2},{4,5},{5,4},{6,7},{7,6},{8,9},{9,8},{10,11... | collective-permute-start | bytes 786440 | tf_op jit(solution)/shard_map/ppermute | solution.py:332
  21.0 4.5 %collective-permute-start.4 = (s16[8,128,128]{2,1,0:T(8,128)(2,1)S(1)}, s16[8,128,128]{2,1,0:T(8,128)(2,1)S(1)}, u32[]{:S(2)}, u32[]{:S(2)}) collective-permute-start(s16[8,128,128]{2,1,0:T(8,128)(2,1)S(1)} %collective-permute-done.3.refs_2_), channel_id=1, source_target_pairs={{0,8},{8,0},{16,24},{24,16},{1,9},{9,1},{17,25},{25,17},{2,10},{10... | collective-permute-start | bytes 786440 | tf_op jit(solution)/shard_map/ppermute | solution.py:300
  23.9 9.6 %collective-permute-start.10 = (bf16[64,16,128]{2,1,0:T(8,128)(2,1)S(1)}, bf16[64,16,128]{2,1,0:T(8,128)(2,1)S(1)}, u32[]{:S(2)}, u32[]{:S(2)}) collective-permute-start(bf16[64,16,128]{2,1,0:T(8,128)(2,1)S(1)} %collective-permute-done.9.refs_3_), channel_id=1, source_target_pairs={{0,2},{1,7},{2,4},{3,1},{4,6},{5,3},{6,0},{7,5},{8,10},{9,15},{10,... | collective-permute-start | bytes 786440 | tf_op jit(solution)/shard_map/ppermute | solution.py:333
  26.8 9.4 %collective-permute-start.5 = (bf16[64,16,128]{2,1,0:T(8,128)(2,1)S(1)}, bf16[64,16,128]{2,1,0:T(8,128)(2,1)S(1)}, u32[]{:S(2)}, u32[]{:S(2)}) collective-permute-start(bf16[64,16,128]{2,1,0:T(8,128)(2,1)S(1)} %forward.3.refs_2_), channel_id=1, source_target_pairs={{0,1},{1,0},{2,3},{3,2},{4,5},{5,4},{6,7},{7,6},{8,9},{9,8},{10,11... | collective-permute-start | bytes 786440 | tf_op jit(solution)/shard_map/ppermute | solution.py:332
  35.3 7.0 %collective-permute-start.12 = (bf16[8,128,128]{2,1,0:T(8,128)(2,1)S(1)}, bf16[8,128,128]{2,1,0:T(8,128)(2,1)S(1)}, u32[]{:S(2)}, u32[]{:S(2)}) collective-permute-start(bf16[8,128,128]{2,1,0:T(8,128)(2,1)S(1)} %outer.3.refs_0_), channel_id=1, source_target_pairs={{0,16},{8,24},{16,0},{24,8},{1,17},{9,25},{17,1},{25,9},{2,18},{10... | collective-permute-start | bytes 786440 | tf_op jit(solution)/shard_map/ppermute | solution.py:363
  36.2 8.7 %collective-permute-start.6 = (bf16[64,16,128]{2,1,0:T(8,128)(2,1)S(1)}, bf16[64,16,128]{2,1,0:T(8,128)(2,1)S(1)}, u32[]{:S(2)}, u32[]{:S(2)}) collective-permute-start(bf16[64,16,128]{2,1,0:T(8,128)(2,1)S(1)} %collective-permute-done.5.refs_3_), channel_id=1, source_target_pairs={{0,2},{1,7},{2,4},{3,1},{4,6},{5,3},{6,0},{7,5},{8,10},{9,15},{10,... | collective-permute-start | bytes 786440 | tf_op jit(solution)/shard_map/ppermute | solution.py:333
  36.2 11.6 %collective-permute-start.11 = (bf16[8,128,128]{2,1,0:T(8,128)(2,1)S(1)}, bf16[8,128,128]{2,1,0:T(8,128)(2,1)S(1)}, u32[]{:S(2)}, u32[]{:S(2)}) collective-permute-start(bf16[8,128,128]{2,1,0:T(8,128)(2,1)S(1)} %outer.3.refs_0_), channel_id=1, source_target_pairs={{0,8},{8,0},{16,24},{24,16},{1,9},{9,1},{17,25},{25,17},{2,10},{10... | collective-permute-start | bytes 786440 | tf_op jit(solution)/shard_map/ppermute | solution.py:368
  39.0 8.8 %copy-start.1 = (f32[2,64,16,128]{3,2,1,0:T(8,128)S(1)}, f32[2,64,16,128]{3,2,1,0:T(8,128)}, u32[]{:S(2)}) copy-start(f32[2,64,16,128]{3,2,1,0:T(8,128)} %param.6) | copy-start | bytes 3145732
  39.0 8.8 %copy-start.2 = (f32[2,64,128]{2,1,0:T(8,128)S(1)}, f32[2,64,128]{2,1,0:T(8,128)}, u32[]{:S(2)}) copy-start(f32[2,64,128]{2,1,0:T(8,128)} %param.7) | copy-start | bytes 196612
  42.4 5.4 %collective-permute-start.13 = (bf16[8,128,128]{2,1,0:T(8,128)(2,1)S(1)}, bf16[8,128,128]{2,1,0:T(8,128)(2,1)S(1)}, u32[]{:S(2)}, u32[]{:S(2)}) collective-permute-start(bf16[8,128,128]{2,1,0:T(8,128)(2,1)S(1)} %collective-permute-done.12.refs_2_), channel_id=1, source_target_pairs={{0,8},{8,0},{16,24},{24,16},{1,9},{9,1},{17,25},{25,17},{2,10},{10... | collective-permute-start | bytes 786440 | tf_op jit(solution)/shard_map/ppermute | solution.py:368
  46.6 6.4 %collective-permute-start.8 = (bf16[8,128,128]{2,1,0:T(8,128)(2,1)S(1)}, bf16[8,128,128]{2,1,0:T(8,128)(2,1)S(1)}, u32[]{:S(2)}, u32[]{:S(2)}) collective-permute-start(bf16[8,128,128]{2,1,0:T(8,128)(2,1)S(1)} %outer.2.refs_0_), channel_id=1, source_target_pairs={{0,16},{8,24},{16,0},{24,8},{1,17},{9,25},{17,1},{25,9},{2,18},{10... | collective-permute-start | bytes 786440 | tf_op jit(solution)/shard_map/ppermute | solution.py:363
  47.8 5.3 %collective-permute-start.7 = (bf16[8,128,128]{2,1,0:T(8,128)(2,1)S(1)}, bf16[8,128,128]{2,1,0:T(8,128)(2,1)S(1)}, u32[]{:S(2)}, u32[]{:S(2)}) collective-permute-start(bf16[8,128,128]{2,1,0:T(8,128)(2,1)S(1)} %outer.2.refs_0_), channel_id=1, source_target_pairs={{0,8},{8,0},{16,24},{24,16},{1,9},{9,1},{17,25},{25,17},{2,10},{10... | collective-permute-start | bytes 786440 | tf_op jit(solution)/shard_map/ppermute | solution.py:368
  53.1 1.5 %collective-permute-start.14 = (bf16[8,128,128]{2,1,0:T(8,128)(2,1)S(1)}, bf16[8,128,128]{2,1,0:T(8,128)(2,1)S(1)}, u32[]{:S(2)}, u32[]{:S(2)}) collective-permute-start(bf16[8,128,128]{2,1,0:T(8,128)(2,1)S(1)} %collective-permute-done.8.refs_2_), channel_id=1, source_target_pairs={{0,8},{8,0},{16,24},{24,16},{1,9},{9,1},{17,25},{25,17},{2,10},{10... | collective-permute-start | bytes 786440 | tf_op jit(solution)/shard_map/ppermute | solution.py:368

commit v4 on v3

--- a/solution.py
+++ b/solution.py
@@ -11,11 +11,11 @@
 CHUNKS = 2
 SHARES = 2
 FIELD_BOUND = 6.0
+PARTIAL_BOUND = 4.25
 CODE_TOP = 32767.0
 VMEM_LIMIT = 24 * 1024 * 1024
-STAGE_VMEM_LIMIT = 46 * 1024 * 1024
-PACK_VMEM_LIMIT = 53 * 1024 * 1024
-LATER_VMEM_LIMIT = 50 * 1024 * 1024
+STAGE_VMEM_LIMIT = 42 * 1024 * 1024
+PACK_VMEM_LIMIT = 52 * 1024 * 1024
 
 
 def dft_tables(parts, local, order, inverse):
@@ -39,55 +39,85 @@
     return np.stack([high, low], axis=1)
 
 
-def code_rows(held, chunk_ref, all_ref, first):
-    per, rows = chunk_ref.shape[:2]
-    for r in range(per):
-        x = held[pl.ds(r, rows, stride=per), :]
-        root = jnp.sqrt(jnp.sqrt(jnp.abs(x) * (1.0 / FIELD_BOUND)))
-        code = jnp.round(jnp.where(x < 0, -root, root) * CODE_TOP)
-        code = code.astype(jnp.int32).astype(jnp.int16)
-        chunk_ref[r] = code
-        if all_ref is not None:
-            all_ref[first + r] = code
-
-
-def chunk_copy(fields_ref, held, per, chunk, sem):
-    rows, _, nodes = fields_ref.shape
-    return pltpu.make_async_copy(
-        fields_ref.at[:, pl.ds(chunk * per, per), :], held.reshape(rows, per, nodes), sem
-    )
-
-
-def first_pack_kernel(fields_ref, chunk_ref, held, sem):
-    copy = chunk_copy(fields_ref, held, chunk_ref.shape[0], 0, sem)
-    copy.start()
-    copy.wait()
-    code_rows(held, chunk_ref, None, 0)
-
-
-def later_pack_kernel(az_ref, fields_ref, tables_ref, first_ref, *refs):
-    chunk_refs, (all_ref, forward_out, back_out, held, sems) = refs[:-5], refs[-5:]
-    per = first_ref.shape[0]
+def encoded(x, bound):
+    root = jnp.sqrt(jnp.sqrt(jnp.abs(x) * (1.0 / bound)))
+    return jnp.round(jnp.where(x < 0, -root, root) * CODE_TOP).astype(jnp.int32).astype(jnp.int16)
+
+
+def decoded(code, bound=FIELD_BOUND):
+    t = code.astype(jnp.int32).astype(jnp.float32) * (bound**0.25 / CODE_TOP)
+    return (t * jnp.abs(t)) * (t * t)
+
+
+def pack_kernel(chunks, az_ref, fields_ref, tables_ref, first_ref, all_ref, forward_out, back_out, held, sems):
+    rows, rhs, nodes = fields_ref.shape
+    per = rhs // chunks
+    copies = [
+        pltpu.make_async_copy(
+            fields_ref.at[:, pl.ds(index * per, per), :], held.at[index].reshape(rows, per, nodes), sems.at[index]
+        )
+        for index in range(chunks)
+    ]
     tables = [
-        pltpu.make_async_copy(tables_ref.at[az_ref[0], 0], forward_out, sems.at[0]),
-        pltpu.make_async_copy(tables_ref.at[az_ref[0], 1], back_out, sems.at[1]),
+        pltpu.make_async_copy(tables_ref.at[az_ref[0], way], out, sems.at[chunks + way])
+        for way, out in enumerate((forward_out, back_out))
     ]
-    for index, chunk_ref in enumerate(chunk_refs):
-        copy = chunk_copy(fields_ref, held, per, index + 1, sems.at[2])
+    for copy in copies + tables:
         copy.start()
-        if index == 0:
-            for table in tables:
-                table.start()
-            all_ref[:per] = first_ref[...]
-        copy.wait()
-        code_rows(held, chunk_ref, all_ref, (index + 1) * per)
+    for index in range(chunks):
+        copies[index].wait()
+        for r in range(per):
+            code = encoded(held[index, pl.ds(r, rows, stride=per), :], FIELD_BOUND)
+            all_ref[index * per + r] = code
+            if index == 0:
+                first_ref[r] = code
     for table in tables:
         table.wait()
 
 
-def decoded(code):
-    t = code.astype(jnp.int32).astype(jnp.float32) * (FIELD_BOUND**0.25 / CODE_TOP)
-    return (t * jnp.abs(t)) * (t * t)
+def exact_product(table_ref, cols, x):
+    high = x.astype(jnp.bfloat16)
+    low = (x - high.astype(jnp.float32)).astype(jnp.bfloat16)
+    table_high, table_low = table_ref[0, :, cols], table_ref[1, :, cols]
+    total = jnp.dot(table_high, high, preferred_element_type=jnp.float32)
+    total += jnp.dot(table_low, high, preferred_element_type=jnp.float32)
+    return total + jnp.dot(table_high, low, preferred_element_type=jnp.float32)
+
+
+def write_modes(held, modes_ref):
+    local, both = modes_ref.shape[:2]
+    rhs, rows = both // 2, 2 * local
+    for k in range(local):
+        real = held[pl.ds(k, rhs, stride=rows), :]
+        imag = held[pl.ds(local + k, rhs, stride=rows), :]
+        modes_ref[k] = jnp.concatenate([real, imag], axis=0).astype(jnp.bfloat16)
+
+
+def split_kernel(first, find, table_ref, own_ref, peer_ref, place_ref, cols_ref, count_ref, tiles_ref,
+                 near_ref, far_ref, out_ref, slot_ref, sem):
+    copy = find(place_ref, cols_ref, count_ref, tiles_ref, out_ref, slot_ref, sem)
+    per, rows, nodes = far_ref.shape
+    odd = lax.rem(lax.broadcasted_iota(jnp.int32, (rows, 2 * nodes), 0), 2) == 1
+    for r in range(0, per, 2):
+        near = jnp.zeros((rows, 2 * nodes), jnp.float32)
+        far = jnp.zeros((rows, 2 * nodes), jnp.float32)
+        for j, ref in enumerate((own_ref, peer_ref)):
+            x = jnp.concatenate([decoded(ref[first + r]), decoded(ref[first + r + 1])], axis=1)
+            cols = slice(j * rows, (j + 1) * rows)
+            near += exact_product(table_ref, cols, x)
+            far += exact_product(table_ref, cols, jnp.where(odd, -x, x))
+        code = encoded(far, PARTIAL_BOUND)
+        for s in range(2):
+            near_ref[r + s] = near[:, s * nodes : (s + 1) * nodes]
+            far_ref[r + s] = code[:, s * nodes : (s + 1) * nodes]
+    copy.wait()
+
+
+def finish_kernel(near_ref, far_ref, modes_ref, held):
+    per, rows = far_ref.shape[:2]
+    for r in range(per):
+        held[r * rows : (r + 1) * rows, :] = near_ref[r] + decoded(far_ref[r], PARTIAL_BOUND)
+    write_modes(held, modes_ref)
 
 
 def forward_kernel(firsts, table_ref, *refs):
@@ -100,20 +130,10 @@
         for j in range(sources):
             at = firsts[j] + r
             x = jnp.concatenate([decoded(coded_refs[j][at]), decoded(coded_refs[j][at + 1])], axis=1)
-            high = x.astype(jnp.bfloat16)
-            low = (x - high.astype(jnp.float32)).astype(jnp.bfloat16)
-            cols = slice(j * rows, (j + 1) * rows)
-            table_high, table_low = table_ref[0, :, cols], table_ref[1, :, cols]
-            total += jnp.dot(table_high, high, preferred_element_type=jnp.float32)
-            total += jnp.dot(table_low, high, preferred_element_type=jnp.float32)
-            total += jnp.dot(table_high, low, preferred_element_type=jnp.float32)
+            total += exact_product(table_ref, slice(j * rows, (j + 1) * rows), x)
         held[r * rows : (r + 1) * rows, :] = total[:, :nodes]
         held[(r + 1) * rows : (r + 2) * rows, :] = total[:, nodes:]
-    local = rows // 2
-    for k in range(local):
-        real = held[pl.ds(k, rhs, stride=rows), :]
-        imag = held[pl.ds(local + k, rhs, stride=rows), :]
-        modes_ref[k] = jnp.concatenate([real, imag], axis=0).astype(jnp.bfloat16)
+    write_modes(held, modes_ref)
 
 
 def stage_kernel(first, tiles_ref, out_ref, sem):
@@ -124,7 +144,7 @@
     copy.wait()
 
 
-def find_kernel(ring, shares, place_ref, cols_ref, count_ref, tiles_ref, out_ref, slot_ref, sem):
+def begin_find(ring, place_ref, cols_ref, count_ref, tiles_ref, out_ref, slot_ref, sem):
     slots, modes = cols_ref.shape
     share = out_ref.shape[0] - 1
     copy = pltpu.make_async_copy(tiles_ref.at[pl.ds(0, share)], out_ref.at[pl.ds(0, share)], sem)
@@ -136,14 +156,18 @@
     far = lax.rem(jnp.where(even, place - 1, place + 1) + ring, ring)
 
     def find(k, carry):
-        base = lax.rem(k, modes // shares) * slots
+        base = lax.rem(k, share // slots) * slots
         for role, wanted in enumerate((place, side, far)):
             slot = jnp.where(cols_ref[0, k] == wanted, 0, jnp.where(cols_ref[1, k] == wanted, 1, 2))
             slot_ref[role * modes + k] = jnp.where(slot < count_ref[k], base + slot, share)
         return carry
 
     lax.fori_loop(0, modes, find, 0)
-    copy.wait()
+    return copy
+
+
+def find_kernel(find, *refs):
+    find(*refs).wait()
 
 
 def tile_product(slot_ref, tile_refs, modes, k, roles, values):
@@ -242,7 +266,6 @@
     tiles_shape = jax.ShapeDtypeStruct((share + 1, 2 * block, block), tile_data.dtype)
     params = pltpu.CompilerParams(vmem_limit_bytes=VMEM_LIMIT)
     pack_params = pltpu.CompilerParams(vmem_limit_bytes=PACK_VMEM_LIMIT)
-    later_params = pltpu.CompilerParams(vmem_limit_bytes=LATER_VMEM_LIMIT)
     stage_params = pltpu.CompilerParams(vmem_limit_bytes=STAGE_VMEM_LIMIT)
     vmem, smem = pl.BlockSpec(memory_space=pltpu.VMEM), pl.BlockSpec(memory_space=pltpu.SMEM)
     hbm = pl.BlockSpec(memory_space=pltpu.HBM)
@@ -250,73 +273,91 @@
     multiply = 4 * rows * rows * parts * per * nodes
     chunk_shape = jax.ShapeDtypeStruct((per, rows, nodes), jnp.int16)
 
-    first = pl.pallas_call(
-        first_pack_kernel,
-        out_shape=chunk_shape,
-        in_specs=[hbm],
-        out_specs=vmem,
-        scratch_shapes=[pltpu.VMEM((rows * per, nodes), jnp.float32), pltpu.SemaphoreType.DMA],
-        cost_estimate=cost(0, move // 2),
+    az = lax.axis_index("az").astype(jnp.int32)[None]
+    place = lax.axis_index("curve").astype(jnp.int32)[None]
+    first, coded, forward_table, back_table = pl.pallas_call(
+        functools.partial(pack_kernel, CHUNKS),
+        out_shape=[chunk_shape, jax.ShapeDtypeStruct((rhs, rows, nodes), jnp.int16), table_shape, table_shape],
+        in_specs=[smem, hbm, hbm],
+        out_specs=[vmem] * 4,
+        scratch_shapes=[
+            pltpu.VMEM((CHUNKS, rows * per, nodes), jnp.float32),
+            pltpu.SemaphoreType.DMA((CHUNKS + 2,)),
+        ],
+        cost_estimate=cost(0, move),
         compiler_params=pack_params,
         name="pack",
-    )(cut_fields)
-    az = lax.axis_index("az").astype(jnp.int32)[None]
-    place = lax.axis_index("curve").astype(jnp.int32)[None]
-    *later, coded, forward_table, back_table = pl.pallas_call(
-        later_pack_kernel,
-        out_shape=[chunk_shape] * (CHUNKS - 1)
-        + [jax.ShapeDtypeStruct((rhs, rows, nodes), jnp.int16), table_shape, table_shape],
-        in_specs=[smem, hbm, hbm, vmem],
-        out_specs=[vmem] * (CHUNKS + 2),
-        scratch_shapes=[pltpu.VMEM((rows * per, nodes), jnp.float32), pltpu.SemaphoreType.DMA((3,))],
-        cost_estimate=cost(0, move),
-        compiler_params=later_params,
-        name="later",
-    )(az, cut_fields, tables, first)
-    chunks = [first] + later
+    )(az, cut_fields, tables)
 
     peer = lax.ppermute(coded, "az", PEER) if paired else None
-    tiles = []
-    head, slot = pl.pallas_call(
-        functools.partial(find_kernel, ring, SHARES),
-        out_shape=[tiles_shape, jax.ShapeDtypeStruct((slots * local,), jnp.int32)],
-        in_specs=[smem, smem, smem, hbm],
-        out_specs=[vmem, smem],
-        scratch_shapes=[pltpu.SemaphoreType.DMA],
-        cost_estimate=cost(0, 2 * tile_data.size // SHARES),
-        compiler_params=stage_params,
-        name="find",
-    )(after(place, coded), tile_cols[:, 0, :].T, tile_count.reshape(local), flat_tiles)
-    tiles.append(head)
+    find = functools.partial(begin_find, ring)
+    find_shapes = [tiles_shape, jax.ShapeDtypeStruct((slots * local,), jnp.int32)]
+    find_operands = (after(place, coded), tile_cols[:, 0, :].T, tile_count.reshape(local), flat_tiles)
+    if paired:
+        near_part, far_part, head, slot = pl.pallas_call(
+            functools.partial(split_kernel, per, find),
+            out_shape=[jax.ShapeDtypeStruct((per, rows, nodes), jnp.float32), chunk_shape] + find_shapes,
+            in_specs=[vmem] * 3 + [smem] * 3 + [hbm],
+            out_specs=[vmem] * 3 + [smem],
+            scratch_shapes=[pltpu.SemaphoreType.DMA],
+            cost_estimate=cost(3 * multiply, move),
+            compiler_params=stage_params,
+            name="split",
+        )(forward_table, coded, peer, *find_operands)
+    else:
+        head, slot = pl.pallas_call(
+            functools.partial(find_kernel, find),
+            out_shape=find_shapes,
+            in_specs=[smem] * 3 + [hbm],
+            out_specs=[vmem, smem],
+            scratch_shapes=[pltpu.SemaphoreType.DMA],
+            compiler_params=stage_params,
+            name="find",
+        )(*find_operands)
+    tiles = [head]
 
     sides = [(i, i ^ 1) for i in range(ring)]
     onward = [(i, (i + 2 if i % 2 == 0 else i - 2) % ring) for i in range(ring)]
-    owns, ready = [], (head,)
-    for index, chunk in enumerate(chunks):
-        if paired:
-            across = lax.ppermute(after(chunk, *ready) if index else chunk, "az", ACROSS)
-            across = after(across, *ready, *tiles[1:])
-            ready = (across,)
-            sources = [coded, peer, across, lax.ppermute(across, "az", PEER)]
-            firsts = (index * per, index * per, 0, 0)
+    modes_shape = jax.ShapeDtypeStruct((local, 2 * per, nodes), jnp.bfloat16)
+    held_modes = pltpu.VMEM((per * rows, nodes), jnp.float32)
+    owns, earlier = [], None
+    for index in range(CHUNKS):
+        if paired and index:
+            across = after(lax.ppermute(after(far_part, earlier), "az", ACROSS), tiles[-1])
+            own = pl.pallas_call(
+                finish_kernel,
+                out_shape=modes_shape,
+                in_specs=[vmem] * 2,
+                out_specs=vmem,
+                scratch_shapes=[held_modes],
+                cost_estimate=cost(0, move // 2),
+                compiler_params=params,
+                name="finish",
+            )(near_part, across)
         else:
-            every = lax.all_gather(chunk, "az")
-            sources, firsts = [every[j] for j in range(parts)], (0,) * parts
-        own = pl.pallas_call(
-            functools.partial(forward_kernel, firsts),
-            out_shape=jax.ShapeDtypeStruct((local, 2 * per, nodes), jnp.bfloat16),
-            in_specs=[vmem] * (1 + parts),
-            out_specs=vmem,
-            scratch_shapes=[pltpu.VMEM((per * rows, nodes), jnp.float32)],
-            cost_estimate=cost(3 * multiply, move),
-            compiler_params=params,
-            name="forward",
-        )(forward_table, *sources)
+            if paired:
+                across = after(lax.ppermute(first, "az", ACROSS), far_part)
+                earlier = across
+                sources = [coded, peer, across, lax.ppermute(across, "az", PEER)]
+                firsts = (0,) * parts
+            else:
+                every = lax.all_gather(coded[index * per : (index + 1) * per], "az")
+                sources, firsts = [every[j] for j in range(parts)], (0,) * parts
+            own = pl.pallas_call(
+                functools.partial(forward_kernel, firsts),
+                out_shape=modes_shape,
+                in_specs=[vmem] * (1 + parts),
+                out_specs=vmem,
+                scratch_shapes=[held_modes],
+                cost_estimate=cost(3 * multiply, move),
+                compiler_params=params,
+                name="forward",
+            )(forward_table, *sources)
         owns.append(own)
         if index == 0:
-            for place_of in range(1, SHARES):
+            for turn in range(1, SHARES):
                 tail = pl.pallas_call(
-                    functools.partial(stage_kernel, place_of * share),
+                    functools.partial(stage_kernel, turn * share),
                     out_shape=tiles_shape,
                     in_specs=[hbm],
                     out_specs=vmem,
@@ -327,9 +368,11 @@
                 )(after(flat_tiles, own))
                 tiles.append(tail)
 
+    sides_in = [lax.ppermute(own, "curve", sides) for own in owns]
+    for index in range(CHUNKS - 1):
+        sides_in[index] = after(sides_in[index], owns[index + 1])
     halo = []
-    for own in owns:
-        side = lax.ppermute(own, "curve", sides)
+    for own, side in zip(owns, sides_in):
         far = lax.ppermute(side, "curve", onward)
         inner = pl.pallas_call(
             inner_kernel,
@@ -341,6 +384,9 @@
             name="inner",
         )(slot, *tiles, own, side)
         halo.append((inner, after(far, inner)))
+    for index in range(CHUNKS - 1):
+        inner, far = halo[index]
+        halo[index] = (inner, after(far, sides_in[index + 1]))
 
     nears = []
     for inner, far in halo:

time: 56.5 us -> 57.2 us (1.012)
  starting transfers between devices: 12 us -> 13.8 us
  waiting for transfers between devices: 17.2 us -> 18.8 us
  Pallas kernels: 24.4 us -> 22.8 us
  local copies, waits for them, and re-layouts: 2.57 us -> 1.34 us
    ppermute x4, waiting for transfers between devices: 4.75 us -> 6.48 us  [the longest x2 3.7 us: on_device(): sides_in = [lax.ppermute(own, 'curve', sides) for own in owns]]
    ppermute x2, waiting for transfers between devices: 2.74 us -> 4.39 us  [on_device(): far = lax.ppermute(side, 'curve', onward)]
    pallas_call x6 -> x5, Pallas kernels: 12 us -> 10.4 us  [the longest x1 3.96 us: on_device(): pl.pallas_call(functools.partial(split_kernel, per, find), out_shape=[jax...]
    ppermute x4, starting transfers between devices: 8.24 us -> 9.49 us  [the longest x2 5.16 us: on_device(): sides_in = [lax.ppermute(own, 'curve', sides) for own in owns]]
    unnamed x9 -> x7, local copies, waits for them, and re-layouts: 2.57 us -> 1.34 us
    ppermute x2 -> x1, waiting for transfers between devices: 1.14 us -> 0.01 us  [on_device(): sources = [coded, peer, across, lax.ppermute(across, 'az', PEER)]]
    ppermute x2, starting transfers between devices: 1.5 us -> 2.16 us  [on_device(): across = lax.ppermute(near, 'az', ACROSS)]
  transfers between devices with their start and end apart: 15 -> 14, of which waited for: 9 -> 9; matrix products, arithmetic and copies ran while one was open for 1% -> 1% of each run, Pallas kernels for 38% -> 31%
where the time goes in v4:
time: 57.2 us; the launch traced here: 57 us
  Pallas kernels  22.8 us (40%)
  waiting for transfers between devices  18.8 us (33%)
  starting transfers between devices  13.8 us (24%)
  local copies, waits for them, and re-layouts  1.34 us (2%)
    ppermute x2, waiting for transfers between devices, on_device(): across = lax.ppermute(near, 'az', ACROSS)  6.43 us
    pallas_call x2, Pallas kernels, on_device(): pl.pallas_call(inner_kernel, out_shape=jax.ShapeDtypeStruct((local * 2 *...  5.65 us
    ppermute x2, starting transfers between devices, on_device(): sides_in = [lax.ppermute(own, 'curve', sides) for own in owns]  5.16 us
    ppermute x2, waiting for transfers between devices, on_device(): far = lax.ppermute(side, 'curve', onward)  4.39 us
    pallas_call x1, Pallas kernels, on_device(): pl.pallas_call(functools.partial(split_kernel, per, find), out_shape=[jax...  3.96 us
    ppermute x2, waiting for transfers between devices, on_device(): sides_in = [lax.ppermute(own, 'curve', sides) for own in owns]  3.7 us
    pallas_call x2, Pallas kernels, on_device(): pl.pallas_call(outer_kernel, out_shape=jax.ShapeDtypeStruct((per, rows, n...  3.56 us
    pallas_call x2, Pallas kernels, on_device(): pl.pallas_call(functools.partial(back_kernel, parts, rhs, index), out_sha...  3.22 us
  transfers between devices with their start and end apart: 14, of which 9 were waited for; matrix products, arithmetic and copies ran while one was open for 1% of the time, Pallas kernels for 31%

profile of v4, /device:TPU:0, one launch (start us, length us, event | category | flops | bytes accessed | tf_op | source)
XLA Modules:
  0.0 57.0 jit_solution(4053716626825382276)
XLA Ops:
  0.0 1.9 %pack.1 = (s16[8,128,128]{2,1,0:T(8,128)(2,1)S(1)}, s16[16,128,128]{2,1,0:T(8,128)(2,1)S(1)}, bf16[2,128,512]{2,1,0:T(8,128)(2,1)S(1)}, bf16[2,128,512]{2,1,0:T(8,128)(2,1)S(1)}) custom-call(s32[1]{0:T(128)} %bitcast.az_ref, f32[128,16,128]{2,1,0:T(8,128)} %bitcast.13, bf16[4,2,2,128,512]{4,3,2,1,0:T(8,128)(2,1)} %constant.10.clone.tables_ref), custom_call_target="tpu_custom_call" | custom-call | bytes 4194304 | tf_op jit(solution)/shard_map/pack/pallas_call | solution.py:278
  1.9 0.5 collective-permute-start
  2.4 2.6 %collective-permute-start.1 = (s16[8,128,128]{2,1,0:T(8,128)(2,1)S(1)}, s16[8,128,128]{2,1,0:T(8,128)(2,1)S(1)}, u32[]{:S(2)}, u32[]{:S(2)}) collective-permute-start(s16[8,128,128]{2,1,0:T(8,128)(2,1)S(1)} %get-tuple-element.31), channel_id=1, source_target_pairs={{0,16},{8,24},{16,0},{24,8},{1,17},{9,25},{17,1},{25,9},{2,18},{10... | collective-permute-start | bytes 786440 | tf_op jit(solution)/shard_map/ppermute | solution.py:339
  5.0 0.7 %copy.10 = s32[64,1,3]{0,2,1:T(4,128)S(1)} copy(s32[64,1,3]{0,1,2:T(1,128)} %param.9) | data formatting | bytes 1536
  5.7 0.0 collective-permute-done.peer_ref.refs_1_
  5.7 0.0 copy-start.2
  5.7 0.7 %copy-done.2 = s32[64,1]{0,1:T(1,128)S(1)} copy-done((s32[64,1]{0,1:T(1,128)S(1)}, s32[64,1]{0,1:T(1,128)}, u32[]{:S(2)}) %copy-start.2) | copy-done | bytes 280
  6.3 4.0 %split.1 = (f32[8,128,128]{2,1,0:T(8,128)S(1)}, s16[8,128,128]{2,1,0:T(8,128)(2,1)S(1)}, bf16[97,256,128]{2,1,0:T(8,128)(2,1)S(1)}, s32[192]{0:T(256)S(1)}) custom-call(bf16[2,128,512]{2,1,0:T(8,128)(2,1)S(1)} %get-tuple-element.26.table_ref, s16[16,128,128]{2,1,0:T(8,128)(2,1)S(1)} %get-tuple-element.27.own_ref.refs_0_, ...), custom_call_target="tpu_custom_call" | custom-call | flops 805306368 | bytes 4194304 | tf_op jit(solution)/shard_map/split/pallas_call | solution.py:297
  10.3 1.6 %collective-permute-done.1.refs_2_ = s16[8,128,128]{2,1,0:T(8,128)(2,1)S(1)} collective-permute-done((s16[8,128,128]{2,1,0:T(8,128)(2,1)S(1)}, s16[8,128,128]{2,1,0:T(8,128)(2,1)S(1)}, u32[]{:S(2)}, u32[]{:S(2)}) %collective-permute-start.1) | collective-permute-done | bytes 262176 | tf_op jit(solution)/shard_map/ppermute | solution.py:339
  11.9 0.0 collective-permute-start.2
  11.9 1.8 %collective-permute-start.3 = (s16[8,128,128]{2,1,0:T(8,128)(2,1)S(1)}, s16[8,128,128]{2,1,0:T(8,128)(2,1)S(1)}, u32[]{:S(2)}, u32[]{:S(2)}) collective-permute-start(s16[8,128,128]{2,1,0:T(8,128)(2,1)S(1)} %get-tuple-element.36), channel_id=1, source_target_pairs={{0,16},{8,24},{16,0},{24,8},{1,17},{9,25},{17,1},{25,9},{2,18},{10... | collective-permute-start | bytes 786440 | tf_op jit(solution)/shard_map/ppermute | solution.py:326
  13.6 0.0 collective-permute-done.2.refs_3_
  13.6 1.3 %forward.1.refs_2_ = bf16[64,16,128]{2,1,0:T(8,128)(2,1)S(1)} custom-call(bf16[2,128,512]{2,1,0:T(8,128)(2,1)S(1)} %get-tuple-element.26.table_ref, s16[16,128,128]{2,1,0:T(8,128)(2,1)S(1)} %get-tuple-element.27.own_ref.refs_0_, s16[16,128,128]{2,1,0:T(8,128)(2,1)S(1)} %collective-permute-done.peer_ref.refs_1_, ...), custom_call_target="tpu_custom_call" | custom-call | flops 805306368 | bytes 4194304 | tf_op jit(solution)/shard_map/forward/pallas_call | solution.py:346
  15.0 1.6 %collective-permute-start.8 = (bf16[64,16,128]{2,1,0:T(8,128)(2,1)S(1)}, bf16[64,16,128]{2,1,0:T(8,128)(2,1)S(1)}, u32[]{:S(2)}, u32[]{:S(2)}) collective-permute-start(bf16[64,16,128]{2,1,0:T(8,128)(2,1)S(1)} %forward.1.refs_2_), channel_id=1, source_target_pairs={{0,1},{1,0},{2,3},{3,2},{4,5},{5,4},{6,7},{7,6},{8,9},{9,8},{10,11... | collective-permute-start | bytes 786440 | tf_op jit(solution)/shard_map/ppermute | solution.py:371
  16.6 2.8 %stage.1.refs_1_ = bf16[97,256,128]{2,1,0:T(8,128)(2,1)S(1)} custom-call(bf16[192,256,128]{2,1,0:T(8,128)(2,1)} %bitcast.21), custom_call_target="tpu_custom_call" | custom-call | bytes 6291456 | tf_op jit(solution)/shard_map/stage/pallas_call | solution.py:359
  19.4 1.2 %collective-permute-done.3.far_ref = s16[8,128,128]{2,1,0:T(8,128)(2,1)S(1)} collective-permute-done((s16[8,128,128]{2,1,0:T(8,128)(2,1)S(1)}, s16[8,128,128]{2,1,0:T(8,128)(2,1)S(1)}, u32[]{:S(2)}, u32[]{:S(2)}) %collective-permute-start.3) | collective-permute-done | bytes 262176 | tf_op jit(solution)/shard_map/ppermute | solution.py:326
  20.6 0.4 finish.1.refs_2_
  21.0 2.5 %collective-permute-done.8.refs_3_ = bf16[64,16,128]{2,1,0:T(8,128)(2,1)S(1)} collective-permute-done((bf16[64,16,128]{2,1,0:T(8,128)(2,1)S(1)}, bf16[64,16,128]{2,1,0:T(8,128)(2,1)S(1)}, u32[]{:S(2)}, u32[]{:S(2)}) %collective-permute-start.8) | collective-permute-done | bytes 262176 | tf_op jit(solution)/shard_map/ppermute | solution.py:371
  23.5 1.6 %collective-permute-start.9 = (bf16[64,16,128]{2,1,0:T(8,128)(2,1)S(1)}, bf16[64,16,128]{2,1,0:T(8,128)(2,1)S(1)}, u32[]{:S(2)}, u32[]{:S(2)}) collective-permute-start(bf16[64,16,128]{2,1,0:T(8,128)(2,1)S(1)} %collective-permute-done.8.refs_3_), channel_id=1, source_target_pairs={{0,2},{1,7},{2,4},{3,1},{4,6},{5,3},{6,0},{7,5},{8,10},{9,15},{10,... | collective-permute-start | bytes 786440 | tf_op jit(solution)/shard_map/ppermute | solution.py:376
  25.1 3.5 %collective-permute-start.4 = (bf16[64,16,128]{2,1,0:T(8,128)(2,1)S(1)}, bf16[64,16,128]{2,1,0:T(8,128)(2,1)S(1)}, u32[]{:S(2)}, u32[]{:S(2)}) collective-permute-start(bf16[64,16,128]{2,1,0:T(8,128)(2,1)S(1)} %finish.1.refs_2_), channel_id=1, source_target_pairs={{0,1},{1,0},{2,3},{3,2},{4,5},{5,4},{6,7},{7,6},{8,9},{9,8},{10,11... | collective-permute-start | bytes 786440 | tf_op jit(solution)/shard_map/ppermute | solution.py:371
  28.6 2.8 %inner.3.refs_3_ = f32[1024,128]{1,0:T(8,128)S(1)} custom-call(s32[192]{0:T(256)S(1)} %get-tuple-element.29.slot_ref, bf16[97,256,128]{2,1,0:T(8,128)(2,1)S(1)} %get-tuple-element.30.refs_0_, bf16[97,256,128]{2,1,0:T(8,128)(2,1)S(1)} %stage.1.refs_1_, bf16[64,16,128]{2,1,0:T(8,128)(2,1)S(1)} %forward.1.refs_2_, ...), custom_call_target="tpu_custom_call" | custom-call | bytes 6291456 | tf_op jit(solution)/shard_map/inner/pallas_call | solution.py:377
  31.4 1.5 %collective-permute-done.9.refs_2_ = bf16[64,16,128]{2,1,0:T(8,128)(2,1)S(1)} collective-permute-done((bf16[64,16,128]{2,1,0:T(8,128)(2,1)S(1)}, bf16[64,16,128]{2,1,0:T(8,128)(2,1)S(1)}, u32[]{:S(2)}, u32[]{:S(2)}) %collective-permute-start.9) | collective-permute-done | bytes 262176 | tf_op jit(solution)/shard_map/ppermute | solution.py:376
  32.9 1.2 %collective-permute-done.4.refs_3_ = bf16[64,16,128]{2,1,0:T(8,128)(2,1)S(1)} collective-permute-done((bf16[64,16,128]{2,1,0:T(8,128)(2,1)S(1)}, bf16[64,16,128]{2,1,0:T(8,128)(2,1)S(1)}, u32[]{:S(2)}, u32[]{:S(2)}) %collective-permute-start.4) | collective-permute-done | bytes 262176 | tf_op jit(solution)/shard_map/ppermute | solution.py:371
  34.2 1.8 %outer.3.refs_0_ = bf16[8,128,128]{2,1,0:T(8,128)(2,1)S(1)} custom-call(s32[192]{0:T(256)S(1)} %get-tuple-element.29.slot_ref, bf16[97,256,128]{2,1,0:T(8,128)(2,1)S(1)} %get-tuple-element.30.refs_0_, bf16[97,256,128]{2,1,0:T(8,128)(2,1)S(1)} %stage.1.refs_1_, bf16[64,16,128]{2,1,0:T(8,128)(2,1)S(1)} %collective-permute-done.9.refs_2_, ...), custom_call_target="tpu_custom_call" | custom-call | bytes 3145728 | tf_op jit(solution)/shard_map/outer/pallas_call | solution.py:394
  36.0 1.5 %collective-permute-start.11 = (bf16[8,128,128]{2,1,0:T(8,128)(2,1)S(1)}, bf16[8,128,128]{2,1,0:T(8,128)(2,1)S(1)}, u32[]{:S(2)}, u32[]{:S(2)}) collective-permute-start(bf16[8,128,128]{2,1,0:T(8,128)(2,1)S(1)} %outer.3.refs_0_), channel_id=1, source_target_pairs={{0,16},{8,24},{16,0},{24,8},{1,17},{9,25},{17,1},{25,9},{2,18},{10... | collective-permute-start | bytes 786440 | tf_op jit(solution)/shard_map/ppermute | solution.py:409
  37.4 0.0 collective-permute-start.5
  37.4 2.8 %inner.2.refs_3_ = f32[1024,128]{1,0:T(8,128)S(1)} custom-call(s32[192]{0:T(256)S(1)} %get-tuple-element.29.slot_ref, bf16[97,256,128]{2,1,0:T(8,128)(2,1)S(1)} %get-tuple-element.30.refs_0_, bf16[97,256,128]{2,1,0:T(8,128)(2,1)S(1)} %stage.1.refs_1_, bf16[64,16,128]{2,1,0:T(8,128)(2,1)S(1)} %finish.1.refs_2_, ...), custom_call_target="tpu_custom_call" | custom-call | bytes 6291456 | tf_op jit(solution)/shard_map/inner/pallas_call | solution.py:377
  40.2 0.0 copy-start
  40.2 0.0 copy-start.1
  40.2 0.1 collective-permute-start.10
  40.3 2.3 %collective-permute-done.11.refs_2_ = bf16[8,128,128]{2,1,0:T(8,128)(2,1)S(1)} collective-permute-done((bf16[8,128,128]{2,1,0:T(8,128)(2,1)S(1)}, bf16[8,128,128]{2,1,0:T(8,128)(2,1)S(1)}, u32[]{:S(2)}, u32[]{:S(2)}) %collective-permute-start.11) | collective-permute-done | bytes 262176 | tf_op jit(solution)/shard_map/ppermute | solution.py:409
  42.7 0.0 collective-permute-start.12
  42.7 2.9 %collective-permute-done.5.refs_2_ = bf16[64,16,128]{2,1,0:T(8,128)(2,1)S(1)} collective-permute-done((bf16[64,16,128]{2,1,0:T(8,128)(2,1)S(1)}, bf16[64,16,128]{2,1,0:T(8,128)(2,1)S(1)}, u32[]{:S(2)}, u32[]{:S(2)}) %collective-permute-start.5) | collective-permute-done | bytes 262176 | tf_op jit(solution)/shard_map/ppermute | solution.py:376
  45.6 1.8 %outer.2.refs_0_ = bf16[8,128,128]{2,1,0:T(8,128)(2,1)S(1)} custom-call(s32[192]{0:T(256)S(1)} %get-tuple-element.29.slot_ref, bf16[97,256,128]{2,1,0:T(8,128)(2,1)S(1)} %get-tuple-element.30.refs_0_, bf16[97,256,128]{2,1,0:T(8,128)(2,1)S(1)} %stage.1.refs_1_, bf16[64,16,128]{2,1,0:T(8,128)(2,1)S(1)} %collective-permute-done.5.refs_2_, ...), custom_call_target="tpu_custom_call" | custom-call | bytes 3145728 | tf_op jit(solution)/shard_map/outer/pallas_call | solution.py:394
  47.4 0.7 %collective-permute-start.7 = (bf16[8,128,128]{2,1,0:T(8,128)(2,1)S(1)}, bf16[8,128,128]{2,1,0:T(8,128)(2,1)S(1)}, u32[]{:S(2)}, u32[]{:S(2)}) collective-permute-start(bf16[8,128,128]{2,1,0:T(8,128)(2,1)S(1)} %outer.2.refs_0_), channel_id=1, source_target_pairs={{0,16},{8,24},{16,0},{24,8},{1,17},{9,25},{17,1},{25,9},{2,18},{10... | collective-permute-start | bytes 786440 | tf_op jit(solution)/shard_map/ppermute | solution.py:409
  48.1 0.0 collective-permute-start.6
  48.1 0.0 collective-permute-done.10.refs_1_
  48.1 0.0 collective-permute-done.12.refs_3_
  48.1 0.0 copy-done
  48.1 0.0 copy-done.1
  48.1 1.6 %back.2.refs_4_ = f32[128,16,128]{2,1,0:T(8,128)} custom-call(bf16[2,128,512]{2,1,0:T(8,128)(2,1)S(1)} %get-tuple-element.25.table_ref, f32[2048,128]{1,0:T(8,128)S(1)} %bitcast.14, f32[128,128]{1,0:T(8,128)S(1)} %bitcast.16, bf16[8,128,128]{2,1,0:T(8,128)(2,1)S(1)} %outer.3.refs_0_, bf16[8,128,128]{2,1,0:T(8,128)(2,1)S(1)} %collective-permute-done.10.refs_1_, ...), custom_call_target="tpu_custom_call" | custom-call | flops 536870912 | bytes 4194304 | tf_op jit(solution)/shard_map/back/pallas_call | solution.py:419
  49.7 4.1 %collective-permute-done.7.refs_2_ = bf16[8,128,128]{2,1,0:T(8,128)(2,1)S(1)} collective-permute-done((bf16[8,128,128]{2,1,0:T(8,128)(2,1)S(1)}, bf16[8,128,128]{2,1,0:T(8,128)(2,1)S(1)}, u32[]{:S(2)}, u32[]{:S(2)}) %collective-permute-start.7) | collective-permute-done | bytes 262176 | tf_op jit(solution)/shard_map/ppermute | solution.py:409
  53.8 0.0 collective-permute-start.13
  53.8 0.0 collective-permute-done.6.refs_1_
  53.8 1.5 %collective-permute-done.13.refs_3_ = bf16[8,128,128]{2,1,0:T(8,128)(2,1)S(1)} collective-permute-done((bf16[8,128,128]{2,1,0:T(8,128)(2,1)S(1)}, bf16[8,128,128]{2,1,0:T(8,128)(2,1)S(1)}, u32[]{:S(2)}, u32[]{:S(2)}) %collective-permute-start.13) | collective-permute-done | bytes 262176 | tf_op jit(solution)/shard_map/ppermute | solution.py:414
  55.3 1.6 %back.3 = f32[128,16,128]{2,1,0:T(8,128)} custom-call(bf16[2,128,512]{2,1,0:T(8,128)(2,1)S(1)} %get-tuple-element.25.table_ref, f32[2048,128]{1,0:T(8,128)S(1)} %bitcast.15, f32[128,128]{1,0:T(8,128)S(1)} %bitcast.17, bf16[8,128,128]{2,1,0:T(8,128)(2,1)S(1)} %outer.2.refs_0_, ...), custom_call_target="tpu_custom_call", output_to_operand_aliasing={{}: (7, {})} | custom-call | flops 536870912 | bytes 4194304 | tf_op jit(solution)/shard_map/back/pallas_call | solution.py:419
Async XLA Ops:
  1.9 3.8 %collective-permute-start = (s16[16,128,128]{2,1,0:T(8,128)(2,1)S(1)}, s16[16,128,128]{2,1,0:T(8,128)(2,1)S(1)}, u32[]{:S(2)}, u32[]{:S(2)}) collective-permute-start(s16[16,128,128]{2,1,0:T(8,128)(2,1)S(1)} %get-tuple-element.27.own_ref.refs_0_), channel_id=1, source_target_pairs={{0,8},{8,0},{16,24},{24,16},{1,9},{9,1},{17,25},{25,17},{2,10},{10... | collective-permute-start | bytes 1572872 | tf_op jit(solution)/shard_map/ppermute | solution.py:292
  2.4 9.5 %collective-permute-start.1 = (s16[8,128,128]{2,1,0:T(8,128)(2,1)S(1)}, s16[8,128,128]{2,1,0:T(8,128)(2,1)S(1)}, u32[]{:S(2)}, u32[]{:S(2)}) collective-permute-start(s16[8,128,128]{2,1,0:T(8,128)(2,1)S(1)} %get-tuple-element.31), channel_id=1, source_target_pairs={{0,16},{8,24},{16,0},{24,8},{1,17},{9,25},{17,1},{25,9},{2,18},{10... | collective-permute-start | bytes 786440 | tf_op jit(solution)/shard_map/ppermute | solution.py:339
  5.7 0.7 %copy-start.2 = (s32[64,1]{0,1:T(1,128)S(1)}, s32[64,1]{0,1:T(1,128)}, u32[]{:S(2)}) copy-start(s32[64,1]{0,1:T(1,128)} %param.10) | copy-start | bytes 772
  11.9 1.8 %collective-permute-start.2 = (s16[8,128,128]{2,1,0:T(8,128)(2,1)S(1)}, s16[8,128,128]{2,1,0:T(8,128)(2,1)S(1)}, u32[]{:S(2)}, u32[]{:S(2)}) collective-permute-start(s16[8,128,128]{2,1,0:T(8,128)(2,1)S(1)} %collective-permute-done.1.refs_2_), channel_id=1, source_target_pairs={{0,8},{8,0},{16,24},{24,16},{1,9},{9,1},{17,25},{25,17},{2,10},{10... | collective-permute-start | bytes 786440 | tf_op jit(solution)/shard_map/ppermute | solution.py:341
  11.9 8.7 %collective-permute-start.3 = (s16[8,128,128]{2,1,0:T(8,128)(2,1)S(1)}, s16[8,128,128]{2,1,0:T(8,128)(2,1)S(1)}, u32[]{:S(2)}, u32[]{:S(2)}) collective-permute-start(s16[8,128,128]{2,1,0:T(8,128)(2,1)S(1)} %get-tuple-element.36), channel_id=1, source_target_pairs={{0,16},{8,24},{16,0},{24,8},{1,17},{9,25},{17,1},{25,9},{2,18},{10... | collective-permute-start | bytes 786440 | tf_op jit(solution)/shard_map/ppermute | solution.py:326
  15.0 8.5 %collective-permute-start.8 = (bf16[64,16,128]{2,1,0:T(8,128)(2,1)S(1)}, bf16[64,16,128]{2,1,0:T(8,128)(2,1)S(1)}, u32[]{:S(2)}, u32[]{:S(2)}) collective-permute-start(bf16[64,16,128]{2,1,0:T(8,128)(2,1)S(1)} %forward.1.refs_2_), channel_id=1, source_target_pairs={{0,1},{1,0},{2,3},{3,2},{4,5},{5,4},{6,7},{7,6},{8,9},{9,8},{10,11... | collective-permute-start | bytes 786440 | tf_op jit(solution)/shard_map/ppermute | solution.py:371
  23.5 9.4 %collective-permute-start.9 = (bf16[64,16,128]{2,1,0:T(8,128)(2,1)S(1)}, bf16[64,16,128]{2,1,0:T(8,128)(2,1)S(1)}, u32[]{:S(2)}, u32[]{:S(2)}) collective-permute-start(bf16[64,16,128]{2,1,0:T(8,128)(2,1)S(1)} %collective-permute-done.8.refs_3_), channel_id=1, source_target_pairs={{0,2},{1,7},{2,4},{3,1},{4,6},{5,3},{6,0},{7,5},{8,10},{9,15},{10,... | collective-permute-start | bytes 786440 | tf_op jit(solution)/shard_map/ppermute | solution.py:376
  25.1 9.1 %collective-permute-start.4 = (bf16[64,16,128]{2,1,0:T(8,128)(2,1)S(1)}, bf16[64,16,128]{2,1,0:T(8,128)(2,1)S(1)}, u32[]{:S(2)}, u32[]{:S(2)}) collective-permute-start(bf16[64,16,128]{2,1,0:T(8,128)(2,1)S(1)} %finish.1.refs_2_), channel_id=1, source_target_pairs={{0,1},{1,0},{2,3},{3,2},{4,5},{5,4},{6,7},{7,6},{8,9},{9,8},{10,11... | collective-permute-start | bytes 786440 | tf_op jit(solution)/shard_map/ppermute | solution.py:371
  36.0 6.7 %collective-permute-start.11 = (bf16[8,128,128]{2,1,0:T(8,128)(2,1)S(1)}, bf16[8,128,128]{2,1,0:T(8,128)(2,1)S(1)}, u32[]{:S(2)}, u32[]{:S(2)}) collective-permute-start(bf16[8,128,128]{2,1,0:T(8,128)(2,1)S(1)} %outer.3.refs_0_), channel_id=1, source_target_pairs={{0,16},{8,24},{16,0},{24,8},{1,17},{9,25},{17,1},{25,9},{2,18},{10... | collective-permute-start | bytes 786440 | tf_op jit(solution)/shard_map/ppermute | solution.py:409
  37.4 8.2 %collective-permute-start.5 = (bf16[64,16,128]{2,1,0:T(8,128)(2,1)S(1)}, bf16[64,16,128]{2,1,0:T(8,128)(2,1)S(1)}, u32[]{:S(2)}, u32[]{:S(2)}) collective-permute-start(bf16[64,16,128]{2,1,0:T(8,128)(2,1)S(1)} %collective-permute-done.4.refs_3_), channel_id=1, source_target_pairs={{0,2},{1,7},{2,4},{3,1},{4,6},{5,3},{6,0},{7,5},{8,10},{9,15},{10,... | collective-permute-start | bytes 786440 | tf_op jit(solution)/shard_map/ppermute | solution.py:376
  40.2 7.8 %copy-start = (f32[2,64,16,128]{3,2,1,0:T(8,128)S(1)}, f32[2,64,16,128]{3,2,1,0:T(8,128)}, u32[]{:S(2)}) copy-start(f32[2,64,16,128]{3,2,1,0:T(8,128)} %param.6) | copy-start | bytes 3145732
  40.2 7.9 %copy-start.1 = (f32[2,64,128]{2,1,0:T(8,128)S(1)}, f32[2,64,128]{2,1,0:T(8,128)}, u32[]{:S(2)}) copy-start(f32[2,64,128]{2,1,0:T(8,128)} %param.7) | copy-start | bytes 196612
  40.2 7.8 %collective-permute-start.10 = (bf16[8,128,128]{2,1,0:T(8,128)(2,1)S(1)}, bf16[8,128,128]{2,1,0:T(8,128)(2,1)S(1)}, u32[]{:S(2)}, u32[]{:S(2)}) collective-permute-start(bf16[8,128,128]{2,1,0:T(8,128)(2,1)S(1)} %outer.3.refs_0_), channel_id=1, source_target_pairs={{0,8},{8,0},{16,24},{24,16},{1,9},{9,1},{17,25},{25,17},{2,10},{10... | collective-permute-start | bytes 786440 | tf_op jit(solution)/shard_map/ppermute | solution.py:414
  42.7 5.4 %collective-permute-start.12 = (bf16[8,128,128]{2,1,0:T(8,128)(2,1)S(1)}, bf16[8,128,128]{2,1,0:T(8,128)(2,1)S(1)}, u32[]{:S(2)}, u32[]{:S(2)}) collective-permute-start(bf16[8,128,128]{2,1,0:T(8,128)(2,1)S(1)} %collective-permute-done.11.refs_2_), channel_id=1, source_target_pairs={{0,8},{8,0},{16,24},{24,16},{1,9},{9,1},{17,25},{25,17},{2,10},{10... | collective-permute-start | bytes 786440 | tf_op jit(solution)/shard_map/ppermute | solution.py:414
  47.4 6.4 %collective-permute-start.7 = (bf16[8,128,128]{2,1,0:T(8,128)(2,1)S(1)}, bf16[8,128,128]{2,1,0:T(8,128)(2,1)S(1)}, u32[]{:S(2)}, u32[]{:S(2)}) collective-permute-start(bf16[8,128,128]{2,1,0:T(8,128)(2,1)S(1)} %outer.2.refs_0_), channel_id=1, source_target_pairs={{0,16},{8,24},{16,0},{24,8},{1,17},{9,25},{17,1},{25,9},{2,18},{10... | collective-permute-start | bytes 786440 | tf_op jit(solution)/shard_map/ppermute | solution.py:409
  48.1 5.7 %collective-permute-start.6 = (bf16[8,128,128]{2,1,0:T(8,128)(2,1)S(1)}, bf16[8,128,128]{2,1,0:T(8,128)(2,1)S(1)}, u32[]{:S(2)}, u32[]{:S(2)}) collective-permute-start(bf16[8,128,128]{2,1,0:T(8,128)(2,1)S(1)} %outer.2.refs_0_), channel_id=1, source_target_pairs={{0,8},{8,0},{16,24},{24,16},{1,9},{9,1},{17,25},{25,17},{2,10},{10... | collective-permute-start | bytes 786440 | tf_op jit(solution)/shard_map/ppermute | solution.py:414
  53.8 1.5 %collective-permute-start.13 = (bf16[8,128,128]{2,1,0:T(8,128)(2,1)S(1)}, bf16[8,128,128]{2,1,0:T(8,128)(2,1)S(1)}, u32[]{:S(2)}, u32[]{:S(2)}) collective-permute-start(bf16[8,128,128]{2,1,0:T(8,128)(2,1)S(1)} %collective-permute-done.7.refs_2_), channel_id=1, source_target_pairs={{0,8},{8,0},{16,24},{24,16},{1,9},{9,1},{17,25},{25,17},{2,10},{10... | collective-permute-start | bytes 786440 | tf_op jit(solution)/shard_map/ppermute | solution.py:414

commit v5 on v4

--- a/solution.py
+++ b/solution.py
@@ -172,34 +172,46 @@
 
 def tile_product(slot_ref, tile_refs, modes, k, roles, values):
     tiles_ref = tile_refs[k * len(tile_refs) // modes]
-    block = tiles_ref.shape[-1]
-    rhs = values[0].shape[0] // 2
-    product = lax.dot_general(
+    return lax.dot_general(
         jnp.concatenate(values, axis=1),
         jnp.concatenate([tiles_ref[slot_ref[role * modes + k]] for role in roles], axis=1),
         (((1,), (1,)), ((), ())),
         preferred_element_type=jnp.float32,
     )
+
+
+def combined(product):
+    rhs, block = product.shape[0] // 2, product.shape[1] // 2
     real = product[:rhs, :block] - product[rhs:, block:]
     imag = product[rhs:, :block] + product[:rhs, block:]
     return real, imag
 
 
-def inner_kernel(slot_ref, *refs):
-    tile_refs, (own_ref, side_ref, part_ref) = refs[:-3], refs[-3:]
-    modes, both = own_ref.shape[:2]
+def put(out_ref, k, both, real, imag):
+    out_ref[k * both : k * both + both // 2, :] = real
+    out_ref[k * both + both // 2 : (k + 1) * both, :] = imag
+
+
+def inner_kernel(chunks, slot_ref, *refs):
+    own_refs, side_ref, part_refs = refs[-2 * chunks - 1 : -chunks - 1], refs[-chunks - 1], refs[-chunks:]
+    tile_refs = refs[: -2 * chunks - 1]
+    modes, both = side_ref.shape[:2]
     for k in range(modes):
-        real, imag = tile_product(slot_ref, tile_refs, modes, k, (0, 1), [own_ref[k], side_ref[k]])
-        part_ref[k * both : k * both + both // 2, :] = real
-        part_ref[k * both + both // 2 : (k + 1) * both, :] = imag
-
-
-def outer_kernel(slot_ref, *refs):
-    tile_refs, (far_ref, part_ref, near_ref, held) = refs[:-4], refs[-4:]
-    modes, both = far_ref.shape[:2]
+        owns = jnp.concatenate([ref[k] for ref in own_refs], axis=0)
+        product = tile_product(slot_ref, tile_refs, modes, k, (0,), [owns])
+        side = tile_product(slot_ref, tile_refs, modes, k, (1,), [side_ref[k]])
+        for index, part_ref in enumerate(part_refs):
+            mine = product[index * both : (index + 1) * both]
+            put(part_ref, k, both, *combined(mine + side if index == 0 else mine))
+
+
+def outer_kernel(roles, slot_ref, *refs):
+    count = len(roles)
+    tile_refs, value_refs, (part_ref, near_ref, held) = refs[: -3 - count], refs[-3 - count : -3], refs[-3:]
+    modes, both = value_refs[0].shape[:2]
     rhs = both // 2
     for k in range(modes):
-        real, imag = tile_product(slot_ref, tile_refs, modes, k, (2,), [far_ref[k]])
+        real, imag = combined(tile_product(slot_ref, tile_refs, modes, k, roles, [ref[k] for ref in value_refs]))
         at_real, at_imag = slice(k * both, k * both + rhs), slice(k * both + rhs, (k + 1) * both)
         held[at_real, :] = real + part_ref[at_real, :]
         held[at_imag, :] = imag + part_ref[at_imag, :]
@@ -368,39 +380,37 @@
                 )(after(flat_tiles, own))
                 tiles.append(tail)
 
-    sides_in = [lax.ppermute(own, "curve", sides) for own in owns]
-    for index in range(CHUNKS - 1):
-        sides_in[index] = after(sides_in[index], owns[index + 1])
-    halo = []
-    for own, side in zip(owns, sides_in):
-        far = lax.ppermute(side, "curve", onward)
-        inner = pl.pallas_call(
-            inner_kernel,
-            out_shape=jax.ShapeDtypeStruct((local * 2 * per, nodes), jnp.float32),
-            in_specs=[smem] + [vmem] * (2 + SHARES),
-            out_specs=vmem,
-            cost_estimate=cost(0, tile_data.size),
-            compiler_params=params,
-            name="inner",
-        )(slot, *tiles, own, side)
-        halo.append((inner, after(far, inner)))
-    for index in range(CHUNKS - 1):
-        inner, far = halo[index]
-        halo[index] = (inner, after(far, sides_in[index + 1]))
+    side_in = [lax.ppermute(own, "curve", sides) for own in owns]
+    side_in[0] = after(side_in[0], *owns[1:])
+    far_in = [lax.ppermute(side, "curve", onward) for side in side_in]
+    part_shape = jax.ShapeDtypeStruct((local * 2 * per, nodes), jnp.float32)
+    parts_of = pl.pallas_call(
+        functools.partial(inner_kernel, CHUNKS),
+        out_shape=[part_shape] * CHUNKS,
+        in_specs=[smem] + [vmem] * (SHARES + CHUNKS + 1),
+        out_specs=[vmem] * CHUNKS,
+        cost_estimate=cost(0, tile_data.size),
+        compiler_params=params,
+        name="inner",
+    )(slot, *tiles, *owns, side_in[0])
 
     nears = []
-    for inner, far in halo:
+    for index in range(CHUNKS):
+        if index == 0:
+            roles, values = (2,), [after(far_in[0], parts_of[0], *side_in[1:])]
+        else:
+            roles, values = (1, 2), [side_in[index], after(far_in[index], nears[0])]
         nears.append(
             pl.pallas_call(
-                outer_kernel,
+                functools.partial(outer_kernel, roles),
                 out_shape=jax.ShapeDtypeStruct((per, rows, nodes), jnp.bfloat16),
-                in_specs=[smem] + [vmem] * (2 + SHARES),
+                in_specs=[smem] + [vmem] * (SHARES + len(roles) + 1),
                 out_specs=vmem,
                 scratch_shapes=[pltpu.VMEM((local * 2 * per, nodes), jnp.float32)],
                 cost_estimate=cost(0, tile_data.size // 2),
                 compiler_params=params,
                 name="outer",
-            )(slot, *tiles, far, inner)
+            )(slot, *tiles, *values, parts_of[index])
         )
 
     out = None
@@ -410,7 +420,7 @@
             if out is not None:
                 across, out = lax.optimization_barrier((across, out))
             elif CHUNKS > 1:
-                across = after(across, halo[-1][0])
+                across = after(across, nears[-1])
             sources = [near, lax.ppermute(near, "az", PEER), across, lax.ppermute(across, "az", PEER)]
         else:
             every = lax.all_gather(near, "az")

time: 57.2 us -> 53.6 us (0.937)
  waiting for transfers between devices: 18.8 us -> 15.9 us
  Pallas kernels: 22.8 us -> 21.4 us
  starting transfers between devices: 13.8 us -> 14.6 us
    ppermute x4, waiting for transfers between devices: 8.09 us -> 6.06 us  [the longest x2 4.55 us: on_device(): far_in = [lax.ppermute(side, 'curve', onward) for side in side_in]]
    pallas_call x4 -> x3, Pallas kernels: 9.21 us -> 7.82 us  [the longest x2 4.66 us: on_device(): pl.pallas_call(functools.partial(outer_kernel, roles), out_shape=jax.Shap...]
    ppermute x2, waiting for transfers between devices: 6.43 us -> 5.53 us  [on_device(): across = lax.ppermute(near, 'az', ACROSS)]
    ppermute x2, starting transfers between devices: 2.16 us -> 2.79 us  [on_device(): across = lax.ppermute(near, 'az', ACROSS)]
  transfers between devices with their start and end apart: 14 -> 14, of which waited for: 9 -> 9; matrix products, arithmetic and copies ran while one was open for 1% -> 1% of each run, Pallas kernels for 31% -> 34%
where the time goes in v5:
time: 53.6 us; the launch traced here: 53.4 us
  Pallas kernels  21.4 us (40%)
  waiting for transfers between devices  15.9 us (30%)
  starting transfers between devices  14.6 us (27%)
  local copies, waits for them, and re-layouts  1.34 us (2%)
    ppermute x2, waiting for transfers between devices, on_device(): across = lax.ppermute(near, 'az', ACROSS)  5.53 us
    pallas_call x2, Pallas kernels, on_device(): pl.pallas_call(functools.partial(outer_kernel, roles), out_shape=jax.Shap...  4.66 us
    ppermute x2, waiting for transfers between devices, on_device(): far_in = [lax.ppermute(side, 'curve', onward) for side in side_in]  4.55 us
    pallas_call x1, Pallas kernels, on_device(): pl.pallas_call(functools.partial(split_kernel, per, find), out_shape=[jax...  3.96 us
    ppermute x2, starting transfers between devices, on_device(): side_in = [lax.ppermute(own, 'curve', sides) for own in owns]  3.46 us
    ppermute x2, starting transfers between devices, on_device(): far_in = [lax.ppermute(side, 'curve', onward) for side in side_in]  3.33 us
    pallas_call x2, Pallas kernels, on_device(): pl.pallas_call(functools.partial(back_kernel, parts, rhs, index), out_sha...  3.22 us
    pallas_call x1, Pallas kernels, on_device(): pl.pallas_call(functools.partial(inner_kernel, CHUNKS), out_shape=[part_s...  3.16 us
  transfers between devices with their start and end apart: 14, of which 9 were waited for; matrix products, arithmetic and copies ran while one was open for 1% of the time, Pallas kernels for 34%

profile of v5, /device:TPU:0, one launch (start us, length us, event | category | flops | bytes accessed | tf_op | source)
XLA Modules:
  0.0 53.4 jit_solution(2538958839791130148)
XLA Ops:
  0.0 1.9 %pack.1 = (s16[8,128,128]{2,1,0:T(8,128)(2,1)S(1)}, s16[16,128,128]{2,1,0:T(8,128)(2,1)S(1)}, bf16[2,128,512]{2,1,0:T(8,128)(2,1)S(1)}, bf16[2,128,512]{2,1,0:T(8,128)(2,1)S(1)}) custom-call(s32[1]{0:T(128)} %bitcast.az_ref, f32[128,16,128]{2,1,0:T(8,128)} %bitcast.13, bf16[4,2,2,128,512]{4,3,2,1,0:T(8,128)(2,1)} %constant.10.clone.tables_ref), custom_call_target="tpu_custom_call" | custom-call | bytes 4194304 | tf_op jit(solution)/shard_map/pack/pallas_call | solution.py:290
  1.9 0.5 collective-permute-start
  2.4 2.6 %collective-permute-start.1 = (s16[8,128,128]{2,1,0:T(8,128)(2,1)S(1)}, s16[8,128,128]{2,1,0:T(8,128)(2,1)S(1)}, u32[]{:S(2)}, u32[]{:S(2)}) collective-permute-start(s16[8,128,128]{2,1,0:T(8,128)(2,1)S(1)} %get-tuple-element.32), channel_id=1, source_target_pairs={{0,16},{8,24},{16,0},{24,8},{1,17},{9,25},{17,1},{25,9},{2,18},{10... | collective-permute-start | bytes 786440 | tf_op jit(solution)/shard_map/ppermute | solution.py:351
  5.0 0.7 %copy.10 = s32[64,1,3]{0,2,1:T(4,128)S(1)} copy(s32[64,1,3]{0,1,2:T(1,128)} %param.9) | data formatting | bytes 1536
  5.7 0.0 collective-permute-done.peer_ref.refs_1_
  5.7 0.0 copy-start.2
  5.7 0.7 %copy-done.2 = s32[64,1]{0,1:T(1,128)S(1)} copy-done((s32[64,1]{0,1:T(1,128)S(1)}, s32[64,1]{0,1:T(1,128)}, u32[]{:S(2)}) %copy-start.2) | copy-done | bytes 280
  6.3 4.0 %split.1 = (f32[8,128,128]{2,1,0:T(8,128)S(1)}, s16[8,128,128]{2,1,0:T(8,128)(2,1)S(1)}, bf16[97,256,128]{2,1,0:T(8,128)(2,1)S(1)}, s32[192]{0:T(256)S(1)}) custom-call(bf16[2,128,512]{2,1,0:T(8,128)(2,1)S(1)} %get-tuple-element.27.table_ref, s16[16,128,128]{2,1,0:T(8,128)(2,1)S(1)} %get-tuple-element.28.own_ref.refs_0_, ...), custom_call_target="tpu_custom_call" | custom-call | flops 805306368 | bytes 4194304 | tf_op jit(solution)/shard_map/split/pallas_call | solution.py:309
  10.3 1.6 %collective-permute-done.1.refs_2_ = s16[8,128,128]{2,1,0:T(8,128)(2,1)S(1)} collective-permute-done((s16[8,128,128]{2,1,0:T(8,128)(2,1)S(1)}, s16[8,128,128]{2,1,0:T(8,128)(2,1)S(1)}, u32[]{:S(2)}, u32[]{:S(2)}) %collective-permute-start.1) | collective-permute-done | bytes 262176 | tf_op jit(solution)/shard_map/ppermute | solution.py:351
  11.9 0.0 collective-permute-start.2
  11.9 1.8 %collective-permute-start.3 = (s16[8,128,128]{2,1,0:T(8,128)(2,1)S(1)}, s16[8,128,128]{2,1,0:T(8,128)(2,1)S(1)}, u32[]{:S(2)}, u32[]{:S(2)}) collective-permute-start(s16[8,128,128]{2,1,0:T(8,128)(2,1)S(1)} %get-tuple-element.37), channel_id=1, source_target_pairs={{0,16},{8,24},{16,0},{24,8},{1,17},{9,25},{17,1},{25,9},{2,18},{10... | collective-permute-start | bytes 786440 | tf_op jit(solution)/shard_map/ppermute | solution.py:338
  13.6 0.0 collective-permute-done.2.refs_3_
  13.6 1.3 %forward.1.refs_2_ = bf16[64,16,128]{2,1,0:T(8,128)(2,1)S(1)} custom-call(bf16[2,128,512]{2,1,0:T(8,128)(2,1)S(1)} %get-tuple-element.27.table_ref, s16[16,128,128]{2,1,0:T(8,128)(2,1)S(1)} %get-tuple-element.28.own_ref.refs_0_, s16[16,128,128]{2,1,0:T(8,128)(2,1)S(1)} %collective-permute-done.peer_ref.refs_1_, ...), custom_call_target="tpu_custom_call" | custom-call | flops 805306368 | bytes 4194304 | tf_op jit(solution)/shard_map/forward/pallas_call | solution.py:358
  15.0 1.6 %collective-permute-start.6 = (bf16[64,16,128]{2,1,0:T(8,128)(2,1)S(1)}, bf16[64,16,128]{2,1,0:T(8,128)(2,1)S(1)}, u32[]{:S(2)}, u32[]{:S(2)}) collective-permute-start(bf16[64,16,128]{2,1,0:T(8,128)(2,1)S(1)} %forward.1.refs_2_), channel_id=1, source_target_pairs={{0,1},{1,0},{2,3},{3,2},{4,5},{5,4},{6,7},{7,6},{8,9},{9,8},{10,11... | collective-permute-start | bytes 786440 | tf_op jit(solution)/shard_map/ppermute | solution.py:383
  16.6 2.8 %stage.1.refs_1_ = bf16[97,256,128]{2,1,0:T(8,128)(2,1)S(1)} custom-call(bf16[192,256,128]{2,1,0:T(8,128)(2,1)} %bitcast.21), custom_call_target="tpu_custom_call" | custom-call | bytes 6291456 | tf_op jit(solution)/shard_map/stage/pallas_call | solution.py:371
  19.4 1.2 %collective-permute-done.3.far_ref = s16[8,128,128]{2,1,0:T(8,128)(2,1)S(1)} collective-permute-done((s16[8,128,128]{2,1,0:T(8,128)(2,1)S(1)}, s16[8,128,128]{2,1,0:T(8,128)(2,1)S(1)}, u32[]{:S(2)}, u32[]{:S(2)}) %collective-permute-start.3) | collective-permute-done | bytes 262176 | tf_op jit(solution)/shard_map/ppermute | solution.py:338
  20.6 0.4 finish.1.refs_3_
  21.0 1.8 %collective-permute-start.4 = (bf16[64,16,128]{2,1,0:T(8,128)(2,1)S(1)}, bf16[64,16,128]{2,1,0:T(8,128)(2,1)S(1)}, u32[]{:S(2)}, u32[]{:S(2)}) collective-permute-start(bf16[64,16,128]{2,1,0:T(8,128)(2,1)S(1)} %finish.1.refs_3_), channel_id=1, source_target_pairs={{0,1},{1,0},{2,3},{3,2},{4,5},{5,4},{6,7},{7,6},{8,9},{9,8},{10,11... | collective-permute-start | bytes 786440 | tf_op jit(solution)/shard_map/ppermute | solution.py:383
  22.9 0.6 %collective-permute-done.6.refs_4_ = bf16[64,16,128]{2,1,0:T(8,128)(2,1)S(1)} collective-permute-done((bf16[64,16,128]{2,1,0:T(8,128)(2,1)S(1)}, bf16[64,16,128]{2,1,0:T(8,128)(2,1)S(1)}, u32[]{:S(2)}, u32[]{:S(2)}) %collective-permute-start.6) | collective-permute-done | bytes 262176 | tf_op jit(solution)/shard_map/ppermute | solution.py:383
  23.5 1.6 %collective-permute-start.7 = (bf16[64,16,128]{2,1,0:T(8,128)(2,1)S(1)}, bf16[64,16,128]{2,1,0:T(8,128)(2,1)S(1)}, u32[]{:S(2)}, u32[]{:S(2)}) collective-permute-start(bf16[64,16,128]{2,1,0:T(8,128)(2,1)S(1)} %collective-permute-done.6.refs_4_), channel_id=1, source_target_pairs={{0,2},{1,7},{2,4},{3,1},{4,6},{5,3},{6,0},{7,5},{8,10},{9,15},{10,... | collective-permute-start | bytes 786440 | tf_op jit(solution)/shard_map/ppermute | solution.py:385
  25.1 3.2 %inner.1 = (f32[1024,128]{1,0:T(8,128)S(1)}, f32[1024,128]{1,0:T(8,128)S(1)}) custom-call(s32[192]{0:T(256)S(1)} %get-tuple-element.30.slot_ref, bf16[97,256,128]{2,1,0:T(8,128)(2,1)S(1)} %get-tuple-element.31.refs_0_, bf16[97,256,128]{2,1,0:T(8,128)(2,1)S(1)} %stage.1.refs_1_, bf16[64,16,128]{2,1,0:T(8,128)(2,1)S(1)} %forward.1.refs_2_, ...), custom_call_target="tpu_custom_call" | custom-call | bytes 6291456 | tf_op jit(solution)/shard_map/inner/pallas_call | solution.py:387
  28.2 0.9 %collective-permute-done.4.refs_2_ = bf16[64,16,128]{2,1,0:T(8,128)(2,1)S(1)} collective-permute-done((bf16[64,16,128]{2,1,0:T(8,128)(2,1)S(1)}, bf16[64,16,128]{2,1,0:T(8,128)(2,1)S(1)}, u32[]{:S(2)}, u32[]{:S(2)}) %collective-permute-start.4) | collective-permute-done | bytes 262176 | tf_op jit(solution)/shard_map/ppermute | solution.py:383
  29.1 1.8 %collective-permute-start.5 = (bf16[64,16,128]{2,1,0:T(8,128)(2,1)S(1)}, bf16[64,16,128]{2,1,0:T(8,128)(2,1)S(1)}, u32[]{:S(2)}, u32[]{:S(2)}) collective-permute-start(bf16[64,16,128]{2,1,0:T(8,128)(2,1)S(1)} %collective-permute-done.4.refs_2_), channel_id=1, source_target_pairs={{0,2},{1,7},{2,4},{3,1},{4,6},{5,3},{6,0},{7,5},{8,10},{9,15},{10,... | collective-permute-start | bytes 786440 | tf_op jit(solution)/shard_map/ppermute | solution.py:385
  30.9 2.3 %collective-permute-done.7.refs_2_ = bf16[64,16,128]{2,1,0:T(8,128)(2,1)S(1)} collective-permute-done((bf16[64,16,128]{2,1,0:T(8,128)(2,1)S(1)}, bf16[64,16,128]{2,1,0:T(8,128)(2,1)S(1)}, u32[]{:S(2)}, u32[]{:S(2)}) %collective-permute-start.7) | collective-permute-done | bytes 262176 | tf_op jit(solution)/shard_map/ppermute | solution.py:385
  33.2 1.8 %outer.2.refs_0_ = bf16[8,128,128]{2,1,0:T(8,128)(2,1)S(1)} custom-call(s32[192]{0:T(256)S(1)} %get-tuple-element.30.slot_ref, bf16[97,256,128]{2,1,0:T(8,128)(2,1)S(1)} %get-tuple-element.31.refs_0_, bf16[97,256,128]{2,1,0:T(8,128)(2,1)S(1)} %stage.1.refs_1_, bf16[64,16,128]{2,1,0:T(8,128)(2,1)S(1)} %collective-permute-done.7.refs_2_, ...), custom_call_target="tpu_custom_call" | custom-call | bytes 3145728 | tf_op jit(solution)/shard_map/outer/pallas_call | solution.py:404
  35.0 1.3 %collective-permute-start.11 = (bf16[8,128,128]{2,1,0:T(8,128)(2,1)S(1)}, bf16[8,128,128]{2,1,0:T(8,128)(2,1)S(1)}, u32[]{:S(2)}, u32[]{:S(2)}) collective-permute-start(bf16[8,128,128]{2,1,0:T(8,128)(2,1)S(1)} %outer.2.refs_0_), channel_id=1, source_target_pairs={{0,16},{8,24},{16,0},{24,8},{1,17},{9,25},{17,1},{25,9},{2,18},{10... | collective-permute-start | bytes 786440 | tf_op jit(solution)/shard_map/ppermute | solution.py:419
  36.3 0.0 collective-permute-start.10
  36.3 2.2 %collective-permute-done.5.refs_3_ = bf16[64,16,128]{2,1,0:T(8,128)(2,1)S(1)} collective-permute-done((bf16[64,16,128]{2,1,0:T(8,128)(2,1)S(1)}, bf16[64,16,128]{2,1,0:T(8,128)(2,1)S(1)}, u32[]{:S(2)}, u32[]{:S(2)}) %collective-permute-start.5) | collective-permute-done | bytes 262176 | tf_op jit(solution)/shard_map/ppermute | solution.py:385
  38.6 0.0 copy-start
  38.6 0.0 copy-start.1
  38.6 2.9 %outer.3.refs_0_ = bf16[8,128,128]{2,1,0:T(8,128)(2,1)S(1)} custom-call(s32[192]{0:T(256)S(1)} %get-tuple-element.30.slot_ref, bf16[97,256,128]{2,1,0:T(8,128)(2,1)S(1)} %get-tuple-element.31.refs_0_, bf16[97,256,128]{2,1,0:T(8,128)(2,1)S(1)} %stage.1.refs_1_, bf16[64,16,128]{2,1,0:T(8,128)(2,1)S(1)} %collective-permute-done.4.refs_2_, ...), custom_call_target="tpu_custom_call" | custom-call | bytes 3145728 | tf_op jit(solution)/shard_map/outer/pallas_call | solution.py:404
  41.4 0.1 collective-permute-done.11.refs_2_
  41.5 0.0 collective-permute-start.12
  41.5 1.4 %collective-permute-start.9 = (bf16[8,128,128]{2,1,0:T(8,128)(2,1)S(1)}, bf16[8,128,128]{2,1,0:T(8,128)(2,1)S(1)}, u32[]{:S(2)}, u32[]{:S(2)}) collective-permute-start(bf16[8,128,128]{2,1,0:T(8,128)(2,1)S(1)} %outer.3.refs_0_), channel_id=1, source_target_pairs={{0,16},{8,24},{16,0},{24,8},{1,17},{9,25},{17,1},{25,9},{2,18},{10... | collective-permute-start | bytes 786440 | tf_op jit(solution)/shard_map/ppermute | solution.py:419
  43.0 0.2 collective-permute-start.8
  43.1 0.0 collective-permute-done.10.refs_1_
  43.1 0.0 collective-permute-done.12.refs_3_
  43.2 0.0 copy-done
  43.2 0.0 copy-done.1
  43.2 1.6 %back.2.refs_4_ = f32[128,16,128]{2,1,0:T(8,128)} custom-call(bf16[2,128,512]{2,1,0:T(8,128)(2,1)S(1)} %get-tuple-element.26.table_ref, f32[2048,128]{1,0:T(8,128)S(1)} %bitcast.14, f32[128,128]{1,0:T(8,128)S(1)} %bitcast.16, bf16[8,128,128]{2,1,0:T(8,128)(2,1)S(1)} %outer.2.refs_0_, bf16[8,128,128]{2,1,0:T(8,128)(2,1)S(1)} %collective-permute-done.10.refs_1_, ...), custom_call_target="tpu_custom_call" | custom-call | flops 536870912 | bytes 4194304 | tf_op jit(solution)/shard_map/back/pallas_call | solution.py:429
  44.8 5.5 %collective-permute-done.9.refs_2_ = bf16[8,128,128]{2,1,0:T(8,128)(2,1)S(1)} collective-permute-done((bf16[8,128,128]{2,1,0:T(8,128)(2,1)S(1)}, bf16[8,128,128]{2,1,0:T(8,128)(2,1)S(1)}, u32[]{:S(2)}, u32[]{:S(2)}) %collective-permute-start.9) | collective-permute-done | bytes 262176 | tf_op jit(solution)/shard_map/ppermute | solution.py:419
  50.3 0.0 collective-permute-start.13
  50.3 0.0 collective-permute-done.8.refs_1_
  50.3 1.5 %collective-permute-done.13.refs_3_ = bf16[8,128,128]{2,1,0:T(8,128)(2,1)S(1)} collective-permute-done((bf16[8,128,128]{2,1,0:T(8,128)(2,1)S(1)}, bf16[8,128,128]{2,1,0:T(8,128)(2,1)S(1)}, u32[]{:S(2)}, u32[]{:S(2)}) %collective-permute-start.13) | collective-permute-done | bytes 262176 | tf_op jit(solution)/shard_map/ppermute | solution.py:424
  51.8 1.6 %back.3 = f32[128,16,128]{2,1,0:T(8,128)} custom-call(bf16[2,128,512]{2,1,0:T(8,128)(2,1)S(1)} %get-tuple-element.26.table_ref, f32[2048,128]{1,0:T(8,128)S(1)} %bitcast.15, f32[128,128]{1,0:T(8,128)S(1)} %bitcast.17, bf16[8,128,128]{2,1,0:T(8,128)(2,1)S(1)} %outer.3.refs_0_, ...), custom_call_target="tpu_custom_call", output_to_operand_aliasing={{}: (7, {})} | custom-call | flops 536870912 | bytes 4194304 | tf_op jit(solution)/shard_map/back/pallas_call | solution.py:429
Async XLA Ops:
  1.9 3.8 %collective-permute-start = (s16[16,128,128]{2,1,0:T(8,128)(2,1)S(1)}, s16[16,128,128]{2,1,0:T(8,128)(2,1)S(1)}, u32[]{:S(2)}, u32[]{:S(2)}) collective-permute-start(s16[16,128,128]{2,1,0:T(8,128)(2,1)S(1)} %get-tuple-element.28.own_ref.refs_0_), channel_id=1, source_target_pairs={{0,8},{8,0},{16,24},{24,16},{1,9},{9,1},{17,25},{25,17},{2,10},{10... | collective-permute-start | bytes 1572872 | tf_op jit(solution)/shard_map/ppermute | solution.py:304
  2.4 9.5 %collective-permute-start.1 = (s16[8,128,128]{2,1,0:T(8,128)(2,1)S(1)}, s16[8,128,128]{2,1,0:T(8,128)(2,1)S(1)}, u32[]{:S(2)}, u32[]{:S(2)}) collective-permute-start(s16[8,128,128]{2,1,0:T(8,128)(2,1)S(1)} %get-tuple-element.32), channel_id=1, source_target_pairs={{0,16},{8,24},{16,0},{24,8},{1,17},{9,25},{17,1},{25,9},{2,18},{10... | collective-permute-start | bytes 786440 | tf_op jit(solution)/shard_map/ppermute | solution.py:351
  5.7 0.7 %copy-start.2 = (s32[64,1]{0,1:T(1,128)S(1)}, s32[64,1]{0,1:T(1,128)}, u32[]{:S(2)}) copy-start(s32[64,1]{0,1:T(1,128)} %param.10) | copy-start | bytes 772
  11.9 1.8 %collective-permute-start.2 = (s16[8,128,128]{2,1,0:T(8,128)(2,1)S(1)}, s16[8,128,128]{2,1,0:T(8,128)(2,1)S(1)}, u32[]{:S(2)}, u32[]{:S(2)}) collective-permute-start(s16[8,128,128]{2,1,0:T(8,128)(2,1)S(1)} %collective-permute-done.1.refs_2_), channel_id=1, source_target_pairs={{0,8},{8,0},{16,24},{24,16},{1,9},{9,1},{17,25},{25,17},{2,10},{10... | collective-permute-start | bytes 786440 | tf_op jit(solution)/shard_map/ppermute | solution.py:353
  11.9 8.7 %collective-permute-start.3 = (s16[8,128,128]{2,1,0:T(8,128)(2,1)S(1)}, s16[8,128,128]{2,1,0:T(8,128)(2,1)S(1)}, u32[]{:S(2)}, u32[]{:S(2)}) collective-permute-start(s16[8,128,128]{2,1,0:T(8,128)(2,1)S(1)} %get-tuple-element.37), channel_id=1, source_target_pairs={{0,16},{8,24},{16,0},{24,8},{1,17},{9,25},{17,1},{25,9},{2,18},{10... | collective-permute-start | bytes 786440 | tf_op jit(solution)/shard_map/ppermute | solution.py:338
  15.0 8.5 %collective-permute-start.6 = (bf16[64,16,128]{2,1,0:T(8,128)(2,1)S(1)}, bf16[64,16,128]{2,1,0:T(8,128)(2,1)S(1)}, u32[]{:S(2)}, u32[]{:S(2)}) collective-permute-start(bf16[64,16,128]{2,1,0:T(8,128)(2,1)S(1)} %forward.1.refs_2_), channel_id=1, source_target_pairs={{0,1},{1,0},{2,3},{3,2},{4,5},{5,4},{6,7},{7,6},{8,9},{9,8},{10,11... | collective-permute-start | bytes 786440 | tf_op jit(solution)/shard_map/ppermute | solution.py:383
  21.0 8.1 %collective-permute-start.4 = (bf16[64,16,128]{2,1,0:T(8,128)(2,1)S(1)}, bf16[64,16,128]{2,1,0:T(8,128)(2,1)S(1)}, u32[]{:S(2)}, u32[]{:S(2)}) collective-permute-start(bf16[64,16,128]{2,1,0:T(8,128)(2,1)S(1)} %finish.1.refs_3_), channel_id=1, source_target_pairs={{0,1},{1,0},{2,3},{3,2},{4,5},{5,4},{6,7},{7,6},{8,9},{9,8},{10,11... | collective-permute-start | bytes 786440 | tf_op jit(solution)/shard_map/ppermute | solution.py:383
  23.5 9.7 %collective-permute-start.7 = (bf16[64,16,128]{2,1,0:T(8,128)(2,1)S(1)}, bf16[64,16,128]{2,1,0:T(8,128)(2,1)S(1)}, u32[]{:S(2)}, u32[]{:S(2)}) collective-permute-start(bf16[64,16,128]{2,1,0:T(8,128)(2,1)S(1)} %collective-permute-done.6.refs_4_), channel_id=1, source_target_pairs={{0,2},{1,7},{2,4},{3,1},{4,6},{5,3},{6,0},{7,5},{8,10},{9,15},{10,... | collective-permute-start | bytes 786440 | tf_op jit(solution)/shard_map/ppermute | solution.py:385
  29.1 9.4 %collective-permute-start.5 = (bf16[64,16,128]{2,1,0:T(8,128)(2,1)S(1)}, bf16[64,16,128]{2,1,0:T(8,128)(2,1)S(1)}, u32[]{:S(2)}, u32[]{:S(2)}) collective-permute-start(bf16[64,16,128]{2,1,0:T(8,128)(2,1)S(1)} %collective-permute-done.4.refs_2_), channel_id=1, source_target_pairs={{0,2},{1,7},{2,4},{3,1},{4,6},{5,3},{6,0},{7,5},{8,10},{9,15},{10,... | collective-permute-start | bytes 786440 | tf_op jit(solution)/shard_map/ppermute | solution.py:385
  35.0 6.5 %collective-permute-start.11 = (bf16[8,128,128]{2,1,0:T(8,128)(2,1)S(1)}, bf16[8,128,128]{2,1,0:T(8,128)(2,1)S(1)}, u32[]{:S(2)}, u32[]{:S(2)}) collective-permute-start(bf16[8,128,128]{2,1,0:T(8,128)(2,1)S(1)} %outer.2.refs_0_), channel_id=1, source_target_pairs={{0,16},{8,24},{16,0},{24,8},{1,17},{9,25},{17,1},{25,9},{2,18},{10... | collective-permute-start | bytes 786440 | tf_op jit(solution)/shard_map/ppermute | solution.py:419
  36.3 6.8 %collective-permute-start.10 = (bf16[8,128,128]{2,1,0:T(8,128)(2,1)S(1)}, bf16[8,128,128]{2,1,0:T(8,128)(2,1)S(1)}, u32[]{:S(2)}, u32[]{:S(2)}) collective-permute-start(bf16[8,128,128]{2,1,0:T(8,128)(2,1)S(1)} %outer.2.refs_0_), channel_id=1, source_target_pairs={{0,8},{8,0},{16,24},{24,16},{1,9},{9,1},{17,25},{25,17},{2,10},{10... | collective-permute-start | bytes 786440 | tf_op jit(solution)/shard_map/ppermute | solution.py:424
  38.6 4.6 %copy-start = (f32[2,64,16,128]{3,2,1,0:T(8,128)S(1)}, f32[2,64,16,128]{3,2,1,0:T(8,128)}, u32[]{:S(2)}) copy-start(f32[2,64,16,128]{3,2,1,0:T(8,128)} %param.6) | copy-start | bytes 3145732
  38.6 4.6 %copy-start.1 = (f32[2,64,128]{2,1,0:T(8,128)S(1)}, f32[2,64,128]{2,1,0:T(8,128)}, u32[]{:S(2)}) copy-start(f32[2,64,128]{2,1,0:T(8,128)} %param.7) | copy-start | bytes 196612
  41.5 1.6 %collective-permute-start.12 = (bf16[8,128,128]{2,1,0:T(8,128)(2,1)S(1)}, bf16[8,128,128]{2,1,0:T(8,128)(2,1)S(1)}, u32[]{:S(2)}, u32[]{:S(2)}) collective-permute-start(bf16[8,128,128]{2,1,0:T(8,128)(2,1)S(1)} %collective-permute-done.11.refs_2_), channel_id=1, source_target_pairs={{0,8},{8,0},{16,24},{24,16},{1,9},{9,1},{17,25},{25,17},{2,10},{10... | collective-permute-start | bytes 786440 | tf_op jit(solution)/shard_map/ppermute | solution.py:424
  41.5 8.7 %collective-permute-start.9 = (bf16[8,128,128]{2,1,0:T(8,128)(2,1)S(1)}, bf16[8,128,128]{2,1,0:T(8,128)(2,1)S(1)}, u32[]{:S(2)}, u32[]{:S(2)}) collective-permute-start(bf16[8,128,128]{2,1,0:T(8,128)(2,1)S(1)} %outer.3.refs_0_), channel_id=1, source_target_pairs={{0,16},{8,24},{16,0},{24,8},{1,17},{9,25},{17,1},{25,9},{2,18},{10... | collective-permute-start | bytes 786440 | tf_op jit(solution)/shard_map/ppermute | solution.py:419
  43.0 7.3 %collective-permute-start.8 = (bf16[8,128,128]{2,1,0:T(8,128)(2,1)S(1)}, bf16[8,128,128]{2,1,0:T(8,128)(2,1)S(1)}, u32[]{:S(2)}, u32[]{:S(2)}) collective-permute-start(bf16[8,128,128]{2,1,0:T(8,128)(2,1)S(1)} %outer.3.refs_0_), channel_id=1, source_target_pairs={{0,8},{8,0},{16,24},{24,16},{1,9},{9,1},{17,25},{25,17},{2,10},{10... | collective-permute-start | bytes 786440 | tf_op jit(solution)/shard_map/ppermute | solution.py:424
  50.3 1.5 %collective-permute-start.13 = (bf16[8,128,128]{2,1,0:T(8,128)(2,1)S(1)}, bf16[8,128,128]{2,1,0:T(8,128)(2,1)S(1)}, u32[]{:S(2)}, u32[]{:S(2)}) collective-permute-start(bf16[8,128,128]{2,1,0:T(8,128)(2,1)S(1)} %collective-permute-done.9.refs_2_), channel_id=1, source_target_pairs={{0,8},{8,0},{16,24},{24,16},{1,9},{9,1},{17,25},{25,17},{2,10},{10... | collective-permute-start | bytes 786440 | tf_op jit(solution)/shard_map/ppermute | solution.py:424

commit v6 on v5

--- a/solution.py
+++ b/solution.py
@@ -170,11 +170,18 @@
     find(*refs).wait()
 
 
-def tile_product(slot_ref, tile_refs, modes, k, roles, values):
-    tiles_ref = tile_refs[k * len(tile_refs) // modes]
+def chosen(slot_ref, modes, roles):
+    group = min(16, modes)
+    for first in range(0, modes, group):
+        places = [[slot_ref[role * modes + first + k] for role in roles] for k in range(group)]
+        for k in range(group):
+            yield first + k, places[k]
+
+
+def tile_product(tiles_ref, places, values):
     return lax.dot_general(
         jnp.concatenate(values, axis=1),
-        jnp.concatenate([tiles_ref[slot_ref[role * modes + k]] for role in roles], axis=1),
+        jnp.concatenate([tiles_ref[place] for place in places], axis=1),
         (((1,), (1,)), ((), ())),
         preferred_element_type=jnp.float32,
     )
@@ -196,10 +203,11 @@
     own_refs, side_ref, part_refs = refs[-2 * chunks - 1 : -chunks - 1], refs[-chunks - 1], refs[-chunks:]
     tile_refs = refs[: -2 * chunks - 1]
     modes, both = side_ref.shape[:2]
-    for k in range(modes):
+    for k, (own_place, side_place) in chosen(slot_ref, modes, (0, 1)):
+        tiles_ref = tile_refs[k * len(tile_refs) // modes]
         owns = jnp.concatenate([ref[k] for ref in own_refs], axis=0)
-        product = tile_product(slot_ref, tile_refs, modes, k, (0,), [owns])
-        side = tile_product(slot_ref, tile_refs, modes, k, (1,), [side_ref[k]])
+        product = tile_product(tiles_ref, [own_place], [owns])
+        side = tile_product(tiles_ref, [side_place], [side_ref[k]])
         for index, part_ref in enumerate(part_refs):
             mine = product[index * both : (index + 1) * both]
             put(part_ref, k, both, *combined(mine + side if index == 0 else mine))
@@ -210,8 +218,9 @@
     tile_refs, value_refs, (part_ref, near_ref, held) = refs[: -3 - count], refs[-3 - count : -3], refs[-3:]
     modes, both = value_refs[0].shape[:2]
     rhs = both // 2
-    for k in range(modes):
-        real, imag = combined(tile_product(slot_ref, tile_refs, modes, k, roles, [ref[k] for ref in value_refs]))
+    for k, places in chosen(slot_ref, modes, roles):
+        tiles_ref = tile_refs[k * len(tile_refs) // modes]
+        real, imag = combined(tile_product(tiles_ref, places, [ref[k] for ref in value_refs]))
         at_real, at_imag = slice(k * both, k * both + rhs), slice(k * both + rhs, (k + 1) * both)
         held[at_real, :] = real + part_ref[at_real, :]
         held[at_imag, :] = imag + part_ref[at_imag, :]
@@ -221,18 +230,35 @@
             near_ref[r, rows, :] = held[pl.ds(part * rhs + r, modes, stride=both), :].astype(jnp.bfloat16)
 
 
-def back_kernel(sources, rhs, chunk, table_ref, fields_ref, impedance_ref, *refs):
-    near_refs, out_ref, held, sem = refs[:sources], refs[-3], refs[-2], refs[-1]
-    per, rows, nodes = near_refs[0].shape
+def back_product(table_ref, near_refs, terms, r):
+    rows = near_refs[0].shape[1]
+    total = None
+    for j, ref in zip(terms, near_refs):
+        x = jnp.concatenate([ref[r], ref[r + 1]], axis=1)
+        for way in range(2):
+            product = jnp.dot(
+                table_ref[way, :, j * rows : (j + 1) * rows], x, preferred_element_type=jnp.float32
+            )
+            total = product if total is None else total + product
+    return total
+
+
+def back_kernel(sources, ahead, chunk, starts, table_ref, fields_ref, impedance_ref, *refs):
+    given, next_refs, refs = refs[:sources], refs[sources : sources + ahead], refs[sources + ahead :]
+    if starts:
+        ready_ref, refs = refs[0], refs[1:]
+    if ahead:
+        out_ref, next_out, held, sem = refs[-4:]
+    else:
+        out_ref, held, sem = refs[-3:]
+    per, rows, nodes = given[0].shape
+    rhs = fields_ref.shape[0] // rows
     local = rows // 2
     z_real, z_imag = impedance_ref[:local], impedance_ref[local:]
     for r in range(0, per, 2):
-        total = jnp.zeros((rows, 2 * nodes), jnp.float32)
-        for j in range(sources):
-            x = jnp.concatenate([near_refs[j][r], near_refs[j][r + 1]], axis=1)
-            cols = slice(j * rows, (j + 1) * rows)
-            total += jnp.dot(table_ref[0, :, cols], x, preferred_element_type=jnp.float32)
-            total += jnp.dot(table_ref[1, :, cols], x, preferred_element_type=jnp.float32)
+        total = back_product(table_ref, given, range(starts, starts + sources), r)
+        if starts:
+            total += ready_ref[r // 2]
         for s in range(2):
             real, imag = total[:local, s * nodes : (s + 1) * nodes], total[local:, s * nodes : (s + 1) * nodes]
             from_row = chunk * per + r + s
@@ -244,6 +270,9 @@
         held.reshape(rows, per, nodes), out_ref.at[:, pl.ds(chunk * per, per), :], sem
     )
     copy.start()
+    if ahead:
+        for r in range(0, per, 2):
+            next_out[r // 2] = back_product(table_ref, next_refs, range(ahead), r)
     copy.wait()
 
 
@@ -413,30 +442,39 @@
             )(slot, *tiles, *values, parts_of[index])
         )
 
-    out = None
+    peers = [lax.ppermute(near, "az", PEER) for near in nears] if paired else []
+    out, ready = None, None
     for index, near in enumerate(nears):
+        starts, ahead = 0, 0
         if paired:
             across = lax.ppermute(near, "az", ACROSS)
-            if out is not None:
-                across, out = lax.optimization_barrier((across, out))
-            elif CHUNKS > 1:
+            if index:
+                starts = 2
+                across, out, ready = lax.optimization_barrier((across, out, ready))
+                given = [across, lax.ppermute(across, "az", PEER), ready, out]
+            else:
                 across = after(across, nears[-1])
-            sources = [near, lax.ppermute(near, "az", PEER), across, lax.ppermute(across, "az", PEER)]
+                given = [near, peers[0], across, lax.ppermute(across, "az", PEER)]
+            if index + 1 < CHUNKS:
+                ahead = 2
+                given[4 - starts : 4 - starts] = [nears[index + 1], peers[index + 1]]
         else:
             every = lax.all_gather(near, "az")
-            sources = [every[j] for j in range(parts)]
-        earlier = [] if out is None else [out]
-        out = pl.pallas_call(
-            functools.partial(back_kernel, parts, rhs, index),
-            out_shape=jax.ShapeDtypeStruct((rows, rhs, nodes), jnp.float32),
-            in_specs=[vmem] * (3 + parts) + [hbm] * len(earlier),
-            out_specs=hbm,
+            given = [every[j] for j in range(parts)] + ([] if out is None else [out])
+        operands = [back_table, flat_fields, flat_impedance] + given
+        results = pl.pallas_call(
+            functools.partial(back_kernel, parts - starts, ahead, index, starts),
+            out_shape=[jax.ShapeDtypeStruct((rows, rhs, nodes), jnp.float32)]
+            + [jax.ShapeDtypeStruct((per // 2, rows, 2 * nodes), jnp.float32)] * (ahead > 0),
+            in_specs=[vmem] * (len(operands) - (out is not None)) + [hbm] * (out is not None),
+            out_specs=[hbm] + [vmem] * (ahead > 0),
             scratch_shapes=[pltpu.VMEM((rows * per, nodes), jnp.float32), pltpu.SemaphoreType.DMA],
-            input_output_aliases={3 + parts: 0} if earlier else {},
+            input_output_aliases={} if out is None else {len(operands) - 1: 0},
             cost_estimate=cost(2 * multiply, move),
             compiler_params=params,
             name="back",
-        )(back_table, flat_fields, flat_impedance, *sources, *earlier)
+        )(*operands)
+        out, ready = results[0], results[-1]
     return out.reshape(fields.shape)
 
 

time: 53.6 us -> 53.4 us (level)
  transfers between devices with their start and end apart: 14 -> 14, of which waited for: 9 -> 8; matrix products, arithmetic and copies ran while one was open for 1% -> 1% of each run, Pallas kernels for 34% -> 34%
where the time goes in v6:
time: 53.4 us; the launch traced here: 53.2 us
  Pallas kernels  21.2 us (40%)
  waiting for transfers between devices  15.6 us (29%)
  starting transfers between devices  14.9 us (28%)
  local copies, waits for them, and re-layouts  1.34 us (3%)
    ppermute x2, waiting for transfers between devices, on_device(): across = lax.ppermute(near, 'az', ACROSS)  5.18 us
    pallas_call x2, Pallas kernels, on_device(): pl.pallas_call(functools.partial(outer_kernel, roles), out_shape=jax.Shap...  4.66 us
    ppermute x2, waiting for transfers between devices, on_device(): far_in = [lax.ppermute(side, 'curve', onward) for side in side_in]  4.55 us
    pallas_call x1, Pallas kernels, on_device(): pl.pallas_call(functools.partial(split_kernel, per, find), out_shape=[jax...  3.96 us
    ppermute x2, starting transfers between devices, on_device(): side_in = [lax.ppermute(own, 'curve', sides) for own in owns]  3.46 us
    ppermute x2, starting transfers between devices, on_device(): far_in = [lax.ppermute(side, 'curve', onward) for side in side_in]  3.33 us
    pallas_call x1, Pallas kernels, on_device(): pl.pallas_call(functools.partial(inner_kernel, CHUNKS), out_shape=[part_s...  3.16 us
    pallas_call x2, Pallas kernels, on_device(): pl.pallas_call(functools.partial(back_kernel, parts - starts, ahead, inde...  3.02 us
  transfers between devices with their start and end apart: 14, of which 8 were waited for; matrix products, arithmetic and copies ran while one was open for 1% of the time, Pallas kernels for 34%

profile of v6, /device:TPU:0, one launch (start us, length us, event | category | flops | bytes accessed | tf_op | source)
XLA Modules:
  0.0 53.2 jit_solution(11107938427676588633)
XLA Ops:
  0.0 1.9 %pack.1 = (s16[8,128,128]{2,1,0:T(8,128)(2,1)S(1)}, s16[16,128,128]{2,1,0:T(8,128)(2,1)S(1)}, bf16[2,128,512]{2,1,0:T(8,128)(2,1)S(1)}, bf16[2,128,512]{2,1,0:T(8,128)(2,1)S(1)}) custom-call(s32[1]{0:T(128)} %bitcast.az_ref, f32[128,16,128]{2,1,0:T(8,128)} %bitcast.13, bf16[4,2,2,128,512]{4,3,2,1,0:T(8,128)(2,1)} %constant.10.clone.tables_ref), custom_call_target="tpu_custom_call" | custom-call | bytes 4194304 | tf_op jit(solution)/shard_map/pack/pallas_call | solution.py:319
  1.9 0.5 collective-permute-start
  2.4 2.6 %collective-permute-start.1 = (s16[8,128,128]{2,1,0:T(8,128)(2,1)S(1)}, s16[8,128,128]{2,1,0:T(8,128)(2,1)S(1)}, u32[]{:S(2)}, u32[]{:S(2)}) collective-permute-start(s16[8,128,128]{2,1,0:T(8,128)(2,1)S(1)} %get-tuple-element.35), channel_id=1, source_target_pairs={{0,16},{8,24},{16,0},{24,8},{1,17},{9,25},{17,1},{25,9},{2,18},{10... | collective-permute-start | bytes 786440 | tf_op jit(solution)/shard_map/ppermute | solution.py:380
  5.0 0.7 %copy.10 = s32[64,1,3]{0,2,1:T(4,128)S(1)} copy(s32[64,1,3]{0,1,2:T(1,128)} %param.9) | data formatting | bytes 1536
  5.7 0.0 collective-permute-done.peer_ref.refs_1_
  5.7 0.0 copy-start.2
  5.7 0.7 %copy-done.2 = s32[64,1]{0,1:T(1,128)S(1)} copy-done((s32[64,1]{0,1:T(1,128)S(1)}, s32[64,1]{0,1:T(1,128)}, u32[]{:S(2)}) %copy-start.2) | copy-done | bytes 280
  6.3 4.0 %split.1 = (f32[8,128,128]{2,1,0:T(8,128)S(1)}, s16[8,128,128]{2,1,0:T(8,128)(2,1)S(1)}, bf16[97,256,128]{2,1,0:T(8,128)(2,1)S(1)}, s32[192]{0:T(256)S(1)}) custom-call(bf16[2,128,512]{2,1,0:T(8,128)(2,1)S(1)} %get-tuple-element.30.table_ref, s16[16,128,128]{2,1,0:T(8,128)(2,1)S(1)} %get-tuple-element.31.own_ref.refs_0_, ...), custom_call_target="tpu_custom_call" | custom-call | flops 805306368 | bytes 4194304 | tf_op jit(solution)/shard_map/split/pallas_call | solution.py:338
  10.3 1.6 %collective-permute-done.1.refs_2_ = s16[8,128,128]{2,1,0:T(8,128)(2,1)S(1)} collective-permute-done((s16[8,128,128]{2,1,0:T(8,128)(2,1)S(1)}, s16[8,128,128]{2,1,0:T(8,128)(2,1)S(1)}, u32[]{:S(2)}, u32[]{:S(2)}) %collective-permute-start.1) | collective-permute-done | bytes 262176 | tf_op jit(solution)/shard_map/ppermute | solution.py:380
  11.9 0.0 collective-permute-start.2
  11.9 1.8 %collective-permute-start.3 = (s16[8,128,128]{2,1,0:T(8,128)(2,1)S(1)}, s16[8,128,128]{2,1,0:T(8,128)(2,1)S(1)}, u32[]{:S(2)}, u32[]{:S(2)}) collective-permute-start(s16[8,128,128]{2,1,0:T(8,128)(2,1)S(1)} %get-tuple-element.40), channel_id=1, source_target_pairs={{0,16},{8,24},{16,0},{24,8},{1,17},{9,25},{17,1},{25,9},{2,18},{10... | collective-permute-start | bytes 786440 | tf_op jit(solution)/shard_map/ppermute | solution.py:367
  13.6 0.0 collective-permute-done.2.refs_3_
  13.6 1.3 %forward.1.refs_2_ = bf16[64,16,128]{2,1,0:T(8,128)(2,1)S(1)} custom-call(bf16[2,128,512]{2,1,0:T(8,128)(2,1)S(1)} %get-tuple-element.30.table_ref, s16[16,128,128]{2,1,0:T(8,128)(2,1)S(1)} %get-tuple-element.31.own_ref.refs_0_, s16[16,128,128]{2,1,0:T(8,128)(2,1)S(1)} %collective-permute-done.peer_ref.refs_1_, ...), custom_call_target="tpu_custom_call" | custom-call | flops 805306368 | bytes 4194304 | tf_op jit(solution)/shard_map/forward/pallas_call | solution.py:387
  15.0 1.6 %collective-permute-start.6 = (bf16[64,16,128]{2,1,0:T(8,128)(2,1)S(1)}, bf16[64,16,128]{2,1,0:T(8,128)(2,1)S(1)}, u32[]{:S(2)}, u32[]{:S(2)}) collective-permute-start(bf16[64,16,128]{2,1,0:T(8,128)(2,1)S(1)} %forward.1.refs_2_), channel_id=1, source_target_pairs={{0,1},{1,0},{2,3},{3,2},{4,5},{5,4},{6,7},{7,6},{8,9},{9,8},{10,11... | collective-permute-start | bytes 786440 | tf_op jit(solution)/shard_map/ppermute | solution.py:412
  16.6 2.8 %stage.1.refs_1_ = bf16[97,256,128]{2,1,0:T(8,128)(2,1)S(1)} custom-call(bf16[192,256,128]{2,1,0:T(8,128)(2,1)} %bitcast.21), custom_call_target="tpu_custom_call" | custom-call | bytes 6291456 | tf_op jit(solution)/shard_map/stage/pallas_call | solution.py:400
  19.4 1.2 %collective-permute-done.3.far_ref = s16[8,128,128]{2,1,0:T(8,128)(2,1)S(1)} collective-permute-done((s16[8,128,128]{2,1,0:T(8,128)(2,1)S(1)}, s16[8,128,128]{2,1,0:T(8,128)(2,1)S(1)}, u32[]{:S(2)}, u32[]{:S(2)}) %collective-permute-start.3) | collective-permute-done | bytes 262176 | tf_op jit(solution)/shard_map/ppermute | solution.py:367
  20.6 0.4 finish.1.refs_3_
  21.0 1.8 %collective-permute-start.4 = (bf16[64,16,128]{2,1,0:T(8,128)(2,1)S(1)}, bf16[64,16,128]{2,1,0:T(8,128)(2,1)S(1)}, u32[]{:S(2)}, u32[]{:S(2)}) collective-permute-start(bf16[64,16,128]{2,1,0:T(8,128)(2,1)S(1)} %finish.1.refs_3_), channel_id=1, source_target_pairs={{0,1},{1,0},{2,3},{3,2},{4,5},{5,4},{6,7},{7,6},{8,9},{9,8},{10,11... | collective-permute-start | bytes 786440 | tf_op jit(solution)/shard_map/ppermute | solution.py:412
  22.9 0.6 %collective-permute-done.6.refs_4_ = bf16[64,16,128]{2,1,0:T(8,128)(2,1)S(1)} collective-permute-done((bf16[64,16,128]{2,1,0:T(8,128)(2,1)S(1)}, bf16[64,16,128]{2,1,0:T(8,128)(2,1)S(1)}, u32[]{:S(2)}, u32[]{:S(2)}) %collective-permute-start.6) | collective-permute-done | bytes 262176 | tf_op jit(solution)/shard_map/ppermute | solution.py:412
  23.5 1.6 %collective-permute-start.7 = (bf16[64,16,128]{2,1,0:T(8,128)(2,1)S(1)}, bf16[64,16,128]{2,1,0:T(8,128)(2,1)S(1)}, u32[]{:S(2)}, u32[]{:S(2)}) collective-permute-start(bf16[64,16,128]{2,1,0:T(8,128)(2,1)S(1)} %collective-permute-done.6.refs_4_), channel_id=1, source_target_pairs={{0,2},{1,7},{2,4},{3,1},{4,6},{5,3},{6,0},{7,5},{8,10},{9,15},{10,... | collective-permute-start | bytes 786440 | tf_op jit(solution)/shard_map/ppermute | solution.py:414
  25.1 3.2 %inner.1 = (f32[1024,128]{1,0:T(8,128)S(1)}, f32[1024,128]{1,0:T(8,128)S(1)}) custom-call(s32[192]{0:T(256)S(1)} %get-tuple-element.33.slot_ref, bf16[97,256,128]{2,1,0:T(8,128)(2,1)S(1)} %get-tuple-element.34.refs_0_, bf16[97,256,128]{2,1,0:T(8,128)(2,1)S(1)} %stage.1.refs_1_, bf16[64,16,128]{2,1,0:T(8,128)(2,1)S(1)} %forward.1.refs_2_, ...), custom_call_target="tpu_custom_call" | custom-call | bytes 6291456 | tf_op jit(solution)/shard_map/inner/pallas_call | solution.py:416
  28.2 0.9 %collective-permute-done.4.refs_2_ = bf16[64,16,128]{2,1,0:T(8,128)(2,1)S(1)} collective-permute-done((bf16[64,16,128]{2,1,0:T(8,128)(2,1)S(1)}, bf16[64,16,128]{2,1,0:T(8,128)(2,1)S(1)}, u32[]{:S(2)}, u32[]{:S(2)}) %collective-permute-start.4) | collective-permute-done | bytes 262176 | tf_op jit(solution)/shard_map/ppermute | solution.py:412
  29.1 1.8 %collective-permute-start.5 = (bf16[64,16,128]{2,1,0:T(8,128)(2,1)S(1)}, bf16[64,16,128]{2,1,0:T(8,128)(2,1)S(1)}, u32[]{:S(2)}, u32[]{:S(2)}) collective-permute-start(bf16[64,16,128]{2,1,0:T(8,128)(2,1)S(1)} %collective-permute-done.4.refs_2_), channel_id=1, source_target_pairs={{0,2},{1,7},{2,4},{3,1},{4,6},{5,3},{6,0},{7,5},{8,10},{9,15},{10,... | collective-permute-start | bytes 786440 | tf_op jit(solution)/shard_map/ppermute | solution.py:414
  30.9 2.3 %collective-permute-done.7.refs_2_ = bf16[64,16,128]{2,1,0:T(8,128)(2,1)S(1)} collective-permute-done((bf16[64,16,128]{2,1,0:T(8,128)(2,1)S(1)}, bf16[64,16,128]{2,1,0:T(8,128)(2,1)S(1)}, u32[]{:S(2)}, u32[]{:S(2)}) %collective-permute-start.7) | collective-permute-done | bytes 262176 | tf_op jit(solution)/shard_map/ppermute | solution.py:414
  33.2 1.8 %outer.2.refs_0_ = bf16[8,128,128]{2,1,0:T(8,128)(2,1)S(1)} custom-call(s32[192]{0:T(256)S(1)} %get-tuple-element.33.slot_ref, bf16[97,256,128]{2,1,0:T(8,128)(2,1)S(1)} %get-tuple-element.34.refs_0_, bf16[97,256,128]{2,1,0:T(8,128)(2,1)S(1)} %stage.1.refs_1_, bf16[64,16,128]{2,1,0:T(8,128)(2,1)S(1)} %collective-permute-done.7.refs_2_, ...), custom_call_target="tpu_custom_call" | custom-call | bytes 3145728 | tf_op jit(solution)/shard_map/outer/pallas_call | solution.py:433
  35.0 1.3 %collective-permute-start.10 = (bf16[8,128,128]{2,1,0:T(8,128)(2,1)S(1)}, bf16[8,128,128]{2,1,0:T(8,128)(2,1)S(1)}, u32[]{:S(2)}, u32[]{:S(2)}) collective-permute-start(bf16[8,128,128]{2,1,0:T(8,128)(2,1)S(1)} %outer.2.refs_0_), channel_id=1, source_target_pairs={{0,16},{8,24},{16,0},{24,8},{1,17},{9,25},{17,1},{25,9},{2,18},{10... | collective-permute-start | bytes 786440 | tf_op jit(solution)/shard_map/ppermute | solution.py:450
  36.3 0.0 collective-permute-start.9
  36.3 2.2 %collective-permute-done.5.refs_3_ = bf16[64,16,128]{2,1,0:T(8,128)(2,1)S(1)} collective-permute-done((bf16[64,16,128]{2,1,0:T(8,128)(2,1)S(1)}, bf16[64,16,128]{2,1,0:T(8,128)(2,1)S(1)}, u32[]{:S(2)}, u32[]{:S(2)}) %collective-permute-start.5) | collective-permute-done | bytes 262176 | tf_op jit(solution)/shard_map/ppermute | solution.py:414
  38.6 0.0 copy-start
  38.6 0.0 copy-start.1
  38.6 2.9 %outer.3.refs_4_ = bf16[8,128,128]{2,1,0:T(8,128)(2,1)S(1)} custom-call(s32[192]{0:T(256)S(1)} %get-tuple-element.33.slot_ref, bf16[97,256,128]{2,1,0:T(8,128)(2,1)S(1)} %get-tuple-element.34.refs_0_, bf16[97,256,128]{2,1,0:T(8,128)(2,1)S(1)} %stage.1.refs_1_, bf16[64,16,128]{2,1,0:T(8,128)(2,1)S(1)} %collective-permute-done.4.refs_2_, ...), custom_call_target="tpu_custom_call" | custom-call | bytes 3145728 | tf_op jit(solution)/shard_map/outer/pallas_call | solution.py:433
  41.4 0.1 collective-permute-start.12
  41.5 0.0 collective-permute-done.10.refs_2_
  41.5 0.5 collective-permute-start.11
  42.0 1.4 %collective-permute-start.8 = (bf16[8,128,128]{2,1,0:T(8,128)(2,1)S(1)}, bf16[8,128,128]{2,1,0:T(8,128)(2,1)S(1)}, u32[]{:S(2)}, u32[]{:S(2)}) collective-permute-start(bf16[8,128,128]{2,1,0:T(8,128)(2,1)S(1)} %outer.3.refs_4_), channel_id=1, source_target_pairs={{0,16},{8,24},{16,0},{24,8},{1,17},{9,25},{17,1},{25,9},{2,18},{10... | collective-permute-start | bytes 786440 | tf_op jit(solution)/shard_map/ppermute | solution.py:450
  43.4 0.0 collective-permute-done.12.refs_5_
  43.4 0.0 collective-permute-done.9.refs_1_
  43.4 0.0 collective-permute-done.11.refs_3_
  43.4 0.0 copy-done
  43.4 0.0 copy-done.1
  43.4 1.7 %back.2 = (f32[128,16,128]{2,1,0:T(8,128)}, f32[4,128,256]{2,1,0:T(8,128)S(1)}) custom-call(bf16[2,128,512]{2,1,0:T(8,128)(2,1)S(1)} %get-tuple-element.29.table_ref, f32[2048,128]{1,0:T(8,128)S(1)} %bitcast.14, f32[128,128]{1,0:T(8,128)S(1)} %bitcast.16, bf16[8,128,128]{2,1,0:T(8,128)(2,1)S(1)} %outer.2.refs_0_, ...), custom_call_target="tpu_custom_call" | custom-call | flops 536870912 | bytes 4194304 | tf_op jit(solution)/shard_map/back/pallas_call | solution.py:465
  45.1 5.2 %collective-permute-done.8.refs_0_ = bf16[8,128,128]{2,1,0:T(8,128)(2,1)S(1)} collective-permute-done((bf16[8,128,128]{2,1,0:T(8,128)(2,1)S(1)}, bf16[8,128,128]{2,1,0:T(8,128)(2,1)S(1)}, u32[]{:S(2)}, u32[]{:S(2)}) %collective-permute-start.8) | collective-permute-done | bytes 262176 | tf_op jit(solution)/shard_map/ppermute | solution.py:450
  50.3 0.0 collective-permute-start.13
  50.3 1.5 %collective-permute-done.13.refs_1_ = bf16[8,128,128]{2,1,0:T(8,128)(2,1)S(1)} collective-permute-done((bf16[8,128,128]{2,1,0:T(8,128)(2,1)S(1)}, bf16[8,128,128]{2,1,0:T(8,128)(2,1)S(1)}, u32[]{:S(2)}, u32[]{:S(2)}) %collective-permute-start.13) | collective-permute-done | bytes 262176 | tf_op jit(solution)/shard_map/ppermute | solution.py:454
  51.9 1.3 %back.3 = f32[128,16,128]{2,1,0:T(8,128)} custom-call(bf16[2,128,512]{2,1,0:T(8,128)(2,1)S(1)} %get-tuple-element.29.table_ref, f32[2048,128]{1,0:T(8,128)S(1)} %bitcast.15, f32[128,128]{1,0:T(8,128)S(1)} %bitcast.17, bf16[8,128,128]{2,1,0:T(8,128)(2,1)S(1)} %collective-permute-done.8.refs_0_, ...), custom_call_target="tpu_custom_call", output_to_operand_aliasing={{}: (6, {})} | custom-call | flops 536870912 | bytes 4194304 | tf_op jit(solution)/shard_map/back/pallas_call | solution.py:465
Async XLA Ops:
  1.9 3.8 %collective-permute-start = (s16[16,128,128]{2,1,0:T(8,128)(2,1)S(1)}, s16[16,128,128]{2,1,0:T(8,128)(2,1)S(1)}, u32[]{:S(2)}, u32[]{:S(2)}) collective-permute-start(s16[16,128,128]{2,1,0:T(8,128)(2,1)S(1)} %get-tuple-element.31.own_ref.refs_0_), channel_id=1, source_target_pairs={{0,8},{8,0},{16,24},{24,16},{1,9},{9,1},{17,25},{25,17},{2,10},{10... | collective-permute-start | bytes 1572872 | tf_op jit(solution)/shard_map/ppermute | solution.py:333
  2.4 9.5 %collective-permute-start.1 = (s16[8,128,128]{2,1,0:T(8,128)(2,1)S(1)}, s16[8,128,128]{2,1,0:T(8,128)(2,1)S(1)}, u32[]{:S(2)}, u32[]{:S(2)}) collective-permute-start(s16[8,128,128]{2,1,0:T(8,128)(2,1)S(1)} %get-tuple-element.35), channel_id=1, source_target_pairs={{0,16},{8,24},{16,0},{24,8},{1,17},{9,25},{17,1},{25,9},{2,18},{10... | collective-permute-start | bytes 786440 | tf_op jit(solution)/shard_map/ppermute | solution.py:380
  5.7 0.7 %copy-start.2 = (s32[64,1]{0,1:T(1,128)S(1)}, s32[64,1]{0,1:T(1,128)}, u32[]{:S(2)}) copy-start(s32[64,1]{0,1:T(1,128)} %param.10) | copy-start | bytes 772
  11.9 1.8 %collective-permute-start.2 = (s16[8,128,128]{2,1,0:T(8,128)(2,1)S(1)}, s16[8,128,128]{2,1,0:T(8,128)(2,1)S(1)}, u32[]{:S(2)}, u32[]{:S(2)}) collective-permute-start(s16[8,128,128]{2,1,0:T(8,128)(2,1)S(1)} %collective-permute-done.1.refs_2_), channel_id=1, source_target_pairs={{0,8},{8,0},{16,24},{24,16},{1,9},{9,1},{17,25},{25,17},{2,10},{10... | collective-permute-start | bytes 786440 | tf_op jit(solution)/shard_map/ppermute | solution.py:382
  11.9 8.7 %collective-permute-start.3 = (s16[8,128,128]{2,1,0:T(8,128)(2,1)S(1)}, s16[8,128,128]{2,1,0:T(8,128)(2,1)S(1)}, u32[]{:S(2)}, u32[]{:S(2)}) collective-permute-start(s16[8,128,128]{2,1,0:T(8,128)(2,1)S(1)} %get-tuple-element.40), channel_id=1, source_target_pairs={{0,16},{8,24},{16,0},{24,8},{1,17},{9,25},{17,1},{25,9},{2,18},{10... | collective-permute-start | bytes 786440 | tf_op jit(solution)/shard_map/ppermute | solution.py:367
  15.0 8.5 %collective-permute-start.6 = (bf16[64,16,128]{2,1,0:T(8,128)(2,1)S(1)}, bf16[64,16,128]{2,1,0:T(8,128)(2,1)S(1)}, u32[]{:S(2)}, u32[]{:S(2)}) collective-permute-start(bf16[64,16,128]{2,1,0:T(8,128)(2,1)S(1)} %forward.1.refs_2_), channel_id=1, source_target_pairs={{0,1},{1,0},{2,3},{3,2},{4,5},{5,4},{6,7},{7,6},{8,9},{9,8},{10,11... | collective-permute-start | bytes 786440 | tf_op jit(solution)/shard_map/ppermute | solution.py:412
  21.0 8.1 %collective-permute-start.4 = (bf16[64,16,128]{2,1,0:T(8,128)(2,1)S(1)}, bf16[64,16,128]{2,1,0:T(8,128)(2,1)S(1)}, u32[]{:S(2)}, u32[]{:S(2)}) collective-permute-start(bf16[64,16,128]{2,1,0:T(8,128)(2,1)S(1)} %finish.1.refs_3_), channel_id=1, source_target_pairs={{0,1},{1,0},{2,3},{3,2},{4,5},{5,4},{6,7},{7,6},{8,9},{9,8},{10,11... | collective-permute-start | bytes 786440 | tf_op jit(solution)/shard_map/ppermute | solution.py:412
  23.5 9.7 %collective-permute-start.7 = (bf16[64,16,128]{2,1,0:T(8,128)(2,1)S(1)}, bf16[64,16,128]{2,1,0:T(8,128)(2,1)S(1)}, u32[]{:S(2)}, u32[]{:S(2)}) collective-permute-start(bf16[64,16,128]{2,1,0:T(8,128)(2,1)S(1)} %collective-permute-done.6.refs_4_), channel_id=1, source_target_pairs={{0,2},{1,7},{2,4},{3,1},{4,6},{5,3},{6,0},{7,5},{8,10},{9,15},{10,... | collective-permute-start | bytes 786440 | tf_op jit(solution)/shard_map/ppermute | solution.py:414
  29.1 9.4 %collective-permute-start.5 = (bf16[64,16,128]{2,1,0:T(8,128)(2,1)S(1)}, bf16[64,16,128]{2,1,0:T(8,128)(2,1)S(1)}, u32[]{:S(2)}, u32[]{:S(2)}) collective-permute-start(bf16[64,16,128]{2,1,0:T(8,128)(2,1)S(1)} %collective-permute-done.4.refs_2_), channel_id=1, source_target_pairs={{0,2},{1,7},{2,4},{3,1},{4,6},{5,3},{6,0},{7,5},{8,10},{9,15},{10,... | collective-permute-start | bytes 786440 | tf_op jit(solution)/shard_map/ppermute | solution.py:414
  35.0 6.5 %collective-permute-start.10 = (bf16[8,128,128]{2,1,0:T(8,128)(2,1)S(1)}, bf16[8,128,128]{2,1,0:T(8,128)(2,1)S(1)}, u32[]{:S(2)}, u32[]{:S(2)}) collective-permute-start(bf16[8,128,128]{2,1,0:T(8,128)(2,1)S(1)} %outer.2.refs_0_), channel_id=1, source_target_pairs={{0,16},{8,24},{16,0},{24,8},{1,17},{9,25},{17,1},{25,9},{2,18},{10... | collective-permute-start | bytes 786440 | tf_op jit(solution)/shard_map/ppermute | solution.py:450
  36.3 7.1 %collective-permute-start.9 = (bf16[8,128,128]{2,1,0:T(8,128)(2,1)S(1)}, bf16[8,128,128]{2,1,0:T(8,128)(2,1)S(1)}, u32[]{:S(2)}, u32[]{:S(2)}) collective-permute-start(bf16[8,128,128]{2,1,0:T(8,128)(2,1)S(1)} %outer.2.refs_0_), channel_id=1, source_target_pairs={{0,8},{8,0},{16,24},{24,16},{1,9},{9,1},{17,25},{25,17},{2,10},{10... | collective-permute-start | bytes 786440 | tf_op jit(solution)/shard_map/ppermute | solution.py:445
  38.6 4.9 %copy-start = (f32[2,64,16,128]{3,2,1,0:T(8,128)S(1)}, f32[2,64,16,128]{3,2,1,0:T(8,128)}, u32[]{:S(2)}) copy-start(f32[2,64,16,128]{3,2,1,0:T(8,128)} %param.6) | copy-start | bytes 3145732
  38.6 4.9 %copy-start.1 = (f32[2,64,128]{2,1,0:T(8,128)S(1)}, f32[2,64,128]{2,1,0:T(8,128)}, u32[]{:S(2)}) copy-start(f32[2,64,128]{2,1,0:T(8,128)} %param.7) | copy-start | bytes 196612
  41.4 2.0 %collective-permute-start.12 = (bf16[8,128,128]{2,1,0:T(8,128)(2,1)S(1)}, bf16[8,128,128]{2,1,0:T(8,128)(2,1)S(1)}, u32[]{:S(2)}, u32[]{:S(2)}) collective-permute-start(bf16[8,128,128]{2,1,0:T(8,128)(2,1)S(1)} %outer.3.refs_4_), channel_id=1, source_target_pairs={{0,8},{8,0},{16,24},{24,16},{1,9},{9,1},{17,25},{25,17},{2,10},{10... | collective-permute-start | bytes 786440 | tf_op jit(solution)/shard_map/ppermute | solution.py:445
  41.5 1.9 %collective-permute-start.11 = (bf16[8,128,128]{2,1,0:T(8,128)(2,1)S(1)}, bf16[8,128,128]{2,1,0:T(8,128)(2,1)S(1)}, u32[]{:S(2)}, u32[]{:S(2)}) collective-permute-start(bf16[8,128,128]{2,1,0:T(8,128)(2,1)S(1)} %collective-permute-done.10.refs_2_), channel_id=1, source_target_pairs={{0,8},{8,0},{16,24},{24,16},{1,9},{9,1},{17,25},{25,17},{2,10},{10... | collective-permute-start | bytes 786440 | tf_op jit(solution)/shard_map/ppermute | solution.py:457
  42.0 8.3 %collective-permute-start.8 = (bf16[8,128,128]{2,1,0:T(8,128)(2,1)S(1)}, bf16[8,128,128]{2,1,0:T(8,128)(2,1)S(1)}, u32[]{:S(2)}, u32[]{:S(2)}) collective-permute-start(bf16[8,128,128]{2,1,0:T(8,128)(2,1)S(1)} %outer.3.refs_4_), channel_id=1, source_target_pairs={{0,16},{8,24},{16,0},{24,8},{1,17},{9,25},{17,1},{25,9},{2,18},{10... | collective-permute-start | bytes 786440 | tf_op jit(solution)/shard_map/ppermute | solution.py:450
  50.3 1.5 %collective-permute-start.13 = (bf16[8,128,128]{2,1,0:T(8,128)(2,1)S(1)}, bf16[8,128,128]{2,1,0:T(8,128)(2,1)S(1)}, u32[]{:S(2)}, u32[]{:S(2)}) collective-permute-start(bf16[8,128,128]{2,1,0:T(8,128)(2,1)S(1)} %collective-permute-done.8.refs_0_), channel_id=1, source_target_pairs={{0,8},{8,0},{16,24},{24,16},{1,9},{9,1},{17,25},{25,17},{2,10},{10... | collective-permute-start | bytes 786440 | tf_op jit(solution)/shard_map/ppermute | solution.py:454

commit v7 on v6

--- a/solution.py
+++ b/solution.py
@@ -93,9 +93,9 @@
         modes_ref[k] = jnp.concatenate([real, imag], axis=0).astype(jnp.bfloat16)
 
 
-def split_kernel(first, find, table_ref, own_ref, peer_ref, place_ref, cols_ref, count_ref, tiles_ref,
-                 near_ref, far_ref, out_ref, slot_ref, sem):
-    copy = find(place_ref, cols_ref, count_ref, tiles_ref, out_ref, slot_ref, sem)
+def split_kernel(first, sort, table_ref, own_ref, peer_ref, place_ref, cols_ref, count_ref, tiles_ref,
+                 near_ref, far_ref, out_ref, live_ref, sem):
+    copy = sort(place_ref, cols_ref, count_ref, tiles_ref, out_ref, live_ref, sem)
     per, rows, nodes = far_ref.shape
     odd = lax.rem(lax.broadcasted_iota(jnp.int32, (rows, 2 * nodes), 0), 2) == 1
     for r in range(0, per, 2):
@@ -136,52 +136,38 @@
     write_modes(held, modes_ref)
 
 
-def stage_kernel(first, tiles_ref, out_ref, sem):
-    share = out_ref.shape[0] - 1
-    copy = pltpu.make_async_copy(tiles_ref.at[pl.ds(first, share)], out_ref.at[pl.ds(0, share)], sem)
-    copy.start()
-    out_ref[share] = jnp.zeros(out_ref.shape[1:], out_ref.dtype)
-    copy.wait()
-
-
-def begin_find(ring, place_ref, cols_ref, count_ref, tiles_ref, out_ref, slot_ref, sem):
+def begin_sort(first, place_ref, cols_ref, count_ref, tiles_ref, out_ref, live_ref, sem):
     slots, modes = cols_ref.shape
-    share = out_ref.shape[0] - 1
-    copy = pltpu.make_async_copy(tiles_ref.at[pl.ds(0, share)], out_ref.at[pl.ds(0, share)], sem)
-    copy.start()
-    out_ref[share] = jnp.zeros(out_ref.shape[1:], out_ref.dtype)
+    share = out_ref.shape[1]
     place = place_ref[0]
     even = lax.rem(place, 2) == 0
     side = jnp.where(even, place + 1, place - 1)
-    far = lax.rem(jnp.where(even, place - 1, place + 1) + ring, ring)
-
-    def find(k, carry):
-        base = lax.rem(k, share // slots) * slots
-        for role, wanted in enumerate((place, side, far)):
-            slot = jnp.where(cols_ref[0, k] == wanted, 0, jnp.where(cols_ref[1, k] == wanted, 1, 2))
-            slot_ref[role * modes + k] = jnp.where(slot < count_ref[k], base + slot, share)
+
+    def begin(k, carry):
+        mode = first + k
+        for t in range(slots):
+            block = cols_ref[t, mode]
+            role = jnp.where(block == place, 0, jnp.where(block == side, 1, 2))
+            pltpu.make_async_copy(tiles_ref.at[mode * slots + t], out_ref.at[role, k], sem).start()
+            live_ref[role * share + k] = (t < count_ref[mode]).astype(jnp.int32)
         return carry
 
-    lax.fori_loop(0, modes, find, 0)
-    return copy
-
-
-def find_kernel(find, *refs):
-    find(*refs).wait()
-
-
-def chosen(slot_ref, modes, roles):
-    group = min(16, modes)
-    for first in range(0, modes, group):
-        places = [[slot_ref[role * modes + first + k] for role in roles] for k in range(group)]
-        for k in range(group):
-            yield first + k, places[k]
-
-
-def tile_product(tiles_ref, places, values):
+    lax.fori_loop(0, share, begin, 0)
+    return pltpu.make_async_copy(out_ref, out_ref, sem)
+
+
+def sort_kernel(sort, *refs):
+    sort(*refs).wait()
+
+
+def tile_product(tiles_ref, live_ref, k, roles, values):
+    share = tiles_ref.shape[1]
+    kept = []
+    for role, value in zip(roles, values):
+        kept.append(jnp.where(live_ref[role * share + k] == 0, jnp.zeros_like(value), value))
     return lax.dot_general(
-        jnp.concatenate(values, axis=1),
-        jnp.concatenate([tiles_ref[place] for place in places], axis=1),
+        jnp.concatenate(kept, axis=1),
+        jnp.concatenate([tiles_ref[role, k] for role in roles], axis=1),
         (((1,), (1,)), ((), ())),
         preferred_element_type=jnp.float32,
     )
@@ -199,28 +185,29 @@
     out_ref[k * both + both // 2 : (k + 1) * both, :] = imag
 
 
-def inner_kernel(chunks, slot_ref, *refs):
-    own_refs, side_ref, part_refs = refs[-2 * chunks - 1 : -chunks - 1], refs[-chunks - 1], refs[-chunks:]
-    tile_refs = refs[: -2 * chunks - 1]
+def inner_kernel(chunks, shares, *refs):
+    live_refs, tile_refs, refs = refs[:shares], refs[shares : 2 * shares], refs[2 * shares :]
+    own_refs, side_ref, part_refs = refs[:chunks], refs[chunks], refs[chunks + 1 :]
     modes, both = side_ref.shape[:2]
-    for k, (own_place, side_place) in chosen(slot_ref, modes, (0, 1)):
-        tiles_ref = tile_refs[k * len(tile_refs) // modes]
+    for k in range(modes):
+        turn, at = divmod(k, modes // shares)
         owns = jnp.concatenate([ref[k] for ref in own_refs], axis=0)
-        product = tile_product(tiles_ref, [own_place], [owns])
-        side = tile_product(tiles_ref, [side_place], [side_ref[k]])
+        product = tile_product(tile_refs[turn], live_refs[turn], at, (0,), [owns])
+        side = tile_product(tile_refs[turn], live_refs[turn], at, (1,), [side_ref[k]])
         for index, part_ref in enumerate(part_refs):
             mine = product[index * both : (index + 1) * both]
             put(part_ref, k, both, *combined(mine + side if index == 0 else mine))
 
 
-def outer_kernel(roles, slot_ref, *refs):
-    count = len(roles)
-    tile_refs, value_refs, (part_ref, near_ref, held) = refs[: -3 - count], refs[-3 - count : -3], refs[-3:]
+def outer_kernel(roles, shares, *refs):
+    live_refs, tile_refs, refs = refs[:shares], refs[shares : 2 * shares], refs[2 * shares :]
+    value_refs, (part_ref, near_ref, held) = refs[:-3], refs[-3:]
     modes, both = value_refs[0].shape[:2]
     rhs = both // 2
-    for k, places in chosen(slot_ref, modes, roles):
-        tiles_ref = tile_refs[k * len(tile_refs) // modes]
-        real, imag = combined(tile_product(tiles_ref, places, [ref[k] for ref in value_refs]))
+    for k in range(modes):
+        turn, at = divmod(k, modes // shares)
+        values = [ref[k] for ref in value_refs]
+        real, imag = combined(tile_product(tile_refs[turn], live_refs[turn], at, roles, values))
         at_real, at_imag = slice(k * both, k * both + rhs), slice(k * both + rhs, (k + 1) * both)
         held[at_real, :] = real + part_ref[at_real, :]
         held[at_imag, :] = imag + part_ref[at_imag, :]
@@ -303,8 +290,11 @@
     cut_fields = fields.reshape(rows, rhs, nodes)
     flat_impedance = impedance.reshape(rows, nodes)
     flat_tiles = tile_data.reshape(local * slots, 2 * block, block)
-    share = local * slots // SHARES
-    tiles_shape = jax.ShapeDtypeStruct((share + 1, 2 * block, block), tile_data.dtype)
+    share = local // SHARES
+    sort_shapes = [
+        jax.ShapeDtypeStruct((slots, share, 2 * block, block), tile_data.dtype),
+        jax.ShapeDtypeStruct((slots * share,), jnp.int32),
+    ]
     params = pltpu.CompilerParams(vmem_limit_bytes=VMEM_LIMIT)
     pack_params = pltpu.CompilerParams(vmem_limit_bytes=PACK_VMEM_LIMIT)
     stage_params = pltpu.CompilerParams(vmem_limit_bytes=STAGE_VMEM_LIMIT)
@@ -331,31 +321,34 @@
     )(az, cut_fields, tables)
 
     peer = lax.ppermute(coded, "az", PEER) if paired else None
-    find = functools.partial(begin_find, ring)
-    find_shapes = [tiles_shape, jax.ShapeDtypeStruct((slots * local,), jnp.int32)]
-    find_operands = (after(place, coded), tile_cols[:, 0, :].T, tile_count.reshape(local), flat_tiles)
+    pattern = (tile_cols[:, 0, :].T, tile_count.reshape(local))
+
+    def sorting(turn, wait_for):
+        return pl.pallas_call(
+            functools.partial(sort_kernel, functools.partial(begin_sort, turn * share)),
+            out_shape=sort_shapes,
+            in_specs=[smem] * 3 + [hbm],
+            out_specs=[vmem, smem],
+            scratch_shapes=[pltpu.SemaphoreType.DMA],
+            cost_estimate=cost(0, 2 * tile_data.size // SHARES),
+            compiler_params=stage_params,
+            name="sort",
+        )(after(place, wait_for), *pattern, flat_tiles)
+
     if paired:
-        near_part, far_part, head, slot = pl.pallas_call(
-            functools.partial(split_kernel, per, find),
-            out_shape=[jax.ShapeDtypeStruct((per, rows, nodes), jnp.float32), chunk_shape] + find_shapes,
+        near_part, far_part, head, live = pl.pallas_call(
+            functools.partial(split_kernel, per, functools.partial(begin_sort, 0)),
+            out_shape=[jax.ShapeDtypeStruct((per, rows, nodes), jnp.float32), chunk_shape] + sort_shapes,
             in_specs=[vmem] * 3 + [smem] * 3 + [hbm],
             out_specs=[vmem] * 3 + [smem],
             scratch_shapes=[pltpu.SemaphoreType.DMA],
             cost_estimate=cost(3 * multiply, move),
             compiler_params=stage_params,
             name="split",
-        )(forward_table, coded, peer, *find_operands)
+        )(forward_table, coded, peer, after(place, coded), *pattern, flat_tiles)
     else:
-        head, slot = pl.pallas_call(
-            functools.partial(find_kernel, find),
-            out_shape=find_shapes,
-            in_specs=[smem] * 3 + [hbm],
-            out_specs=[vmem, smem],
-            scratch_shapes=[pltpu.SemaphoreType.DMA],
-            compiler_params=stage_params,
-            name="find",
-        )(*find_operands)
-    tiles = [head]
+        head, live = sorting(0, coded)
+    tiles, lives = [head], [live]
 
     sides = [(i, i ^ 1) for i in range(ring)]
     onward = [(i, (i + 2 if i % 2 == 0 else i - 2) % ring) for i in range(ring)]
@@ -397,31 +390,23 @@
         owns.append(own)
         if index == 0:
             for turn in range(1, SHARES):
-                tail = pl.pallas_call(
-                    functools.partial(stage_kernel, turn * share),
-                    out_shape=tiles_shape,
-                    in_specs=[hbm],
-                    out_specs=vmem,
-                    scratch_shapes=[pltpu.SemaphoreType.DMA],
-                    cost_estimate=cost(0, 2 * tile_data.size // SHARES),
-                    compiler_params=stage_params,
-                    name="stage",
-                )(after(flat_tiles, own))
+                tail, live = sorting(turn, own)
                 tiles.append(tail)
+                lives.append(live)
 
     side_in = [lax.ppermute(own, "curve", sides) for own in owns]
     side_in[0] = after(side_in[0], *owns[1:])
     far_in = [lax.ppermute(side, "curve", onward) for side in side_in]
     part_shape = jax.ShapeDtypeStruct((local * 2 * per, nodes), jnp.float32)
     parts_of = pl.pallas_call(
-        functools.partial(inner_kernel, CHUNKS),
+        functools.partial(inner_kernel, CHUNKS, SHARES),
         out_shape=[part_shape] * CHUNKS,
-        in_specs=[smem] + [vmem] * (SHARES + CHUNKS + 1),
+        in_specs=[smem] * SHARES + [vmem] * (SHARES + CHUNKS + 1),
         out_specs=[vmem] * CHUNKS,
         cost_estimate=cost(0, tile_data.size),
         compiler_params=params,
         name="inner",
-    )(slot, *tiles, *owns, side_in[0])
+    )(*lives, *tiles, *owns, side_in[0])
 
     nears = []
     for index in range(CHUNKS):
@@ -431,15 +416,15 @@
             roles, values = (1, 2), [side_in[index], after(far_in[index], nears[0])]
         nears.append(
             pl.pallas_call(
-                functools.partial(outer_kernel, roles),
+                functools.partial(outer_kernel, roles, SHARES),
                 out_shape=jax.ShapeDtypeStruct((per, rows, nodes), jnp.bfloat16),
-                in_specs=[smem] + [vmem] * (SHARES + len(roles) + 1),
+                in_specs=[smem] * SHARES + [vmem] * (SHARES + len(roles) + 1),
                 out_specs=vmem,
                 scratch_shapes=[pltpu.VMEM((local * 2 * per, nodes), jnp.float32)],
                 cost_estimate=cost(0, tile_data.size // 2),
                 compiler_params=params,
                 name="outer",
-            )(slot, *tiles, *values, parts_of[index])
+            )(*lives, *tiles, *values, parts_of[index])
         )
 
     peers = [lax.ppermute(near, "az", PEER) for near in nears] if paired else []

time: 53.4 us -> 53.4 us (level)
  Pallas kernels: 21.2 us -> 22.8 us
  waiting for transfers between devices: 15.6 us -> 14.2 us
    pallas_call x5, Pallas kernels: 14.6 us -> 16.1 us  [the longest x2 4.67 us: on_device(): pl.pallas_call(functools.partial(outer_kernel, roles, SHARES), out_shape=...]
    ppermute x1, waiting for transfers between devices: 1.19 us -> 0.01 us  [on_device(): lax.ppermute(after(far_part, earlier), 'az', ACROSS)]
    unnamed x7 -> x9, local copies, waits for them, and re-layouts: 1.34 us -> 1.35 us
  transfers between devices with their start and end apart: 14 -> 14, of which waited for: 8 -> 7; matrix products, arithmetic and copies ran while one was open for 1% -> 1% of each run, Pallas kernels for 34% -> 37%
where the time goes in v7:
time: 53.4 us; the launch traced here: 53.2 us
  Pallas kernels  22.8 us (43%)
  starting transfers between devices  14.7 us (28%)
  waiting for transfers between devices  14.2 us (27%)
  local copies, waits for them, and re-layouts  1.35 us (3%)
    ppermute x2, waiting for transfers between devices, on_device(): across = lax.ppermute(near, 'az', ACROSS)  5.16 us
    pallas_call x2, Pallas kernels, on_device(): pl.pallas_call(functools.partial(outer_kernel, roles, SHARES), out_shape=...  4.67 us
    ppermute x2, waiting for transfers between devices, on_device(): far_in = [lax.ppermute(side, 'curve', onward) for side in side_in]  4.29 us
    pallas_call x1, Pallas kernels, sorting(): pl.pallas_call(functools.partial(sort_kernel, functools.partial(begin_sor...  4.14 us
    pallas_call x1, Pallas kernels, on_device(): pl.pallas_call(functools.partial(split_kernel, per, functools.partial(beg...  4.14 us
    ppermute x2, starting transfers between devices, on_device(): side_in = [lax.ppermute(own, 'curve', sides) for own in owns]  3.29 us
    ppermute x2, starting transfers between devices, on_device(): far_in = [lax.ppermute(side, 'curve', onward) for side in side_in]  3.15 us
    pallas_call x1, Pallas kernels, on_device(): pl.pallas_call(functools.partial(inner_kernel, CHUNKS, SHARES), out_shape...  3.15 us
  transfers between devices with their start and end apart: 14, of which 7 were waited for; matrix products, arithmetic and copies ran while one was open for 1% of the time, Pallas kernels for 37%

profile of v7, /device:TPU:0, one launch (start us, length us, event | category | flops | bytes accessed | tf_op | source)
XLA Modules:
  0.0 53.2 jit_solution(1115130918561876170)
XLA Ops:
  0.0 1.9 %pack.1 = (s16[8,128,128]{2,1,0:T(8,128)(2,1)S(1)}, s16[16,128,128]{2,1,0:T(8,128)(2,1)S(1)}, bf16[2,128,512]{2,1,0:T(8,128)(2,1)S(1)}, bf16[2,128,512]{2,1,0:T(8,128)(2,1)S(1)}) custom-call(s32[1]{0:T(128)} %bitcast.az_ref, f32[128,16,128]{2,1,0:T(8,128)} %bitcast.13, bf16[4,2,2,128,512]{4,3,2,1,0:T(8,128)(2,1)} %constant.10.clone.tables_ref), custom_call_target="tpu_custom_call" | custom-call | bytes 4194304 | tf_op jit(solution)/shard_map/pack/pallas_call | solution.py:309
  1.9 0.5 collective-permute-start
  2.4 2.6 %collective-permute-start.1 = (s16[8,128,128]{2,1,0:T(8,128)(2,1)S(1)}, s16[8,128,128]{2,1,0:T(8,128)(2,1)S(1)}, u32[]{:S(2)}, u32[]{:S(2)}) collective-permute-start(s16[8,128,128]{2,1,0:T(8,128)(2,1)S(1)} %get-tuple-element.36), channel_id=1, source_target_pairs={{0,16},{8,24},{16,0},{24,8},{1,17},{9,25},{17,1},{25,9},{2,18},{10... | collective-permute-start | bytes 786440 | tf_op jit(solution)/shard_map/ppermute | solution.py:373
  5.0 0.7 %copy.10 = s32[64,1,3]{0,2,1:T(4,128)S(1)} copy(s32[64,1,3]{0,1,2:T(1,128)} %param.9) | data formatting | bytes 1536
  5.7 0.0 collective-permute-done.peer_ref.refs_1_
  5.7 0.0 copy-start.2
  5.7 0.7 %copy-done.2 = s32[64,1]{0,1:T(1,128)S(1)} copy-done((s32[64,1]{0,1:T(1,128)S(1)}, s32[64,1]{0,1:T(1,128)}, u32[]{:S(2)}) %copy-start.2) | copy-done | bytes 280
  6.3 0.0 copy-start.3
  6.3 4.1 %split.1 = (f32[8,128,128]{2,1,0:T(8,128)S(1)}, s16[8,128,128]{2,1,0:T(8,128)(2,1)S(1)}, bf16[3,32,256,128]{3,2,1,0:T(8,128)(2,1)S(1)}, s32[96]{0:T(128)S(1)}) custom-call(bf16[2,128,512]{2,1,0:T(8,128)(2,1)S(1)} %get-tuple-element.32.table_ref, s16[16,128,128]{2,1,0:T(8,128)(2,1)S(1)} %get-tuple-element.33.own_ref.refs_0_, ...), custom_call_target="tpu_custom_call" | custom-call | flops 805306368 | bytes 4194304 | tf_op jit(solution)/shard_map/split/pallas_call | solution.py:339
  10.5 1.4 %collective-permute-done.1.refs_2_ = s16[8,128,128]{2,1,0:T(8,128)(2,1)S(1)} collective-permute-done((s16[8,128,128]{2,1,0:T(8,128)(2,1)S(1)}, s16[8,128,128]{2,1,0:T(8,128)(2,1)S(1)}, u32[]{:S(2)}, u32[]{:S(2)}) %collective-permute-start.1) | collective-permute-done | bytes 262176 | tf_op jit(solution)/shard_map/ppermute | solution.py:373
  11.9 0.0 collective-permute-start.2
  11.9 1.8 %collective-permute-start.3 = (s16[8,128,128]{2,1,0:T(8,128)(2,1)S(1)}, s16[8,128,128]{2,1,0:T(8,128)(2,1)S(1)}, u32[]{:S(2)}, u32[]{:S(2)}) collective-permute-start(s16[8,128,128]{2,1,0:T(8,128)(2,1)S(1)} %get-tuple-element.44), channel_id=1, source_target_pairs={{0,16},{8,24},{16,0},{24,8},{1,17},{9,25},{17,1},{25,9},{2,18},{10... | collective-permute-start | bytes 786440 | tf_op jit(solution)/shard_map/ppermute | solution.py:360
  13.6 0.0 collective-permute-done.2.refs_3_
  13.6 1.3 %forward.1.refs_4_ = bf16[64,16,128]{2,1,0:T(8,128)(2,1)S(1)} custom-call(bf16[2,128,512]{2,1,0:T(8,128)(2,1)S(1)} %get-tuple-element.32.table_ref, s16[16,128,128]{2,1,0:T(8,128)(2,1)S(1)} %get-tuple-element.33.own_ref.refs_0_, s16[16,128,128]{2,1,0:T(8,128)(2,1)S(1)} %collective-permute-done.peer_ref.refs_1_, ...), custom_call_target="tpu_custom_call" | custom-call | flops 805306368 | bytes 4194304 | tf_op jit(solution)/shard_map/forward/pallas_call | solution.py:380
  15.0 1.6 %collective-permute-start.6 = (bf16[64,16,128]{2,1,0:T(8,128)(2,1)S(1)}, bf16[64,16,128]{2,1,0:T(8,128)(2,1)S(1)}, u32[]{:S(2)}, u32[]{:S(2)}) collective-permute-start(bf16[64,16,128]{2,1,0:T(8,128)(2,1)S(1)} %forward.1.refs_4_), channel_id=1, source_target_pairs={{0,1},{1,0},{2,3},{3,2},{4,5},{5,4},{6,7},{7,6},{8,9},{9,8},{10,11... | collective-permute-start | bytes 786440 | tf_op jit(solution)/shard_map/ppermute | solution.py:397
  16.6 0.0 copy-done.3
  16.6 4.1 %sort.1 = (bf16[3,32,256,128]{3,2,1,0:T(8,128)(2,1)S(1)}, s32[96]{0:T(128)S(1)}) custom-call(s32[1]{0:T(128)} %bitcast.4.place_ref.refs_0_, s32[3,64]{1,0:T(4,128)S(1)} %bitcast.19, s32[64]{0:T(128)S(1)} %bitcast.21, bf16[192,256,128]{2,1,0:T(8,128)(2,1)} %bitcast.23), custom_call_target="tpu_custom_call" | custom-call | bytes 6291456 | tf_op jit(solution)/shard_map/sort/pallas_call | solution.py:327
  20.8 0.0 collective-permute-done.3.far_ref
  20.8 0.4 finish.1.refs_5_
  21.2 1.7 %collective-permute-start.4 = (bf16[64,16,128]{2,1,0:T(8,128)(2,1)S(1)}, bf16[64,16,128]{2,1,0:T(8,128)(2,1)S(1)}, u32[]{:S(2)}, u32[]{:S(2)}) collective-permute-start(bf16[64,16,128]{2,1,0:T(8,128)(2,1)S(1)} %finish.1.refs_5_), channel_id=1, source_target_pairs={{0,1},{1,0},{2,3},{3,2},{4,5},{5,4},{6,7},{7,6},{8,9},{9,8},{10,11... | collective-permute-start | bytes 786440 | tf_op jit(solution)/shard_map/ppermute | solution.py:397
  22.9 0.6 %collective-permute-done.6.refs_6_ = bf16[64,16,128]{2,1,0:T(8,128)(2,1)S(1)} collective-permute-done((bf16[64,16,128]{2,1,0:T(8,128)(2,1)S(1)}, bf16[64,16,128]{2,1,0:T(8,128)(2,1)S(1)}, u32[]{:S(2)}, u32[]{:S(2)}) %collective-permute-start.6) | collective-permute-done | bytes 262176 | tf_op jit(solution)/shard_map/ppermute | solution.py:397
  23.5 1.6 %collective-permute-start.7 = (bf16[64,16,128]{2,1,0:T(8,128)(2,1)S(1)}, bf16[64,16,128]{2,1,0:T(8,128)(2,1)S(1)}, u32[]{:S(2)}, u32[]{:S(2)}) collective-permute-start(bf16[64,16,128]{2,1,0:T(8,128)(2,1)S(1)} %collective-permute-done.6.refs_6_), channel_id=1, source_target_pairs={{0,2},{1,7},{2,4},{3,1},{4,6},{5,3},{6,0},{7,5},{8,10},{9,15},{10,... | collective-permute-start | bytes 786440 | tf_op jit(solution)/shard_map/ppermute | solution.py:399
  25.1 3.1 %inner.1 = (f32[1024,128]{1,0:T(8,128)S(1)}, f32[1024,128]{1,0:T(8,128)S(1)}) custom-call(s32[96]{0:T(128)S(1)} %get-tuple-element.35.refs_0_, s32[96]{0:T(128)S(1)} %get-tuple-element.40.refs_1_, bf16[3,32,256,128]{3,2,1,0:T(8,128)(2,1)S(1)} %get-tuple-element.41.refs_2_, bf16[3,32,256,128]{3,2,1,0:T(8,128)(2,1)S(1)} %get-tuple-element.42.refs_3_, ...), custom_call_target="tpu_custom_call" | custom-call | bytes 6291456 | tf_op jit(solution)/shard_map/inner/pallas_call | solution.py:401
  28.2 1.2 %collective-permute-done.4.refs_4_ = bf16[64,16,128]{2,1,0:T(8,128)(2,1)S(1)} collective-permute-done((bf16[64,16,128]{2,1,0:T(8,128)(2,1)S(1)}, bf16[64,16,128]{2,1,0:T(8,128)(2,1)S(1)}, u32[]{:S(2)}, u32[]{:S(2)}) %collective-permute-start.4) | collective-permute-done | bytes 262176 | tf_op jit(solution)/shard_map/ppermute | solution.py:397
  29.4 1.6 %collective-permute-start.5 = (bf16[64,16,128]{2,1,0:T(8,128)(2,1)S(1)}, bf16[64,16,128]{2,1,0:T(8,128)(2,1)S(1)}, u32[]{:S(2)}, u32[]{:S(2)}) collective-permute-start(bf16[64,16,128]{2,1,0:T(8,128)(2,1)S(1)} %collective-permute-done.4.refs_4_), channel_id=1, source_target_pairs={{0,2},{1,7},{2,4},{3,1},{4,6},{5,3},{6,0},{7,5},{8,10},{9,15},{10,... | collective-permute-start | bytes 786440 | tf_op jit(solution)/shard_map/ppermute | solution.py:399
  31.0 2.0 %collective-permute-done.7.refs_4_ = bf16[64,16,128]{2,1,0:T(8,128)(2,1)S(1)} collective-permute-done((bf16[64,16,128]{2,1,0:T(8,128)(2,1)S(1)}, bf16[64,16,128]{2,1,0:T(8,128)(2,1)S(1)}, u32[]{:S(2)}, u32[]{:S(2)}) %collective-permute-start.7) | collective-permute-done | bytes 262176 | tf_op jit(solution)/shard_map/ppermute | solution.py:399
  33.0 1.8 %outer.2.refs_0_ = bf16[8,128,128]{2,1,0:T(8,128)(2,1)S(1)} custom-call(s32[96]{0:T(128)S(1)} %get-tuple-element.35.refs_0_, s32[96]{0:T(128)S(1)} %get-tuple-element.40.refs_1_, bf16[3,32,256,128]{3,2,1,0:T(8,128)(2,1)S(1)} %get-tuple-element.41.refs_2_, bf16[3,32,256,128]{3,2,1,0:T(8,128)(2,1)S(1)} %get-tuple-element.42.refs_3_, ...), custom_call_target="tpu_custom_call" | custom-call | bytes 3145728 | tf_op jit(solution)/shard_map/outer/pallas_call | solution.py:418
  34.8 1.5 %collective-permute-start.10 = (bf16[8,128,128]{2,1,0:T(8,128)(2,1)S(1)}, bf16[8,128,128]{2,1,0:T(8,128)(2,1)S(1)}, u32[]{:S(2)}, u32[]{:S(2)}) collective-permute-start(bf16[8,128,128]{2,1,0:T(8,128)(2,1)S(1)} %outer.2.refs_0_), channel_id=1, source_target_pairs={{0,16},{8,24},{16,0},{24,8},{1,17},{9,25},{17,1},{25,9},{2,18},{10... | collective-permute-start | bytes 786440 | tf_op jit(solution)/shard_map/ppermute | solution.py:435
  36.3 0.0 collective-permute-start.9
  36.3 2.3 %collective-permute-done.5.refs_5_ = bf16[64,16,128]{2,1,0:T(8,128)(2,1)S(1)} collective-permute-done((bf16[64,16,128]{2,1,0:T(8,128)(2,1)S(1)}, bf16[64,16,128]{2,1,0:T(8,128)(2,1)S(1)}, u32[]{:S(2)}, u32[]{:S(2)}) %collective-permute-start.5) | collective-permute-done | bytes 262176 | tf_op jit(solution)/shard_map/ppermute | solution.py:399
  38.6 0.0 copy-start
  38.6 0.0 copy-start.1
  38.6 2.9 %outer.3.refs_4_ = bf16[8,128,128]{2,1,0:T(8,128)(2,1)S(1)} custom-call(s32[96]{0:T(128)S(1)} %get-tuple-element.35.refs_0_, s32[96]{0:T(128)S(1)} %get-tuple-element.40.refs_1_, bf16[3,32,256,128]{3,2,1,0:T(8,128)(2,1)S(1)} %get-tuple-element.41.refs_2_, bf16[3,32,256,128]{3,2,1,0:T(8,128)(2,1)S(1)} %get-tuple-element.42.refs_3_, ...), custom_call_target="tpu_custom_call" | custom-call | bytes 3145728 | tf_op jit(solution)/shard_map/outer/pallas_call | solution.py:418
  41.4 0.1 collective-permute-start.12
  41.5 0.0 collective-permute-done.10.refs_2_
  41.5 0.5 collective-permute-start.11
  42.0 1.4 %collective-permute-start.8 = (bf16[8,128,128]{2,1,0:T(8,128)(2,1)S(1)}, bf16[8,128,128]{2,1,0:T(8,128)(2,1)S(1)}, u32[]{:S(2)}, u32[]{:S(2)}) collective-permute-start(bf16[8,128,128]{2,1,0:T(8,128)(2,1)S(1)} %outer.3.refs_4_), channel_id=1, source_target_pairs={{0,16},{8,24},{16,0},{24,8},{1,17},{9,25},{17,1},{25,9},{2,18},{10... | collective-permute-start | bytes 786440 | tf_op jit(solution)/shard_map/ppermute | solution.py:435
  43.4 0.0 collective-permute-done.12.refs_5_
  43.4 0.0 collective-permute-done.9.refs_1_
  43.4 0.0 collective-permute-done.11.refs_3_
  43.4 0.0 copy-done
  43.4 0.0 copy-done.1
  43.4 1.7 %back.2 = (f32[128,16,128]{2,1,0:T(8,128)}, f32[4,128,256]{2,1,0:T(8,128)S(1)}) custom-call(bf16[2,128,512]{2,1,0:T(8,128)(2,1)S(1)} %get-tuple-element.31.table_ref, f32[2048,128]{1,0:T(8,128)S(1)} %bitcast.14, f32[128,128]{1,0:T(8,128)S(1)} %bitcast.16, bf16[8,128,128]{2,1,0:T(8,128)(2,1)S(1)} %outer.2.refs_0_, ...), custom_call_target="tpu_custom_call" | custom-call | flops 536870912 | bytes 4194304 | tf_op jit(solution)/shard_map/back/pallas_call | solution.py:450
  45.2 5.2 %collective-permute-done.8.refs_0_ = bf16[8,128,128]{2,1,0:T(8,128)(2,1)S(1)} collective-permute-done((bf16[8,128,128]{2,1,0:T(8,128)(2,1)S(1)}, bf16[8,128,128]{2,1,0:T(8,128)(2,1)S(1)}, u32[]{:S(2)}, u32[]{:S(2)}) %collective-permute-start.8) | collective-permute-done | bytes 262176 | tf_op jit(solution)/shard_map/ppermute | solution.py:435
  50.3 0.0 collective-permute-start.13
  50.3 1.5 %collective-permute-done.13.refs_1_ = bf16[8,128,128]{2,1,0:T(8,128)(2,1)S(1)} collective-permute-done((bf16[8,128,128]{2,1,0:T(8,128)(2,1)S(1)}, bf16[8,128,128]{2,1,0:T(8,128)(2,1)S(1)}, u32[]{:S(2)}, u32[]{:S(2)}) %collective-permute-start.13) | collective-permute-done | bytes 262176 | tf_op jit(solution)/shard_map/ppermute | solution.py:439
  51.9 1.3 %back.3 = f32[128,16,128]{2,1,0:T(8,128)} custom-call(bf16[2,128,512]{2,1,0:T(8,128)(2,1)S(1)} %get-tuple-element.31.table_ref, f32[2048,128]{1,0:T(8,128)S(1)} %bitcast.15, f32[128,128]{1,0:T(8,128)S(1)} %bitcast.17, bf16[8,128,128]{2,1,0:T(8,128)(2,1)S(1)} %collective-permute-done.8.refs_0_, ...), custom_call_target="tpu_custom_call", output_to_operand_aliasing={{}: (6, {})} | custom-call | flops 536870912 | bytes 4194304 | tf_op jit(solution)/shard_map/back/pallas_call | solution.py:450
Async XLA Ops:
  1.9 3.8 %collective-permute-start = (s16[16,128,128]{2,1,0:T(8,128)(2,1)S(1)}, s16[16,128,128]{2,1,0:T(8,128)(2,1)S(1)}, u32[]{:S(2)}, u32[]{:S(2)}) collective-permute-start(s16[16,128,128]{2,1,0:T(8,128)(2,1)S(1)} %get-tuple-element.33.own_ref.refs_0_), channel_id=1, source_target_pairs={{0,8},{8,0},{16,24},{24,16},{1,9},{9,1},{17,25},{25,17},{2,10},{10... | collective-permute-start | bytes 1572872 | tf_op jit(solution)/shard_map/ppermute | solution.py:323
  2.4 9.5 %collective-permute-start.1 = (s16[8,128,128]{2,1,0:T(8,128)(2,1)S(1)}, s16[8,128,128]{2,1,0:T(8,128)(2,1)S(1)}, u32[]{:S(2)}, u32[]{:S(2)}) collective-permute-start(s16[8,128,128]{2,1,0:T(8,128)(2,1)S(1)} %get-tuple-element.36), channel_id=1, source_target_pairs={{0,16},{8,24},{16,0},{24,8},{1,17},{9,25},{17,1},{25,9},{2,18},{10... | collective-permute-start | bytes 786440 | tf_op jit(solution)/shard_map/ppermute | solution.py:373
  5.7 0.7 %copy-start.2 = (s32[64,1]{0,1:T(1,128)S(1)}, s32[64,1]{0,1:T(1,128)}, u32[]{:S(2)}) copy-start(s32[64,1]{0,1:T(1,128)} %param.10) | copy-start | bytes 772
  6.3 10.3 %copy-start.3 = (s32[64,1]{0,1:T(1,128)S(1)}, s32[64,1]{0,1:T(1,128)}, u32[]{:S(2)}) copy-start(s32[64,1]{0,1:T(1,128)} %param.10) | copy-start | bytes 772
  11.9 1.8 %collective-permute-start.2 = (s16[8,128,128]{2,1,0:T(8,128)(2,1)S(1)}, s16[8,128,128]{2,1,0:T(8,128)(2,1)S(1)}, u32[]{:S(2)}, u32[]{:S(2)}) collective-permute-start(s16[8,128,128]{2,1,0:T(8,128)(2,1)S(1)} %collective-permute-done.1.refs_2_), channel_id=1, source_target_pairs={{0,8},{8,0},{16,24},{24,16},{1,9},{9,1},{17,25},{25,17},{2,10},{10... | collective-permute-start | bytes 786440 | tf_op jit(solution)/shard_map/ppermute | solution.py:375
  11.9 8.9 %collective-permute-start.3 = (s16[8,128,128]{2,1,0:T(8,128)(2,1)S(1)}, s16[8,128,128]{2,1,0:T(8,128)(2,1)S(1)}, u32[]{:S(2)}, u32[]{:S(2)}) collective-permute-start(s16[8,128,128]{2,1,0:T(8,128)(2,1)S(1)} %get-tuple-element.44), channel_id=1, source_target_pairs={{0,16},{8,24},{16,0},{24,8},{1,17},{9,25},{17,1},{25,9},{2,18},{10... | collective-permute-start | bytes 786440 | tf_op jit(solution)/shard_map/ppermute | solution.py:360
  15.0 8.5 %collective-permute-start.6 = (bf16[64,16,128]{2,1,0:T(8,128)(2,1)S(1)}, bf16[64,16,128]{2,1,0:T(8,128)(2,1)S(1)}, u32[]{:S(2)}, u32[]{:S(2)}) collective-permute-start(bf16[64,16,128]{2,1,0:T(8,128)(2,1)S(1)} %forward.1.refs_4_), channel_id=1, source_target_pairs={{0,1},{1,0},{2,3},{3,2},{4,5},{5,4},{6,7},{7,6},{8,9},{9,8},{10,11... | collective-permute-start | bytes 786440 | tf_op jit(solution)/shard_map/ppermute | solution.py:397
  21.2 8.2 %collective-permute-start.4 = (bf16[64,16,128]{2,1,0:T(8,128)(2,1)S(1)}, bf16[64,16,128]{2,1,0:T(8,128)(2,1)S(1)}, u32[]{:S(2)}, u32[]{:S(2)}) collective-permute-start(bf16[64,16,128]{2,1,0:T(8,128)(2,1)S(1)} %finish.1.refs_5_), channel_id=1, source_target_pairs={{0,1},{1,0},{2,3},{3,2},{4,5},{5,4},{6,7},{7,6},{8,9},{9,8},{10,11... | collective-permute-start | bytes 786440 | tf_op jit(solution)/shard_map/ppermute | solution.py:397
  23.5 9.5 %collective-permute-start.7 = (bf16[64,16,128]{2,1,0:T(8,128)(2,1)S(1)}, bf16[64,16,128]{2,1,0:T(8,128)(2,1)S(1)}, u32[]{:S(2)}, u32[]{:S(2)}) collective-permute-start(bf16[64,16,128]{2,1,0:T(8,128)(2,1)S(1)} %collective-permute-done.6.refs_6_), channel_id=1, source_target_pairs={{0,2},{1,7},{2,4},{3,1},{4,6},{5,3},{6,0},{7,5},{8,10},{9,15},{10,... | collective-permute-start | bytes 786440 | tf_op jit(solution)/shard_map/ppermute | solution.py:399
  29.4 9.2 %collective-permute-start.5 = (bf16[64,16,128]{2,1,0:T(8,128)(2,1)S(1)}, bf16[64,16,128]{2,1,0:T(8,128)(2,1)S(1)}, u32[]{:S(2)}, u32[]{:S(2)}) collective-permute-start(bf16[64,16,128]{2,1,0:T(8,128)(2,1)S(1)} %collective-permute-done.4.refs_4_), channel_id=1, source_target_pairs={{0,2},{1,7},{2,4},{3,1},{4,6},{5,3},{6,0},{7,5},{8,10},{9,15},{10,... | collective-permute-start | bytes 786440 | tf_op jit(solution)/shard_map/ppermute | solution.py:399
  34.8 6.8 %collective-permute-start.10 = (bf16[8,128,128]{2,1,0:T(8,128)(2,1)S(1)}, bf16[8,128,128]{2,1,0:T(8,128)(2,1)S(1)}, u32[]{:S(2)}, u32[]{:S(2)}) collective-permute-start(bf16[8,128,128]{2,1,0:T(8,128)(2,1)S(1)} %outer.2.refs_0_), channel_id=1, source_target_pairs={{0,16},{8,24},{16,0},{24,8},{1,17},{9,25},{17,1},{25,9},{2,18},{10... | collective-permute-start | bytes 786440 | tf_op jit(solution)/shard_map/ppermute | solution.py:435
  36.3 7.2 %collective-permute-start.9 = (bf16[8,128,128]{2,1,0:T(8,128)(2,1)S(1)}, bf16[8,128,128]{2,1,0:T(8,128)(2,1)S(1)}, u32[]{:S(2)}, u32[]{:S(2)}) collective-permute-start(bf16[8,128,128]{2,1,0:T(8,128)(2,1)S(1)} %outer.2.refs_0_), channel_id=1, source_target_pairs={{0,8},{8,0},{16,24},{24,16},{1,9},{9,1},{17,25},{25,17},{2,10},{10... | collective-permute-start | bytes 786440 | tf_op jit(solution)/shard_map/ppermute | solution.py:430
  38.6 4.9 %copy-start = (f32[2,64,16,128]{3,2,1,0:T(8,128)S(1)}, f32[2,64,16,128]{3,2,1,0:T(8,128)}, u32[]{:S(2)}) copy-start(f32[2,64,16,128]{3,2,1,0:T(8,128)} %param.6) | copy-start | bytes 3145732
  38.6 4.9 %copy-start.1 = (f32[2,64,128]{2,1,0:T(8,128)S(1)}, f32[2,64,128]{2,1,0:T(8,128)}, u32[]{:S(2)}) copy-start(f32[2,64,128]{2,1,0:T(8,128)} %param.7) | copy-start | bytes 196612
  41.4 2.0 %collective-permute-start.12 = (bf16[8,128,128]{2,1,0:T(8,128)(2,1)S(1)}, bf16[8,128,128]{2,1,0:T(8,128)(2,1)S(1)}, u32[]{:S(2)}, u32[]{:S(2)}) collective-permute-start(bf16[8,128,128]{2,1,0:T(8,128)(2,1)S(1)} %outer.3.refs_4_), channel_id=1, source_target_pairs={{0,8},{8,0},{16,24},{24,16},{1,9},{9,1},{17,25},{25,17},{2,10},{10... | collective-permute-start | bytes 786440 | tf_op jit(solution)/shard_map/ppermute | solution.py:430
  41.5 1.9 %collective-permute-start.11 = (bf16[8,128,128]{2,1,0:T(8,128)(2,1)S(1)}, bf16[8,128,128]{2,1,0:T(8,128)(2,1)S(1)}, u32[]{:S(2)}, u32[]{:S(2)}) collective-permute-start(bf16[8,128,128]{2,1,0:T(8,128)(2,1)S(1)} %collective-permute-done.10.refs_2_), channel_id=1, source_target_pairs={{0,8},{8,0},{16,24},{24,16},{1,9},{9,1},{17,25},{25,17},{2,10},{10... | collective-permute-start | bytes 786440 | tf_op jit(solution)/shard_map/ppermute | solution.py:442
  42.0 8.3 %collective-permute-start.8 = (bf16[8,128,128]{2,1,0:T(8,128)(2,1)S(1)}, bf16[8,128,128]{2,1,0:T(8,128)(2,1)S(1)}, u32[]{:S(2)}, u32[]{:S(2)}) collective-permute-start(bf16[8,128,128]{2,1,0:T(8,128)(2,1)S(1)} %outer.3.refs_4_), channel_id=1, source_target_pairs={{0,16},{8,24},{16,0},{24,8},{1,17},{9,25},{17,1},{25,9},{2,18},{10... | collective-permute-start | bytes 786440 | tf_op jit(solution)/shard_map/ppermute | solution.py:435
  50.3 1.5 %collective-permute-start.13 = (bf16[8,128,128]{2,1,0:T(8,128)(2,1)S(1)}, bf16[8,128,128]{2,1,0:T(8,128)(2,1)S(1)}, u32[]{:S(2)}, u32[]{:S(2)}) collective-permute-start(bf16[8,128,128]{2,1,0:T(8,128)(2,1)S(1)} %collective-permute-done.8.refs_0_), channel_id=1, source_target_pairs={{0,8},{8,0},{16,24},{24,16},{1,9},{9,1},{17,25},{25,17},{2,10},{10... | collective-permute-start | bytes 786440 | tf_op jit(solution)/shard_map/ppermute | solution.py:439

commit v8 on v7

--- a/solution.py
+++ b/solution.py
@@ -149,7 +149,8 @@
             block = cols_ref[t, mode]
             role = jnp.where(block == place, 0, jnp.where(block == side, 1, 2))
             pltpu.make_async_copy(tiles_ref.at[mode * slots + t], out_ref.at[role, k], sem).start()
-            live_ref[role * share + k] = (t < count_ref[mode]).astype(jnp.int32)
+            used = jnp.where(t < count_ref[mode], 1.0, 0.0)
+            live_ref[role, k] = jnp.full(live_ref.shape[2:], used, jnp.float32).astype(jnp.bfloat16)
         return carry
 
     lax.fori_loop(0, share, begin, 0)
@@ -161,10 +162,10 @@
 
 
 def tile_product(tiles_ref, live_ref, k, roles, values):
-    share = tiles_ref.shape[1]
     kept = []
     for role, value in zip(roles, values):
-        kept.append(jnp.where(live_ref[role * share + k] == 0, jnp.zeros_like(value), value))
+        live = live_ref[role, k]
+        kept.append(value * jnp.concatenate([live] * (value.shape[0] // live.shape[0]), axis=0))
     return lax.dot_general(
         jnp.concatenate(kept, axis=1),
         jnp.concatenate([tiles_ref[role, k] for role in roles], axis=1),
@@ -293,7 +294,7 @@
     share = local // SHARES
     sort_shapes = [
         jax.ShapeDtypeStruct((slots, share, 2 * block, block), tile_data.dtype),
-        jax.ShapeDtypeStruct((slots * share,), jnp.int32),
+        jax.ShapeDtypeStruct((slots, share, 2 * per, nodes), jnp.bfloat16),
     ]
     params = pltpu.CompilerParams(vmem_limit_bytes=VMEM_LIMIT)
     pack_params = pltpu.CompilerParams(vmem_limit_bytes=PACK_VMEM_LIMIT)
@@ -328,7 +329,7 @@
             functools.partial(sort_kernel, functools.partial(begin_sort, turn * share)),
             out_shape=sort_shapes,
             in_specs=[smem] * 3 + [hbm],
-            out_specs=[vmem, smem],
+            out_specs=[vmem] * 2,
             scratch_shapes=[pltpu.SemaphoreType.DMA],
             cost_estimate=cost(0, 2 * tile_data.size // SHARES),
             compiler_params=stage_params,
@@ -340,7 +341,7 @@
             functools.partial(split_kernel, per, functools.partial(begin_sort, 0)),
             out_shape=[jax.ShapeDtypeStruct((per, rows, nodes), jnp.float32), chunk_shape] + sort_shapes,
             in_specs=[vmem] * 3 + [smem] * 3 + [hbm],
-            out_specs=[vmem] * 3 + [smem],
+            out_specs=[vmem] * 4,
             scratch_shapes=[pltpu.SemaphoreType.DMA],
             cost_estimate=cost(3 * multiply, move),
             compiler_params=stage_params,
@@ -401,7 +402,7 @@
     parts_of = pl.pallas_call(
         functools.partial(inner_kernel, CHUNKS, SHARES),
         out_shape=[part_shape] * CHUNKS,
-        in_specs=[smem] * SHARES + [vmem] * (SHARES + CHUNKS + 1),
+        in_specs=[vmem] * (2 * SHARES + CHUNKS + 1),
         out_specs=[vmem] * CHUNKS,
         cost_estimate=cost(0, tile_data.size),
         compiler_params=params,
@@ -418,7 +419,7 @@
             pl.pallas_call(
                 functools.partial(outer_kernel, roles, SHARES),
                 out_shape=jax.ShapeDtypeStruct((per, rows, nodes), jnp.bfloat16),
-                in_specs=[smem] * SHARES + [vmem] * (SHARES + len(roles) + 1),
+                in_specs=[vmem] * (2 * SHARES + len(roles) + 1),
                 out_specs=vmem,
                 scratch_shapes=[pltpu.VMEM((local * 2 * per, nodes), jnp.float32)],
                 cost_estimate=cost(0, tile_data.size // 2),

time: 53.4 us -> 52.9 us (level)
  Pallas kernels: 22.8 us -> 20 us
  waiting for transfers between devices: 14.2 us -> 16.3 us
    pallas_call x2, Pallas kernels: 4.67 us -> 3.59 us  [on_device(): pl.pallas_call(functools.partial(outer_kernel, roles, SHARES), out_shape=...]
    ppermute x2, waiting for transfers between devices: 4.29 us -> 5.07 us  [on_device(): far_in = [lax.ppermute(side, 'curve', onward) for side in side_in]]
    pallas_call x1, Pallas kernels: 4.14 us -> 3.54 us  [sorting(): pl.pallas_call(functools.partial(sort_kernel, functools.partial(begin_sor...]
    ppermute x1, waiting for transfers between devices: 1.41 us -> 2.01 us  [on_device(): across = after(lax.ppermute(first, 'az', ACROSS), far_part)]
    pallas_call x1, Pallas kernels: 4.14 us -> 3.54 us  [on_device(): pl.pallas_call(functools.partial(split_kernel, per, functools.partial(beg...]
    pallas_call x1, Pallas kernels: 3.15 us -> 2.61 us  [on_device(): pl.pallas_call(functools.partial(inner_kernel, CHUNKS, SHARES), out_shape...]
    unnamed x9 -> x7, local copies, waits for them, and re-layouts: 1.35 us -> 1.34 us
  transfers between devices with their start and end apart: 14 -> 14, of which waited for: 7 -> 8; matrix products, arithmetic and copies ran while one was open for 1% -> 1% of each run, Pallas kernels for 37% -> 32%
where the time goes in v8:
time: 52.9 us; the launch traced here: 52.7 us
  Pallas kernels  20 us (38%)
  waiting for transfers between devices  16.3 us (31%)
  starting transfers between devices  14.9 us (28%)
  local copies, waits for them, and re-layouts  1.34 us (3%)
    ppermute x2, waiting for transfers between devices, on_device(): across = lax.ppermute(near, 'az', ACROSS)  5.17 us
    ppermute x2, waiting for transfers between devices, on_device(): far_in = [lax.ppermute(side, 'curve', onward) for side in side_in]  5.07 us
    pallas_call x2, Pallas kernels, on_device(): pl.pallas_call(functools.partial(outer_kernel, roles, SHARES), out_shape=...  3.59 us
    pallas_call x1, Pallas kernels, on_device(): pl.pallas_call(functools.partial(split_kernel, per, functools.partial(beg...  3.54 us
    pallas_call x1, Pallas kernels, sorting(): pl.pallas_call(functools.partial(sort_kernel, functools.partial(begin_sor...  3.54 us
    ppermute x2, starting transfers between devices, on_device(): side_in = [lax.ppermute(own, 'curve', sides) for own in owns]  3.46 us
    ppermute x2, starting transfers between devices, on_device(): far_in = [lax.ppermute(side, 'curve', onward) for side in side_in]  3.32 us
    pallas_call x2, Pallas kernels, on_device(): pl.pallas_call(functools.partial(back_kernel, parts - starts, ahead, inde...  3.06 us
  transfers between devices with their start and end apart: 14, of which 8 were waited for; matrix products, arithmetic and copies ran while one was open for 1% of the time, Pallas kernels for 32%

profile of v8, /device:TPU:0, one launch (start us, length us, event | category | flops | bytes accessed | tf_op | source)
XLA Modules:
  0.0 52.7 jit_solution(838701689821473520)
XLA Ops:
  0.0 1.9 %pack.1 = (s16[8,128,128]{2,1,0:T(8,128)(2,1)S(1)}, s16[16,128,128]{2,1,0:T(8,128)(2,1)S(1)}, bf16[2,128,512]{2,1,0:T(8,128)(2,1)S(1)}, bf16[2,128,512]{2,1,0:T(8,128)(2,1)S(1)}) custom-call(s32[1]{0:T(128)} %bitcast.az_ref, f32[128,16,128]{2,1,0:T(8,128)} %bitcast.13, bf16[4,2,2,128,512]{4,3,2,1,0:T(8,128)(2,1)} %constant.10.clone.tables_ref), custom_call_target="tpu_custom_call" | custom-call | bytes 4194304 | tf_op jit(solution)/shard_map/pack/pallas_call | solution.py:310
  1.9 0.5 collective-permute-start
  2.4 2.6 %collective-permute-start.1 = (s16[8,128,128]{2,1,0:T(8,128)(2,1)S(1)}, s16[8,128,128]{2,1,0:T(8,128)(2,1)S(1)}, u32[]{:S(2)}, u32[]{:S(2)}) collective-permute-start(s16[8,128,128]{2,1,0:T(8,128)(2,1)S(1)} %get-tuple-element.36), channel_id=1, source_target_pairs={{0,16},{8,24},{16,0},{24,8},{1,17},{9,25},{17,1},{25,9},{2,18},{10... | collective-permute-start | bytes 786440 | tf_op jit(solution)/shard_map/ppermute | solution.py:374
  5.0 0.7 %copy.10 = s32[64,1,3]{0,2,1:T(4,128)S(1)} copy(s32[64,1,3]{0,1,2:T(1,128)} %param.9) | data formatting | bytes 1536
  5.7 0.0 collective-permute-done.peer_ref.refs_1_
  5.7 0.0 copy-start.2
  5.7 0.7 %copy-done.2 = s32[64,1]{0,1:T(1,128)S(1)} copy-done((s32[64,1]{0,1:T(1,128)S(1)}, s32[64,1]{0,1:T(1,128)}, u32[]{:S(2)}) %copy-start.2) | copy-done | bytes 280
  6.3 3.5 %split.1 = (f32[8,128,128]{2,1,0:T(8,128)S(1)}, s16[8,128,128]{2,1,0:T(8,128)(2,1)S(1)}, bf16[3,32,256,128]{3,2,1,0:T(8,128)(2,1)S(1)}, bf16[3,32,16,128]{3,2,1,0:T(8,128)(2,1)S(1)}) custom-call(bf16[2,128,512]{2,1,0:T(8,128)(2,1)S(1)} %get-tuple-element.32.table_ref, s16[16,128,128]{2,1,0:T(8,128)(2,1)S(1)} %get-tuple-element.33.own_ref.refs_0_, ...), custom_call_target="tpu_custom_call" | custom-call | flops 805306368 | bytes 4194304 | tf_op jit(solution)/shard_map/split/pallas_call | solution.py:340
  9.9 2.0 %collective-permute-done.1.refs_2_ = s16[8,128,128]{2,1,0:T(8,128)(2,1)S(1)} collective-permute-done((s16[8,128,128]{2,1,0:T(8,128)(2,1)S(1)}, s16[8,128,128]{2,1,0:T(8,128)(2,1)S(1)}, u32[]{:S(2)}, u32[]{:S(2)}) %collective-permute-start.1) | collective-permute-done | bytes 262176 | tf_op jit(solution)/shard_map/ppermute | solution.py:374
  11.9 0.0 collective-permute-start.2
  11.9 1.8 %collective-permute-start.3 = (s16[8,128,128]{2,1,0:T(8,128)(2,1)S(1)}, s16[8,128,128]{2,1,0:T(8,128)(2,1)S(1)}, u32[]{:S(2)}, u32[]{:S(2)}) collective-permute-start(s16[8,128,128]{2,1,0:T(8,128)(2,1)S(1)} %get-tuple-element.44), channel_id=1, source_target_pairs={{0,16},{8,24},{16,0},{24,8},{1,17},{9,25},{17,1},{25,9},{2,18},{10... | collective-permute-start | bytes 786440 | tf_op jit(solution)/shard_map/ppermute | solution.py:361
  13.6 0.0 collective-permute-done.2.refs_3_
  13.6 1.3 %forward.1.refs_4_ = bf16[64,16,128]{2,1,0:T(8,128)(2,1)S(1)} custom-call(bf16[2,128,512]{2,1,0:T(8,128)(2,1)S(1)} %get-tuple-element.32.table_ref, s16[16,128,128]{2,1,0:T(8,128)(2,1)S(1)} %get-tuple-element.33.own_ref.refs_0_, s16[16,128,128]{2,1,0:T(8,128)(2,1)S(1)} %collective-permute-done.peer_ref.refs_1_, ...), custom_call_target="tpu_custom_call" | custom-call | flops 805306368 | bytes 4194304 | tf_op jit(solution)/shard_map/forward/pallas_call | solution.py:381
  15.0 1.6 %collective-permute-start.6 = (bf16[64,16,128]{2,1,0:T(8,128)(2,1)S(1)}, bf16[64,16,128]{2,1,0:T(8,128)(2,1)S(1)}, u32[]{:S(2)}, u32[]{:S(2)}) collective-permute-start(bf16[64,16,128]{2,1,0:T(8,128)(2,1)S(1)} %forward.1.refs_4_), channel_id=1, source_target_pairs={{0,1},{1,0},{2,3},{3,2},{4,5},{5,4},{6,7},{7,6},{8,9},{9,8},{10,11... | collective-permute-start | bytes 786440 | tf_op jit(solution)/shard_map/ppermute | solution.py:398
  16.6 3.5 %sort.1 = (bf16[3,32,256,128]{3,2,1,0:T(8,128)(2,1)S(1)}, bf16[3,32,16,128]{3,2,1,0:T(8,128)(2,1)S(1)}) custom-call(s32[1]{0:T(128)} %bitcast.4.place_ref.refs_0_, s32[3,64]{1,0:T(4,128)S(1)} %bitcast.19, s32[64]{0:T(128)S(1)} %bitcast.21, bf16[192,256,128]{2,1,0:T(8,128)(2,1)} %bitcast.23), custom_call_target="tpu_custom_call" | custom-call | bytes 6291456 | tf_op jit(solution)/shard_map/sort/pallas_call | solution.py:328
  20.2 0.4 collective-permute-done.3.far_ref
  20.6 0.4 finish.1.refs_5_
  21.0 1.8 %collective-permute-start.4 = (bf16[64,16,128]{2,1,0:T(8,128)(2,1)S(1)}, bf16[64,16,128]{2,1,0:T(8,128)(2,1)S(1)}, u32[]{:S(2)}, u32[]{:S(2)}) collective-permute-start(bf16[64,16,128]{2,1,0:T(8,128)(2,1)S(1)} %finish.1.refs_5_), channel_id=1, source_target_pairs={{0,1},{1,0},{2,3},{3,2},{4,5},{5,4},{6,7},{7,6},{8,9},{9,8},{10,11... | collective-permute-start | bytes 786440 | tf_op jit(solution)/shard_map/ppermute | solution.py:398
  22.9 0.6 %collective-permute-done.6.refs_6_ = bf16[64,16,128]{2,1,0:T(8,128)(2,1)S(1)} collective-permute-done((bf16[64,16,128]{2,1,0:T(8,128)(2,1)S(1)}, bf16[64,16,128]{2,1,0:T(8,128)(2,1)S(1)}, u32[]{:S(2)}, u32[]{:S(2)}) %collective-permute-start.6) | collective-permute-done | bytes 262176 | tf_op jit(solution)/shard_map/ppermute | solution.py:398
  23.5 1.6 %collective-permute-start.7 = (bf16[64,16,128]{2,1,0:T(8,128)(2,1)S(1)}, bf16[64,16,128]{2,1,0:T(8,128)(2,1)S(1)}, u32[]{:S(2)}, u32[]{:S(2)}) collective-permute-start(bf16[64,16,128]{2,1,0:T(8,128)(2,1)S(1)} %collective-permute-done.6.refs_6_), channel_id=1, source_target_pairs={{0,2},{1,7},{2,4},{3,1},{4,6},{5,3},{6,0},{7,5},{8,10},{9,15},{10,... | collective-permute-start | bytes 786440 | tf_op jit(solution)/shard_map/ppermute | solution.py:400
  25.1 2.6 %inner.1 = (f32[1024,128]{1,0:T(8,128)S(1)}, f32[1024,128]{1,0:T(8,128)S(1)}) custom-call(bf16[3,32,16,128]{3,2,1,0:T(8,128)(2,1)S(1)} %get-tuple-element.35.refs_0_, bf16[3,32,16,128]{3,2,1,0:T(8,128)(2,1)S(1)} %get-tuple-element.40.refs_1_, bf16[3,32,256,128]{3,2,1,0:T(8,128)(2,1)S(1)} %get-tuple-element.41.refs_2_, ...), custom_call_target="tpu_custom_call" | custom-call | bytes 6291456 | tf_op jit(solution)/shard_map/inner/pallas_call | solution.py:402
  27.7 1.4 %collective-permute-done.4.refs_4_ = bf16[64,16,128]{2,1,0:T(8,128)(2,1)S(1)} collective-permute-done((bf16[64,16,128]{2,1,0:T(8,128)(2,1)S(1)}, bf16[64,16,128]{2,1,0:T(8,128)(2,1)S(1)}, u32[]{:S(2)}, u32[]{:S(2)}) %collective-permute-start.4) | collective-permute-done | bytes 262176 | tf_op jit(solution)/shard_map/ppermute | solution.py:398
  29.1 1.7 %collective-permute-start.5 = (bf16[64,16,128]{2,1,0:T(8,128)(2,1)S(1)}, bf16[64,16,128]{2,1,0:T(8,128)(2,1)S(1)}, u32[]{:S(2)}, u32[]{:S(2)}) collective-permute-start(bf16[64,16,128]{2,1,0:T(8,128)(2,1)S(1)} %collective-permute-done.4.refs_4_), channel_id=1, source_target_pairs={{0,2},{1,7},{2,4},{3,1},{4,6},{5,3},{6,0},{7,5},{8,10},{9,15},{10,... | collective-permute-start | bytes 786440 | tf_op jit(solution)/shard_map/ppermute | solution.py:400
  30.9 2.4 %collective-permute-done.7.refs_4_ = bf16[64,16,128]{2,1,0:T(8,128)(2,1)S(1)} collective-permute-done((bf16[64,16,128]{2,1,0:T(8,128)(2,1)S(1)}, bf16[64,16,128]{2,1,0:T(8,128)(2,1)S(1)}, u32[]{:S(2)}, u32[]{:S(2)}) %collective-permute-start.7) | collective-permute-done | bytes 262176 | tf_op jit(solution)/shard_map/ppermute | solution.py:400
  33.2 1.3 %outer.2.refs_0_ = bf16[8,128,128]{2,1,0:T(8,128)(2,1)S(1)} custom-call(bf16[3,32,16,128]{3,2,1,0:T(8,128)(2,1)S(1)} %get-tuple-element.35.refs_0_, bf16[3,32,16,128]{3,2,1,0:T(8,128)(2,1)S(1)} %get-tuple-element.40.refs_1_, bf16[3,32,256,128]{3,2,1,0:T(8,128)(2,1)S(1)} %get-tuple-element.41.refs_2_, ...), custom_call_target="tpu_custom_call" | custom-call | bytes 3145728 | tf_op jit(solution)/shard_map/outer/pallas_call | solution.py:419
  34.5 1.3 %collective-permute-start.10 = (bf16[8,128,128]{2,1,0:T(8,128)(2,1)S(1)}, bf16[8,128,128]{2,1,0:T(8,128)(2,1)S(1)}, u32[]{:S(2)}, u32[]{:S(2)}) collective-permute-start(bf16[8,128,128]{2,1,0:T(8,128)(2,1)S(1)} %outer.2.refs_0_), channel_id=1, source_target_pairs={{0,16},{8,24},{16,0},{24,8},{1,17},{9,25},{17,1},{25,9},{2,18},{10... | collective-permute-start | bytes 786440 | tf_op jit(solution)/shard_map/ppermute | solution.py:436
  35.8 0.0 collective-permute-start.9
  35.8 2.7 %collective-permute-done.5.refs_5_ = bf16[64,16,128]{2,1,0:T(8,128)(2,1)S(1)} collective-permute-done((bf16[64,16,128]{2,1,0:T(8,128)(2,1)S(1)}, bf16[64,16,128]{2,1,0:T(8,128)(2,1)S(1)}, u32[]{:S(2)}, u32[]{:S(2)}) %collective-permute-start.5) | collective-permute-done | bytes 262176 | tf_op jit(solution)/shard_map/ppermute | solution.py:400
  38.6 0.0 copy-start
  38.6 0.0 copy-start.1
  38.6 2.3 %outer.3.refs_4_ = bf16[8,128,128]{2,1,0:T(8,128)(2,1)S(1)} custom-call(bf16[3,32,16,128]{3,2,1,0:T(8,128)(2,1)S(1)} %get-tuple-element.35.refs_0_, bf16[3,32,16,128]{3,2,1,0:T(8,128)(2,1)S(1)} %get-tuple-element.40.refs_1_, bf16[3,32,256,128]{3,2,1,0:T(8,128)(2,1)S(1)} %get-tuple-element.41.refs_2_, ...), custom_call_target="tpu_custom_call" | custom-call | bytes 3145728 | tf_op jit(solution)/shard_map/outer/pallas_call | solution.py:419
  40.9 0.1 collective-permute-start.12
  41.0 0.0 collective-permute-done.10.refs_2_
  41.0 0.5 collective-permute-start.11
  41.5 1.4 %collective-permute-start.8 = (bf16[8,128,128]{2,1,0:T(8,128)(2,1)S(1)}, bf16[8,128,128]{2,1,0:T(8,128)(2,1)S(1)}, u32[]{:S(2)}, u32[]{:S(2)}) collective-permute-start(bf16[8,128,128]{2,1,0:T(8,128)(2,1)S(1)} %outer.3.refs_4_), channel_id=1, source_target_pairs={{0,16},{8,24},{16,0},{24,8},{1,17},{9,25},{17,1},{25,9},{2,18},{10... | collective-permute-start | bytes 786440 | tf_op jit(solution)/shard_map/ppermute | solution.py:436
  42.9 0.0 collective-permute-done.12.refs_5_
  42.9 0.0 collective-permute-done.9.refs_1_
  42.9 0.0 collective-permute-done.11.refs_3_
  42.9 0.0 copy-done
  42.9 0.0 copy-done.1
  42.9 1.7 %back.2 = (f32[128,16,128]{2,1,0:T(8,128)}, f32[4,128,256]{2,1,0:T(8,128)S(1)}) custom-call(bf16[2,128,512]{2,1,0:T(8,128)(2,1)S(1)} %get-tuple-element.31.table_ref, f32[2048,128]{1,0:T(8,128)S(1)} %bitcast.14, f32[128,128]{1,0:T(8,128)S(1)} %bitcast.16, bf16[8,128,128]{2,1,0:T(8,128)(2,1)S(1)} %outer.2.refs_0_, ...), custom_call_target="tpu_custom_call" | custom-call | flops 536870912 | bytes 4194304 | tf_op jit(solution)/shard_map/back/pallas_call | solution.py:451
  44.6 5.2 %collective-permute-done.8.refs_0_ = bf16[8,128,128]{2,1,0:T(8,128)(2,1)S(1)} collective-permute-done((bf16[8,128,128]{2,1,0:T(8,128)(2,1)S(1)}, bf16[8,128,128]{2,1,0:T(8,128)(2,1)S(1)}, u32[]{:S(2)}, u32[]{:S(2)}) %collective-permute-start.8) | collective-permute-done | bytes 262176 | tf_op jit(solution)/shard_map/ppermute | solution.py:436
  49.8 0.0 collective-permute-start.13
  49.8 1.5 %collective-permute-done.13.refs_1_ = bf16[8,128,128]{2,1,0:T(8,128)(2,1)S(1)} collective-permute-done((bf16[8,128,128]{2,1,0:T(8,128)(2,1)S(1)}, bf16[8,128,128]{2,1,0:T(8,128)(2,1)S(1)}, u32[]{:S(2)}, u32[]{:S(2)}) %collective-permute-start.13) | collective-permute-done | bytes 262176 | tf_op jit(solution)/shard_map/ppermute | solution.py:440
  51.3 1.4 %back.3 = f32[128,16,128]{2,1,0:T(8,128)} custom-call(bf16[2,128,512]{2,1,0:T(8,128)(2,1)S(1)} %get-tuple-element.31.table_ref, f32[2048,128]{1,0:T(8,128)S(1)} %bitcast.15, f32[128,128]{1,0:T(8,128)S(1)} %bitcast.17, bf16[8,128,128]{2,1,0:T(8,128)(2,1)S(1)} %collective-permute-done.8.refs_0_, ...), custom_call_target="tpu_custom_call", output_to_operand_aliasing={{}: (6, {})} | custom-call | flops 536870912 | bytes 4194304 | tf_op jit(solution)/shard_map/back/pallas_call | solution.py:451
Async XLA Ops:
  1.9 3.8 %collective-permute-start = (s16[16,128,128]{2,1,0:T(8,128)(2,1)S(1)}, s16[16,128,128]{2,1,0:T(8,128)(2,1)S(1)}, u32[]{:S(2)}, u32[]{:S(2)}) collective-permute-start(s16[16,128,128]{2,1,0:T(8,128)(2,1)S(1)} %get-tuple-element.33.own_ref.refs_0_), channel_id=1, source_target_pairs={{0,8},{8,0},{16,24},{24,16},{1,9},{9,1},{17,25},{25,17},{2,10},{10... | collective-permute-start | bytes 1572872 | tf_op jit(solution)/shard_map/ppermute | solution.py:324
  2.4 9.5 %collective-permute-start.1 = (s16[8,128,128]{2,1,0:T(8,128)(2,1)S(1)}, s16[8,128,128]{2,1,0:T(8,128)(2,1)S(1)}, u32[]{:S(2)}, u32[]{:S(2)}) collective-permute-start(s16[8,128,128]{2,1,0:T(8,128)(2,1)S(1)} %get-tuple-element.36), channel_id=1, source_target_pairs={{0,16},{8,24},{16,0},{24,8},{1,17},{9,25},{17,1},{25,9},{2,18},{10... | collective-permute-start | bytes 786440 | tf_op jit(solution)/shard_map/ppermute | solution.py:374
  5.7 0.7 %copy-start.2 = (s32[64,1]{0,1:T(1,128)S(1)}, s32[64,1]{0,1:T(1,128)}, u32[]{:S(2)}) copy-start(s32[64,1]{0,1:T(1,128)} %param.10) | copy-start | bytes 772
  11.9 1.8 %collective-permute-start.2 = (s16[8,128,128]{2,1,0:T(8,128)(2,1)S(1)}, s16[8,128,128]{2,1,0:T(8,128)(2,1)S(1)}, u32[]{:S(2)}, u32[]{:S(2)}) collective-permute-start(s16[8,128,128]{2,1,0:T(8,128)(2,1)S(1)} %collective-permute-done.1.refs_2_), channel_id=1, source_target_pairs={{0,8},{8,0},{16,24},{24,16},{1,9},{9,1},{17,25},{25,17},{2,10},{10... | collective-permute-start | bytes 786440 | tf_op jit(solution)/shard_map/ppermute | solution.py:376
  11.9 8.7 %collective-permute-start.3 = (s16[8,128,128]{2,1,0:T(8,128)(2,1)S(1)}, s16[8,128,128]{2,1,0:T(8,128)(2,1)S(1)}, u32[]{:S(2)}, u32[]{:S(2)}) collective-permute-start(s16[8,128,128]{2,1,0:T(8,128)(2,1)S(1)} %get-tuple-element.44), channel_id=1, source_target_pairs={{0,16},{8,24},{16,0},{24,8},{1,17},{9,25},{17,1},{25,9},{2,18},{10... | collective-permute-start | bytes 786440 | tf_op jit(solution)/shard_map/ppermute | solution.py:361
  15.0 8.5 %collective-permute-start.6 = (bf16[64,16,128]{2,1,0:T(8,128)(2,1)S(1)}, bf16[64,16,128]{2,1,0:T(8,128)(2,1)S(1)}, u32[]{:S(2)}, u32[]{:S(2)}) collective-permute-start(bf16[64,16,128]{2,1,0:T(8,128)(2,1)S(1)} %forward.1.refs_4_), channel_id=1, source_target_pairs={{0,1},{1,0},{2,3},{3,2},{4,5},{5,4},{6,7},{7,6},{8,9},{9,8},{10,11... | collective-permute-start | bytes 786440 | tf_op jit(solution)/shard_map/ppermute | solution.py:398
  21.0 8.1 %collective-permute-start.4 = (bf16[64,16,128]{2,1,0:T(8,128)(2,1)S(1)}, bf16[64,16,128]{2,1,0:T(8,128)(2,1)S(1)}, u32[]{:S(2)}, u32[]{:S(2)}) collective-permute-start(bf16[64,16,128]{2,1,0:T(8,128)(2,1)S(1)} %finish.1.refs_5_), channel_id=1, source_target_pairs={{0,1},{1,0},{2,3},{3,2},{4,5},{5,4},{6,7},{7,6},{8,9},{9,8},{10,11... | collective-permute-start | bytes 786440 | tf_op jit(solution)/shard_map/ppermute | solution.py:398
  23.5 9.7 %collective-permute-start.7 = (bf16[64,16,128]{2,1,0:T(8,128)(2,1)S(1)}, bf16[64,16,128]{2,1,0:T(8,128)(2,1)S(1)}, u32[]{:S(2)}, u32[]{:S(2)}) collective-permute-start(bf16[64,16,128]{2,1,0:T(8,128)(2,1)S(1)} %collective-permute-done.6.refs_6_), channel_id=1, source_target_pairs={{0,2},{1,7},{2,4},{3,1},{4,6},{5,3},{6,0},{7,5},{8,10},{9,15},{10,... | collective-permute-start | bytes 786440 | tf_op jit(solution)/shard_map/ppermute | solution.py:400
  29.1 9.4 %collective-permute-start.5 = (bf16[64,16,128]{2,1,0:T(8,128)(2,1)S(1)}, bf16[64,16,128]{2,1,0:T(8,128)(2,1)S(1)}, u32[]{:S(2)}, u32[]{:S(2)}) collective-permute-start(bf16[64,16,128]{2,1,0:T(8,128)(2,1)S(1)} %collective-permute-done.4.refs_4_), channel_id=1, source_target_pairs={{0,2},{1,7},{2,4},{3,1},{4,6},{5,3},{6,0},{7,5},{8,10},{9,15},{10,... | collective-permute-start | bytes 786440 | tf_op jit(solution)/shard_map/ppermute | solution.py:400
  34.5 6.5 %collective-permute-start.10 = (bf16[8,128,128]{2,1,0:T(8,128)(2,1)S(1)}, bf16[8,128,128]{2,1,0:T(8,128)(2,1)S(1)}, u32[]{:S(2)}, u32[]{:S(2)}) collective-permute-start(bf16[8,128,128]{2,1,0:T(8,128)(2,1)S(1)} %outer.2.refs_0_), channel_id=1, source_target_pairs={{0,16},{8,24},{16,0},{24,8},{1,17},{9,25},{17,1},{25,9},{2,18},{10... | collective-permute-start | bytes 786440 | tf_op jit(solution)/shard_map/ppermute | solution.py:436
  35.8 7.0 %collective-permute-start.9 = (bf16[8,128,128]{2,1,0:T(8,128)(2,1)S(1)}, bf16[8,128,128]{2,1,0:T(8,128)(2,1)S(1)}, u32[]{:S(2)}, u32[]{:S(2)}) collective-permute-start(bf16[8,128,128]{2,1,0:T(8,128)(2,1)S(1)} %outer.2.refs_0_), channel_id=1, source_target_pairs={{0,8},{8,0},{16,24},{24,16},{1,9},{9,1},{17,25},{25,17},{2,10},{10... | collective-permute-start | bytes 786440 | tf_op jit(solution)/shard_map/ppermute | solution.py:431
  38.6 4.3 %copy-start = (f32[2,64,16,128]{3,2,1,0:T(8,128)S(1)}, f32[2,64,16,128]{3,2,1,0:T(8,128)}, u32[]{:S(2)}) copy-start(f32[2,64,16,128]{3,2,1,0:T(8,128)} %param.6) | copy-start | bytes 3145732
  38.6 4.3 %copy-start.1 = (f32[2,64,128]{2,1,0:T(8,128)S(1)}, f32[2,64,128]{2,1,0:T(8,128)}, u32[]{:S(2)}) copy-start(f32[2,64,128]{2,1,0:T(8,128)} %param.7) | copy-start | bytes 196612
  40.9 2.0 %collective-permute-start.12 = (bf16[8,128,128]{2,1,0:T(8,128)(2,1)S(1)}, bf16[8,128,128]{2,1,0:T(8,128)(2,1)S(1)}, u32[]{:S(2)}, u32[]{:S(2)}) collective-permute-start(bf16[8,128,128]{2,1,0:T(8,128)(2,1)S(1)} %outer.3.refs_4_), channel_id=1, source_target_pairs={{0,8},{8,0},{16,24},{24,16},{1,9},{9,1},{17,25},{25,17},{2,10},{10... | collective-permute-start | bytes 786440 | tf_op jit(solution)/shard_map/ppermute | solution.py:431
  41.0 1.9 %collective-permute-start.11 = (bf16[8,128,128]{2,1,0:T(8,128)(2,1)S(1)}, bf16[8,128,128]{2,1,0:T(8,128)(2,1)S(1)}, u32[]{:S(2)}, u32[]{:S(2)}) collective-permute-start(bf16[8,128,128]{2,1,0:T(8,128)(2,1)S(1)} %collective-permute-done.10.refs_2_), channel_id=1, source_target_pairs={{0,8},{8,0},{16,24},{24,16},{1,9},{9,1},{17,25},{25,17},{2,10},{10... | collective-permute-start | bytes 786440 | tf_op jit(solution)/shard_map/ppermute | solution.py:443
  41.5 8.3 %collective-permute-start.8 = (bf16[8,128,128]{2,1,0:T(8,128)(2,1)S(1)}, bf16[8,128,128]{2,1,0:T(8,128)(2,1)S(1)}, u32[]{:S(2)}, u32[]{:S(2)}) collective-permute-start(bf16[8,128,128]{2,1,0:T(8,128)(2,1)S(1)} %outer.3.refs_4_), channel_id=1, source_target_pairs={{0,16},{8,24},{16,0},{24,8},{1,17},{9,25},{17,1},{25,9},{2,18},{10... | collective-permute-start | bytes 786440 | tf_op jit(solution)/shard_map/ppermute | solution.py:436
  49.8 1.5 %collective-permute-start.13 = (bf16[8,128,128]{2,1,0:T(8,128)(2,1)S(1)}, bf16[8,128,128]{2,1,0:T(8,128)(2,1)S(1)}, u32[]{:S(2)}, u32[]{:S(2)}) collective-permute-start(bf16[8,128,128]{2,1,0:T(8,128)(2,1)S(1)} %collective-permute-done.8.refs_0_), channel_id=1, source_target_pairs={{0,8},{8,0},{16,24},{24,16},{1,9},{9,1},{17,25},{25,17},{2,10},{10... | collective-permute-start | bytes 786440 | tf_op jit(solution)/shard_map/ppermute | solution.py:440

commit v9 on v8

--- a/solution.py
+++ b/solution.py
@@ -49,7 +49,7 @@
     return (t * jnp.abs(t)) * (t * t)
 
 
-def pack_kernel(chunks, az_ref, fields_ref, tables_ref, first_ref, all_ref, forward_out, back_out, held, sems):
+def pack_kernel(chunks, fields_ref, tables_ref, first_ref, all_ref, forward_out, back_out, held, sems):
     rows, rhs, nodes = fields_ref.shape
     per = rhs // chunks
     copies = [
@@ -59,7 +59,7 @@
         for index in range(chunks)
     ]
     tables = [
-        pltpu.make_async_copy(tables_ref.at[az_ref[0], way], out, sems.at[chunks + way])
+        pltpu.make_async_copy(tables_ref.at[lax.axis_index("az"), way], out, sems.at[chunks + way])
         for way, out in enumerate((forward_out, back_out))
     ]
     for copy in copies + tables:
@@ -93,9 +93,9 @@
         modes_ref[k] = jnp.concatenate([real, imag], axis=0).astype(jnp.bfloat16)
 
 
-def split_kernel(first, sort, table_ref, own_ref, peer_ref, place_ref, cols_ref, count_ref, tiles_ref,
+def split_kernel(first, sort, table_ref, own_ref, peer_ref, cols_ref, count_ref, tiles_ref,
                  near_ref, far_ref, out_ref, live_ref, sem):
-    copy = sort(place_ref, cols_ref, count_ref, tiles_ref, out_ref, live_ref, sem)
+    copy = sort(cols_ref, count_ref, tiles_ref, out_ref, live_ref, sem)
     per, rows, nodes = far_ref.shape
     odd = lax.rem(lax.broadcasted_iota(jnp.int32, (rows, 2 * nodes), 0), 2) == 1
     for r in range(0, per, 2):
@@ -136,10 +136,10 @@
     write_modes(held, modes_ref)
 
 
-def begin_sort(first, place_ref, cols_ref, count_ref, tiles_ref, out_ref, live_ref, sem):
+def begin_sort(first, cols_ref, count_ref, tiles_ref, out_ref, live_ref, sem):
     slots, modes = cols_ref.shape
     share = out_ref.shape[1]
-    place = place_ref[0]
+    place = lax.axis_index("curve")
     even = lax.rem(place, 2) == 0
     side = jnp.where(even, place + 1, place - 1)
 
@@ -231,14 +231,16 @@
     return total
 
 
-def back_kernel(sources, ahead, chunk, starts, table_ref, fields_ref, impedance_ref, *refs):
-    given, next_refs, refs = refs[:sources], refs[sources : sources + ahead], refs[sources + ahead :]
-    if starts:
-        ready_ref, refs = refs[0], refs[1:]
-    if ahead:
-        out_ref, next_out, held, sem = refs[-4:]
-    else:
-        out_ref, held, sem = refs[-3:]
+def lead_kernel(counts, table_ref, *refs):
+    near_refs, out_refs = refs[: -len(counts)], refs[-len(counts) :]
+    for count, out_ref in zip(counts, out_refs):
+        for r in range(0, near_refs[0].shape[0], 2):
+            out_ref[r // 2] = back_product(table_ref, near_refs[:count], range(count), r)
+        near_refs = near_refs[count:]
+
+
+def back_kernel(sources, chunk, starts, table_ref, fields_ref, impedance_ref, *refs):
+    given, (out_ref, held, sem) = refs[:sources], refs[-3:]
     per, rows, nodes = given[0].shape
     rhs = fields_ref.shape[0] // rows
     local = rows // 2
@@ -246,7 +248,7 @@
     for r in range(0, per, 2):
         total = back_product(table_ref, given, range(starts, starts + sources), r)
         if starts:
-            total += ready_ref[r // 2]
+            total += refs[sources][r // 2]
         for s in range(2):
             real, imag = total[:local, s * nodes : (s + 1) * nodes], total[local:, s * nodes : (s + 1) * nodes]
             from_row = chunk * per + r + s
@@ -258,9 +260,6 @@
         held.reshape(rows, per, nodes), out_ref.at[:, pl.ds(chunk * per, per), :], sem
     )
     copy.start()
-    if ahead:
-        for r in range(0, per, 2):
-            next_out[r // 2] = back_product(table_ref, next_refs, range(ahead), r)
     copy.wait()
 
 
@@ -305,12 +304,10 @@
     multiply = 4 * rows * rows * parts * per * nodes
     chunk_shape = jax.ShapeDtypeStruct((per, rows, nodes), jnp.int16)
 
-    az = lax.axis_index("az").astype(jnp.int32)[None]
-    place = lax.axis_index("curve").astype(jnp.int32)[None]
     first, coded, forward_table, back_table = pl.pallas_call(
         functools.partial(pack_kernel, CHUNKS),
         out_shape=[chunk_shape, jax.ShapeDtypeStruct((rhs, rows, nodes), jnp.int16), table_shape, table_shape],
-        in_specs=[smem, hbm, hbm],
+        in_specs=[hbm, hbm],
         out_specs=[vmem] * 4,
         scratch_shapes=[
             pltpu.VMEM((CHUNKS, rows * per, nodes), jnp.float32),
@@ -319,7 +316,7 @@
         cost_estimate=cost(0, move),
         compiler_params=pack_params,
         name="pack",
-    )(az, cut_fields, tables)
+    )(cut_fields, tables)
 
     peer = lax.ppermute(coded, "az", PEER) if paired else None
     pattern = (tile_cols[:, 0, :].T, tile_count.reshape(local))
@@ -328,25 +325,25 @@
         return pl.pallas_call(
             functools.partial(sort_kernel, functools.partial(begin_sort, turn * share)),
             out_shape=sort_shapes,
-            in_specs=[smem] * 3 + [hbm],
+            in_specs=[smem] * 2 + [hbm],
             out_specs=[vmem] * 2,
             scratch_shapes=[pltpu.SemaphoreType.DMA],
             cost_estimate=cost(0, 2 * tile_data.size // SHARES),
             compiler_params=stage_params,
             name="sort",
-        )(after(place, wait_for), *pattern, flat_tiles)
+        )(*pattern, after(flat_tiles, wait_for))
 
     if paired:
         near_part, far_part, head, live = pl.pallas_call(
             functools.partial(split_kernel, per, functools.partial(begin_sort, 0)),
             out_shape=[jax.ShapeDtypeStruct((per, rows, nodes), jnp.float32), chunk_shape] + sort_shapes,
-            in_specs=[vmem] * 3 + [smem] * 3 + [hbm],
+            in_specs=[vmem] * 3 + [smem] * 2 + [hbm],
             out_specs=[vmem] * 4,
             scratch_shapes=[pltpu.SemaphoreType.DMA],
             cost_estimate=cost(3 * multiply, move),
             compiler_params=stage_params,
             name="split",
-        )(forward_table, coded, peer, after(place, coded), *pattern, flat_tiles)
+        )(forward_table, coded, peer, *pattern, flat_tiles)
     else:
         head, live = sorting(0, coded)
     tiles, lives = [head], [live]
@@ -397,7 +394,6 @@
 
     side_in = [lax.ppermute(own, "curve", sides) for own in owns]
     side_in[0] = after(side_in[0], *owns[1:])
-    far_in = [lax.ppermute(side, "curve", onward) for side in side_in]
     part_shape = jax.ShapeDtypeStruct((local * 2 * per, nodes), jnp.float32)
     parts_of = pl.pallas_call(
         functools.partial(inner_kernel, CHUNKS, SHARES),
@@ -409,6 +405,8 @@
         name="inner",
     )(*lives, *tiles, *owns, side_in[0])
 
+    side_in[1:] = [after(side, *parts_of) for side in side_in[1:]]
+    far_in = [lax.ppermute(side, "curve", onward) for side in side_in]
     nears = []
     for index in range(CHUNKS):
         if index == 0:
@@ -428,39 +426,45 @@
             )(*lives, *tiles, *values, parts_of[index])
         )
 
-    peers = [lax.ppermute(near, "az", PEER) for near in nears] if paired else []
-    out, ready = None, None
+    if paired:
+        peers = [lax.ppermute(near, "az", PEER) for near in nears]
+        across = [lax.ppermute(near, "az", ACROSS) for near in nears]
+        counts = [2] * (CHUNKS - 1) + [1]
+        led = [x for near, peer_near, count in zip(nears, peers, counts) for x in (near, peer_near)[:count]]
+        ready = pl.pallas_call(
+            functools.partial(lead_kernel, counts),
+            out_shape=[jax.ShapeDtypeStruct((per // 2, rows, 2 * nodes), jnp.float32)] * CHUNKS,
+            in_specs=[vmem] * (1 + len(led)),
+            out_specs=[vmem] * CHUNKS,
+            cost_estimate=cost(2 * multiply, move),
+            compiler_params=params,
+            name="lead",
+        )(back_table, *led)
+        across[:-1] = [after(x, nears[-1]) for x in across[:-1]]
+        across[-1] = after(across[-1], *ready)
+        crossed = [lax.ppermute(x, "az", PEER) for x in across]
+        crossed[:-1] = [after(x, across[-1]) for x in crossed[:-1]]
+    out = None
     for index, near in enumerate(nears):
-        starts, ahead = 0, 0
+        starts = 0
         if paired:
-            across = lax.ppermute(near, "az", ACROSS)
-            if index:
-                starts = 2
-                across, out, ready = lax.optimization_barrier((across, out, ready))
-                given = [across, lax.ppermute(across, "az", PEER), ready, out]
-            else:
-                across = after(across, nears[-1])
-                given = [near, peers[0], across, lax.ppermute(across, "az", PEER)]
-            if index + 1 < CHUNKS:
-                ahead = 2
-                given[4 - starts : 4 - starts] = [nears[index + 1], peers[index + 1]]
+            starts = counts[index]
+            given = [near, peers[index], across[index], crossed[index]][starts:] + [ready[index]]
         else:
             every = lax.all_gather(near, "az")
-            given = [every[j] for j in range(parts)] + ([] if out is None else [out])
-        operands = [back_table, flat_fields, flat_impedance] + given
-        results = pl.pallas_call(
-            functools.partial(back_kernel, parts - starts, ahead, index, starts),
-            out_shape=[jax.ShapeDtypeStruct((rows, rhs, nodes), jnp.float32)]
-            + [jax.ShapeDtypeStruct((per // 2, rows, 2 * nodes), jnp.float32)] * (ahead > 0),
+            given = [every[j] for j in range(parts)]
+        operands = [back_table, flat_fields, flat_impedance] + given + ([] if out is None else [out])
+        out = pl.pallas_call(
+            functools.partial(back_kernel, parts - starts, index, starts),
+            out_shape=jax.ShapeDtypeStruct((rows, rhs, nodes), jnp.float32),
             in_specs=[vmem] * (len(operands) - (out is not None)) + [hbm] * (out is not None),
-            out_specs=[hbm] + [vmem] * (ahead > 0),
+            out_specs=hbm,
             scratch_shapes=[pltpu.VMEM((rows * per, nodes), jnp.float32), pltpu.SemaphoreType.DMA],
             input_output_aliases={} if out is None else {len(operands) - 1: 0},
             cost_estimate=cost(2 * multiply, move),
             compiler_params=params,
             name="back",
         )(*operands)
-        out, ready = results[0], results[-1]
     return out.reshape(fields.shape)
 
 

time: 52.9 us -> 51 us (0.964)
  waiting for transfers between devices: 16.3 us -> 14 us
    ppermute x6, waiting for transfers between devices: 6.71 us -> 4.44 us  [the longest x2 4.27 us: on_device(): across = [lax.ppermute(near, 'az', ACROSS) for near in nears]]
    pallas_call x2 -> x3, Pallas kernels: 3.06 us -> 3.4 us  [the longest x2 2.85 us: on_device(): pl.pallas_call(functools.partial(back_kernel, parts - starts, index, star...]
  transfers between devices with their start and end apart: 14 -> 14, of which waited for: 8 -> 8; matrix products, arithmetic and copies ran while one was open for 1% -> 1% of each run, Pallas kernels for 32% -> 33%
where the time goes in v9:
time: 51 us; the launch traced here: 50.7 us
  Pallas kernels  20.3 us (40%)
  starting transfers between devices  14.9 us (29%)
  waiting for transfers between devices  14 us (27%)
  local copies, waits for them, and re-layouts  1.35 us (3%)
    ppermute x2, waiting for transfers between devices, on_device(): far_in = [lax.ppermute(side, 'curve', onward) for side in side_in]  5.09 us
    ppermute x2, waiting for transfers between devices, on_device(): across = [lax.ppermute(near, 'az', ACROSS) for near in nears]  4.27 us
    pallas_call x2, Pallas kernels, on_device(): pl.pallas_call(functools.partial(outer_kernel, roles, SHARES), out_shape=...  3.57 us
    pallas_call x1, Pallas kernels, on_device(): pl.pallas_call(functools.partial(split_kernel, per, functools.partial(beg...  3.55 us
    pallas_call x1, Pallas kernels, sorting(): pl.pallas_call(functools.partial(sort_kernel, functools.partial(begin_sor...  3.54 us
    ppermute x2, starting transfers between devices, on_device(): side_in = [lax.ppermute(own, 'curve', sides) for own in owns]  3.46 us
    ppermute x2, starting transfers between devices, on_device(): far_in = [lax.ppermute(side, 'curve', onward) for side in side_in]  3.32 us
    pallas_call x2, Pallas kernels, on_device(): pl.pallas_call(functools.partial(back_kernel, parts - starts, index, star...  2.85 us
  transfers between devices with their start and end apart: 14, of which 8 were waited for; matrix products, arithmetic and copies ran while one was open for 1% of the time, Pallas kernels for 33%

profile of v9, /device:TPU:0, one launch (start us, length us, event | category | flops | bytes accessed | tf_op | source)
XLA Modules:
  0.0 50.7 jit_solution(16849773875312127133)
XLA Ops:
  0.0 1.9 %pack.1 = (s16[8,128,128]{2,1,0:T(8,128)(2,1)S(1)}, s16[16,128,128]{2,1,0:T(8,128)(2,1)S(1)}, bf16[2,128,512]{2,1,0:T(8,128)(2,1)S(1)}, bf16[2,128,512]{2,1,0:T(8,128)(2,1)S(1)}) custom-call(f32[128,16,128]{2,1,0:T(8,128)} %bitcast.11, bf16[4,2,2,128,512]{4,3,2,1,0:T(8,128)(2,1)} %constant.2.clone.tables_ref), custom_call_target="tpu_custom_call" | custom-call | bytes 4194304 | tf_op jit(solution)/shard_map/pack/pallas_call | solution.py:307
  1.9 0.5 %collective-permute-start = (s16[16,128,128]{2,1,0:T(8,128)(2,1)S(1)}, s16[16,128,128]{2,1,0:T(8,128)(2,1)S(1)}, u32[]{:S(2)}, u32[]{:S(2)}) collective-permute-start(s16[16,128,128]{2,1,0:T(8,128)(2,1)S(1)} %get-tuple-element.32.own_ref.refs_0_), channel_id=1, source_target_pairs={{0,8},{8,0},{16,24},{24,16},{1,9},{9,1},{17,25},{25,17},{2,10},{10... | collective-permute-start | bytes 1572872 | tf_op jit(solution)/shard_map/ppermute | solution.py:321
  2.4 2.6 %collective-permute-start.1 = (s16[8,128,128]{2,1,0:T(8,128)(2,1)S(1)}, s16[8,128,128]{2,1,0:T(8,128)(2,1)S(1)}, u32[]{:S(2)}, u32[]{:S(2)}) collective-permute-start(s16[8,128,128]{2,1,0:T(8,128)(2,1)S(1)} %get-tuple-element.34), channel_id=1, source_target_pairs={{0,16},{8,24},{16,0},{24,8},{1,17},{9,25},{17,1},{25,9},{2,18},{10... | collective-permute-start | bytes 786440 | tf_op jit(solution)/shard_map/ppermute | solution.py:371
  5.0 0.7 %copy.10 = s32[64,1,3]{0,2,1:T(4,128)S(1)} copy(s32[64,1,3]{0,1,2:T(1,128)} %param.9) | data formatting | bytes 1536
  5.7 0.0 collective-permute-done.peer_ref.refs_1_
  5.7 0.0 copy-start.2
  5.7 0.7 %copy-done.2 = s32[64,1]{0,1:T(1,128)S(1)} copy-done((s32[64,1]{0,1:T(1,128)S(1)}, s32[64,1]{0,1:T(1,128)}, u32[]{:S(2)}) %copy-start.2) | copy-done | bytes 280
  6.3 3.5 %split.1 = (f32[8,128,128]{2,1,0:T(8,128)S(1)}, s16[8,128,128]{2,1,0:T(8,128)(2,1)S(1)}, bf16[3,32,256,128]{3,2,1,0:T(8,128)(2,1)S(1)}, bf16[3,32,16,128]{3,2,1,0:T(8,128)(2,1)S(1)}) custom-call(bf16[2,128,512]{2,1,0:T(8,128)(2,1)S(1)} %get-tuple-element.31.table_ref, s16[16,128,128]{2,1,0:T(8,128)(2,1)S(1)} %get-tuple-element.32.own_ref.refs_0_, ...), custom_call_target="tpu_custom_call" | custom-call | flops 805306368 | bytes 4194304 | tf_op jit(solution)/shard_map/split/pallas_call | solution.py:337
  9.9 2.0 %collective-permute-done.1.refs_2_ = s16[8,128,128]{2,1,0:T(8,128)(2,1)S(1)} collective-permute-done((s16[8,128,128]{2,1,0:T(8,128)(2,1)S(1)}, s16[8,128,128]{2,1,0:T(8,128)(2,1)S(1)}, u32[]{:S(2)}, u32[]{:S(2)}) %collective-permute-start.1) | collective-permute-done | bytes 262176 | tf_op jit(solution)/shard_map/ppermute | solution.py:371
  11.9 0.0 collective-permute-start.2
  11.9 1.8 %collective-permute-start.3 = (s16[8,128,128]{2,1,0:T(8,128)(2,1)S(1)}, s16[8,128,128]{2,1,0:T(8,128)(2,1)S(1)}, u32[]{:S(2)}, u32[]{:S(2)}) collective-permute-start(s16[8,128,128]{2,1,0:T(8,128)(2,1)S(1)} %get-tuple-element.42), channel_id=1, source_target_pairs={{0,16},{8,24},{16,0},{24,8},{1,17},{9,25},{17,1},{25,9},{2,18},{10... | collective-permute-start | bytes 786440 | tf_op jit(solution)/shard_map/ppermute | solution.py:358
  13.6 0.0 collective-permute-done.2.refs_3_
  13.6 1.4 %forward.1.refs_4_ = bf16[64,16,128]{2,1,0:T(8,128)(2,1)S(1)} custom-call(bf16[2,128,512]{2,1,0:T(8,128)(2,1)S(1)} %get-tuple-element.31.table_ref, s16[16,128,128]{2,1,0:T(8,128)(2,1)S(1)} %get-tuple-element.32.own_ref.refs_0_, s16[16,128,128]{2,1,0:T(8,128)(2,1)S(1)} %collective-permute-done.peer_ref.refs_1_, ...), custom_call_target="tpu_custom_call" | custom-call | flops 805306368 | bytes 4194304 | tf_op jit(solution)/shard_map/forward/pallas_call | solution.py:378
  15.0 1.6 %collective-permute-start.5 = (bf16[64,16,128]{2,1,0:T(8,128)(2,1)S(1)}, bf16[64,16,128]{2,1,0:T(8,128)(2,1)S(1)}, u32[]{:S(2)}, u32[]{:S(2)}) collective-permute-start(bf16[64,16,128]{2,1,0:T(8,128)(2,1)S(1)} %forward.1.refs_4_), channel_id=1, source_target_pairs={{0,1},{1,0},{2,3},{3,2},{4,5},{5,4},{6,7},{7,6},{8,9},{9,8},{10,11... | collective-permute-start | bytes 786440 | tf_op jit(solution)/shard_map/ppermute | solution.py:395
  16.6 3.5 %sort.1 = (bf16[3,32,256,128]{3,2,1,0:T(8,128)(2,1)S(1)}, bf16[3,32,16,128]{3,2,1,0:T(8,128)(2,1)S(1)}) custom-call(s32[3,64]{1,0:T(4,128)S(1)} %bitcast.17, s32[64]{0:T(128)S(1)} %bitcast.19, bf16[192,256,128]{2,1,0:T(8,128)(2,1)} %bitcast.21), custom_call_target="tpu_custom_call" | custom-call | bytes 6291456 | tf_op jit(solution)/shard_map/sort/pallas_call | solution.py:325
  20.2 0.4 collective-permute-done.3.far_ref
  20.6 0.4 finish.1.refs_5_
  21.0 1.8 %collective-permute-start.4 = (bf16[64,16,128]{2,1,0:T(8,128)(2,1)S(1)}, bf16[64,16,128]{2,1,0:T(8,128)(2,1)S(1)}, u32[]{:S(2)}, u32[]{:S(2)}) collective-permute-start(bf16[64,16,128]{2,1,0:T(8,128)(2,1)S(1)} %finish.1.refs_5_), channel_id=1, source_target_pairs={{0,1},{1,0},{2,3},{3,2},{4,5},{5,4},{6,7},{7,6},{8,9},{9,8},{10,11... | collective-permute-start | bytes 786440 | tf_op jit(solution)/shard_map/ppermute | solution.py:395
  22.9 0.6 %collective-permute-done.5.refs_6_ = bf16[64,16,128]{2,1,0:T(8,128)(2,1)S(1)} collective-permute-done((bf16[64,16,128]{2,1,0:T(8,128)(2,1)S(1)}, bf16[64,16,128]{2,1,0:T(8,128)(2,1)S(1)}, u32[]{:S(2)}, u32[]{:S(2)}) %collective-permute-start.5) | collective-permute-done | bytes 262176 | tf_op jit(solution)/shard_map/ppermute | solution.py:395
  23.5 1.6 %collective-permute-start.7 = (bf16[64,16,128]{2,1,0:T(8,128)(2,1)S(1)}, bf16[64,16,128]{2,1,0:T(8,128)(2,1)S(1)}, u32[]{:S(2)}, u32[]{:S(2)}) collective-permute-start(bf16[64,16,128]{2,1,0:T(8,128)(2,1)S(1)} %collective-permute-done.5.refs_6_), channel_id=1, source_target_pairs={{0,2},{1,7},{2,4},{3,1},{4,6},{5,3},{6,0},{7,5},{8,10},{9,15},{10,... | collective-permute-start | bytes 786440 | tf_op jit(solution)/shard_map/ppermute | solution.py:409
  25.1 2.6 %inner.1 = (f32[1024,128]{1,0:T(8,128)S(1)}, f32[1024,128]{1,0:T(8,128)S(1)}) custom-call(bf16[3,32,16,128]{3,2,1,0:T(8,128)(2,1)S(1)} %get-tuple-element.33.refs_0_, bf16[3,32,16,128]{3,2,1,0:T(8,128)(2,1)S(1)} %get-tuple-element.38.refs_1_, bf16[3,32,256,128]{3,2,1,0:T(8,128)(2,1)S(1)} %get-tuple-element.39.refs_2_, ...), custom_call_target="tpu_custom_call" | custom-call | bytes 6291456 | tf_op jit(solution)/shard_map/inner/pallas_call | solution.py:398
  27.7 1.4 %collective-permute-done.4.refs_4_ = bf16[64,16,128]{2,1,0:T(8,128)(2,1)S(1)} collective-permute-done((bf16[64,16,128]{2,1,0:T(8,128)(2,1)S(1)}, bf16[64,16,128]{2,1,0:T(8,128)(2,1)S(1)}, u32[]{:S(2)}, u32[]{:S(2)}) %collective-permute-start.4) | collective-permute-done | bytes 262176 | tf_op jit(solution)/shard_map/ppermute | solution.py:395
  29.1 1.7 %collective-permute-start.6 = (bf16[64,16,128]{2,1,0:T(8,128)(2,1)S(1)}, bf16[64,16,128]{2,1,0:T(8,128)(2,1)S(1)}, u32[]{:S(2)}, u32[]{:S(2)}) collective-permute-start(bf16[64,16,128]{2,1,0:T(8,128)(2,1)S(1)} %collective-permute-done.4.refs_4_), channel_id=1, source_target_pairs={{0,2},{1,7},{2,4},{3,1},{4,6},{5,3},{6,0},{7,5},{8,10},{9,15},{10,... | collective-permute-start | bytes 786440 | tf_op jit(solution)/shard_map/ppermute | solution.py:409
  30.9 2.4 %collective-permute-done.7.refs_4_ = bf16[64,16,128]{2,1,0:T(8,128)(2,1)S(1)} collective-permute-done((bf16[64,16,128]{2,1,0:T(8,128)(2,1)S(1)}, bf16[64,16,128]{2,1,0:T(8,128)(2,1)S(1)}, u32[]{:S(2)}, u32[]{:S(2)}) %collective-permute-start.7) | collective-permute-done | bytes 262176 | tf_op jit(solution)/shard_map/ppermute | solution.py:409
  33.2 1.2 %outer.2.refs_0_ = bf16[8,128,128]{2,1,0:T(8,128)(2,1)S(1)} custom-call(bf16[3,32,16,128]{3,2,1,0:T(8,128)(2,1)S(1)} %get-tuple-element.33.refs_0_, bf16[3,32,16,128]{3,2,1,0:T(8,128)(2,1)S(1)} %get-tuple-element.38.refs_1_, bf16[3,32,256,128]{3,2,1,0:T(8,128)(2,1)S(1)} %get-tuple-element.39.refs_2_, ...), custom_call_target="tpu_custom_call" | custom-call | bytes 3145728 | tf_op jit(solution)/shard_map/outer/pallas_call | solution.py:417
  34.5 0.0 copy-start
  34.5 0.0 copy-start.1
  34.5 1.3 %collective-permute-start.12 = (bf16[8,128,128]{2,1,0:T(8,128)(2,1)S(1)}, bf16[8,128,128]{2,1,0:T(8,128)(2,1)S(1)}, u32[]{:S(2)}, u32[]{:S(2)}) collective-permute-start(bf16[8,128,128]{2,1,0:T(8,128)(2,1)S(1)} %outer.2.refs_0_), channel_id=1, source_target_pairs={{0,16},{8,24},{16,0},{24,8},{1,17},{9,25},{17,1},{25,9},{2,18},{10... | collective-permute-start | bytes 786440 | tf_op jit(solution)/shard_map/ppermute | solution.py:431
  35.8 0.0 collective-permute-start.10
  35.8 2.7 %collective-permute-done.6.refs_5_ = bf16[64,16,128]{2,1,0:T(8,128)(2,1)S(1)} collective-permute-done((bf16[64,16,128]{2,1,0:T(8,128)(2,1)S(1)}, bf16[64,16,128]{2,1,0:T(8,128)(2,1)S(1)}, u32[]{:S(2)}, u32[]{:S(2)}) %collective-permute-start.6) | collective-permute-done | bytes 262176 | tf_op jit(solution)/shard_map/ppermute | solution.py:409
  38.6 2.3 %outer.3.refs_2_ = bf16[8,128,128]{2,1,0:T(8,128)(2,1)S(1)} custom-call(bf16[3,32,16,128]{3,2,1,0:T(8,128)(2,1)S(1)} %get-tuple-element.33.refs_0_, bf16[3,32,16,128]{3,2,1,0:T(8,128)(2,1)S(1)} %get-tuple-element.38.refs_1_, bf16[3,32,256,128]{3,2,1,0:T(8,128)(2,1)S(1)} %get-tuple-element.39.refs_2_, ...), custom_call_target="tpu_custom_call" | custom-call | bytes 3145728 | tf_op jit(solution)/shard_map/outer/pallas_call | solution.py:417
  40.9 1.4 %collective-permute-start.9 = (bf16[8,128,128]{2,1,0:T(8,128)(2,1)S(1)}, bf16[8,128,128]{2,1,0:T(8,128)(2,1)S(1)}, u32[]{:S(2)}, u32[]{:S(2)}) collective-permute-start(bf16[8,128,128]{2,1,0:T(8,128)(2,1)S(1)} %outer.3.refs_2_), channel_id=1, source_target_pairs={{0,16},{8,24},{16,0},{24,8},{1,17},{9,25},{17,1},{25,9},{2,18},{10... | collective-permute-start | bytes 786440 | tf_op jit(solution)/shard_map/ppermute | solution.py:431
  42.3 0.0 collective-permute-start.8
  42.3 0.0 collective-permute-done.12.refs_0_
  42.4 0.5 %collective-permute-start.13 = (bf16[8,128,128]{2,1,0:T(8,128)(2,1)S(1)}, bf16[8,128,128]{2,1,0:T(8,128)(2,1)S(1)}, u32[]{:S(2)}, u32[]{:S(2)}) collective-permute-start(bf16[8,128,128]{2,1,0:T(8,128)(2,1)S(1)} %collective-permute-done.12.refs_0_), channel_id=1, source_target_pairs={{0,8},{8,0},{16,24},{24,16},{1,9},{9,1},{17,25},{25,17},{2,10},{10... | collective-permute-start | bytes 786440 | tf_op jit(solution)/shard_map/ppermute | solution.py:445
  42.9 0.0 collective-permute-done.10.refs_1_
  42.9 0.6 %lead.1 = (f32[4,128,256]{2,1,0:T(8,128)S(1)}, f32[4,128,256]{2,1,0:T(8,128)S(1)}) custom-call(bf16[2,128,512]{2,1,0:T(8,128)(2,1)S(1)} %get-tuple-element.30.table_ref, bf16[8,128,128]{2,1,0:T(8,128)(2,1)S(1)} %outer.2.refs_0_, bf16[8,128,128]{2,1,0:T(8,128)(2,1)S(1)} %collective-permute-done.10.refs_1_, bf16[8,128,128]{2,1,0:T(8,128)(2,1)S(1)} %outer.3.refs_2_), custom_call_target="tpu_custom_call" | custom-call | flops 536870912 | bytes 4194304 | tf_op jit(solution)/shard_map/lead/pallas_call | solution.py:434
  43.4 4.3 %collective-permute-done.9.refs_1_ = bf16[8,128,128]{2,1,0:T(8,128)(2,1)S(1)} collective-permute-done((bf16[8,128,128]{2,1,0:T(8,128)(2,1)S(1)}, bf16[8,128,128]{2,1,0:T(8,128)(2,1)S(1)}, u32[]{:S(2)}, u32[]{:S(2)}) %collective-permute-start.9) | collective-permute-done | bytes 262176 | tf_op jit(solution)/shard_map/ppermute | solution.py:431
  47.7 0.0 collective-permute-start.11
  47.7 0.0 collective-permute-done.13.refs_1_
  47.7 0.0 copy-done
  47.7 0.0 copy-done.1
  47.7 1.3 %back.2.refs_4_ = f32[128,16,128]{2,1,0:T(8,128)} custom-call(bf16[2,128,512]{2,1,0:T(8,128)(2,1)S(1)} %get-tuple-element.30.table_ref, f32[2048,128]{1,0:T(8,128)S(1)} %bitcast.12, f32[128,128]{1,0:T(8,128)S(1)} %bitcast.14, bf16[8,128,128]{2,1,0:T(8,128)(2,1)S(1)} %collective-permute-done.12.refs_0_, ...), custom_call_target="tpu_custom_call" | custom-call | flops 536870912 | bytes 4194304 | tf_op jit(solution)/shard_map/back/pallas_call | solution.py:457
  49.1 0.0 collective-permute-done.8.refs_0_
  49.1 0.2 collective-permute-done.11.refs_2_
  49.2 1.5 %back.3 = f32[128,16,128]{2,1,0:T(8,128)} custom-call(bf16[2,128,512]{2,1,0:T(8,128)(2,1)S(1)} %get-tuple-element.30.table_ref, f32[2048,128]{1,0:T(8,128)S(1)} %bitcast.13, f32[128,128]{1,0:T(8,128)S(1)} %bitcast.15, bf16[8,128,128]{2,1,0:T(8,128)(2,1)S(1)} %collective-permute-done.8.refs_0_, ...), custom_call_target="tpu_custom_call", output_to_operand_aliasing={{}: (7, {})} | custom-call | flops 536870912 | bytes 4194304 | tf_op jit(solution)/shard_map/back/pallas_call | solution.py:457
Async XLA Ops:
  1.9 3.8 %collective-permute-start = (s16[16,128,128]{2,1,0:T(8,128)(2,1)S(1)}, s16[16,128,128]{2,1,0:T(8,128)(2,1)S(1)}, u32[]{:S(2)}, u32[]{:S(2)}) collective-permute-start(s16[16,128,128]{2,1,0:T(8,128)(2,1)S(1)} %get-tuple-element.32.own_ref.refs_0_), channel_id=1, source_target_pairs={{0,8},{8,0},{16,24},{24,16},{1,9},{9,1},{17,25},{25,17},{2,10},{10... | collective-permute-start | bytes 1572872 | tf_op jit(solution)/shard_map/ppermute | solution.py:321
  2.4 9.5 %collective-permute-start.1 = (s16[8,128,128]{2,1,0:T(8,128)(2,1)S(1)}, s16[8,128,128]{2,1,0:T(8,128)(2,1)S(1)}, u32[]{:S(2)}, u32[]{:S(2)}) collective-permute-start(s16[8,128,128]{2,1,0:T(8,128)(2,1)S(1)} %get-tuple-element.34), channel_id=1, source_target_pairs={{0,16},{8,24},{16,0},{24,8},{1,17},{9,25},{17,1},{25,9},{2,18},{10... | collective-permute-start | bytes 786440 | tf_op jit(solution)/shard_map/ppermute | solution.py:371
  5.7 0.7 %copy-start.2 = (s32[64,1]{0,1:T(1,128)S(1)}, s32[64,1]{0,1:T(1,128)}, u32[]{:S(2)}) copy-start(s32[64,1]{0,1:T(1,128)} %param.10) | copy-start | bytes 772
  11.9 1.8 %collective-permute-start.2 = (s16[8,128,128]{2,1,0:T(8,128)(2,1)S(1)}, s16[8,128,128]{2,1,0:T(8,128)(2,1)S(1)}, u32[]{:S(2)}, u32[]{:S(2)}) collective-permute-start(s16[8,128,128]{2,1,0:T(8,128)(2,1)S(1)} %collective-permute-done.1.refs_2_), channel_id=1, source_target_pairs={{0,8},{8,0},{16,24},{24,16},{1,9},{9,1},{17,25},{25,17},{2,10},{10... | collective-permute-start | bytes 786440 | tf_op jit(solution)/shard_map/ppermute | solution.py:373
  11.9 8.7 %collective-permute-start.3 = (s16[8,128,128]{2,1,0:T(8,128)(2,1)S(1)}, s16[8,128,128]{2,1,0:T(8,128)(2,1)S(1)}, u32[]{:S(2)}, u32[]{:S(2)}) collective-permute-start(s16[8,128,128]{2,1,0:T(8,128)(2,1)S(1)} %get-tuple-element.42), channel_id=1, source_target_pairs={{0,16},{8,24},{16,0},{24,8},{1,17},{9,25},{17,1},{25,9},{2,18},{10... | collective-permute-start | bytes 786440 | tf_op jit(solution)/shard_map/ppermute | solution.py:358
  15.0 8.5 %collective-permute-start.5 = (bf16[64,16,128]{2,1,0:T(8,128)(2,1)S(1)}, bf16[64,16,128]{2,1,0:T(8,128)(2,1)S(1)}, u32[]{:S(2)}, u32[]{:S(2)}) collective-permute-start(bf16[64,16,128]{2,1,0:T(8,128)(2,1)S(1)} %forward.1.refs_4_), channel_id=1, source_target_pairs={{0,1},{1,0},{2,3},{3,2},{4,5},{5,4},{6,7},{7,6},{8,9},{9,8},{10,11... | collective-permute-start | bytes 786440 | tf_op jit(solution)/shard_map/ppermute | solution.py:395
  21.0 8.1 %collective-permute-start.4 = (bf16[64,16,128]{2,1,0:T(8,128)(2,1)S(1)}, bf16[64,16,128]{2,1,0:T(8,128)(2,1)S(1)}, u32[]{:S(2)}, u32[]{:S(2)}) collective-permute-start(bf16[64,16,128]{2,1,0:T(8,128)(2,1)S(1)} %finish.1.refs_5_), channel_id=1, source_target_pairs={{0,1},{1,0},{2,3},{3,2},{4,5},{5,4},{6,7},{7,6},{8,9},{9,8},{10,11... | collective-permute-start | bytes 786440 | tf_op jit(solution)/shard_map/ppermute | solution.py:395
  23.5 9.7 %collective-permute-start.7 = (bf16[64,16,128]{2,1,0:T(8,128)(2,1)S(1)}, bf16[64,16,128]{2,1,0:T(8,128)(2,1)S(1)}, u32[]{:S(2)}, u32[]{:S(2)}) collective-permute-start(bf16[64,16,128]{2,1,0:T(8,128)(2,1)S(1)} %collective-permute-done.5.refs_6_), channel_id=1, source_target_pairs={{0,2},{1,7},{2,4},{3,1},{4,6},{5,3},{6,0},{7,5},{8,10},{9,15},{10,... | collective-permute-start | bytes 786440 | tf_op jit(solution)/shard_map/ppermute | solution.py:409
  29.1 9.4 %collective-permute-start.6 = (bf16[64,16,128]{2,1,0:T(8,128)(2,1)S(1)}, bf16[64,16,128]{2,1,0:T(8,128)(2,1)S(1)}, u32[]{:S(2)}, u32[]{:S(2)}) collective-permute-start(bf16[64,16,128]{2,1,0:T(8,128)(2,1)S(1)} %collective-permute-done.4.refs_4_), channel_id=1, source_target_pairs={{0,2},{1,7},{2,4},{3,1},{4,6},{5,3},{6,0},{7,5},{8,10},{9,15},{10,... | collective-permute-start | bytes 786440 | tf_op jit(solution)/shard_map/ppermute | solution.py:409
  34.5 13.2 %copy-start = (f32[2,64,16,128]{3,2,1,0:T(8,128)S(1)}, f32[2,64,16,128]{3,2,1,0:T(8,128)}, u32[]{:S(2)}) copy-start(f32[2,64,16,128]{3,2,1,0:T(8,128)} %param.6) | copy-start | bytes 3145732
  34.5 13.2 %copy-start.1 = (f32[2,64,128]{2,1,0:T(8,128)S(1)}, f32[2,64,128]{2,1,0:T(8,128)}, u32[]{:S(2)}) copy-start(f32[2,64,128]{2,1,0:T(8,128)} %param.7) | copy-start | bytes 196612
  34.5 7.8 %collective-permute-start.12 = (bf16[8,128,128]{2,1,0:T(8,128)(2,1)S(1)}, bf16[8,128,128]{2,1,0:T(8,128)(2,1)S(1)}, u32[]{:S(2)}, u32[]{:S(2)}) collective-permute-start(bf16[8,128,128]{2,1,0:T(8,128)(2,1)S(1)} %outer.2.refs_0_), channel_id=1, source_target_pairs={{0,16},{8,24},{16,0},{24,8},{1,17},{9,25},{17,1},{25,9},{2,18},{10... | collective-permute-start | bytes 786440 | tf_op jit(solution)/shard_map/ppermute | solution.py:431
  35.8 7.0 %collective-permute-start.10 = (bf16[8,128,128]{2,1,0:T(8,128)(2,1)S(1)}, bf16[8,128,128]{2,1,0:T(8,128)(2,1)S(1)}, u32[]{:S(2)}, u32[]{:S(2)}) collective-permute-start(bf16[8,128,128]{2,1,0:T(8,128)(2,1)S(1)} %outer.2.refs_0_), channel_id=1, source_target_pairs={{0,8},{8,0},{16,24},{24,16},{1,9},{9,1},{17,25},{25,17},{2,10},{10... | collective-permute-start | bytes 786440 | tf_op jit(solution)/shard_map/ppermute | solution.py:430
  40.9 6.8 %collective-permute-start.9 = (bf16[8,128,128]{2,1,0:T(8,128)(2,1)S(1)}, bf16[8,128,128]{2,1,0:T(8,128)(2,1)S(1)}, u32[]{:S(2)}, u32[]{:S(2)}) collective-permute-start(bf16[8,128,128]{2,1,0:T(8,128)(2,1)S(1)} %outer.3.refs_2_), channel_id=1, source_target_pairs={{0,16},{8,24},{16,0},{24,8},{1,17},{9,25},{17,1},{25,9},{2,18},{10... | collective-permute-start | bytes 786440 | tf_op jit(solution)/shard_map/ppermute | solution.py:431
  42.3 6.7 %collective-permute-start.8 = (bf16[8,128,128]{2,1,0:T(8,128)(2,1)S(1)}, bf16[8,128,128]{2,1,0:T(8,128)(2,1)S(1)}, u32[]{:S(2)}, u32[]{:S(2)}) collective-permute-start(bf16[8,128,128]{2,1,0:T(8,128)(2,1)S(1)} %outer.3.refs_2_), channel_id=1, source_target_pairs={{0,8},{8,0},{16,24},{24,16},{1,9},{9,1},{17,25},{25,17},{2,10},{10... | collective-permute-start | bytes 786440 | tf_op jit(solution)/shard_map/ppermute | solution.py:430
  42.4 5.3 %collective-permute-start.13 = (bf16[8,128,128]{2,1,0:T(8,128)(2,1)S(1)}, bf16[8,128,128]{2,1,0:T(8,128)(2,1)S(1)}, u32[]{:S(2)}, u32[]{:S(2)}) collective-permute-start(bf16[8,128,128]{2,1,0:T(8,128)(2,1)S(1)} %collective-permute-done.12.refs_0_), channel_id=1, source_target_pairs={{0,8},{8,0},{16,24},{24,16},{1,9},{9,1},{17,25},{25,17},{2,10},{10... | collective-permute-start | bytes 786440 | tf_op jit(solution)/shard_map/ppermute | solution.py:445
  47.7 1.5 %collective-permute-start.11 = (bf16[8,128,128]{2,1,0:T(8,128)(2,1)S(1)}, bf16[8,128,128]{2,1,0:T(8,128)(2,1)S(1)}, u32[]{:S(2)}, u32[]{:S(2)}) collective-permute-start(bf16[8,128,128]{2,1,0:T(8,128)(2,1)S(1)} %collective-permute-done.9.refs_1_), channel_id=1, source_target_pairs={{0,8},{8,0},{16,24},{24,16},{1,9},{9,1},{17,25},{25,17},{2,10},{10... | collective-permute-start | bytes 786440 | tf_op jit(solution)/shard_map/ppermute | solution.py:445

commit v10 on v9

--- a/solution.py
+++ b/solution.py
@@ -40,7 +40,7 @@
 
 
 def encoded(x, bound):
-    root = jnp.sqrt(jnp.sqrt(jnp.abs(x) * (1.0 / bound)))
+    root = lax.rsqrt(lax.rsqrt(jnp.maximum(jnp.abs(x) * (1.0 / bound), 1e-30)))
     return jnp.round(jnp.where(x < 0, -root, root) * CODE_TOP).astype(jnp.int32).astype(jnp.int16)
 
 
@@ -94,10 +94,17 @@
 
 
 def split_kernel(first, sort, table_ref, own_ref, peer_ref, cols_ref, count_ref, tiles_ref,
-                 near_ref, far_ref, out_ref, live_ref, sem):
+                 lead_ref, near_ref, far_ref, out_ref, live_ref, sem):
     copy = sort(cols_ref, count_ref, tiles_ref, out_ref, live_ref, sem)
     per, rows, nodes = far_ref.shape
     odd = lax.rem(lax.broadcasted_iota(jnp.int32, (rows, 2 * nodes), 0), 2) == 1
+    for r in range(0, first, 2):
+        lead = jnp.zeros((rows, 2 * nodes), jnp.float32)
+        for j, ref in enumerate((own_ref, peer_ref)):
+            x = jnp.concatenate([decoded(ref[r]), decoded(ref[r + 1])], axis=1)
+            lead += exact_product(table_ref, slice(j * rows, (j + 1) * rows), x)
+        for s in range(2):
+            lead_ref[r + s] = lead[:, s * nodes : (s + 1) * nodes]
     for r in range(0, per, 2):
         near = jnp.zeros((rows, 2 * nodes), jnp.float32)
         far = jnp.zeros((rows, 2 * nodes), jnp.float32)
@@ -120,19 +127,20 @@
     write_modes(held, modes_ref)
 
 
-def forward_kernel(firsts, table_ref, *refs):
-    sources = len(firsts)
-    coded_refs, modes_ref, held = refs[:sources], refs[sources], refs[sources + 1]
+def forward_kernel(starts, table_ref, *refs):
+    coded_refs, modes_ref, held = refs[:-2], refs[-2], refs[-1]
+    if starts:
+        ready_ref, coded_refs = coded_refs[0], coded_refs[1:]
     rhs = modes_ref.shape[1] // 2
     rows, nodes = coded_refs[0].shape[1:]
     for r in range(0, rhs, 2):
         total = jnp.zeros((rows, 2 * nodes), jnp.float32)
-        for j in range(sources):
-            at = firsts[j] + r
-            x = jnp.concatenate([decoded(coded_refs[j][at]), decoded(coded_refs[j][at + 1])], axis=1)
+        for j, ref in enumerate(coded_refs, starts):
+            x = jnp.concatenate([decoded(ref[r]), decoded(ref[r + 1])], axis=1)
             total += exact_product(table_ref, slice(j * rows, (j + 1) * rows), x)
-        held[r * rows : (r + 1) * rows, :] = total[:, :nodes]
-        held[(r + 1) * rows : (r + 2) * rows, :] = total[:, nodes:]
+        for s in range(2):
+            part = total[:, s * nodes : (s + 1) * nodes]
+            held[(r + s) * rows : (r + s + 1) * rows, :] = part + ready_ref[r + s] if starts else part
     write_modes(held, modes_ref)
 
 
@@ -334,11 +342,11 @@
         )(*pattern, after(flat_tiles, wait_for))
 
     if paired:
-        near_part, far_part, head, live = pl.pallas_call(
+        lead_part, near_part, far_part, head, live = pl.pallas_call(
             functools.partial(split_kernel, per, functools.partial(begin_sort, 0)),
-            out_shape=[jax.ShapeDtypeStruct((per, rows, nodes), jnp.float32), chunk_shape] + sort_shapes,
+            out_shape=[jax.ShapeDtypeStruct((per, rows, nodes), jnp.float32)] * 2 + [chunk_shape] + sort_shapes,
             in_specs=[vmem] * 3 + [smem] * 2 + [hbm],
-            out_specs=[vmem] * 4,
+            out_specs=[vmem] * 5,
             scratch_shapes=[pltpu.SemaphoreType.DMA],
             cost_estimate=cost(3 * multiply, move),
             compiler_params=stage_params,
@@ -370,15 +378,14 @@
             if paired:
                 across = after(lax.ppermute(first, "az", ACROSS), far_part)
                 earlier = across
-                sources = [coded, peer, across, lax.ppermute(across, "az", PEER)]
-                firsts = (0,) * parts
+                starts, sources = 2, [lead_part, across, lax.ppermute(across, "az", PEER)]
             else:
                 every = lax.all_gather(coded[index * per : (index + 1) * per], "az")
-                sources, firsts = [every[j] for j in range(parts)], (0,) * parts
+                starts, sources = 0, [every[j] for j in range(parts)]
             own = pl.pallas_call(
-                functools.partial(forward_kernel, firsts),
+                functools.partial(forward_kernel, starts),
                 out_shape=modes_shape,
-                in_specs=[vmem] * (1 + parts),
+                in_specs=[vmem] * (1 + len(sources)),
                 out_specs=vmem,
                 scratch_shapes=[held_modes],
                 cost_estimate=cost(3 * multiply, move),

time: 51 us -> 50 us (0.980)
  Pallas kernels: 20.3 us -> 19.6 us
where the time goes in v10:
time: 50 us; the launch traced here: 49.7 us
  Pallas kernels  19.6 us (39%)
  starting transfers between devices  15.2 us (30%)
  waiting for transfers between devices  13.5 us (27%)
  local copies, waits for them, and re-layouts  1.35 us (3%)
    ppermute x2, waiting for transfers between devices, on_device(): far_in = [lax.ppermute(side, 'curve', onward) for side in side_in]  4.6 us
    ppermute x2, waiting for transfers between devices, on_device(): across = [lax.ppermute(near, 'az', ACROSS) for near in nears]  3.84 us
    pallas_call x2, Pallas kernels, on_device(): pl.pallas_call(functools.partial(outer_kernel, roles, SHARES), out_shape=...  3.56 us
    pallas_call x1, Pallas kernels, on_device(): pl.pallas_call(functools.partial(split_kernel, per, functools.partial(beg...  3.55 us
    pallas_call x1, Pallas kernels, sorting(): pl.pallas_call(functools.partial(sort_kernel, functools.partial(begin_sor...  3.54 us
    ppermute x2, starting transfers between devices, on_device(): side_in = [lax.ppermute(own, 'curve', sides) for own in owns]  3.45 us
    ppermute x2, starting transfers between devices, on_device(): far_in = [lax.ppermute(side, 'curve', onward) for side in side_in]  3.37 us
    ppermute x2, starting transfers between devices, on_device(): across = [lax.ppermute(near, 'az', ACROSS) for near in nears]  3 us
  transfers between devices with their start and end apart: 14, of which 8 were waited for; matrix products, arithmetic and copies ran while one was open for 1% of the time, Pallas kernels for 33%

profile of v10, /device:TPU:0, one launch (start us, length us, event | category | flops | bytes accessed | tf_op | source)
XLA Modules:
  0.0 49.7 jit_solution(2015132589546670808)
XLA Ops:
  0.0 1.6 %pack.1 = (s16[8,128,128]{2,1,0:T(8,128)(2,1)S(1)}, s16[16,128,128]{2,1,0:T(8,128)(2,1)S(1)}, bf16[2,128,512]{2,1,0:T(8,128)(2,1)S(1)}, bf16[2,128,512]{2,1,0:T(8,128)(2,1)S(1)}) custom-call(f32[128,16,128]{2,1,0:T(8,128)} %bitcast.11, bf16[4,2,2,128,512]{4,3,2,1,0:T(8,128)(2,1)} %constant.2.clone.tables_ref), custom_call_target="tpu_custom_call" | custom-call | bytes 4194304 | tf_op jit(solution)/shard_map/pack/pallas_call | solution.py:315
  1.6 0.5 %collective-permute-start = (s16[16,128,128]{2,1,0:T(8,128)(2,1)S(1)}, s16[16,128,128]{2,1,0:T(8,128)(2,1)S(1)}, u32[]{:S(2)}, u32[]{:S(2)}) collective-permute-start(s16[16,128,128]{2,1,0:T(8,128)(2,1)S(1)} %get-tuple-element.33.own_ref), channel_id=1, source_target_pairs={{0,8},{8,0},{16,24},{24,16},{1,9},{9,1},{17,25},{25,17},{2,10},{10... | collective-permute-start | bytes 1572872 | tf_op jit(solution)/shard_map/ppermute | solution.py:329
  2.1 2.6 %collective-permute-start.1 = (s16[8,128,128]{2,1,0:T(8,128)(2,1)S(1)}, s16[8,128,128]{2,1,0:T(8,128)(2,1)S(1)}, u32[]{:S(2)}, u32[]{:S(2)}) collective-permute-start(s16[8,128,128]{2,1,0:T(8,128)(2,1)S(1)} %get-tuple-element.36), channel_id=1, source_target_pairs={{0,16},{8,24},{16,0},{24,8},{1,17},{9,25},{17,1},{25,9},{2,18},{10... | collective-permute-start | bytes 786440 | tf_op jit(solution)/shard_map/ppermute | solution.py:379
  4.7 0.7 %copy.10 = s32[64,1,3]{0,2,1:T(4,128)S(1)} copy(s32[64,1,3]{0,1,2:T(1,128)} %param.9) | data formatting | bytes 1536
  5.3 0.0 collective-permute-done.peer_ref
  5.3 0.0 copy-start.2
  5.3 0.7 %copy-done.2 = s32[64,1]{0,1:T(1,128)S(1)} copy-done((s32[64,1]{0,1:T(1,128)S(1)}, s32[64,1]{0,1:T(1,128)}, u32[]{:S(2)}) %copy-start.2) | copy-done | bytes 280
  6.0 3.5 %split.1 = (f32[8,128,128]{2,1,0:T(8,128)S(1)}, f32[8,128,128]{2,1,0:T(8,128)S(1)}, s16[8,128,128]{2,1,0:T(8,128)(2,1)S(1)}, bf16[3,32,256,128]{3,2,1,0:T(8,128)(2,1)S(1)}, bf16[3,32,16,128]{3,2,1,0:T(8,128)(2,1)S(1)}) custom-call(bf16[2,128,512]{2,1,0:T(8,128)(2,1)S(1)} %get-tuple-element.32.table_ref, s16[16,128,128]{2,1,0:T(8,128)(2,1)S(1)} %get-tuple-element.33.own_ref, ...), custom_call_target="tpu_custom_call" | custom-call | flops 805306368 | bytes 4194304 | tf_op jit(solution)/shard_map/split/pallas_call | solution.py:345
  9.6 2.0 %collective-permute-done.1.refs_1_ = s16[8,128,128]{2,1,0:T(8,128)(2,1)S(1)} collective-permute-done((s16[8,128,128]{2,1,0:T(8,128)(2,1)S(1)}, s16[8,128,128]{2,1,0:T(8,128)(2,1)S(1)}, u32[]{:S(2)}, u32[]{:S(2)}) %collective-permute-start.1) | collective-permute-done | bytes 262176 | tf_op jit(solution)/shard_map/ppermute | solution.py:379
  11.6 0.0 collective-permute-start.2
  11.6 1.8 %collective-permute-start.3 = (s16[8,128,128]{2,1,0:T(8,128)(2,1)S(1)}, s16[8,128,128]{2,1,0:T(8,128)(2,1)S(1)}, u32[]{:S(2)}, u32[]{:S(2)}) collective-permute-start(s16[8,128,128]{2,1,0:T(8,128)(2,1)S(1)} %get-tuple-element.44), channel_id=1, source_target_pairs={{0,16},{8,24},{16,0},{24,8},{1,17},{9,25},{17,1},{25,9},{2,18},{10... | collective-permute-start | bytes 786440 | tf_op jit(solution)/shard_map/ppermute | solution.py:366
  13.3 0.0 collective-permute-done.2.refs_2_
  13.3 0.9 %forward.1.refs_4_ = bf16[64,16,128]{2,1,0:T(8,128)(2,1)S(1)} custom-call(bf16[2,128,512]{2,1,0:T(8,128)(2,1)S(1)} %get-tuple-element.32.table_ref, f32[8,128,128]{2,1,0:T(8,128)S(1)} %get-tuple-element.35.refs_0_, s16[8,128,128]{2,1,0:T(8,128)(2,1)S(1)} %collective-permute-done.1.refs_1_, s16[8,128,128]{2,1,0:T(8,128)(2,1)S(1)} %collective-permute-done.2.refs_2_), custom_call_target="tpu_custom_call" | custom-call | flops 805306368 | bytes 4194304 | tf_op jit(solution)/shard_map/forward/pallas_call | solution.py:385
  14.3 1.6 %collective-permute-start.5 = (bf16[64,16,128]{2,1,0:T(8,128)(2,1)S(1)}, bf16[64,16,128]{2,1,0:T(8,128)(2,1)S(1)}, u32[]{:S(2)}, u32[]{:S(2)}) collective-permute-start(bf16[64,16,128]{2,1,0:T(8,128)(2,1)S(1)} %forward.1.refs_4_), channel_id=1, source_target_pairs={{0,1},{1,0},{2,3},{3,2},{4,5},{5,4},{6,7},{7,6},{8,9},{9,8},{10,11... | collective-permute-start | bytes 786440 | tf_op jit(solution)/shard_map/ppermute | solution.py:402
  15.9 3.5 %sort.1 = (bf16[3,32,256,128]{3,2,1,0:T(8,128)(2,1)S(1)}, bf16[3,32,16,128]{3,2,1,0:T(8,128)(2,1)S(1)}) custom-call(s32[3,64]{1,0:T(4,128)S(1)} %bitcast.17, s32[64]{0:T(128)S(1)} %bitcast.19, bf16[192,256,128]{2,1,0:T(8,128)(2,1)} %bitcast.21), custom_call_target="tpu_custom_call" | custom-call | bytes 6291456 | tf_op jit(solution)/shard_map/sort/pallas_call | solution.py:333
  19.5 0.8 %collective-permute-done.3.far_ref = s16[8,128,128]{2,1,0:T(8,128)(2,1)S(1)} collective-permute-done((s16[8,128,128]{2,1,0:T(8,128)(2,1)S(1)}, s16[8,128,128]{2,1,0:T(8,128)(2,1)S(1)}, u32[]{:S(2)}, u32[]{:S(2)}) %collective-permute-start.3) | collective-permute-done | bytes 262176 | tf_op jit(solution)/shard_map/ppermute | solution.py:366
  20.3 0.4 finish.1.refs_5_
  20.7 1.8 %collective-permute-start.4 = (bf16[64,16,128]{2,1,0:T(8,128)(2,1)S(1)}, bf16[64,16,128]{2,1,0:T(8,128)(2,1)S(1)}, u32[]{:S(2)}, u32[]{:S(2)}) collective-permute-start(bf16[64,16,128]{2,1,0:T(8,128)(2,1)S(1)} %finish.1.refs_5_), channel_id=1, source_target_pairs={{0,1},{1,0},{2,3},{3,2},{4,5},{5,4},{6,7},{7,6},{8,9},{9,8},{10,11... | collective-permute-start | bytes 786440 | tf_op jit(solution)/shard_map/ppermute | solution.py:402
  22.6 0.2 collective-permute-done.5.refs_6_
  22.8 1.6 %collective-permute-start.7 = (bf16[64,16,128]{2,1,0:T(8,128)(2,1)S(1)}, bf16[64,16,128]{2,1,0:T(8,128)(2,1)S(1)}, u32[]{:S(2)}, u32[]{:S(2)}) collective-permute-start(bf16[64,16,128]{2,1,0:T(8,128)(2,1)S(1)} %collective-permute-done.5.refs_6_), channel_id=1, source_target_pairs={{0,2},{1,7},{2,4},{3,1},{4,6},{5,3},{6,0},{7,5},{8,10},{9,15},{10,... | collective-permute-start | bytes 786440 | tf_op jit(solution)/shard_map/ppermute | solution.py:416
  24.4 2.6 %inner.1 = (f32[1024,128]{1,0:T(8,128)S(1)}, f32[1024,128]{1,0:T(8,128)S(1)}) custom-call(bf16[3,32,16,128]{3,2,1,0:T(8,128)(2,1)S(1)} %get-tuple-element.34.refs_0_, bf16[3,32,16,128]{3,2,1,0:T(8,128)(2,1)S(1)} %get-tuple-element.40.refs_1_, bf16[3,32,256,128]{3,2,1,0:T(8,128)(2,1)S(1)} %get-tuple-element.41.refs_2_, ...), custom_call_target="tpu_custom_call" | custom-call | bytes 6291456 | tf_op jit(solution)/shard_map/inner/pallas_call | solution.py:405
  27.0 1.8 %collective-permute-done.4.refs_4_ = bf16[64,16,128]{2,1,0:T(8,128)(2,1)S(1)} collective-permute-done((bf16[64,16,128]{2,1,0:T(8,128)(2,1)S(1)}, bf16[64,16,128]{2,1,0:T(8,128)(2,1)S(1)}, u32[]{:S(2)}, u32[]{:S(2)}) %collective-permute-start.4) | collective-permute-done | bytes 262176 | tf_op jit(solution)/shard_map/ppermute | solution.py:402
  28.8 1.8 %collective-permute-start.6 = (bf16[64,16,128]{2,1,0:T(8,128)(2,1)S(1)}, bf16[64,16,128]{2,1,0:T(8,128)(2,1)S(1)}, u32[]{:S(2)}, u32[]{:S(2)}) collective-permute-start(bf16[64,16,128]{2,1,0:T(8,128)(2,1)S(1)} %collective-permute-done.4.refs_4_), channel_id=1, source_target_pairs={{0,2},{1,7},{2,4},{3,1},{4,6},{5,3},{6,0},{7,5},{8,10},{9,15},{10,... | collective-permute-start | bytes 786440 | tf_op jit(solution)/shard_map/ppermute | solution.py:416
  30.6 1.7 %collective-permute-done.7.refs_4_ = bf16[64,16,128]{2,1,0:T(8,128)(2,1)S(1)} collective-permute-done((bf16[64,16,128]{2,1,0:T(8,128)(2,1)S(1)}, bf16[64,16,128]{2,1,0:T(8,128)(2,1)S(1)}, u32[]{:S(2)}, u32[]{:S(2)}) %collective-permute-start.7) | collective-permute-done | bytes 262176 | tf_op jit(solution)/shard_map/ppermute | solution.py:416
  32.2 1.2 %outer.2.refs_0_ = bf16[8,128,128]{2,1,0:T(8,128)(2,1)S(1)} custom-call(bf16[3,32,16,128]{3,2,1,0:T(8,128)(2,1)S(1)} %get-tuple-element.34.refs_0_, bf16[3,32,16,128]{3,2,1,0:T(8,128)(2,1)S(1)} %get-tuple-element.40.refs_1_, bf16[3,32,256,128]{3,2,1,0:T(8,128)(2,1)S(1)} %get-tuple-element.41.refs_2_, ...), custom_call_target="tpu_custom_call" | custom-call | bytes 3145728 | tf_op jit(solution)/shard_map/outer/pallas_call | solution.py:424
  33.5 0.0 copy-start
  33.5 0.0 copy-start.1
  33.5 1.4 %collective-permute-start.12 = (bf16[8,128,128]{2,1,0:T(8,128)(2,1)S(1)}, bf16[8,128,128]{2,1,0:T(8,128)(2,1)S(1)}, u32[]{:S(2)}, u32[]{:S(2)}) collective-permute-start(bf16[8,128,128]{2,1,0:T(8,128)(2,1)S(1)} %outer.2.refs_0_), channel_id=1, source_target_pairs={{0,16},{8,24},{16,0},{24,8},{1,17},{9,25},{17,1},{25,9},{2,18},{10... | collective-permute-start | bytes 786440 | tf_op jit(solution)/shard_map/ppermute | solution.py:438
  34.9 0.0 collective-permute-start.10
  34.9 2.9 %collective-permute-done.6.refs_5_ = bf16[64,16,128]{2,1,0:T(8,128)(2,1)S(1)} collective-permute-done((bf16[64,16,128]{2,1,0:T(8,128)(2,1)S(1)}, bf16[64,16,128]{2,1,0:T(8,128)(2,1)S(1)}, u32[]{:S(2)}, u32[]{:S(2)}) %collective-permute-start.6) | collective-permute-done | bytes 262176 | tf_op jit(solution)/shard_map/ppermute | solution.py:416
  37.9 2.3 %outer.3.refs_2_ = bf16[8,128,128]{2,1,0:T(8,128)(2,1)S(1)} custom-call(bf16[3,32,16,128]{3,2,1,0:T(8,128)(2,1)S(1)} %get-tuple-element.34.refs_0_, bf16[3,32,16,128]{3,2,1,0:T(8,128)(2,1)S(1)} %get-tuple-element.40.refs_1_, bf16[3,32,256,128]{3,2,1,0:T(8,128)(2,1)S(1)} %get-tuple-element.41.refs_2_, ...), custom_call_target="tpu_custom_call" | custom-call | bytes 3145728 | tf_op jit(solution)/shard_map/outer/pallas_call | solution.py:424
  40.2 1.6 %collective-permute-start.9 = (bf16[8,128,128]{2,1,0:T(8,128)(2,1)S(1)}, bf16[8,128,128]{2,1,0:T(8,128)(2,1)S(1)}, u32[]{:S(2)}, u32[]{:S(2)}) collective-permute-start(bf16[8,128,128]{2,1,0:T(8,128)(2,1)S(1)} %outer.3.refs_2_), channel_id=1, source_target_pairs={{0,16},{8,24},{16,0},{24,8},{1,17},{9,25},{17,1},{25,9},{2,18},{10... | collective-permute-start | bytes 786440 | tf_op jit(solution)/shard_map/ppermute | solution.py:438
  41.8 0.0 collective-permute-start.8
  41.8 0.0 collective-permute-done.12.refs_0_
  41.8 0.5 %collective-permute-start.13 = (bf16[8,128,128]{2,1,0:T(8,128)(2,1)S(1)}, bf16[8,128,128]{2,1,0:T(8,128)(2,1)S(1)}, u32[]{:S(2)}, u32[]{:S(2)}) collective-permute-start(bf16[8,128,128]{2,1,0:T(8,128)(2,1)S(1)} %collective-permute-done.12.refs_0_), channel_id=1, source_target_pairs={{0,8},{8,0},{16,24},{24,16},{1,9},{9,1},{17,25},{25,17},{2,10},{10... | collective-permute-start | bytes 786440 | tf_op jit(solution)/shard_map/ppermute | solution.py:452
  42.3 0.0 collective-permute-done.10.refs_1_
  42.3 0.6 %lead.1 = (f32[4,128,256]{2,1,0:T(8,128)S(1)}, f32[4,128,256]{2,1,0:T(8,128)S(1)}) custom-call(bf16[2,128,512]{2,1,0:T(8,128)(2,1)S(1)} %get-tuple-element.31.table_ref, bf16[8,128,128]{2,1,0:T(8,128)(2,1)S(1)} %outer.2.refs_0_, bf16[8,128,128]{2,1,0:T(8,128)(2,1)S(1)} %collective-permute-done.10.refs_1_, bf16[8,128,128]{2,1,0:T(8,128)(2,1)S(1)} %outer.3.refs_2_), custom_call_target="tpu_custom_call" | custom-call | flops 536870912 | bytes 4194304 | tf_op jit(solution)/shard_map/lead/pallas_call | solution.py:441
  42.9 3.8 %collective-permute-done.9.refs_1_ = bf16[8,128,128]{2,1,0:T(8,128)(2,1)S(1)} collective-permute-done((bf16[8,128,128]{2,1,0:T(8,128)(2,1)S(1)}, bf16[8,128,128]{2,1,0:T(8,128)(2,1)S(1)}, u32[]{:S(2)}, u32[]{:S(2)}) %collective-permute-start.9) | collective-permute-done | bytes 262176 | tf_op jit(solution)/shard_map/ppermute | solution.py:438
  46.7 0.0 collective-permute-start.11
  46.7 0.0 collective-permute-done.13.refs_1_
  46.7 0.0 copy-done
  46.7 0.0 copy-done.1
  46.7 1.3 %back.2.refs_4_ = f32[128,16,128]{2,1,0:T(8,128)} custom-call(bf16[2,128,512]{2,1,0:T(8,128)(2,1)S(1)} %get-tuple-element.31.table_ref, f32[2048,128]{1,0:T(8,128)S(1)} %bitcast.12, f32[128,128]{1,0:T(8,128)S(1)} %bitcast.14, bf16[8,128,128]{2,1,0:T(8,128)(2,1)S(1)} %collective-permute-done.12.refs_0_, ...), custom_call_target="tpu_custom_call" | custom-call | flops 536870912 | bytes 4194304 | tf_op jit(solution)/shard_map/back/pallas_call | solution.py:464
  48.1 0.0 collective-permute-done.8.refs_0_
  48.1 0.2 collective-permute-done.11.refs_2_
  48.2 1.5 %back.3 = f32[128,16,128]{2,1,0:T(8,128)} custom-call(bf16[2,128,512]{2,1,0:T(8,128)(2,1)S(1)} %get-tuple-element.31.table_ref, f32[2048,128]{1,0:T(8,128)S(1)} %bitcast.13, f32[128,128]{1,0:T(8,128)S(1)} %bitcast.15, bf16[8,128,128]{2,1,0:T(8,128)(2,1)S(1)} %collective-permute-done.8.refs_0_, ...), custom_call_target="tpu_custom_call", output_to_operand_aliasing={{}: (7, {})} | custom-call | flops 536870912 | bytes 4194304 | tf_op jit(solution)/shard_map/back/pallas_call | solution.py:464
Async XLA Ops:
  1.6 3.8 %collective-permute-start = (s16[16,128,128]{2,1,0:T(8,128)(2,1)S(1)}, s16[16,128,128]{2,1,0:T(8,128)(2,1)S(1)}, u32[]{:S(2)}, u32[]{:S(2)}) collective-permute-start(s16[16,128,128]{2,1,0:T(8,128)(2,1)S(1)} %get-tuple-element.33.own_ref), channel_id=1, source_target_pairs={{0,8},{8,0},{16,24},{24,16},{1,9},{9,1},{17,25},{25,17},{2,10},{10... | collective-permute-start | bytes 1572872 | tf_op jit(solution)/shard_map/ppermute | solution.py:329
  2.1 9.5 %collective-permute-start.1 = (s16[8,128,128]{2,1,0:T(8,128)(2,1)S(1)}, s16[8,128,128]{2,1,0:T(8,128)(2,1)S(1)}, u32[]{:S(2)}, u32[]{:S(2)}) collective-permute-start(s16[8,128,128]{2,1,0:T(8,128)(2,1)S(1)} %get-tuple-element.36), channel_id=1, source_target_pairs={{0,16},{8,24},{16,0},{24,8},{1,17},{9,25},{17,1},{25,9},{2,18},{10... | collective-permute-start | bytes 786440 | tf_op jit(solution)/shard_map/ppermute | solution.py:379
  5.3 0.7 %copy-start.2 = (s32[64,1]{0,1:T(1,128)S(1)}, s32[64,1]{0,1:T(1,128)}, u32[]{:S(2)}) copy-start(s32[64,1]{0,1:T(1,128)} %param.10) | copy-start | bytes 772
  11.6 1.8 %collective-permute-start.2 = (s16[8,128,128]{2,1,0:T(8,128)(2,1)S(1)}, s16[8,128,128]{2,1,0:T(8,128)(2,1)S(1)}, u32[]{:S(2)}, u32[]{:S(2)}) collective-permute-start(s16[8,128,128]{2,1,0:T(8,128)(2,1)S(1)} %collective-permute-done.1.refs_1_), channel_id=1, source_target_pairs={{0,8},{8,0},{16,24},{24,16},{1,9},{9,1},{17,25},{25,17},{2,10},{10... | collective-permute-start | bytes 786440 | tf_op jit(solution)/shard_map/ppermute | solution.py:381
  11.6 8.7 %collective-permute-start.3 = (s16[8,128,128]{2,1,0:T(8,128)(2,1)S(1)}, s16[8,128,128]{2,1,0:T(8,128)(2,1)S(1)}, u32[]{:S(2)}, u32[]{:S(2)}) collective-permute-start(s16[8,128,128]{2,1,0:T(8,128)(2,1)S(1)} %get-tuple-element.44), channel_id=1, source_target_pairs={{0,16},{8,24},{16,0},{24,8},{1,17},{9,25},{17,1},{25,9},{2,18},{10... | collective-permute-start | bytes 786440 | tf_op jit(solution)/shard_map/ppermute | solution.py:366
  14.3 8.5 %collective-permute-start.5 = (bf16[64,16,128]{2,1,0:T(8,128)(2,1)S(1)}, bf16[64,16,128]{2,1,0:T(8,128)(2,1)S(1)}, u32[]{:S(2)}, u32[]{:S(2)}) collective-permute-start(bf16[64,16,128]{2,1,0:T(8,128)(2,1)S(1)} %forward.1.refs_4_), channel_id=1, source_target_pairs={{0,1},{1,0},{2,3},{3,2},{4,5},{5,4},{6,7},{7,6},{8,9},{9,8},{10,11... | collective-permute-start | bytes 786440 | tf_op jit(solution)/shard_map/ppermute | solution.py:402
  20.7 8.0 %collective-permute-start.4 = (bf16[64,16,128]{2,1,0:T(8,128)(2,1)S(1)}, bf16[64,16,128]{2,1,0:T(8,128)(2,1)S(1)}, u32[]{:S(2)}, u32[]{:S(2)}) collective-permute-start(bf16[64,16,128]{2,1,0:T(8,128)(2,1)S(1)} %finish.1.refs_5_), channel_id=1, source_target_pairs={{0,1},{1,0},{2,3},{3,2},{4,5},{5,4},{6,7},{7,6},{8,9},{9,8},{10,11... | collective-permute-start | bytes 786440 | tf_op jit(solution)/shard_map/ppermute | solution.py:402
  22.8 9.4 %collective-permute-start.7 = (bf16[64,16,128]{2,1,0:T(8,128)(2,1)S(1)}, bf16[64,16,128]{2,1,0:T(8,128)(2,1)S(1)}, u32[]{:S(2)}, u32[]{:S(2)}) collective-permute-start(bf16[64,16,128]{2,1,0:T(8,128)(2,1)S(1)} %collective-permute-done.5.refs_6_), channel_id=1, source_target_pairs={{0,2},{1,7},{2,4},{3,1},{4,6},{5,3},{6,0},{7,5},{8,10},{9,15},{10,... | collective-permute-start | bytes 786440 | tf_op jit(solution)/shard_map/ppermute | solution.py:416
  28.8 9.1 %collective-permute-start.6 = (bf16[64,16,128]{2,1,0:T(8,128)(2,1)S(1)}, bf16[64,16,128]{2,1,0:T(8,128)(2,1)S(1)}, u32[]{:S(2)}, u32[]{:S(2)}) collective-permute-start(bf16[64,16,128]{2,1,0:T(8,128)(2,1)S(1)} %collective-permute-done.4.refs_4_), channel_id=1, source_target_pairs={{0,2},{1,7},{2,4},{3,1},{4,6},{5,3},{6,0},{7,5},{8,10},{9,15},{10,... | collective-permute-start | bytes 786440 | tf_op jit(solution)/shard_map/ppermute | solution.py:416
  33.5 13.2 %copy-start = (f32[2,64,16,128]{3,2,1,0:T(8,128)S(1)}, f32[2,64,16,128]{3,2,1,0:T(8,128)}, u32[]{:S(2)}) copy-start(f32[2,64,16,128]{3,2,1,0:T(8,128)} %param.6) | copy-start | bytes 3145732
  33.5 13.2 %copy-start.1 = (f32[2,64,128]{2,1,0:T(8,128)S(1)}, f32[2,64,128]{2,1,0:T(8,128)}, u32[]{:S(2)}) copy-start(f32[2,64,128]{2,1,0:T(8,128)} %param.7) | copy-start | bytes 196612
  33.5 8.3 %collective-permute-start.12 = (bf16[8,128,128]{2,1,0:T(8,128)(2,1)S(1)}, bf16[8,128,128]{2,1,0:T(8,128)(2,1)S(1)}, u32[]{:S(2)}, u32[]{:S(2)}) collective-permute-start(bf16[8,128,128]{2,1,0:T(8,128)(2,1)S(1)} %outer.2.refs_0_), channel_id=1, source_target_pairs={{0,16},{8,24},{16,0},{24,8},{1,17},{9,25},{17,1},{25,9},{2,18},{10... | collective-permute-start | bytes 786440 | tf_op jit(solution)/shard_map/ppermute | solution.py:438
  34.9 7.3 %collective-permute-start.10 = (bf16[8,128,128]{2,1,0:T(8,128)(2,1)S(1)}, bf16[8,128,128]{2,1,0:T(8,128)(2,1)S(1)}, u32[]{:S(2)}, u32[]{:S(2)}) collective-permute-start(bf16[8,128,128]{2,1,0:T(8,128)(2,1)S(1)} %outer.2.refs_0_), channel_id=1, source_target_pairs={{0,8},{8,0},{16,24},{24,16},{1,9},{9,1},{17,25},{25,17},{2,10},{10... | collective-permute-start | bytes 786440 | tf_op jit(solution)/shard_map/ppermute | solution.py:437
  40.2 6.5 %collective-permute-start.9 = (bf16[8,128,128]{2,1,0:T(8,128)(2,1)S(1)}, bf16[8,128,128]{2,1,0:T(8,128)(2,1)S(1)}, u32[]{:S(2)}, u32[]{:S(2)}) collective-permute-start(bf16[8,128,128]{2,1,0:T(8,128)(2,1)S(1)} %outer.3.refs_2_), channel_id=1, source_target_pairs={{0,16},{8,24},{16,0},{24,8},{1,17},{9,25},{17,1},{25,9},{2,18},{10... | collective-permute-start | bytes 786440 | tf_op jit(solution)/shard_map/ppermute | solution.py:438
  41.8 6.3 %collective-permute-start.8 = (bf16[8,128,128]{2,1,0:T(8,128)(2,1)S(1)}, bf16[8,128,128]{2,1,0:T(8,128)(2,1)S(1)}, u32[]{:S(2)}, u32[]{:S(2)}) collective-permute-start(bf16[8,128,128]{2,1,0:T(8,128)(2,1)S(1)} %outer.3.refs_2_), channel_id=1, source_target_pairs={{0,8},{8,0},{16,24},{24,16},{1,9},{9,1},{17,25},{25,17},{2,10},{10... | collective-permute-start | bytes 786440 | tf_op jit(solution)/shard_map/ppermute | solution.py:437
  41.8 4.9 %collective-permute-start.13 = (bf16[8,128,128]{2,1,0:T(8,128)(2,1)S(1)}, bf16[8,128,128]{2,1,0:T(8,128)(2,1)S(1)}, u32[]{:S(2)}, u32[]{:S(2)}) collective-permute-start(bf16[8,128,128]{2,1,0:T(8,128)(2,1)S(1)} %collective-permute-done.12.refs_0_), channel_id=1, source_target_pairs={{0,8},{8,0},{16,24},{24,16},{1,9},{9,1},{17,25},{25,17},{2,10},{10... | collective-permute-start | bytes 786440 | tf_op jit(solution)/shard_map/ppermute | solution.py:452
  46.7 1.5 %collective-permute-start.11 = (bf16[8,128,128]{2,1,0:T(8,128)(2,1)S(1)}, bf16[8,128,128]{2,1,0:T(8,128)(2,1)S(1)}, u32[]{:S(2)}, u32[]{:S(2)}) collective-permute-start(bf16[8,128,128]{2,1,0:T(8,128)(2,1)S(1)} %collective-permute-done.9.refs_1_), channel_id=1, source_target_pairs={{0,8},{8,0},{16,24},{24,16},{1,9},{9,1},{17,25},{25,17},{2,10},{10... | collective-permute-start | bytes 786440 | tf_op jit(solution)/shard_map/ppermute | solution.py:452

commit v11 on v10

--- a/solution.py
+++ b/solution.py
@@ -15,7 +15,7 @@
 CODE_TOP = 32767.0
 VMEM_LIMIT = 24 * 1024 * 1024
 STAGE_VMEM_LIMIT = 42 * 1024 * 1024
-PACK_VMEM_LIMIT = 52 * 1024 * 1024
+PACK_VMEM_LIMIT = 53 * 1024 * 1024
 
 
 def dft_tables(parts, local, order, inverse):
@@ -49,7 +49,7 @@
     return (t * jnp.abs(t)) * (t * t)
 
 
-def pack_kernel(chunks, fields_ref, tables_ref, first_ref, all_ref, forward_out, back_out, held, sems):
+def pack_kernel(chunks, fields_ref, first_ref, all_ref, held, sems):
     rows, rhs, nodes = fields_ref.shape
     per = rhs // chunks
     copies = [
@@ -58,11 +58,7 @@
         )
         for index in range(chunks)
     ]
-    tables = [
-        pltpu.make_async_copy(tables_ref.at[lax.axis_index("az"), way], out, sems.at[chunks + way])
-        for way, out in enumerate((forward_out, back_out))
-    ]
-    for copy in copies + tables:
+    for copy in copies:
         copy.start()
     for index in range(chunks):
         copies[index].wait()
@@ -71,8 +67,21 @@
             all_ref[index * per + r] = code
             if index == 0:
                 first_ref[r] = code
-    for table in tables:
-        table.wait()
+
+
+def begin_tables(tables_ref, forward_out, back_out, sems):
+    copies = [
+        pltpu.make_async_copy(tables_ref.at[lax.axis_index("az"), way], out, sems.at[way])
+        for way, out in enumerate((forward_out, back_out))
+    ]
+    for copy in copies:
+        copy.start()
+    return copies
+
+
+def table_kernel(*refs):
+    for copy in begin_tables(*refs):
+        copy.wait()
 
 
 def exact_product(table_ref, cols, x):
@@ -93,9 +102,12 @@
         modes_ref[k] = jnp.concatenate([real, imag], axis=0).astype(jnp.bfloat16)
 
 
-def split_kernel(first, sort, table_ref, own_ref, peer_ref, cols_ref, count_ref, tiles_ref,
-                 lead_ref, near_ref, far_ref, out_ref, live_ref, sem):
+def split_kernel(first, sort, own_ref, peer_ref, cols_ref, count_ref, tiles_ref, tables_ref,
+                 table_ref, back_ref, lead_ref, near_ref, far_ref, out_ref, live_ref, sem, table_sems):
+    tables = begin_tables(tables_ref, table_ref, back_ref, table_sems)
     copy = sort(cols_ref, count_ref, tiles_ref, out_ref, live_ref, sem)
+    for table in tables:
+        table.wait()
     per, rows, nodes = far_ref.shape
     odd = lax.rem(lax.broadcasted_iota(jnp.int32, (rows, 2 * nodes), 0), 2) == 1
     for r in range(0, first, 2):
@@ -312,19 +324,19 @@
     multiply = 4 * rows * rows * parts * per * nodes
     chunk_shape = jax.ShapeDtypeStruct((per, rows, nodes), jnp.int16)
 
-    first, coded, forward_table, back_table = pl.pallas_call(
+    first, coded = pl.pallas_call(
         functools.partial(pack_kernel, CHUNKS),
-        out_shape=[chunk_shape, jax.ShapeDtypeStruct((rhs, rows, nodes), jnp.int16), table_shape, table_shape],
-        in_specs=[hbm, hbm],
-        out_specs=[vmem] * 4,
+        out_shape=[chunk_shape, jax.ShapeDtypeStruct((rhs, rows, nodes), jnp.int16)],
+        in_specs=[hbm],
+        out_specs=[vmem] * 2,
         scratch_shapes=[
             pltpu.VMEM((CHUNKS, rows * per, nodes), jnp.float32),
-            pltpu.SemaphoreType.DMA((CHUNKS + 2,)),
+            pltpu.SemaphoreType.DMA((CHUNKS,)),
         ],
         cost_estimate=cost(0, move),
         compiler_params=pack_params,
         name="pack",
-    )(cut_fields, tables)
+    )(cut_fields)
 
     peer = lax.ppermute(coded, "az", PEER) if paired else None
     pattern = (tile_cols[:, 0, :].T, tile_count.reshape(local))
@@ -342,18 +354,30 @@
         )(*pattern, after(flat_tiles, wait_for))
 
     if paired:
-        lead_part, near_part, far_part, head, live = pl.pallas_call(
+        forward_table, back_table, lead_part, near_part, far_part, head, live = pl.pallas_call(
             functools.partial(split_kernel, per, functools.partial(begin_sort, 0)),
-            out_shape=[jax.ShapeDtypeStruct((per, rows, nodes), jnp.float32)] * 2 + [chunk_shape] + sort_shapes,
-            in_specs=[vmem] * 3 + [smem] * 2 + [hbm],
-            out_specs=[vmem] * 5,
-            scratch_shapes=[pltpu.SemaphoreType.DMA],
+            out_shape=[table_shape] * 2
+            + [jax.ShapeDtypeStruct((per, rows, nodes), jnp.float32)] * 2
+            + [chunk_shape]
+            + sort_shapes,
+            in_specs=[vmem] * 2 + [smem] * 2 + [hbm] * 2,
+            out_specs=[vmem] * 7,
+            scratch_shapes=[pltpu.SemaphoreType.DMA, pltpu.SemaphoreType.DMA((2,))],
             cost_estimate=cost(3 * multiply, move),
             compiler_params=stage_params,
             name="split",
-        )(forward_table, coded, peer, *pattern, flat_tiles)
+        )(coded, peer, *pattern, flat_tiles, tables)
     else:
         head, live = sorting(0, coded)
+        forward_table, back_table = pl.pallas_call(
+            table_kernel,
+            out_shape=[table_shape] * 2,
+            in_specs=[hbm],
+            out_specs=[vmem] * 2,
+            scratch_shapes=[pltpu.SemaphoreType.DMA((2,))],
+            compiler_params=params,
+            name="table",
+        )(tables)
     tiles, lives = [head], [live]
 
     sides = [(i, i ^ 1) for i in range(ring)]

time: 50 us -> 50 us (level)
  waiting for transfers between devices: 13.5 us -> 11.8 us
  local copies, waits for them, and re-layouts: 1.35 us -> 2.94 us
    ppermute x1, waiting for transfers between devices: 2 us -> 0.35 us  [on_device(): across = after(lax.ppermute(first, 'az', ACROSS), far_part)]
    unnamed x7 -> x11, local copies, waits for them, and re-layouts: 1.35 us -> 2.94 us
where the time goes in v11:
time: 50 us; the launch traced here: 49.7 us
  Pallas kernels  19.6 us (39%)
  starting transfers between devices  15.2 us (30%)
  waiting for transfers between devices  11.8 us (24%)
  local copies, waits for them, and re-layouts  2.94 us (6%)
    ppermute x2, waiting for transfers between devices, on_device(): far_in = [lax.ppermute(side, 'curve', onward) for side in side_in]  4.6 us
    ppermute x2, waiting for transfers between devices, on_device(): across = [lax.ppermute(near, 'az', ACROSS) for near in nears]  3.84 us
    pallas_call x1, Pallas kernels, on_device(): pl.pallas_call(functools.partial(split_kernel, per, functools.partial(beg...  3.61 us
    pallas_call x2, Pallas kernels, on_device(): pl.pallas_call(functools.partial(outer_kernel, roles, SHARES), out_shape=...  3.58 us
    pallas_call x1, Pallas kernels, sorting(): pl.pallas_call(functools.partial(sort_kernel, functools.partial(begin_sor...  3.54 us
    ppermute x2, starting transfers between devices, on_device(): side_in = [lax.ppermute(own, 'curve', sides) for own in owns]  3.46 us
    ppermute x2, starting transfers between devices, on_device(): far_in = [lax.ppermute(side, 'curve', onward) for side in side_in]  3.37 us
    ppermute x2, starting transfers between devices, on_device(): across = [lax.ppermute(near, 'az', ACROSS) for near in nears]  3 us
  transfers between devices with their start and end apart: 14, of which 8 were waited for; matrix products, arithmetic and copies ran while one was open for 1% of the time, Pallas kernels for 33%

profile of v11, /device:TPU:0, one launch (start us, length us, event | category | flops | bytes accessed | tf_op | source)
XLA Modules:
  0.0 49.7 jit_solution(1723282101046085651)
XLA Ops:
  0.0 1.6 %pack.1 = (s16[8,128,128]{2,1,0:T(8,128)(2,1)S(1)}, s16[16,128,128]{2,1,0:T(8,128)(2,1)S(1)}) custom-call(f32[128,16,128]{2,1,0:T(8,128)} %bitcast.11), custom_call_target="tpu_custom_call" | custom-call | bytes 4194304 | tf_op jit(solution)/shard_map/pack/pallas_call | solution.py:327
  1.6 0.5 %collective-permute-start = (s16[16,128,128]{2,1,0:T(8,128)(2,1)S(1)}, s16[16,128,128]{2,1,0:T(8,128)(2,1)S(1)}, u32[]{:S(2)}, u32[]{:S(2)}) collective-permute-start(s16[16,128,128]{2,1,0:T(8,128)(2,1)S(1)} %get-tuple-element.31.own_ref), channel_id=1, source_target_pairs={{0,8},{8,0},{16,24},{24,16},{1,9},{9,1},{17,25},{25,17},{2,10},{10... | collective-permute-start | bytes 1572872 | tf_op jit(solution)/shard_map/ppermute | solution.py:341
  2.1 2.6 %collective-permute-start.1 = (s16[8,128,128]{2,1,0:T(8,128)(2,1)S(1)}, s16[8,128,128]{2,1,0:T(8,128)(2,1)S(1)}, u32[]{:S(2)}, u32[]{:S(2)}) collective-permute-start(s16[8,128,128]{2,1,0:T(8,128)(2,1)S(1)} %get-tuple-element.36), channel_id=1, source_target_pairs={{0,16},{8,24},{16,0},{24,8},{1,17},{9,25},{17,1},{25,9},{2,18},{10... | collective-permute-start | bytes 786440 | tf_op jit(solution)/shard_map/ppermute | solution.py:403
  4.6 0.7 %copy.10 = s32[64,1,3]{0,2,1:T(4,128)S(1)} copy(s32[64,1,3]{0,1,2:T(1,128)} %param.9) | data formatting | bytes 1536
  5.3 0.0 collective-permute-done.peer_ref
  5.3 0.0 copy-start.1
  5.3 1.6 %copy-done.1 = bf16[4,2,2,128,512]{4,3,2,1,0:T(8,128)(2,1)S(1)} copy-done((bf16[4,2,2,128,512]{4,3,2,1,0:T(8,128)(2,1)S(1)}, bf16[4,2,2,128,512]{4,3,2,1,0:T(8,128)(2,1)}, u32[]{:S(2)}) %copy-start.1) | copy-done | bytes 2097176
  6.9 0.0 copy-start.3
  6.9 0.7 %copy-done.3 = s32[64,1]{0,1:T(1,128)S(1)} copy-done((s32[64,1]{0,1:T(1,128)S(1)}, s32[64,1]{0,1:T(1,128)}, u32[]{:S(2)}) %copy-start.3) | copy-done | bytes 280
  7.6 0.0 copy-start.4
  7.6 3.6 %split.1 = (bf16[2,128,512]{2,1,0:T(8,128)(2,1)S(1)}, bf16[2,128,512]{2,1,0:T(8,128)(2,1)S(1)}, f32[8,128,128]{2,1,0:T(8,128)S(1)}, f32[8,128,128]{2,1,0:T(8,128...) custom-call(s16[16,128,128]{2,1,0:T(8,128)(2,1)S(1)} %get-tuple-elem, ...), custom_call_target="tpu_custom_call" | custom-call | flops 805306368 | bytes 4194304 | tf_op jit(solution)/shard_map/split/pallas_call | solution.py:357
  11.2 0.3 collective-permute-done.1.refs_1_
  11.5 0.0 collective-permute-start.2
  11.5 1.8 %collective-permute-start.3 = (s16[8,128,128]{2,1,0:T(8,128)(2,1)S(1)}, s16[8,128,128]{2,1,0:T(8,128)(2,1)S(1)}, u32[]{:S(2)}, u32[]{:S(2)}) collective-permute-start(s16[8,128,128]{2,1,0:T(8,128)(2,1)S(1)} %get-tuple-element.44), channel_id=1, source_target_pairs={{0,16},{8,24},{16,0},{24,8},{1,17},{9,25},{17,1},{25,9},{2,18},{10... | collective-permute-start | bytes 786440 | tf_op jit(solution)/shard_map/ppermute | solution.py:390
  13.3 0.0 collective-permute-done.2.refs_2_
  13.3 0.9 %forward.1.refs_4_ = bf16[64,16,128]{2,1,0:T(8,128)(2,1)S(1)} custom-call(bf16[2,128,512]{2,1,0:T(8,128)(2,1)S(1)} %get-tuple-element.34.table_ref, f32[8,128,128]{2,1,0:T(8,128)S(1)} %get-tuple-element.35.refs_0_, s16[8,128,128]{2,1,0:T(8,128)(2,1)S(1)} %collective-permute-done.1.refs_1_, s16[8,128,128]{2,1,0:T(8,128)(2,1)S(1)} %collective-permute-done.2.refs_2_), custom_call_target="tpu_custom_call" | custom-call | flops 805306368 | bytes 4194304 | tf_op jit(solution)/shard_map/forward/pallas_call | solution.py:409
  14.2 1.6 %collective-permute-start.5 = (bf16[64,16,128]{2,1,0:T(8,128)(2,1)S(1)}, bf16[64,16,128]{2,1,0:T(8,128)(2,1)S(1)}, u32[]{:S(2)}, u32[]{:S(2)}) collective-permute-start(bf16[64,16,128]{2,1,0:T(8,128)(2,1)S(1)} %forward.1.refs_4_), channel_id=1, source_target_pairs={{0,1},{1,0},{2,3},{3,2},{4,5},{5,4},{6,7},{7,6},{8,9},{9,8},{10,11... | collective-permute-start | bytes 786440 | tf_op jit(solution)/shard_map/ppermute | solution.py:426
  15.9 0.0 copy-done.4
  15.9 3.5 %sort.1 = (bf16[3,32,256,128]{3,2,1,0:T(8,128)(2,1)S(1)}, bf16[3,32,16,128]{3,2,1,0:T(8,128)(2,1)S(1)}) custom-call(s32[3,64]{1,0:T(4,128)S(1)} %bitcast.17, s32[64]{0:T(128)S(1)} %bitcast.19, bf16[192,256,128]{2,1,0:T(8,128)(2,1)} %bitcast.21), custom_call_target="tpu_custom_call" | custom-call | bytes 6291456 | tf_op jit(solution)/shard_map/sort/pallas_call | solution.py:345
  19.4 0.8 %collective-permute-done.3.far_ref = s16[8,128,128]{2,1,0:T(8,128)(2,1)S(1)} collective-permute-done((s16[8,128,128]{2,1,0:T(8,128)(2,1)S(1)}, s16[8,128,128]{2,1,0:T(8,128)(2,1)S(1)}, u32[]{:S(2)}, u32[]{:S(2)}) %collective-permute-start.3) | collective-permute-done | bytes 262176 | tf_op jit(solution)/shard_map/ppermute | solution.py:390
  20.3 0.4 finish.1.refs_5_
  20.7 1.8 %collective-permute-start.4 = (bf16[64,16,128]{2,1,0:T(8,128)(2,1)S(1)}, bf16[64,16,128]{2,1,0:T(8,128)(2,1)S(1)}, u32[]{:S(2)}, u32[]{:S(2)}) collective-permute-start(bf16[64,16,128]{2,1,0:T(8,128)(2,1)S(1)} %finish.1.refs_5_), channel_id=1, source_target_pairs={{0,1},{1,0},{2,3},{3,2},{4,5},{5,4},{6,7},{7,6},{8,9},{9,8},{10,11... | collective-permute-start | bytes 786440 | tf_op jit(solution)/shard_map/ppermute | solution.py:426
  22.5 0.2 collective-permute-done.5.refs_6_
  22.8 1.6 %collective-permute-start.7 = (bf16[64,16,128]{2,1,0:T(8,128)(2,1)S(1)}, bf16[64,16,128]{2,1,0:T(8,128)(2,1)S(1)}, u32[]{:S(2)}, u32[]{:S(2)}) collective-permute-start(bf16[64,16,128]{2,1,0:T(8,128)(2,1)S(1)} %collective-permute-done.5.refs_6_), channel_id=1, source_target_pairs={{0,2},{1,7},{2,4},{3,1},{4,6},{5,3},{6,0},{7,5},{8,10},{9,15},{10,... | collective-permute-start | bytes 786440 | tf_op jit(solution)/shard_map/ppermute | solution.py:440
  24.3 2.6 %inner.1 = (f32[1024,128]{1,0:T(8,128)S(1)}, f32[1024,128]{1,0:T(8,128)S(1)}) custom-call(bf16[3,32,16,128]{3,2,1,0:T(8,128)(2,1)S(1)} %get-tuple-element.33.refs_0_, bf16[3,32,16,128]{3,2,1,0:T(8,128)(2,1)S(1)} %get-tuple-element.40.refs_1_, bf16[3,32,256,128]{3,2,1,0:T(8,128)(2,1)S(1)} %get-tuple-element.41.refs_2_, ...), custom_call_target="tpu_custom_call" | custom-call | bytes 6291456 | tf_op jit(solution)/shard_map/inner/pallas_call | solution.py:429
  26.9 1.8 %collective-permute-done.4.refs_4_ = bf16[64,16,128]{2,1,0:T(8,128)(2,1)S(1)} collective-permute-done((bf16[64,16,128]{2,1,0:T(8,128)(2,1)S(1)}, bf16[64,16,128]{2,1,0:T(8,128)(2,1)S(1)}, u32[]{:S(2)}, u32[]{:S(2)}) %collective-permute-start.4) | collective-permute-done | bytes 262176 | tf_op jit(solution)/shard_map/ppermute | solution.py:426
  28.7 1.8 %collective-permute-start.6 = (bf16[64,16,128]{2,1,0:T(8,128)(2,1)S(1)}, bf16[64,16,128]{2,1,0:T(8,128)(2,1)S(1)}, u32[]{:S(2)}, u32[]{:S(2)}) collective-permute-start(bf16[64,16,128]{2,1,0:T(8,128)(2,1)S(1)} %collective-permute-done.4.refs_4_), channel_id=1, source_target_pairs={{0,2},{1,7},{2,4},{3,1},{4,6},{5,3},{6,0},{7,5},{8,10},{9,15},{10,... | collective-permute-start | bytes 786440 | tf_op jit(solution)/shard_map/ppermute | solution.py:440
  30.5 1.7 %collective-permute-done.7.refs_4_ = bf16[64,16,128]{2,1,0:T(8,128)(2,1)S(1)} collective-permute-done((bf16[64,16,128]{2,1,0:T(8,128)(2,1)S(1)}, bf16[64,16,128]{2,1,0:T(8,128)(2,1)S(1)}, u32[]{:S(2)}, u32[]{:S(2)}) %collective-permute-start.7) | collective-permute-done | bytes 262176 | tf_op jit(solution)/shard_map/ppermute | solution.py:440
  32.2 1.3 %outer.2.refs_0_ = bf16[8,128,128]{2,1,0:T(8,128)(2,1)S(1)} custom-call(bf16[3,32,16,128]{3,2,1,0:T(8,128)(2,1)S(1)} %get-tuple-element.33.refs_0_, bf16[3,32,16,128]{3,2,1,0:T(8,128)(2,1)S(1)} %get-tuple-element.40.refs_1_, bf16[3,32,256,128]{3,2,1,0:T(8,128)(2,1)S(1)} %get-tuple-element.41.refs_2_, ...), custom_call_target="tpu_custom_call" | custom-call | bytes 3145728 | tf_op jit(solution)/shard_map/outer/pallas_call | solution.py:448
  33.4 0.0 copy-start
  33.5 0.0 copy-start.2
  33.5 1.4 %collective-permute-start.12 = (bf16[8,128,128]{2,1,0:T(8,128)(2,1)S(1)}, bf16[8,128,128]{2,1,0:T(8,128)(2,1)S(1)}, u32[]{:S(2)}, u32[]{:S(2)}) collective-permute-start(bf16[8,128,128]{2,1,0:T(8,128)(2,1)S(1)} %outer.2.refs_0_), channel_id=1, source_target_pairs={{0,16},{8,24},{16,0},{24,8},{1,17},{9,25},{17,1},{25,9},{2,18},{10... | collective-permute-start | bytes 786440 | tf_op jit(solution)/shard_map/ppermute | solution.py:462
  34.9 0.0 collective-permute-start.10
  34.9 2.9 %collective-permute-done.6.refs_5_ = bf16[64,16,128]{2,1,0:T(8,128)(2,1)S(1)} collective-permute-done((bf16[64,16,128]{2,1,0:T(8,128)(2,1)S(1)}, bf16[64,16,128]{2,1,0:T(8,128)(2,1)S(1)}, u32[]{:S(2)}, u32[]{:S(2)}) %collective-permute-start.6) | collective-permute-done | bytes 262176 | tf_op jit(solution)/shard_map/ppermute | solution.py:440
  37.9 2.3 %outer.3.refs_2_ = bf16[8,128,128]{2,1,0:T(8,128)(2,1)S(1)} custom-call(bf16[3,32,16,128]{3,2,1,0:T(8,128)(2,1)S(1)} %get-tuple-element.33.refs_0_, bf16[3,32,16,128]{3,2,1,0:T(8,128)(2,1)S(1)} %get-tuple-element.40.refs_1_, bf16[3,32,256,128]{3,2,1,0:T(8,128)(2,1)S(1)} %get-tuple-element.41.refs_2_, ...), custom_call_target="tpu_custom_call" | custom-call | bytes 3145728 | tf_op jit(solution)/shard_map/outer/pallas_call | solution.py:448
  40.2 1.6 %collective-permute-start.9 = (bf16[8,128,128]{2,1,0:T(8,128)(2,1)S(1)}, bf16[8,128,128]{2,1,0:T(8,128)(2,1)S(1)}, u32[]{:S(2)}, u32[]{:S(2)}) collective-permute-start(bf16[8,128,128]{2,1,0:T(8,128)(2,1)S(1)} %outer.3.refs_2_), channel_id=1, source_target_pairs={{0,16},{8,24},{16,0},{24,8},{1,17},{9,25},{17,1},{25,9},{2,18},{10... | collective-permute-start | bytes 786440 | tf_op jit(solution)/shard_map/ppermute | solution.py:462
  41.8 0.0 collective-permute-start.8
  41.8 0.0 collective-permute-done.12.refs_0_
  41.8 0.5 %collective-permute-start.13 = (bf16[8,128,128]{2,1,0:T(8,128)(2,1)S(1)}, bf16[8,128,128]{2,1,0:T(8,128)(2,1)S(1)}, u32[]{:S(2)}, u32[]{:S(2)}) collective-permute-start(bf16[8,128,128]{2,1,0:T(8,128)(2,1)S(1)} %collective-permute-done.12.refs_0_), channel_id=1, source_target_pairs={{0,8},{8,0},{16,24},{24,16},{1,9},{9,1},{17,25},{25,17},{2,10},{10... | collective-permute-start | bytes 786440 | tf_op jit(solution)/shard_map/ppermute | solution.py:476
  42.3 0.0 collective-permute-done.10.refs_1_
  42.3 0.6 %lead.1 = (f32[4,128,256]{2,1,0:T(8,128)S(1)}, f32[4,128,256]{2,1,0:T(8,128)S(1)}) custom-call(bf16[2,128,512]{2,1,0:T(8,128)(2,1)S(1)} %get-tuple-element.32.table_ref, bf16[8,128,128]{2,1,0:T(8,128)(2,1)S(1)} %outer.2.refs_0_, bf16[8,128,128]{2,1,0:T(8,128)(2,1)S(1)} %collective-permute-done.10.refs_1_, bf16[8,128,128]{2,1,0:T(8,128)(2,1)S(1)} %outer.3.refs_2_), custom_call_target="tpu_custom_call" | custom-call | flops 536870912 | bytes 4194304 | tf_op jit(solution)/shard_map/lead/pallas_call | solution.py:465
  42.8 3.8 %collective-permute-done.9.refs_1_ = bf16[8,128,128]{2,1,0:T(8,128)(2,1)S(1)} collective-permute-done((bf16[8,128,128]{2,1,0:T(8,128)(2,1)S(1)}, bf16[8,128,128]{2,1,0:T(8,128)(2,1)S(1)}, u32[]{:S(2)}, u32[]{:S(2)}) %collective-permute-start.9) | collective-permute-done | bytes 262176 | tf_op jit(solution)/shard_map/ppermute | solution.py:462
  46.7 0.0 collective-permute-start.11
  46.7 0.0 collective-permute-done.13.refs_1_
  46.7 0.0 copy-done
  46.7 0.0 copy-done.2
  46.7 1.3 %back.2.refs_4_ = f32[128,16,128]{2,1,0:T(8,128)} custom-call(bf16[2,128,512]{2,1,0:T(8,128)(2,1)S(1)} %get-tuple-element.32.table_ref, f32[2048,128]{1,0:T(8,128)S(1)} %bitcast.12, f32[128,128]{1,0:T(8,128)S(1)} %bitcast.14, bf16[8,128,128]{2,1,0:T(8,128)(2,1)S(1)} %collective-permute-done.12.refs_0_, ...), custom_call_target="tpu_custom_call" | custom-call | flops 536870912 | bytes 4194304 | tf_op jit(solution)/shard_map/back/pallas_call | solution.py:488
  48.0 0.0 collective-permute-done.8.refs_0_
  48.0 0.2 collective-permute-done.11.refs_2_
  48.2 1.5 %back.3 = f32[128,16,128]{2,1,0:T(8,128)} custom-call(bf16[2,128,512]{2,1,0:T(8,128)(2,1)S(1)} %get-tuple-element.32.table_ref, f32[2048,128]{1,0:T(8,128)S(1)} %bitcast.13, f32[128,128]{1,0:T(8,128)S(1)} %bitcast.15, bf16[8,128,128]{2,1,0:T(8,128)(2,1)S(1)} %collective-permute-done.8.refs_0_, ...), custom_call_target="tpu_custom_call", output_to_operand_aliasing={{}: (7, {})} | custom-call | flops 536870912 | bytes 4194304 | tf_op jit(solution)/shard_map/back/pallas_call | solution.py:488
Async XLA Ops:
  1.6 3.8 %collective-permute-start = (s16[16,128,128]{2,1,0:T(8,128)(2,1)S(1)}, s16[16,128,128]{2,1,0:T(8,128)(2,1)S(1)}, u32[]{:S(2)}, u32[]{:S(2)}) collective-permute-start(s16[16,128,128]{2,1,0:T(8,128)(2,1)S(1)} %get-tuple-element.31.own_ref), channel_id=1, source_target_pairs={{0,8},{8,0},{16,24},{24,16},{1,9},{9,1},{17,25},{25,17},{2,10},{10... | collective-permute-start | bytes 1572872 | tf_op jit(solution)/shard_map/ppermute | solution.py:341
  2.1 9.5 %collective-permute-start.1 = (s16[8,128,128]{2,1,0:T(8,128)(2,1)S(1)}, s16[8,128,128]{2,1,0:T(8,128)(2,1)S(1)}, u32[]{:S(2)}, u32[]{:S(2)}) collective-permute-start(s16[8,128,128]{2,1,0:T(8,128)(2,1)S(1)} %get-tuple-element.36), channel_id=1, source_target_pairs={{0,16},{8,24},{16,0},{24,8},{1,17},{9,25},{17,1},{25,9},{2,18},{10... | collective-permute-start | bytes 786440 | tf_op jit(solution)/shard_map/ppermute | solution.py:403
  5.3 1.6 %copy-start.1 = (bf16[4,2,2,128,512]{4,3,2,1,0:T(8,128)(2,1)S(1)}, bf16[4,2,2,128,512]{4,3,2,1,0:T(8,128)(2,1)}, u32[]{:S(2)}) copy-start(bf16[4,2,2,128,512]{4,3,2,1,0:T(8,128)(2,1)} %constant.2.clone.tables_ref) | copy-start | bytes 6291460
  6.9 0.7 %copy-start.3 = (s32[64,1]{0,1:T(1,128)S(1)}, s32[64,1]{0,1:T(1,128)}, u32[]{:S(2)}) copy-start(s32[64,1]{0,1:T(1,128)} %param.10) | copy-start | bytes 772
  7.6 8.3 %copy-start.4 = (s32[64,1]{0,1:T(1,128)S(1)}, s32[64,1]{0,1:T(1,128)}, u32[]{:S(2)}) copy-start(s32[64,1]{0,1:T(1,128)} %param.10) | copy-start | bytes 772
  11.5 1.8 %collective-permute-start.2 = (s16[8,128,128]{2,1,0:T(8,128)(2,1)S(1)}, s16[8,128,128]{2,1,0:T(8,128)(2,1)S(1)}, u32[]{:S(2)}, u32[]{:S(2)}) collective-permute-start(s16[8,128,128]{2,1,0:T(8,128)(2,1)S(1)} %collective-permute-done.1.refs_1_), channel_id=1, source_target_pairs={{0,8},{8,0},{16,24},{24,16},{1,9},{9,1},{17,25},{25,17},{2,10},{10... | collective-permute-start | bytes 786440 | tf_op jit(solution)/shard_map/ppermute | solution.py:405
  11.5 8.7 %collective-permute-start.3 = (s16[8,128,128]{2,1,0:T(8,128)(2,1)S(1)}, s16[8,128,128]{2,1,0:T(8,128)(2,1)S(1)}, u32[]{:S(2)}, u32[]{:S(2)}) collective-permute-start(s16[8,128,128]{2,1,0:T(8,128)(2,1)S(1)} %get-tuple-element.44), channel_id=1, source_target_pairs={{0,16},{8,24},{16,0},{24,8},{1,17},{9,25},{17,1},{25,9},{2,18},{10... | collective-permute-start | bytes 786440 | tf_op jit(solution)/shard_map/ppermute | solution.py:390
  14.2 8.5 %collective-permute-start.5 = (bf16[64,16,128]{2,1,0:T(8,128)(2,1)S(1)}, bf16[64,16,128]{2,1,0:T(8,128)(2,1)S(1)}, u32[]{:S(2)}, u32[]{:S(2)}) collective-permute-start(bf16[64,16,128]{2,1,0:T(8,128)(2,1)S(1)} %forward.1.refs_4_), channel_id=1, source_target_pairs={{0,1},{1,0},{2,3},{3,2},{4,5},{5,4},{6,7},{7,6},{8,9},{9,8},{10,11... | collective-permute-start | bytes 786440 | tf_op jit(solution)/shard_map/ppermute | solution.py:426
  20.7 8.0 %collective-permute-start.4 = (bf16[64,16,128]{2,1,0:T(8,128)(2,1)S(1)}, bf16[64,16,128]{2,1,0:T(8,128)(2,1)S(1)}, u32[]{:S(2)}, u32[]{:S(2)}) collective-permute-start(bf16[64,16,128]{2,1,0:T(8,128)(2,1)S(1)} %finish.1.refs_5_), channel_id=1, source_target_pairs={{0,1},{1,0},{2,3},{3,2},{4,5},{5,4},{6,7},{7,6},{8,9},{9,8},{10,11... | collective-permute-start | bytes 786440 | tf_op jit(solution)/shard_map/ppermute | solution.py:426
  22.8 9.4 %collective-permute-start.7 = (bf16[64,16,128]{2,1,0:T(8,128)(2,1)S(1)}, bf16[64,16,128]{2,1,0:T(8,128)(2,1)S(1)}, u32[]{:S(2)}, u32[]{:S(2)}) collective-permute-start(bf16[64,16,128]{2,1,0:T(8,128)(2,1)S(1)} %collective-permute-done.5.refs_6_), channel_id=1, source_target_pairs={{0,2},{1,7},{2,4},{3,1},{4,6},{5,3},{6,0},{7,5},{8,10},{9,15},{10,... | collective-permute-start | bytes 786440 | tf_op jit(solution)/shard_map/ppermute | solution.py:440
  28.7 9.1 %collective-permute-start.6 = (bf16[64,16,128]{2,1,0:T(8,128)(2,1)S(1)}, bf16[64,16,128]{2,1,0:T(8,128)(2,1)S(1)}, u32[]{:S(2)}, u32[]{:S(2)}) collective-permute-start(bf16[64,16,128]{2,1,0:T(8,128)(2,1)S(1)} %collective-permute-done.4.refs_4_), channel_id=1, source_target_pairs={{0,2},{1,7},{2,4},{3,1},{4,6},{5,3},{6,0},{7,5},{8,10},{9,15},{10,... | collective-permute-start | bytes 786440 | tf_op jit(solution)/shard_map/ppermute | solution.py:440
  33.4 13.2 %copy-start = (f32[2,64,16,128]{3,2,1,0:T(8,128)S(1)}, f32[2,64,16,128]{3,2,1,0:T(8,128)}, u32[]{:S(2)}) copy-start(f32[2,64,16,128]{3,2,1,0:T(8,128)} %param.6) | copy-start | bytes 3145732
  33.5 13.2 %copy-start.2 = (f32[2,64,128]{2,1,0:T(8,128)S(1)}, f32[2,64,128]{2,1,0:T(8,128)}, u32[]{:S(2)}) copy-start(f32[2,64,128]{2,1,0:T(8,128)} %param.7) | copy-start | bytes 196612
  33.5 8.3 %collective-permute-start.12 = (bf16[8,128,128]{2,1,0:T(8,128)(2,1)S(1)}, bf16[8,128,128]{2,1,0:T(8,128)(2,1)S(1)}, u32[]{:S(2)}, u32[]{:S(2)}) collective-permute-start(bf16[8,128,128]{2,1,0:T(8,128)(2,1)S(1)} %outer.2.refs_0_), channel_id=1, source_target_pairs={{0,16},{8,24},{16,0},{24,8},{1,17},{9,25},{17,1},{25,9},{2,18},{10... | collective-permute-start | bytes 786440 | tf_op jit(solution)/shard_map/ppermute | solution.py:462
  34.9 7.4 %collective-permute-start.10 = (bf16[8,128,128]{2,1,0:T(8,128)(2,1)S(1)}, bf16[8,128,128]{2,1,0:T(8,128)(2,1)S(1)}, u32[]{:S(2)}, u32[]{:S(2)}) collective-permute-start(bf16[8,128,128]{2,1,0:T(8,128)(2,1)S(1)} %outer.2.refs_0_), channel_id=1, source_target_pairs={{0,8},{8,0},{16,24},{24,16},{1,9},{9,1},{17,25},{25,17},{2,10},{10... | collective-permute-start | bytes 786440 | tf_op jit(solution)/shard_map/ppermute | solution.py:461
  40.2 6.5 %collective-permute-start.9 = (bf16[8,128,128]{2,1,0:T(8,128)(2,1)S(1)}, bf16[8,128,128]{2,1,0:T(8,128)(2,1)S(1)}, u32[]{:S(2)}, u32[]{:S(2)}) collective-permute-start(bf16[8,128,128]{2,1,0:T(8,128)(2,1)S(1)} %outer.3.refs_2_), channel_id=1, source_target_pairs={{0,16},{8,24},{16,0},{24,8},{1,17},{9,25},{17,1},{25,9},{2,18},{10... | collective-permute-start | bytes 786440 | tf_op jit(solution)/shard_map/ppermute | solution.py:462
  41.8 6.3 %collective-permute-start.8 = (bf16[8,128,128]{2,1,0:T(8,128)(2,1)S(1)}, bf16[8,128,128]{2,1,0:T(8,128)(2,1)S(1)}, u32[]{:S(2)}, u32[]{:S(2)}) collective-permute-start(bf16[8,128,128]{2,1,0:T(8,128)(2,1)S(1)} %outer.3.refs_2_), channel_id=1, source_target_pairs={{0,8},{8,0},{16,24},{24,16},{1,9},{9,1},{17,25},{25,17},{2,10},{10... | collective-permute-start | bytes 786440 | tf_op jit(solution)/shard_map/ppermute | solution.py:461
  41.8 4.9 %collective-permute-start.13 = (bf16[8,128,128]{2,1,0:T(8,128)(2,1)S(1)}, bf16[8,128,128]{2,1,0:T(8,128)(2,1)S(1)}, u32[]{:S(2)}, u32[]{:S(2)}) collective-permute-start(bf16[8,128,128]{2,1,0:T(8,128)(2,1)S(1)} %collective-permute-done.12.refs_0_), channel_id=1, source_target_pairs={{0,8},{8,0},{16,24},{24,16},{1,9},{9,1},{17,25},{25,17},{2,10},{10... | collective-permute-start | bytes 786440 | tf_op jit(solution)/shard_map/ppermute | solution.py:476
  46.7 1.5 %collective-permute-start.11 = (bf16[8,128,128]{2,1,0:T(8,128)(2,1)S(1)}, bf16[8,128,128]{2,1,0:T(8,128)(2,1)S(1)}, u32[]{:S(2)}, u32[]{:S(2)}) collective-permute-start(bf16[8,128,128]{2,1,0:T(8,128)(2,1)S(1)} %collective-permute-done.9.refs_1_), channel_id=1, source_target_pairs={{0,8},{8,0},{16,24},{24,16},{1,9},{9,1},{17,25},{25,17},{2,10},{10... | collective-permute-start | bytes 786440 | tf_op jit(solution)/shard_map/ppermute | solution.py:476
